TPU v7x, 32 devices: a whole 2x2x4 slice. The times are simulated.
32 devices in a mesh: view: 4 (over x, core), vol: 8 (over z, y).
Axes of the slice: x: 2, y: 2, z: 4, core: 2. Of those that a mesh axis runs over, the one named last changes fastest.
Arguments:
- raw_views: bfloat16 [12, 256, 64, 128], P('view', 'vol'), may hold values from 0.18 to 5.41, as said below
- weights: float32 [12, 64, 8], P('view'), may hold values from 0.05 to 1
- offsets: int32 [12, 64], P('view'), may hold values from 0 to 56, as said below
- psf_taps: float32 [12, 3, 9], P('view'), may hold values from 0.01 to 1
Outputs:
- joined_volume: float32 [256, 64, 128], P(None, 'vol')
Inputs may be any that keep to these rules, and one draw needn't show every extreme that they name: offsets[v, x] - x + 4 lies in -3 to 4 except where clipped to 0 or 56. `raw_views`: positive intensities.
All inputs are finite; a program needn't handle non-finite values.
Results may differ from a plain program's by a relative error of at most 0.0003.
The roundings to bfloat16 on the way count: a program that leaves them out, or rounds other values in their place, can miss the bound.
Values may be sent and summed in bfloat16 or wider, within the bound.
No kernel may reach another device: no remote copies, remote signals or barrier semaphores. Data moves between devices by JAX's collectives and lax.ppermute only.
A program may use at most 64 MiB of HBM per device.

v0:
```python
import jax
import jax.numpy as jnp
from jax import lax
from jax.sharding import PartitionSpec as P

ITERS = 2


def extended_2(shard, sides, width):
    for axis, dim in sides:
        devices, length = (lax.axis_size(axis), shard.shape[dim])
        up = [(i, (i + 1) % devices) for i in range(devices - 1)]
        down = [(j, i) for i, j in up]
        last = lax.slice_in_dim(shard, length - width, length, axis=dim)
        first = lax.slice_in_dim(shard, 0, width, axis=dim)
        before = lax.ppermute(last, axis, up)
        after = lax.ppermute(first, axis, down)
        shard = jnp.concatenate([before, shard, after], axis=dim)
    return shard


def pad_axis(field, axis, width):
    widths = [(0, 0)] * field.ndim
    widths[axis] = (width, width)
    return jnp.pad(field, widths)


def correlate(extended, taps, axis, length):
    result = taps[0] * lax.slice_in_dim(extended, 0, length, axis=axis)
    for offset in range(1, taps.shape[0]):
        result = result + taps[offset] * lax.slice_in_dim(
            extended, offset, offset + length, axis=axis
        )
    return result


def blur_forward(extended, taps, length):
    rim_width = (taps.shape[1] - 1) // 2
    along_x = correlate(extended, taps[1], 1, length)
    along_z = correlate(pad_axis(along_x, 0, rim_width), taps[0], 0, along_x.shape[0])
    return correlate(pad_axis(along_z, 2, rim_width), taps[2], 2, along_z.shape[2])


def blur_back_yz(field, taps):
    rim_width = (taps.shape[1] - 1) // 2
    along_y = correlate(pad_axis(field, 2, rim_width), taps[2][::-1], 2, field.shape[2])
    return correlate(pad_axis(along_y, 0, rim_width), taps[0][::-1], 0, field.shape[0])


def resample_view(planes, weight_rows, first_rows):
    result = jnp.zeros((planes.shape[0], first_rows.shape[0], planes.shape[2]), jnp.float32)
    for offset in range(weight_rows.shape[1]):
        gathered = jnp.take(planes, first_rows + offset, axis=1).astype(jnp.float32)
        result = result + weight_rows[None, :, offset, None] * gathered
    return result.astype(jnp.bfloat16)


def update_estimate(joined_volume, logs, total_views):
    summed = lax.psum(logs, "view")
    return joined_volume * jnp.exp(summed / total_views)


def per_device(raw_views, weights, offsets, psf_taps):
    count = raw_views.shape[0]
    total_views = count * lax.axis_size("view")
    rim_width = (psf_taps.shape[2] - 1) // 2
    weight_norm = weights / jnp.sum(weights, axis=-1, keepdims=True)
    taps_norm = psf_taps / jnp.sum(psf_taps, axis=-1, keepdims=True)
    local_views = jnp.stack(
        [
            resample_view(raw_views[index], weight_norm[index], offsets[index])
            for index in range(count)
        ]
    )
    bricks = lax.all_to_all(local_views, "vol", split_axis=2, concat_axis=1, tiled=True)
    width = bricks.shape[2]
    local_sum = bricks[0].astype(jnp.float32)
    for index in range(1, count):
        local_sum = local_sum + bricks[index].astype(jnp.float32)
    joined_volume = lax.psum(local_sum, "view") / total_views
    for turn in range(ITERS):
        extended = extended_2(joined_volume, (("vol", 1),), rim_width)
        partials = []
        for index in range(count):
            blurred = blur_forward(extended, taps_norm[index], width)
            ratio = bricks[index].astype(jnp.float32) / blurred
            partials.append(blur_back_yz(ratio, taps_norm[index]))
        ratio_wide = extended_2(jnp.stack(partials), (("vol", 2),), rim_width)
        logs = jnp.zeros(joined_volume.shape, jnp.float32)
        for index in range(count):
            back = correlate(ratio_wide[index], taps_norm[index, 1][::-1], 1, width)
            logs = logs + jnp.log(back)
        joined_volume = update_estimate(joined_volume, logs, total_views)
    return joined_volume


def solution(mesh):
    placed = (
        P("view", "vol", None, None),
        P("view", None, None),
        P("view", None),
        P("view", None, None),
    )
    return jax.shard_map(
        per_device, mesh=mesh, in_specs=placed, out_specs=P(None, "vol", None), check_vma=False
    )
```

profile of v0, /device:TPU:0, one launch (start us, length us, event | category | flops | bytes accessed | tf_op | source)
XLA Modules:
  0.0 709.0 jit_solution(3959235660179055947)
XLA Ops:
  10.4 2.4 fusion.333
  15.9 1.4 gather_fusion.3
  20.2 1.4 gather_fusion
  21.6 1.9 copy_bitcast_fusion
  29.1 1.4 gather_fusion.19
  30.6 1.4 gather_fusion.18
  33.4 1.4 gather_fusion.16
  34.9 1.4 gather_fusion.15
  39.2 1.5 gather_fusion.12
  40.6 1.5 gather_fusion.11
  45.0 1.4 gather_fusion.8
  46.5 3.6 fusion.328
  50.3 1.8 fusion.330
  52.3 1.7 fusion.329
  54.5 44.1 %all_to_all.15 = bf16[3,32,64,128]{3,1,0,2:T(8,128)(2,1)S(1)} all-to-all(bf16[3,32,64,128]{3,1,0,2:T(8,128)(2,1)S(1)} %copy.15), channel_id=1, replica_groups=mesh['view'=4,'vol'=8] {'vol'}, dimensions={2} | all-to-all | bytes 3145728 | tf_op jit(solution)/shard_map/all_to_all | solution.py:75
  103.3 35.0 %all-reduce.28.cloned.1.call-done = f32[256,8,128]{2,1,0:T(8,128)} async-done(((f32[256,8,128]{2,1,0:T(8,128)}), f32[256,8,128]{2,1,0:T(8,128)}) %all-reduce.28.cloned.1.call-update) | async-done | bytes 1048592 | tf_op jit(solution)/shard_map/psum | solution.py:80
  142.2 5.5 collective-permute-start
  153.1 3.5 collective-permute-done.1
  156.6 10.9 %collective-permute-done = f32[256,4,128]{2,1,0:T(4,128)} collective-permute-done((f32[256,4,128]{2,1,0:T(4,128)}, f32[256,4,128]{2,1,0:T(4,128)}, u32[]{:S(2)}, u32[]{:S(2)}) %collective-permute-start) | collective-permute-done | bytes 524320 | tf_op jit(solution)/shard_map/ppermute | solution.py:16
  167.4 9.6 %multiply_add_fusion.11 = f32[256,8,128]{2,1,0:T(8,128)S(1)} fusion(f32[256,8,128]{2,1,0:T(8,128)S(1)} %copy-done.1, f32[]{:T(128)} %bitcast.78, f32[]{:T(128)} %bitcast.77, f32[]{:T(128)} %bitcast.76, f32[]{:T(128)S(6)} %mul.1801, f32[]{:T(128)} %bitcast.74, f32[]{:T(128)} %bitcast.73, f32[]{:T(128)} %bitcast.72, f32[]{:T(128)} %bitcast.71, f32[]{:T(128)} %bitcast.66, ...), kind=kLoop, calls=%fused_computation.598 | loop fusion | flops 6553600 | bytes 4194340 | tf_op jit(solution)/shard_map/add | solution.py:31
  177.1 6.1 multiply_add_fusion.10
  183.2 8.0 %fusion.21 = f32[256,8,128]{2,1,0:T(8,128)S(1)} fusion(f32[256,8,128]{2,1,0:T(8,128)S(1)} %multiply_add_fusion.10, f32[1,8,32,8,128]{4,3,2,1,0:T(8,128)S(1)} %copy-done.8, f32[]{:T(128)} %bitcast.92, f32[]{:T(128)} %bitcast.91, f32[]{:T(128)} %bitcast.90, f32[]{:T(128)} %bitcast.89, f32[]{:T(128)} %bitcast.88, f32[]{:T(128)} %bitcast.87, f32[]{:T(128)} %bitcast.86, ...), kind=kLoop, calls=%fused_computation.176 | loop fusion | flops 4718592 | bytes 3145764 | tf_op jit(solution)/shard_map/div | solution.py:86
  191.3 8.0 %fusion.37 = f32[256,8,128]{2,1,0:T(8,128)S(1)} fusion(f32[256,8,128]{2,1,0:T(8,128)S(1)} %fusion.21, f32[]{:T(128)} %bitcast.92, f32[]{:T(128)} %bitcast.91, f32[]{:T(128)} %bitcast.90, f32[]{:T(128)} %bitcast.89, f32[]{:T(128)} %bitcast.88, f32[]{:T(128)} %bitcast.87, f32[]{:T(128)} %bitcast.86, f32[]{:T(128)} %bitcast.69, f32[]{:T(128)} %bitcast.68), kind=kLoop, calls=%fused_computation.192 | loop fusion | flops 4456448 | bytes 2097188 | tf_op jit(solution)/shard_map/add | solution.py:31
  199.2 6.1 add_bitcast_fusion.5
  205.3 9.7 %multiply_add_fusion.9 = f32[256,8,128]{2,1,0:T(8,128)S(1)} fusion(f32[256,8,128]{2,1,0:T(8,128)S(1)} %copy-done.1, f32[]{:T(128)} %bitcast.106, f32[]{:T(128)} %bitcast.105, f32[]{:T(128)} %bitcast.104, f32[]{:T(128)} %bitcast.103, f32[]{:T(128)S(6)} %mul.1873, f32[]{:T(128)} %bitcast.101, f32[]{:T(128)} %bitcast.100, f32[]{:T(128)} %bitcast.99, ...), kind=kLoop, calls=%fused_computation.579 | loop fusion | flops 6553600 | bytes 4194340 | tf_op jit(solution)/shard_map/add | solution.py:31
  215.1 6.3 multiply_add_fusion.8
  221.3 7.9 %fusion.54 = f32[256,8,128]{2,1,0:T(8,128)S(1)} fusion(f32[256,8,128]{2,1,0:T(8,128)S(1)} %multiply_add_fusion.8, f32[1,8,32,8,128]{4,3,2,1,0:T(8,128)S(1)} %copy-done.5, f32[]{:T(128)} %bitcast.120, f32[]{:T(128)} %bitcast.119, f32[]{:T(128)} %bitcast.118, f32[]{:T(128)} %bitcast.117, f32[]{:T(128)} %bitcast.116, f32[]{:T(128)} %bitcast.115, f32[]{:T(128)} %bitcast.114, ...), kind=kLoop, calls=%fused_computation.209 | loop fusion | flops 4718592 | bytes 3145764 | tf_op jit(solution)/shard_map/div | solution.py:86
  229.2 7.9 %fusion.70 = f32[256,8,128]{2,1,0:T(8,128)S(1)} fusion(f32[256,8,128]{2,1,0:T(8,128)S(1)} %fusion.54, f32[]{:T(128)} %bitcast.120, f32[]{:T(128)} %bitcast.119, f32[]{:T(128)} %bitcast.118, f32[]{:T(128)} %bitcast.117, f32[]{:T(128)} %bitcast.116, f32[]{:T(128)} %bitcast.115, f32[]{:T(128)} %bitcast.114, f32[]{:T(128)} %bitcast.96, f32[]{:T(128)} %bitcast.95), kind=kLoop, calls=%fused_computation.225 | loop fusion | flops 4456448 | bytes 2097188 | tf_op jit(solution)/shard_map/add | solution.py:31
  237.1 6.2 add_bitcast_fusion.4
  243.3 10.1 %multiply_add_fusion.7 = f32[256,8,128]{2,1,0:T(8,128)S(1)} fusion(f32[256,8,128]{2,1,0:T(8,128)S(1)} %copy-done.1, f32[]{:T(128)} %bitcast.134, f32[]{:T(128)} %bitcast.133, f32[]{:T(128)} %bitcast.132, f32[]{:T(128)} %bitcast.131, f32[]{:T(128)S(6)} %mul.1946, f32[]{:T(128)} %bitcast.129, f32[]{:T(128)} %bitcast.128, f32[]{:T(128)} %bitcast.127, ...), kind=kLoop, calls=%fused_computation.560 | loop fusion | flops 6553600 | bytes 4194340 | tf_op jit(solution)/shard_map/add | solution.py:31
  253.4 5.9 multiply_add_fusion.6
  259.3 7.9 %fusion.87 = f32[256,8,128]{2,1,0:T(8,128)S(1)} fusion(f32[256,8,128]{2,1,0:T(8,128)S(1)} %multiply_add_fusion.6, f32[1,8,32,8,128]{4,3,2,1,0:T(8,128)S(1)} %copy.18, f32[]{:T(128)} %bitcast.148, f32[]{:T(128)} %bitcast.147, f32[]{:T(128)} %bitcast.146, f32[]{:T(128)} %bitcast.145, f32[]{:T(128)} %bitcast.144, f32[]{:T(128)} %bitcast.143, f32[]{:T(128)} %bitcast.142, ...), kind=kLoop, calls=%fused_computation.242 | loop fusion | flops 4718592 | bytes 3145764 | tf_op jit(solution)/shard_map/div | solution.py:86
  267.2 7.9 %fusion.103 = f32[256,8,128]{2,1,0:T(8,128)S(1)} fusion(f32[256,8,128]{2,1,0:T(8,128)S(1)} %fusion.87, f32[]{:T(128)} %bitcast.148, f32[]{:T(128)} %bitcast.147, f32[]{:T(128)} %bitcast.146, f32[]{:T(128)} %bitcast.145, f32[]{:T(128)} %bitcast.144, f32[]{:T(128)} %bitcast.143, f32[]{:T(128)} %bitcast.142, f32[]{:T(128)} %bitcast.124, f32[]{:T(128)} %bitcast.123), kind=kLoop, calls=%fused_computation.258 | loop fusion | flops 4456448 | bytes 2097188 | tf_op jit(solution)/shard_map/add | solution.py:31
  275.0 5.9 add_bitcast_fusion.3
  281.6 4.5 collective-permute-start.2
  287.4 66.1 %collective-permute-done.2 = f32[3,256,4,128]{3,2,1,0:T(4,128)S(1)} collective-permute-done((f32[3,256,4,128]{3,2,1,0:T(4,128)S(1)}, f32[3,256,4,128]{3,2,1,0:T(4,128)S(1)}, u32[]{:S(2)}, u32[]{:S(2)}) %collective-permute-start.2) | collective-permute-done | bytes 1572896 | tf_op jit(solution)/shard_map/ppermute | solution.py:16
  355.0 1.8 slice_bitcast_fusion.5
  356.8 28.6 %fusion.241 = f32[256,8,128]{2,1,0:T(8,128)} fusion(f32[256,16,128]{2,1,0:T(8,128)S(1)} %get-tuple-element.52, f32[256,16,128]{2,1,0:T(8,128)} %get-tuple-element.53, f32[256,16,128]{2,1,0:T(8,128)S(1)} %get-tuple-element.51, f32[]{:T(128)} %bitcast.130, f32[]{:T(128)} %bitcast.102, f32[]{:T(128)} %bitcast.75, f32[]{:T(128)} %bitcast.134, f32[]{:T(128)} %bitcast.133, ...), kind=kLoop, calls=%fused_computation.426 | loop fusion | flops 13893632 | bytes 29360236 | tf_op jit(solution)/shard_map/add | solution.py:92
  385.5 37.0 %all-reduce.30.cloned.1.call-done = f32[256,8,128]{2,1,0:T(8,128)} async-done(((f32[256,8,128]{2,1,0:T(8,128)}), f32[256,8,128]{2,1,0:T(8,128)}) %all-reduce.30.cloned.1.call-update) | async-done | bytes 1048592 | tf_op jit(solution)/shard_map/psum | solution.py:59
  422.5 1.7 exponential_multiply_fusion.1
  425.7 4.7 collective-permute-start.4
  430.4 9.3 %collective-permute-done.5 = f32[256,4,128]{2,1,0:T(4,128)S(1)} collective-permute-done((f32[256,4,128]{2,1,0:T(4,128)S(1)}, f32[256,4,128]{2,1,0:T(4,128)S(1)}, u32[]{:S(2)}, u32[]{:S(2)}) %collective-permute-start.5) | collective-permute-done | bytes 524320 | tf_op jit(solution)/shard_map/ppermute | solution.py:17
  439.8 10.9 %collective-permute-done.4 = f32[256,4,128]{2,1,0:T(4,128)S(1)} collective-permute-done((f32[256,4,128]{2,1,0:T(4,128)S(1)}, f32[256,4,128]{2,1,0:T(4,128)S(1)}, u32[]{:S(2)}, u32[]{:S(2)}) %collective-permute-start.4) | collective-permute-done | bytes 524320 | tf_op jit(solution)/shard_map/ppermute | solution.py:16
  450.6 7.8 %multiply_add_fusion.5 = f32[256,8,128]{2,1,0:T(8,128)S(1)} fusion(f32[256,8,128]{2,1,0:T(8,128)S(1)} %exponential_multiply_fusion.1, f32[]{:T(128)} %bitcast.75, f32[]{:T(128)} %bitcast.78, f32[]{:T(128)} %bitcast.77, f32[]{:T(128)} %bitcast.76, f32[]{:T(128)} %bitcast.74, f32[]{:T(128)} %bitcast.73, f32[]{:T(128)} %bitcast.72, f32[]{:T(128)} %bitcast.71, ...), kind=kLoop, calls=%fused_computation.540 | loop fusion | flops 6553600 | bytes 3145764 | tf_op jit(solution)/shard_map/add | solution.py:31
  458.4 6.1 multiply_add_fusion.4
  464.5 8.0 %fusion.120 = f32[256,8,128]{2,1,0:T(8,128)S(1)} fusion(f32[256,8,128]{2,1,0:T(8,128)S(1)} %multiply_add_fusion.4, f32[1,8,32,8,128]{4,3,2,1,0:T(8,128)S(1)} %copy-done.9, f32[]{:T(128)} %bitcast.92, f32[]{:T(128)} %bitcast.91, f32[]{:T(128)} %bitcast.90, f32[]{:T(128)} %bitcast.89, f32[]{:T(128)} %bitcast.88, f32[]{:T(128)} %bitcast.87, f32[]{:T(128)} %bitcast.86, ...), kind=kLoop, calls=%fused_computation.275 | loop fusion | flops 4718592 | bytes 3145764 | tf_op jit(solution)/shard_map/div | solution.py:86
  472.5 8.0 %fusion.136 = f32[256,8,128]{2,1,0:T(8,128)S(1)} fusion(f32[256,8,128]{2,1,0:T(8,128)S(1)} %fusion.120, f32[]{:T(128)} %bitcast.92, f32[]{:T(128)} %bitcast.91, f32[]{:T(128)} %bitcast.90, f32[]{:T(128)} %bitcast.89, f32[]{:T(128)} %bitcast.88, f32[]{:T(128)} %bitcast.87, f32[]{:T(128)} %bitcast.86, f32[]{:T(128)} %bitcast.69, f32[]{:T(128)} %bitcast.68), kind=kLoop, calls=%fused_computation.291 | loop fusion | flops 4456448 | bytes 2097188 | tf_op jit(solution)/shard_map/add | solution.py:31
  480.5 6.1 add_bitcast_fusion.2
  486.6 7.7 %multiply_add_fusion.3 = f32[256,8,128]{2,1,0:T(8,128)S(1)} fusion(f32[256,8,128]{2,1,0:T(8,128)S(1)} %exponential_multiply_fusion.1, f32[]{:T(128)} %bitcast.102, f32[]{:T(128)} %bitcast.106, f32[]{:T(128)} %bitcast.105, f32[]{:T(128)} %bitcast.104, f32[]{:T(128)} %bitcast.103, f32[]{:T(128)} %bitcast.101, f32[]{:T(128)} %bitcast.100, f32[]{:T(128)} %bitcast.99, ...), kind=kLoop, calls=%fused_computation.521 | loop fusion | flops 6553600 | bytes 3145764 | tf_op jit(solution)/shard_map/add | solution.py:31
  494.3 6.2 multiply_add_fusion.2
  500.5 7.9 %fusion.153 = f32[256,8,128]{2,1,0:T(8,128)S(1)} fusion(f32[256,8,128]{2,1,0:T(8,128)S(1)} %multiply_add_fusion.2, f32[1,8,32,8,128]{4,3,2,1,0:T(8,128)S(1)} %copy-done.6, f32[]{:T(128)} %bitcast.120, f32[]{:T(128)} %bitcast.119, f32[]{:T(128)} %bitcast.118, f32[]{:T(128)} %bitcast.117, f32[]{:T(128)} %bitcast.116, f32[]{:T(128)} %bitcast.115, ...), kind=kLoop, calls=%fused_computation.308 | loop fusion | flops 4718592 | bytes 3145764 | tf_op jit(solution)/shard_map/div | solution.py:86
  508.4 7.9 %fusion.169 = f32[256,8,128]{2,1,0:T(8,128)S(1)} fusion(f32[256,8,128]{2,1,0:T(8,128)S(1)} %fusion.153, f32[]{:T(128)} %bitcast.120, f32[]{:T(128)} %bitcast.119, f32[]{:T(128)} %bitcast.118, f32[]{:T(128)} %bitcast.117, f32[]{:T(128)} %bitcast.116, f32[]{:T(128)} %bitcast.115, f32[]{:T(128)} %bitcast.114, f32[]{:T(128)} %bitcast.96, f32[]{:T(128)} %bitcast.95), kind=kLoop, calls=%fused_computation.324 | loop fusion | flops 4456448 | bytes 2097188 | tf_op jit(solution)/shard_map/add | solution.py:31
  516.3 6.2 add_bitcast_fusion.1
  522.5 8.0 %multiply_add_fusion.1 = f32[256,8,128]{2,1,0:T(8,128)S(1)} fusion(f32[256,8,128]{2,1,0:T(8,128)S(1)} %exponential_multiply_fusion.1, f32[]{:T(128)} %bitcast.130, f32[]{:T(128)} %bitcast.134, f32[]{:T(128)} %bitcast.133, f32[]{:T(128)} %bitcast.132, f32[]{:T(128)} %bitcast.131, f32[]{:T(128)} %bitcast.129, f32[]{:T(128)} %bitcast.128, f32[]{:T(128)} %bitcast.127, ...), kind=kLoop, calls=%fused_computation.502 | loop fusion | flops 6553600 | bytes 3145764 | tf_op jit(solution)/shard_map/add | solution.py:31
  530.5 5.9 multiply_add_fusion
  536.4 7.9 %fusion.186 = f32[256,8,128]{2,1,0:T(8,128)S(1)} fusion(f32[256,8,128]{2,1,0:T(8,128)S(1)} %multiply_add_fusion, f32[1,8,32,8,128]{4,3,2,1,0:T(8,128)S(1)} %copy-done.3, f32[]{:T(128)} %bitcast.148, f32[]{:T(128)} %bitcast.147, f32[]{:T(128)} %bitcast.146, f32[]{:T(128)} %bitcast.145, f32[]{:T(128)} %bitcast.144, f32[]{:T(128)} %bitcast.143, f32[]{:T(128)} %bitcast.142, ...), kind=kLoop, calls=%fused_computation.341 | loop fusion | flops 4718592 | bytes 3145764 | tf_op jit(solution)/shard_map/div | solution.py:86
  544.3 7.9 %fusion.202 = f32[256,8,128]{2,1,0:T(8,128)S(1)} fusion(f32[256,8,128]{2,1,0:T(8,128)S(1)} %fusion.186, f32[]{:T(128)} %bitcast.148, f32[]{:T(128)} %bitcast.147, f32[]{:T(128)} %bitcast.146, f32[]{:T(128)} %bitcast.145, f32[]{:T(128)} %bitcast.144, f32[]{:T(128)} %bitcast.143, f32[]{:T(128)} %bitcast.142, f32[]{:T(128)} %bitcast.124, f32[]{:T(128)} %bitcast.123), kind=kLoop, calls=%fused_computation.357 | loop fusion | flops 4456448 | bytes 2097188 | tf_op jit(solution)/shard_map/add | solution.py:31
  552.2 5.9 add_bitcast_fusion
  558.8 4.5 collective-permute-start.6
  564.6 66.1 %collective-permute-done.6 = f32[3,256,4,128]{3,2,1,0:T(4,128)S(1)} collective-permute-done((f32[3,256,4,128]{3,2,1,0:T(4,128)S(1)}, f32[3,256,4,128]{3,2,1,0:T(4,128)S(1)}, u32[]{:S(2)}, u32[]{:S(2)}) %collective-permute-start.6) | collective-permute-done | bytes 1572896 | tf_op jit(solution)/shard_map/ppermute | solution.py:16
  632.1 1.8 slice_bitcast_fusion.2
  633.9 28.7 %fusion.212 = f32[256,8,128]{2,1,0:T(8,128)} fusion(f32[256,16,128]{2,1,0:T(8,128)S(1)} %get-tuple-element.49, f32[256,16,128]{2,1,0:T(8,128)} %get-tuple-element.50, f32[256,16,128]{2,1,0:T(8,128)S(1)} %get-tuple-element.48, f32[]{:T(128)} %bitcast.130, f32[]{:T(128)} %bitcast.102, f32[]{:T(128)} %bitcast.75, f32[]{:T(128)} %bitcast.134, f32[]{:T(128)} %bitcast.133, ...), kind=kLoop, calls=%fused_computation.368 | loop fusion | flops 13893632 | bytes 29360236 | tf_op jit(solution)/shard_map/add | solution.py:92
  662.6 37.0 %all-reduce.32.cloned.1.call-done = f32[256,8,128]{2,1,0:T(8,128)} async-done(((f32[256,8,128]{2,1,0:T(8,128)}), f32[256,8,128]{2,1,0:T(8,128)}) %all-reduce.32.cloned.1.call-update) | async-done | bytes 1048592 | tf_op jit(solution)/shard_map/psum | solution.py:59
  699.6 2.7 exponential_multiply_fusion
  (128 shorter events, 43.6 us)
Async XLA Ops:
  6.5 131.8 %all-reduce.28.cloned.1.call-start = ((), (), s32[]{:S(2)}) async-start(), calls=%async_computation.1 | async-start | bytes 2097152 | tf_op jit(solution)/shard_map/psum | solution.py:80
  40.6 5.8 copy-start.10
  46.4 3.7 copy-start.11
  46.4 3.7 copy-start.12
  46.4 3.7 copy-start.13
  46.5 3.7 copy-start.14
  46.5 3.7 copy-start.15
  46.5 3.7 copy-start.17
  46.5 3.7 copy-start.19
  46.5 3.7 copy-start.22
  50.2 1.9 copy-start.16
  50.2 1.9 copy-start.18
  50.2 1.9 copy-start.20
  50.2 1.9 copy-start.21
  50.2 1.9 copy-start.23
  50.2 1.9 copy-start.24
  50.2 1.9 copy-start.25
  50.2 2.1 copy-start.26
  99.7 1.3 copy-start.7
  100.3 159.0 %copy-start.2 = (f32[1,8,32,8,128]{4,3,2,1,0:T(8,128)}, f32[1,8,32,8,128]{4,3,2,1,0:T(8,128)S(1)}, u32[]{:S(2)}) copy-start(f32[1,8,32,8,128]{4,3,2,1,0:T(8,128)S(1)} %copy.18) | copy-start | bytes 3145732
  100.9 1.0 copy-start.4
  101.9 1.3 copy-start.27
  103.1 319.4 %all-reduce.30.cloned.1.call-start = ((), (), s32[]{:S(2)}) async-start(), calls=%async_computation.2 | async-start | bytes 2097152 | tf_op jit(solution)/shard_map/psum | solution.py:59
  138.4 29.1 %copy-start.1 = (f32[256,8,128]{2,1,0:T(8,128)S(1)}, f32[256,8,128]{2,1,0:T(8,128)}, u32[]{:S(2)}) copy-start(f32[256,8,128]{2,1,0:T(8,128)} %all-reduce.28.cloned.1.call-done) | copy-start | bytes 3145732
  140.9 15.6 %collective-permute-start.1 = (f32[256,4,128]{2,1,0:T(4,128)}, f32[256,4,128]{2,1,0:T(4,128)}, u32[]{:S(2)}, u32[]{:S(2)}) collective-permute-start(f32[256,4,128]{2,1,0:T(4,128)} %get-tuple-element.66), channel_id=1, source_target_pairs={{1,0},{2,1},{3,2},{4,3},{5,4},{6,5},{7,6},{9,8},{10,9},{11,10},{12... | collective-permute-start | bytes 1572872 | tf_op jit(solution)/shard_map/ppermute | solution.py:17
  142.2 25.2 %collective-permute-start = (f32[256,4,128]{2,1,0:T(4,128)}, f32[256,4,128]{2,1,0:T(4,128)}, u32[]{:S(2)}, u32[]{:S(2)}) collective-permute-start(f32[256,4,128]{2,1,0:T(4,128)} %get-tuple-element.67), channel_id=1, source_target_pairs={{0,1},{1,2},{2,3},{3,4},{4,5},{5,6},{6,7},{8,9},{9,10},{10,11},{11... | collective-permute-start | bytes 1572872 | tf_op jit(solution)/shard_map/ppermute | solution.py:16
  177.1 6.2 copy-start.8
  215.0 6.3 copy-start.5
  281.6 71.9 %collective-permute-start.2 = (f32[3,256,4,128]{3,2,1,0:T(4,128)S(1)}, f32[3,256,4,128]{3,2,1,0:T(4,128)S(1)}, u32[]{:S(2)}, u32[]{:S(2)}) collective-permute-start(f32[3,256,4,128]{3,2,1,0:T(4,128)S(1)} %get-tuple-element.56), channel_id=1, source_target_pairs={{0,1},{1,2},{2,3},{3,4},{4,5},{5,6},{6,7},{8,9},{9,10},{10,11},{11... | collective-permute-start | bytes 4718600 | tf_op jit(solution)/shard_map/ppermute | solution.py:16
  286.1 67.4 %collective-permute-start.3 = (f32[3,256,4,128]{3,2,1,0:T(4,128)S(1)}, f32[3,256,4,128]{3,2,1,0:T(4,128)S(1)}, u32[]{:S(2)}, u32[]{:S(2)}) collective-permute-start(f32[3,256,4,128]{3,2,1,0:T(4,128)S(1)} %get-tuple-element.57), channel_id=1, source_target_pairs={{1,0},{2,1},{3,2},{4,3},{5,4},{6,5},{7,6},{9,8},{10,9},{11,10},{12... | collective-permute-start | bytes 4718600 | tf_op jit(solution)/shard_map/ppermute | solution.py:17
  385.4 314.1 %all-reduce.32.cloned.1.call-start = ((), (), s32[]{:S(2)}) async-start(), calls=%async_computation.3 | async-start | bytes 2097152 | tf_op jit(solution)/shard_map/psum | solution.py:59
  424.2 98.2 %copy-start = (f32[256,8,128]{2,1,0:T(8,128)}, f32[256,8,128]{2,1,0:T(8,128)S(1)}, u32[]{:S(2)}) copy-start(f32[256,8,128]{2,1,0:T(8,128)S(1)} %exponential_multiply_fusion.1) | copy-start | bytes 3145732
  424.4 15.3 %collective-permute-start.5 = (f32[256,4,128]{2,1,0:T(4,128)S(1)}, f32[256,4,128]{2,1,0:T(4,128)S(1)}, u32[]{:S(2)}, u32[]{:S(2)}) collective-permute-start(f32[256,4,128]{2,1,0:T(4,128)S(1)} %get-tuple-element.64), channel_id=1, source_target_pairs={{1,0},{2,1},{3,2},{4,3},{5,4},{6,5},{7,6},{9,8},{10,9},{11,10},{12... | collective-permute-start | bytes 1572872 | tf_op jit(solution)/shard_map/ppermute | solution.py:17
  425.7 38.8 %copy-start.9 = (f32[1,8,32,8,128]{4,3,2,1,0:T(8,128)S(1)}, f32[1,8,32,8,128]{4,3,2,1,0:T(8,128)}, u32[]{:S(2)}) copy-start(f32[1,8,32,8,128]{4,3,2,1,0:T(8,128)} %copy-done.7) | copy-start | bytes 3145732
  425.7 24.9 %collective-permute-start.4 = (f32[256,4,128]{2,1,0:T(4,128)S(1)}, f32[256,4,128]{2,1,0:T(4,128)S(1)}, u32[]{:S(2)}, u32[]{:S(2)}) collective-permute-start(f32[256,4,128]{2,1,0:T(4,128)S(1)} %get-tuple-element.65), channel_id=1, source_target_pairs={{0,1},{1,2},{2,3},{3,4},{4,5},{5,6},{6,7},{8,9},{9,10},{10,11},{11... | collective-permute-start | bytes 1572872 | tf_op jit(solution)/shard_map/ppermute | solution.py:16
  486.6 13.9 %copy-start.6 = (f32[1,8,32,8,128]{4,3,2,1,0:T(8,128)S(1)}, f32[1,8,32,8,128]{4,3,2,1,0:T(8,128)}, u32[]{:S(2)}) copy-start(f32[1,8,32,8,128]{4,3,2,1,0:T(8,128)} %copy-done.4) | copy-start | bytes 3145732
  522.5 14.0 %copy-start.3 = (f32[1,8,32,8,128]{4,3,2,1,0:T(8,128)S(1)}, f32[1,8,32,8,128]{4,3,2,1,0:T(8,128)}, u32[]{:S(2)}) copy-start(f32[1,8,32,8,128]{4,3,2,1,0:T(8,128)} %copy-done.2) | copy-start | bytes 3145732
  558.8 71.9 %collective-permute-start.6 = (f32[3,256,4,128]{3,2,1,0:T(4,128)S(1)}, f32[3,256,4,128]{3,2,1,0:T(4,128)S(1)}, u32[]{:S(2)}, u32[]{:S(2)}) collective-permute-start(f32[3,256,4,128]{3,2,1,0:T(4,128)S(1)} %get-tuple-element.54), channel_id=1, source_target_pairs={{0,1},{1,2},{2,3},{3,4},{4,5},{5,6},{6,7},{8,9},{9,10},{10,11},{11... | collective-permute-start | bytes 4718600 | tf_op jit(solution)/shard_map/ppermute | solution.py:16
  563.3 67.4 %collective-permute-start.7 = (f32[3,256,4,128]{3,2,1,0:T(4,128)S(1)}, f32[3,256,4,128]{3,2,1,0:T(4,128)S(1)}, u32[]{:S(2)}, u32[]{:S(2)}) collective-permute-start(f32[3,256,4,128]{3,2,1,0:T(4,128)S(1)} %get-tuple-element.55), channel_id=1, source_target_pairs={{1,0},{2,1},{3,2},{4,3},{5,4},{6,5},{7,6},{9,8},{10,9},{11,10},{12... | collective-permute-start | bytes 4718600 | tf_op jit(solution)/shard_map/ppermute | solution.py:17
Sparse Core Ops, SparseCore 0:
  103.2 35.0 all-reduce.27
  385.5 36.8 all-reduce.29
  662.7 36.8 all-reduce.31
where the time goes:
time: 719 us; the launch traced here: 709 us
  other arithmetic  300 us (42%)
  waiting for transfers between devices  276 us (38%)
  local copies, waits for them, and re-layouts  48.7 us (7%)
  blocking collectives  44.1 us (6%)
  starting transfers between devices  24.4 us (3%)
  between operations  16 us (2%)
    ppermute x4, waiting for transfers between devices, extended_2(): before = lax.ppermute(last, axis, up)  154 us
    add x18, other arithmetic, correlate(): result + taps[offset] * lax.slice_in_dim(extended, offset, offset + lengt...  137 us
    psum x2, waiting for transfers between devices, update_estimate(): summed = lax.psum(logs, 'view')  74 us
    add x2, other arithmetic, per_device(): logs = logs + jnp.log(back)  57.3 us
    div x6, other arithmetic, per_device(): ratio = bricks[index].astype(jnp.float32) / blurred  47.5 us
    all_to_all x1, blocking collectives, per_device(): lax.all_to_all(local_views, 'vol', split_axis=2, concat_axis=1, tiled=True)  44.1 us
    another operation x8, other arithmetic, per_device(): ratio_wide = extended_2(jnp.stack(partials), (('vol', 2),), rim_width)  36.7 us
    psum x1, waiting for transfers between devices, per_device(): joined_volume = lax.psum(local_sum, 'view') / total_views  35 us
  transfers between devices with their start and end apart: 11, of which 9 were waited for; matrix products, arithmetic and copies ran while one was open for 1% of the time, Pallas kernels for 0%

commit v1 on v0

v1 whole, which is shorter than its diff:
```python
import functools

import jax
import jax.numpy as jnp
from jax import lax
from jax.experimental import pallas as pl
from jax.experimental.pallas import tpu as pltpu
from jax.sharding import PartitionSpec as P

ITERS = 2
CORES = 2
VMEM = pl.BlockSpec(memory_space=pltpu.VMEM)
SMEM = pl.BlockSpec(memory_space=pltpu.SMEM)
PARAMS = pltpu.CompilerParams(vmem_limit_bytes=48 * 1024 * 1024)


def halves(value):
    high = value.astype(jnp.bfloat16)
    low = (value - high.astype(jnp.float32)).astype(jnp.bfloat16)
    return high, low


def resample_kernel(weights_ref, offsets_ref, raw_ref, out_ref):
    weights = weights_ref[0]
    rows, band = weights.shape
    weights = weights / jnp.sum(weights, axis=-1, keepdims=True)
    first = offsets_ref[0]
    source = lax.broadcasted_iota(jnp.int32, (rows, rows), 1)
    matrix = jnp.zeros((rows, rows), jnp.float32)
    for k in range(band):
        matrix = jnp.where(source == first + k, weights[:, k : k + 1], matrix)
    high = matrix.astype(jnp.bfloat16)
    rest = matrix - high.astype(jnp.float32)
    middle = rest.astype(jnp.bfloat16)
    low = (rest - middle.astype(jnp.float32)).astype(jnp.bfloat16)
    left = jnp.concatenate([high, middle, low], axis=0)

    def two_planes(step, carry):
        z = step * 2
        planes = jnp.concatenate([raw_ref[0, z], raw_ref[0, z + 1]], axis=1)
        parts = jnp.dot(left, planes, preferred_element_type=jnp.float32)
        total = parts[:rows] + (parts[rows : 2 * rows] + parts[2 * rows :])
        total = total.astype(jnp.bfloat16)
        width = raw_ref.shape[3]
        out_ref[0, z] = total[:, :width]
        out_ref[0, z + 1] = total[:, width:]
        return carry

    lax.fori_loop(0, raw_ref.shape[1] // 2, two_planes, 0)


def resample(raw, weights, offsets):
    views, planes, rows, width = raw.shape
    block = lambda v: (v, 0, 0, 0)
    return pl.pallas_call(
        resample_kernel,
        grid=(views,),
        out_shape=jax.ShapeDtypeStruct(raw.shape, jnp.bfloat16),
        in_specs=[
            pl.BlockSpec((1,) + weights.shape[1:], lambda v: (v, 0, 0)),
            pl.BlockSpec((1, rows, 1), lambda v: (v, 0, 0)),
            pl.BlockSpec((1, planes, rows, width), block),
        ],
        out_specs=pl.BlockSpec((1, planes, rows, width), block),
        compiler_params=PARAMS,
    )(weights, offsets[:, :, None], raw)


def bands_kernel(taps_ref, out_ref):
    view = pl.program_id(0)
    count = taps_ref.shape[2]
    width = out_ref.shape[2] // 2
    shape = (width, width)
    shift = lax.broadcasted_iota(jnp.int32, shape, 0) - lax.broadcasted_iota(jnp.int32, shape, 1)
    for way in range(2):
        band = jnp.zeros(shape, jnp.float32)
        for t in range(count):
            at = t - count // 2
            band = jnp.where(shift == (-at if way else at), taps_ref[view, 2, t], band)
        high, low = halves(band)
        out_ref[0, way, :width, :width] = high
        out_ref[0, way, width:, :width] = high
        out_ref[0, way, :width, width:] = low
        out_ref[0, way, width:, width:] = jnp.zeros_like(low)


def bands(taps, width):
    views = taps.shape[0]
    return pl.pallas_call(
        bands_kernel,
        grid=(views,),
        out_shape=jax.ShapeDtypeStruct((views, 2, 2 * width, 2 * width), jnp.bfloat16),
        in_specs=[SMEM],
        out_specs=pl.BlockSpec((1, 2, 2 * width, 2 * width), lambda v: (v, 0, 0, 0)),
        compiler_params=PARAMS,
    )(taps)


def start_kernel(views, place_ref, *refs):
    mains, rims, (out_ref, start_ref, window) = refs[:4], refs[4:8], refs[8:]
    step = pl.program_id(0)
    chip, core = place_ref[0], place_ref[1]
    planes = start_ref.shape[0]
    main, rim = mains[0].shape[1], rims[0].shape[1]

    @pl.when(step == 0)
    def _():
        start_ref[...] = jnp.zeros_like(start_ref)

    for group in range(4):
        for z in range(main):
            window[rim * (1 - chip) + z] = mains[group][0, z]
        for z in range(rim):
            window[main * chip + z] = rims[group][0, z]
        for z in range(planes + 2 * rim):
            plane = window[planes * core + z]
            out_ref[group, 0, z] = plane
            if rim <= z < rim + planes:
                start_ref[z - rim] += plane.astype(jnp.float32)

    @pl.when(step == pl.num_programs(0) - 1)
    def _():
        start_ref[...] = start_ref[...] / views


def gather_start(place, mains, rims, planes):
    count, main, rows, width = mains[0].shape
    rim = rims[0].shape[1]
    take = lambda v: (v, 0, 0, 0)
    bricks, start = pl.pallas_call(
        functools.partial(start_kernel, 4 * count),
        grid=(count,),
        out_shape=(
            jax.ShapeDtypeStruct((4, count, planes + 2 * rim, rows, width), jnp.bfloat16),
            jax.ShapeDtypeStruct((planes, rows, width), jnp.float32),
        ),
        in_specs=[SMEM]
        + [pl.BlockSpec((1, main, rows, width), take)] * 4
        + [pl.BlockSpec((1, rim, rows, width), take)] * 4,
        out_specs=(
            pl.BlockSpec((4, 1, planes + 2 * rim, rows, width), lambda v: (0, v, 0, 0, 0)),
            pl.BlockSpec((planes, rows, width), lambda v: (0, 0, 0)),
        ),
        scratch_shapes=[pltpu.VMEM((main + rim, rows, width), jnp.bfloat16)],
        compiler_params=PARAMS,
    )(place, *mains, *rims)
    return bricks.reshape((4 * count,) + bricks.shape[2:]), start


def update_kernel(taps_ref, bands_ref, brick_ref, before_ref, own_ref, after_ref, out_ref, wide, left, ratio, back, logs):
    view = pl.program_id(0)
    taps = taps_ref.shape[2]
    rim = taps // 2
    planes, rows, width = own_ref.shape
    outer = planes + 2 * rim
    edge = 8

    @pl.when(view == 0)
    def _():
        logs[...] = jnp.zeros_like(logs)
        for scratch in (wide, back):
            depth = scratch.shape[0]
            scratch[:, :edge, :] = jnp.zeros((depth, edge, width), jnp.float32)
            scratch[:, edge + rows :, :] = jnp.zeros((depth, edge, width), jnp.float32)

    gain_z = [taps_ref[view, 0, t] for t in range(taps)]
    gain_x = [taps_ref[view, 1, t] for t in range(taps)]

    def correlate(gains, terms):
        total = gains[0] * terms[0]
        for t in range(1, taps):
            total = total + gains[t] * terms[t]
        return total

    def along_z(k, carry):
        at = pl.ds(pl.multiple_of(k * 8, 8), 8)
        column = [ref[z, at, :] for ref in (before_ref, own_ref, after_ref) for z in range(ref.shape[0])]
        for z in range(outer):
            wide[z, pl.ds(pl.multiple_of(k * 8, 8) + edge, 8), :] = correlate(gain_z, column[z : z + taps])
        return carry

    lax.fori_loop(0, rows // 8, along_z, 0)

    def along_x(source, gains, z):
        for k in range(rows // 16):
            parts = []
            for half in range(2):
                first = edge - rim + 16 * k + 8 * half
                parts.append(correlate(gains, [source[z, pl.ds(first + t, 8), :] for t in range(taps)]))
            high, low = halves(jnp.concatenate(parts, axis=0))
            at = pl.ds(pl.multiple_of(z * rows + 16 * k, 16), 16)
            left[at, :width] = high
            left[at, width:] = low

    def forward_x(z, carry):
        along_x(wide, gain_x, z)
        return carry

    lax.fori_loop(0, outer, forward_x, 0)

    product = jnp.dot(left[...], bands_ref[0, 0], preferred_element_type=jnp.float32)
    blurred = product[:, :width] + product[:, width:]
    ratio[...] = brick_ref[0].astype(jnp.float32) / blurred.reshape(outer, rows, width)

    def back_z(k, carry):
        at = pl.ds(pl.multiple_of(k * 8, 8), 8)
        column = [ratio[z, at, :] for z in range(outer)]
        for z in range(planes):
            back[z, pl.ds(pl.multiple_of(k * 8, 8) + edge, 8), :] = correlate(gain_z[::-1], column[z : z + taps])
        return carry

    lax.fori_loop(0, rows // 8, back_z, 0)

    def back_x(z, carry):
        along_x(back, gain_x[::-1], z)
        return carry

    lax.fori_loop(0, planes, back_x, 0)

    product = jnp.dot(left[: planes * rows, :], bands_ref[0, 1], preferred_element_type=jnp.float32)
    logs[...] += jnp.log(product[:, :width] + product[:, width:]).reshape(logs.shape)

    @pl.when(view == pl.num_programs(0) - 1)
    def _():
        out_ref[...] = own_ref[...] * jnp.exp(logs[...] / pl.num_programs(0))


def update(taps, band, bricks, before, own, after):
    views, outer, rows, width = bricks.shape
    planes = own.shape[0]
    return pl.pallas_call(
        update_kernel,
        grid=(views,),
        out_shape=jax.ShapeDtypeStruct(own.shape, jnp.float32),
        in_specs=[
            SMEM,
            pl.BlockSpec((1,) + band.shape[1:], lambda v: (v, 0, 0, 0)),
            pl.BlockSpec((1, outer, rows, width), lambda v: (v, 0, 0, 0)),
            VMEM,
            VMEM,
            VMEM,
        ],
        out_specs=VMEM,
        scratch_shapes=[
            pltpu.VMEM((outer, rows + 16, width), jnp.float32),
            pltpu.VMEM((outer * rows, 2 * width), jnp.bfloat16),
            pltpu.VMEM((outer, rows, width), jnp.float32),
            pltpu.VMEM((planes, rows + 16, width), jnp.float32),
            pltpu.VMEM((planes, rows, width), jnp.float32),
        ],
        compiler_params=PARAMS,
    )(taps, band, bricks, before, own, after)


def partner(value, bit, members):
    return lax.ppermute(value, "view", [(i, i ^ bit) for i in range(members)])


def z_rims(own, width, members, blocks):
    planes = own.shape[0]
    hops = -(-width // planes)
    axes = ("view", "vol")
    at = lambda line: (line % members) * blocks + line // members
    total = members * blocks
    before, after = [], []
    for hop in range(hops, 0, -1):
        count = min(planes, width - (hop - 1) * planes)
        up = [(at(i), at(i + hop)) for i in range(total - hop)]
        before.append(lax.ppermute(own[planes - count :], axes, up))
    for hop in range(1, hops + 1):
        count = min(planes, width - (hop - 1) * planes)
        down = [(at(i + hop), at(i)) for i in range(total - hop)]
        after.append(lax.ppermute(own[:count], axes, down))
    join = lambda parts: parts[0] if len(parts) == 1 else jnp.concatenate(parts)
    return join(before), join(after)


def per_device(raw_views, weights, offsets, psf_taps):
    views, depth, rows, width = raw_views.shape
    members, blocks = lax.axis_size("view"), lax.axis_size("vol")
    rim = (psf_taps.shape[2] - 1) // 2
    planes = depth // members
    me = lax.axis_index("view")
    chip, core = me // CORES, me % CORES

    up = [(i, i + 1) for i in range(blocks - 1)]
    down = [(i + 1, i) for i in range(blocks - 1)]
    raw_rims = jnp.concatenate(
        [
            lax.ppermute(raw_views[:, depth - rim :], "vol", up),
            lax.ppermute(raw_views[:, :rim], "vol", down),
        ],
        axis=1,
    )
    all_taps = lax.all_gather(psf_taps, "view")
    all_taps = jnp.concatenate([all_taps[me ^ k] for k in range(members)])
    all_taps = all_taps / jnp.sum(all_taps, axis=-1, keepdims=True)
    band = bands(all_taps, width)

    inner = resample(raw_views, weights, offsets)
    main = 2 * planes + rim
    step = 2 * planes - rim
    own_main = lax.dynamic_slice_in_dim(inner, chip * step, main, axis=1)
    far_main = partner(lax.dynamic_slice_in_dim(inner, (1 - chip) * step, main, axis=1), 2, members)
    rims = resample(raw_rims, weights, offsets)
    own_rim = lax.dynamic_slice_in_dim(rims, chip * rim, rim, axis=1)
    far_rim = partner(lax.dynamic_slice_in_dim(rims, (1 - chip) * rim, rim, axis=1), 2, members)
    mains = [own_main, partner(own_main, 1, members), far_main, partner(far_main, 1, members)]
    rims = [own_rim, partner(own_rim, 1, members), far_rim, partner(far_rim, 1, members)]
    place = jnp.stack([chip, core]).astype(jnp.int32)
    bricks, joined = gather_start(place, mains, rims, planes)

    for turn in range(ITERS):
        before, after = z_rims(joined, 2 * rim, members, blocks)
        joined = update(all_taps, band, bricks, before, joined, after)

    columns = lax.all_to_all(joined, "vol", split_axis=1, concat_axis=0, tiled=True)
    far = partner(columns, 2, members)
    pair = jnp.stack([columns, far])
    parts = [columns, None, far, None]
    near = partner(pair, 1, members)
    parts[1], parts[3] = near[0], near[1]
    width_x = columns.shape[1]
    result = jnp.zeros((blocks, members, planes, width_x, width), jnp.float32)
    for k in range(members):
        piece = parts[k].reshape(blocks, 1, planes, width_x, width)
        result = lax.dynamic_update_slice(result, piece, (0, me ^ k, 0, 0, 0))
    return result.reshape(blocks * depth, width_x, width)


def solution(mesh):
    placed = (
        P("view", "vol", None, None),
        P("view", None, None),
        P("view", None),
        P("view", None, None),
    )
    return jax.shard_map(
        per_device, mesh=mesh, in_specs=placed, out_specs=P(None, "vol", None), check_vma=False
    )
```

time: 719 us -> 174 us (0.24); the launches traced: 709 us -> 174 us
  other arithmetic: 300 us -> 1.17 us
  waiting for transfers between devices: 276 us -> 46.2 us
  Pallas kernels: 0 us -> 68.7 us
  local copies, waits for them, and re-layouts: 48.7 us -> 8.64 us
  between operations: 16 us -> 0.31 us
  blocking collectives: 44.1 us -> 31.9 us
  starting transfers between devices: 24.4 us -> 16.8 us
    add x21 -> x0, other arithmetic: 195 us -> none  [the longest x18 137 us: correlate(): result + taps[offset] * lax.slice_in_dim(extended, offset, offset + lengt...]
    ppermute x8 -> x14, waiting for transfers between devices: 167 us -> 46.2 us  [the longest x8 36 us: partner(): return lax.ppermute(value, 'view', [(i, i ^ bit) for i in range(members)])]
    psum x3 -> x0, waiting for transfers between devices: 109 us -> none  [the longest x2 74 us: update_estimate(): summed = lax.psum(logs, 'view')]
    pallas_call x0 -> x6, Pallas kernels: none -> 68.7 us  [the longest x2 51 us: update(): pl.pallas_call(update_kernel, grid=(views,), out_shape=jax.ShapeDtypeStru...]
    div x9 -> x1, other arithmetic: 49.7 us -> 0.1 us  [per_device(): all_taps = all_taps / jnp.sum(all_taps, axis=-1, keepdims=True)]
    another operation x12 -> x2, other arithmetic: 43.9 us -> 0.11 us  [the longest x1 0.07 us: per_device(): place = jnp.stack([chip, core]).astype(jnp.int32)]
    gather x24 -> x0, local copies, waits for them, and re-layouts: 31.2 us -> none  [resample_view(): gathered = jnp.take(planes, first_rows + offset, axis=1).astype(jnp.float32)]
    all_to_all x1, blocking collectives: 44.1 us -> 22.1 us  [per_device(): lax.all_to_all(joined, 'vol', split_axis=1, concat_axis=0, tiled=True)]
  transfers between devices with their start and end apart: 11 -> 14, of which waited for: 9 -> 7; matrix products, arithmetic and copies ran while one was open for 1% -> 1% of each run, Pallas kernels for 0% -> 3%
where the time goes in v1:
time: 174 us
  Pallas kernels  68.7 us (39%)
  waiting for transfers between devices  46.2 us (27%)
  blocking collectives  31.9 us (18%)
  starting transfers between devices  16.8 us (10%)
  local copies, waits for them, and re-layouts  8.64 us (5%)
    pallas_call x2, Pallas kernels, update(): pl.pallas_call(update_kernel, grid=(views,), out_shape=jax.ShapeDtypeStru...  51 us
    ppermute x8, waiting for transfers between devices, partner(): return lax.ppermute(value, 'view', [(i, i ^ bit) for i in range(members)])  36 us
    all_to_all x1, blocking collectives, per_device(): lax.all_to_all(joined, 'vol', split_axis=1, concat_axis=0, tiled=True)  22.1 us
    pallas_call x2, Pallas kernels, resample(): pl.pallas_call(resample_kernel, grid=(views,), out_shape=jax.ShapeDtypeSt...  11.3 us
    all_gather x1, blocking collectives, per_device(): all_taps = lax.all_gather(psf_taps, 'view')  9.78 us
    ppermute x1, waiting for transfers between devices, per_device(): lax.ppermute(raw_views[:, depth - rim:], 'vol', up)  8.05 us
    unnamed x15, local copies, waits for them, and re-layouts  6.38 us
    ppermute x8, starting transfers between devices, partner(): return lax.ppermute(value, 'view', [(i, i ^ bit) for i in range(members)])  4.71 us
  transfers between devices with their start and end apart: 14, of which 7 were waited for; matrix products, arithmetic and copies ran while one was open for 1% of the time, Pallas kernels for 3%

profile of v1, /device:TPU:0, one launch (start us, length us, event | category | flops | bytes accessed | tf_op | source)
XLA Modules:
  0.0 173.7 jit_solution(13341499013840787415)
XLA Ops:
  0.0 0.8 copy.26.weights_ref
  0.8 0.8 copy.27.offsets_ref
  1.6 0.0 copy-start
  1.6 1.4 copy-done
  3.0 8.5 %shard_map.47 = bf16[3,32,64,128]{3,2,1,0:T(8,128)(2,1)S(1)} custom-call(f32[3,64,8]{2,1,0:T(8,128)S(1)} %copy.26.weights_ref, s32[3,64,1]{2,1,0:T(8,128)S(1)} %copy.27.offsets_ref, bf16[3,32,64,128]{3,2,1,0:T(8,128)(2,1)S(1)} %copy-done), custom_call_target="tpu_custom_call" | custom-call | tf_op jit(solution)/shard_map/pallas_call | solution.py:55
  11.5 0.2 constant_dynamic-slice_fusion.2
  11.8 3.0 %collective-permute-start.1 = (bf16[3,20,64,128]{3,2,1,0:T(8,128)(2,1)S(1)}, bf16[3,20,64,128]{3,2,1,0:T(8,128)(2,1)S(1)}, u32[]{:S(2)}, u32[]{:S(2)}) collective-permute-start(bf16[3,20,64,128]{3,2,1,0:T(8,128)(2,1)S(1)} %get-tuple-element.11), channel_id=1, source_target_pairs={{0,16},{8,24},{16,0},{24,8},{1,17},{9,25},{17,1},{25,9},{2,18},{10... | collective-permute-start | bytes 2949128 | tf_op jit(solution)/shard_map/ppermute | solution.py:256
  14.8 0.0 collective-permute-start
  14.8 21.7 %collective-permute-done.1.refs_2_ = bf16[3,20,64,128]{3,2,1,0:T(8,128)(2,1)S(1)} collective-permute-done((bf16[3,20,64,128]{3,2,1,0:T(8,128)(2,1)S(1)}, bf16[3,20,64,128]{3,2,1,0:T(8,128)(2,1)S(1)}, u32[]{:S(2)}, u32[]{:S(2)}) %collective-permute-start.1) | collective-permute-done | bytes 983072 | tf_op jit(solution)/shard_map/ppermute | solution.py:256
  36.5 0.0 collective-permute-start.2
  36.5 0.7 fusion.4
  37.2 3.7 %collective-permute-start.3 = (bf16[3,4,64,128]{3,2,1,0:T(8,128)(2,1)}, bf16[3,4,64,128]{3,2,1,0:T(8,128)(2,1)S(1)}, u32[]{:S(2)}, u32[]{:S(2)}) collective-permute-start(bf16[3,4,64,128]{3,2,1,0:T(8,128)(2,1)} %get-tuple-element.9), channel_id=1, source_target_pairs={{0,1},{1,2},{2,3},{3,4},{4,5},{5,6},{6,7},{8,9},{9,10},{10,11},{11... | collective-permute-start | bytes 589832 | tf_op jit(solution)/shard_map/ppermute | solution.py:290
  40.9 1.3 collective-permute-start.4
  42.2 8.0 %collective-permute-done.3 = bf16[3,4,64,128]{3,2,1,0:T(8,128)(2,1)S(1)} collective-permute-done((bf16[3,4,64,128]{3,2,1,0:T(8,128)(2,1)}, bf16[3,4,64,128]{3,2,1,0:T(8,128)(2,1)S(1)}, u32[]{:S(2)}, u32[]{:S(2)}) %collective-permute-start.3) | collective-permute-done | bytes 196640 | tf_op jit(solution)/shard_map/ppermute | solution.py:290
  50.3 0.0 collective-permute-done.4
  50.3 1.0 pad_maximum_fusion.1.raw_ref
  51.2 2.8 %shard_map.48 = bf16[3,8,64,128]{3,2,1,0:T(8,128)(2,1)S(1)} custom-call(f32[3,64,8]{2,1,0:T(8,128)S(1)} %copy.26.weights_ref, s32[3,64,1]{2,1,0:T(8,128)S(1)} %copy.27.offsets_ref, bf16[3,8,64,128]{3,2,1,0:T(8,128)(2,1)S(1)} %pad_maximum_fusion.1.raw_ref), custom_call_target="tpu_custom_call" | custom-call | tf_op jit(solution)/shard_map/pallas_call | solution.py:55
  54.1 1.6 collective-permute-start.6
  55.7 0.0 collective-permute-start.5
  55.7 4.4 %collective-permute-done.6.refs_6_ = bf16[3,4,64,128]{3,2,1,0:T(8,128)(2,1)S(1)} collective-permute-done((bf16[3,4,64,128]{3,2,1,0:T(8,128)(2,1)S(1)}, bf16[3,4,64,128]{3,2,1,0:T(8,128)(2,1)S(1)}, u32[]{:S(2)}, u32[]{:S(2)}) %collective-permute-start.6) | collective-permute-done | bytes 196640 | tf_op jit(solution)/shard_map/ppermute | solution.py:256
  60.1 0.0 collective-permute-start.7
  60.1 0.0 copy-start.1
  60.1 0.7 copy-done.1
  60.7 0.1 pad_add_fusion.place_ref
  60.8 0.0 collective-permute-done.5.refs_5_
  60.8 0.0 copy-start.3
  60.8 0.7 copy-done.3
  61.5 0.1 collective-permute-done.7.refs_7_
  61.6 0.0 collective-permute-done.refs_1_
  61.6 0.0 collective-permute-done.2.refs_3_
  61.6 0.0 copy-start.2
  61.6 0.9 copy-done.2
  62.6 0.0 copy-start.4
  62.6 0.9 copy-done.4
  63.5 0.0 copy-start.6
  63.5 4.0 %shard_map.49 = (bf16[4,3,16,64,128]{4,3,2,1,0:T(8,128)(2,1)}, f32[8,64,128]{2,1,0:T(8,128)S(1)}) custom-call(s32[2]{0:T(128)S(1)} %pad_add_fusion.place_ref, bf16[3,20,64,128]{3,2,1,0:T(8,128)(2,1)S(1)} %get-tuple-element.12.refs_0_, bf16[3,20,64,128]{3,2,1,0:T(8,128)(2,1)S(1)} %collective-permute-done.refs_1_, ...), custom_call_target="tpu_custom_call" | custom-call | tf_op jit(solution)/shard_map/pallas_call | solution.py:130
  67.5 2.3 %collective-permute-start.8 = (f32[8,64,128]{2,1,0:T(8,128)S(1)}, f32[8,64,128]{2,1,0:T(8,128)S(1)}, u32[]{:S(2)}, u32[]{:S(2)}) collective-permute-start(f32[8,64,128]{2,1,0:T(8,128)S(1)} %get-tuple-element.8.own_ref), channel_id=1, source_target_pairs={{0,8},{8,16},{16,24},{24,1},{1,9},{9,17},{17,25},{25,2},{2,10},{10... | collective-permute-start | bytes 786440 | tf_op jit(solution)/shard_map/ppermute | solution.py:269
  69.8 1.3 collective-permute-start.9
  71.1 0.0 copy-done.6
  71.1 9.8 %all-gather = f32[12,3,9]{2,1,0:T(4,128)S(1)} all-gather(f32[3,3,9]{2,1,0:T(4,128)S(1)} %copy-done.6), channel_id=2, replica_groups=mesh['view'=4,'vol'=8] {'view'}, dimensions={0}, use_global_device_ids=true | all-gather | bytes 1620 | tf_op jit(solution)/shard_map/all_gather | solution.py:295
  80.9 0.1 fusion.1.taps_ref
  81.0 2.4 %shard_map.46.bands_ref = bf16[12,2,256,256]{3,2,1,0:T(8,128)(2,1)S(1)} custom-call(f32[12,3,9]{2,1,0:T(4,128)S(1)} %fusion.1.taps_ref), custom_call_target="tpu_custom_call" | custom-call | tf_op jit(solution)/shard_map/pallas_call | solution.py:89
  83.4 0.0 collective-permute-done.8.before_ref
  83.4 0.0 collective-permute-done.9.after_ref
  83.4 25.5 %shard_map.50.own_ref = f32[8,64,128]{2,1,0:T(8,128)S(1)} custom-call(f32[12,3,9]{2,1,0:T(4,128)S(1)} %fusion.1.taps_ref, bf16[12,2,256,256]{3,2,1,0:T(8,128)(2,1)S(1)} %shard_map.46.bands_ref, bf16[12,16,64,128]{3,2,1,0:T(8,128)(2,1)} %bitcast.34, f32[8,64,128]{2,1,0:T(8,128)S(1)} %collective-permute-done.8.before_ref, ...), custom_call_target="tpu_custom_call" | custom-call | tf_op jit(solution)/shard_map/pallas_call | solution.py:231
  108.9 2.2 %collective-permute-start.10 = (f32[8,64,128]{2,1,0:T(8,128)S(1)}, f32[8,64,128]{2,1,0:T(8,128)S(1)}, u32[]{:S(2)}, u32[]{:S(2)}) collective-permute-start(f32[8,64,128]{2,1,0:T(8,128)S(1)} %shard_map.50.own_ref), channel_id=1, source_target_pairs={{0,8},{8,16},{16,24},{24,1},{1,9},{9,17},{17,25},{25,2},{2,10},{10... | collective-permute-start | bytes 786440 | tf_op jit(solution)/shard_map/ppermute | solution.py:269
  111.2 1.3 collective-permute-start.11
  112.5 0.0 collective-permute-done.10.before_ref
  112.5 2.1 %collective-permute-done.11.after_ref = f32[8,64,128]{2,1,0:T(8,128)S(1)} collective-permute-done((f32[8,64,128]{2,1,0:T(8,128)S(1)}, f32[8,64,128]{2,1,0:T(8,128)S(1)}, u32[]{:S(2)}, u32[]{:S(2)}) %collective-permute-start.11) | collective-permute-done | bytes 262176 | tf_op jit(solution)/shard_map/ppermute | solution.py:273
  114.6 25.5 %shard_map.51 = f32[8,64,128]{2,1,0:T(8,128)S(1)} custom-call(f32[12,3,9]{2,1,0:T(4,128)S(1)} %fusion.1.taps_ref, bf16[12,2,256,256]{3,2,1,0:T(8,128)(2,1)S(1)} %shard_map.46.bands_ref, bf16[12,16,64,128]{3,2,1,0:T(8,128)(2,1)} %bitcast.35, f32[8,64,128]{2,1,0:T(8,128)S(1)} %collective-permute-done.10.before_ref, f32[8,64,128]{2,1,0:T(8,128)S(1)} %shard_map.50.own_ref, ...), custom_call_target="tpu_custom_call" | custom-call | tf_op jit(solution)/shard_map/pallas_call | solution.py:231
  140.1 0.2 copy.30
  140.2 22.1 %all_to_all.18 = f32[8,64,128]{2,0,1:T(8,128)S(1)} all-to-all(f32[8,64,128]{2,0,1:T(8,128)S(1)} %copy.30), channel_id=1, replica_groups=mesh['view'=4,'vol'=8] {'vol'}, dimensions={1} | all-to-all | bytes 524288 | tf_op jit(solution)/shard_map/all_to_all | solution.py:317
  162.4 0.1 collective-permute-start.12
  162.5 8.0 %collective-permute-done.12 = f32[64,8,128]{2,1,0:T(8,128)S(1)} collective-permute-done((f32[64,8,128]{2,1,0:T(8,128)S(1)}, f32[64,8,128]{2,1,0:T(8,128)S(1)}, u32[]{:S(2)}, u32[]{:S(2)}) %collective-permute-start.12) | collective-permute-done | bytes 262176 | tf_op jit(solution)/shard_map/ppermute | solution.py:256
  170.6 0.1 collective-permute-start.13
  170.6 0.1 broadcast_in_dim.8
  170.8 0.1 copy_dynamic-update-slice_fusion
  170.8 1.7 collective-permute-done.13
  172.7 0.0 copy-start.5
  172.7 1.0 copy-done.5
  (8 shorter events, 0.2 us)
Async XLA Ops:
  1.6 1.4 copy-start
  11.8 24.8 %collective-permute-start.1 = (bf16[3,20,64,128]{3,2,1,0:T(8,128)(2,1)S(1)}, bf16[3,20,64,128]{3,2,1,0:T(8,128)(2,1)S(1)}, u32[]{:S(2)}, u32[]{:S(2)}) collective-permute-start(bf16[3,20,64,128]{3,2,1,0:T(8,128)(2,1)S(1)} %get-tuple-element.11), channel_id=1, source_target_pairs={{0,16},{8,24},{16,0},{24,8},{1,17},{9,25},{17,1},{25,9},{2,18},{10... | collective-permute-start | bytes 2949128 | tf_op jit(solution)/shard_map/ppermute | solution.py:256
  14.8 46.9 %collective-permute-start = (bf16[3,20,64,128]{3,2,1,0:T(8,128)(2,1)S(1)}, bf16[3,20,64,128]{3,2,1,0:T(8,128)(2,1)S(1)}, u32[]{:S(2)}, u32[]{:S(2)}) collective-permute-start(bf16[3,20,64,128]{3,2,1,0:T(8,128)(2,1)S(1)} %get-tuple-element.12.refs_0_), channel_id=1, source_target_pairs={{0,8},{8,0},{16,24},{24,16},{1,9},{9,1},{17,25},{25,17},{2,10},{10... | collective-permute-start | bytes 2949128 | tf_op jit(solution)/shard_map/ppermute | solution.py:256
  36.5 25.1 %collective-permute-start.2 = (bf16[3,20,64,128]{3,2,1,0:T(8,128)(2,1)S(1)}, bf16[3,20,64,128]{3,2,1,0:T(8,128)(2,1)}, u32[]{:S(2)}, u32[]{:S(2)}) collective-permute-start(bf16[3,20,64,128]{3,2,1,0:T(8,128)(2,1)S(1)} %collective-permute-done.1.refs_2_), channel_id=1, source_target_pairs={{0,8},{8,0},{16,24},{24,16},{1,9},{9,1},{17,25},{25,17},{2,10},{10... | collective-permute-start | bytes 2949128 | tf_op jit(solution)/shard_map/ppermute | solution.py:256
  37.2 13.0 %collective-permute-start.3 = (bf16[3,4,64,128]{3,2,1,0:T(8,128)(2,1)}, bf16[3,4,64,128]{3,2,1,0:T(8,128)(2,1)S(1)}, u32[]{:S(2)}, u32[]{:S(2)}) collective-permute-start(bf16[3,4,64,128]{3,2,1,0:T(8,128)(2,1)} %get-tuple-element.9), channel_id=1, source_target_pairs={{0,1},{1,2},{2,3},{3,4},{4,5},{5,6},{6,7},{8,9},{9,10},{10,11},{11... | collective-permute-start | bytes 589832 | tf_op jit(solution)/shard_map/ppermute | solution.py:290
  40.9 9.4 %collective-permute-start.4 = (bf16[3,4,64,128]{3,2,1,0:T(8,128)(2,1)S(1)}, bf16[3,4,64,128]{3,2,1,0:T(8,128)(2,1)}, u32[]{:S(2)}, u32[]{:S(2)}) collective-permute-start(bf16[3,4,64,128]{3,2,1,0:T(8,128)(2,1)S(1)} %get-tuple-element.10), channel_id=1, source_target_pairs={{1,0},{2,1},{3,2},{4,3},{5,4},{6,5},{7,6},{9,8},{10,9},{11,10},{12... | collective-permute-start | bytes 589832 | tf_op jit(solution)/shard_map/ppermute | solution.py:291
  54.1 5.9 %collective-permute-start.6 = (bf16[3,4,64,128]{3,2,1,0:T(8,128)(2,1)S(1)}, bf16[3,4,64,128]{3,2,1,0:T(8,128)(2,1)S(1)}, u32[]{:S(2)}, u32[]{:S(2)}) collective-permute-start(bf16[3,4,64,128]{3,2,1,0:T(8,128)(2,1)S(1)} %get-tuple-element.15), channel_id=1, source_target_pairs={{0,16},{8,24},{16,0},{24,8},{1,17},{9,25},{17,1},{25,9},{2,18},{10... | collective-permute-start | bytes 589832 | tf_op jit(solution)/shard_map/ppermute | solution.py:256
  55.7 5.2 %collective-permute-start.5 = (bf16[3,4,64,128]{3,2,1,0:T(8,128)(2,1)S(1)}, bf16[3,4,64,128]{3,2,1,0:T(8,128)(2,1)S(1)}, u32[]{:S(2)}, u32[]{:S(2)}) collective-permute-start(bf16[3,4,64,128]{3,2,1,0:T(8,128)(2,1)S(1)} %get-tuple-element.16.refs_4_), channel_id=1, source_target_pairs={{0,8},{8,0},{16,24},{24,16},{1,9},{9,1},{17,25},{25,17},{2,10},{10... | collective-permute-start | bytes 589832 | tf_op jit(solution)/shard_map/ppermute | solution.py:256
  60.1 1.6 collective-permute-start.7
  60.1 0.7 copy-start.1
  60.8 0.7 copy-start.3
  61.6 0.9 copy-start.2
  62.6 0.9 copy-start.4
  63.5 7.6 %copy-start.6 = (f32[3,3,9]{2,1,0:T(4,128)S(1)}, f32[3,3,9]{2,1,0:T(4,128)}, u32[]{:S(2)}) copy-start(f32[3,3,9]{2,1,0:T(4,128)} %param.7) | copy-start | bytes 976
  67.5 15.9 %collective-permute-start.8 = (f32[8,64,128]{2,1,0:T(8,128)S(1)}, f32[8,64,128]{2,1,0:T(8,128)S(1)}, u32[]{:S(2)}, u32[]{:S(2)}) collective-permute-start(f32[8,64,128]{2,1,0:T(8,128)S(1)} %get-tuple-element.8.own_ref), channel_id=1, source_target_pairs={{0,8},{8,16},{16,24},{24,1},{1,9},{9,17},{17,25},{25,2},{2,10},{10... | collective-permute-start | bytes 786440 | tf_op jit(solution)/shard_map/ppermute | solution.py:269
  69.8 13.6 %collective-permute-start.9 = (f32[8,64,128]{2,1,0:T(8,128)S(1)}, f32[8,64,128]{2,1,0:T(8,128)S(1)}, u32[]{:S(2)}, u32[]{:S(2)}) collective-permute-start(f32[8,64,128]{2,1,0:T(8,128)S(1)} %get-tuple-element.8.own_ref), channel_id=1, source_target_pairs={{8,0},{16,8},{24,16},{1,24},{9,1},{17,9},{25,17},{2,25},{10,2},{18... | collective-permute-start | bytes 786440 | tf_op jit(solution)/shard_map/ppermute | solution.py:273
  108.9 3.5 %collective-permute-start.10 = (f32[8,64,128]{2,1,0:T(8,128)S(1)}, f32[8,64,128]{2,1,0:T(8,128)S(1)}, u32[]{:S(2)}, u32[]{:S(2)}) collective-permute-start(f32[8,64,128]{2,1,0:T(8,128)S(1)} %shard_map.50.own_ref), channel_id=1, source_target_pairs={{0,8},{8,16},{16,24},{24,1},{1,9},{9,17},{17,25},{25,2},{2,10},{10... | collective-permute-start | bytes 786440 | tf_op jit(solution)/shard_map/ppermute | solution.py:269
  111.2 3.4 %collective-permute-start.11 = (f32[8,64,128]{2,1,0:T(8,128)S(1)}, f32[8,64,128]{2,1,0:T(8,128)S(1)}, u32[]{:S(2)}, u32[]{:S(2)}) collective-permute-start(f32[8,64,128]{2,1,0:T(8,128)S(1)} %shard_map.50.own_ref), channel_id=1, source_target_pairs={{8,0},{16,8},{24,16},{1,24},{9,1},{17,9},{25,17},{2,25},{10,2},{18... | collective-permute-start | bytes 786440 | tf_op jit(solution)/shard_map/ppermute | solution.py:273
  162.4 8.1 %collective-permute-start.12 = (f32[64,8,128]{2,1,0:T(8,128)S(1)}, f32[64,8,128]{2,1,0:T(8,128)S(1)}, u32[]{:S(2)}, u32[]{:S(2)}) collective-permute-start(f32[64,8,128]{2,1,0:T(8,128)S(1)} %bitcast.41), channel_id=1, source_target_pairs={{0,16},{8,24},{16,0},{24,8},{1,17},{9,25},{17,1},{25,9},{2,18},{10... | collective-permute-start | bytes 786440 | tf_op jit(solution)/shard_map/ppermute | solution.py:256
  170.6 2.0 %collective-permute-start.13 = (f32[2,64,8,128]{3,2,1,0:T(8,128)S(1)}, f32[2,64,8,128]{3,2,1,0:T(8,128)S(1)}, u32[]{:S(2)}, u32[]{:S(2)}) collective-permute-start(f32[2,64,8,128]{3,2,1,0:T(8,128)S(1)} %pad_maximum_fusion), channel_id=1, source_target_pairs={{0,8},{8,0},{16,24},{24,16},{1,9},{9,1},{17,25},{25,17},{2,10},{10... | collective-permute-start | bytes 1572872 | tf_op jit(solution)/shard_map/ppermute | solution.py:256
  172.7 1.0 copy-start.5

commit v2 on v1

--- a/solution.py
+++ b/solution.py
@@ -33,20 +33,20 @@
     rest = matrix - high.astype(jnp.float32)
     middle = rest.astype(jnp.bfloat16)
     low = (rest - middle.astype(jnp.float32)).astype(jnp.bfloat16)
-    left = jnp.concatenate([high, middle, low], axis=0)
-
-    def two_planes(step, carry):
-        z = step * 2
-        planes = jnp.concatenate([raw_ref[0, z], raw_ref[0, z + 1]], axis=1)
-        parts = jnp.dot(left, planes, preferred_element_type=jnp.float32)
-        total = parts[:rows] + (parts[rows : 2 * rows] + parts[2 * rows :])
-        total = total.astype(jnp.bfloat16)
-        width = raw_ref.shape[3]
-        out_ref[0, z] = total[:, :width]
-        out_ref[0, z + 1] = total[:, width:]
-        return carry
-
-    lax.fori_loop(0, raw_ref.shape[1] // 2, two_planes, 0)
+    left = jnp.concatenate([high, middle, low], axis=1)
+    width = raw_ref.shape[3]
+
+    def eight_planes(step, carry):
+        for pair in range(4):
+            z = step * 8 + pair * 2
+            planes = jnp.concatenate([raw_ref[0, z], raw_ref[0, z + 1]], axis=1)
+            planes = jnp.concatenate([planes, planes, planes], axis=0)
+            total = jnp.dot(left, planes, preferred_element_type=jnp.float32).astype(jnp.bfloat16)
+            out_ref[0, z] = total[:, :width]
+            out_ref[0, z + 1] = total[:, width:]
+        return carry
+
+    lax.fori_loop(0, raw_ref.shape[1] // 8, eight_planes, 0)
 
 
 def resample(raw, weights, offsets):
@@ -63,6 +63,7 @@
         ],
         out_specs=pl.BlockSpec((1, planes, rows, width), block),
         compiler_params=PARAMS,
+        cost_estimate=pl.CostEstimate(flops=0, bytes_accessed=16 * raw.size, transcendentals=0),
     )(weights, offsets[:, :, None], raw)
 
 
@@ -292,19 +293,23 @@
         ],
         axis=1,
     )
-    all_taps = lax.all_gather(psf_taps, "view")
-    all_taps = jnp.concatenate([all_taps[me ^ k] for k in range(members)])
+    pair_taps = jnp.stack([psf_taps, partner(psf_taps, 2, members)])
+    near_taps = partner(pair_taps, 1, members)
+    all_taps = jnp.stack([pair_taps[0], near_taps[0], pair_taps[1], near_taps[1]])
+    all_taps = all_taps.reshape((-1,) + psf_taps.shape[1:])
     all_taps = all_taps / jnp.sum(all_taps, axis=-1, keepdims=True)
     band = bands(all_taps, width)
 
     inner = resample(raw_views, weights, offsets)
     main = 2 * planes + rim
     step = 2 * planes - rim
+    inner, raw_rims = lax.optimization_barrier((inner, raw_rims))
     own_main = lax.dynamic_slice_in_dim(inner, chip * step, main, axis=1)
     far_main = partner(lax.dynamic_slice_in_dim(inner, (1 - chip) * step, main, axis=1), 2, members)
     rims = resample(raw_rims, weights, offsets)
     own_rim = lax.dynamic_slice_in_dim(rims, chip * rim, rim, axis=1)
     far_rim = partner(lax.dynamic_slice_in_dim(rims, (1 - chip) * rim, rim, axis=1), 2, members)
+    far_main, band, own_rim = lax.optimization_barrier((far_main, band, own_rim))
     mains = [own_main, partner(own_main, 1, members), far_main, partner(far_main, 1, members)]
     rims = [own_rim, partner(own_rim, 1, members), far_rim, partner(far_rim, 1, members)]
     place = jnp.stack([chip, core]).astype(jnp.int32)

time: 174 us -> 162 us (0.931)
  blocking collectives: 31.9 us -> 22.5 us
  starting transfers between devices: 16.8 us -> 23.3 us
  Pallas kernels: 68.7 us -> 63.5 us
  waiting for transfers between devices: 46.2 us -> 44.3 us
    all_gather x1 -> x0, blocking collectives: 9.78 us -> none  [per_device(): all_taps = lax.all_gather(psf_taps, 'view')]
    ppermute x1, waiting for transfers between devices: 8.05 us -> 0.01 us  [per_device(): lax.ppermute(raw_views[:, depth - rim:], 'vol', up)]
    pallas_call x2, Pallas kernels: 11.3 us -> 5.06 us  [resample(): pl.pallas_call(resample_kernel, grid=(views,), out_shape=jax.ShapeDtypeSt...]
    ppermute x2, starting transfers between devices: 4.52 us -> 9.72 us  [z_rims(): before.append(lax.ppermute(own[planes - count:], axes, up))]
    unnamed x15 -> x19, local copies, waits for them, and re-layouts: 6.38 us -> 3.23 us
    ppermute x2, waiting for transfers between devices: 2.12 us -> 5.1 us  [z_rims(): after.append(lax.ppermute(own[:count], axes, down))]
    ppermute x8 -> x10, waiting for transfers between devices: 36 us -> 38.8 us  [partner(): return lax.ppermute(value, 'view', [(i, i ^ bit) for i in range(members)])]
    ppermute x8 -> x10, starting transfers between devices: 4.71 us -> 4.81 us  [partner(): return lax.ppermute(value, 'view', [(i, i ^ bit) for i in range(members)])]
  transfers between devices with their start and end apart: 14 -> 16, of which waited for: 7 -> 10; matrix products, arithmetic and copies ran while one was open for 1% -> 1% of each run, Pallas kernels for 3% -> 5%
where the time goes in v2:
time: 162 us
  Pallas kernels  63.5 us (39%)
  waiting for transfers between devices  44.3 us (27%)
  starting transfers between devices  23.3 us (14%)
  blocking collectives  22.5 us (14%)
  local copies, waits for them, and re-layouts  7.21 us (4%)
    pallas_call x2, Pallas kernels, update(): pl.pallas_call(update_kernel, grid=(views,), out_shape=jax.ShapeDtypeStru...  51 us
    ppermute x10, waiting for transfers between devices, partner(): return lax.ppermute(value, 'view', [(i, i ^ bit) for i in range(members)])  38.8 us
    all_to_all x1, blocking collectives, per_device(): lax.all_to_all(joined, 'vol', split_axis=1, concat_axis=0, tiled=True)  22.5 us
    ppermute x2, starting transfers between devices, z_rims(): before.append(lax.ppermute(own[planes - count:], axes, up))  9.72 us
    ppermute x2, waiting for transfers between devices, z_rims(): after.append(lax.ppermute(own[:count], axes, down))  5.1 us
    pallas_call x1, Pallas kernels, gather_start(): pl.pallas_call(functools.partial(start_kernel, 4 * count), grid=(count,),...  5.07 us
    pallas_call x2, Pallas kernels, resample(): pl.pallas_call(resample_kernel, grid=(views,), out_shape=jax.ShapeDtypeSt...  5.06 us
    ppermute x1, starting transfers between devices, per_device(): lax.ppermute(raw_views[:, depth - rim:], 'vol', up)  4.88 us
  transfers between devices with their start and end apart: 16, of which 10 were waited for; matrix products, arithmetic and copies ran while one was open for 1% of the time, Pallas kernels for 5%

profile of v2, /device:TPU:0, one launch (start us, length us, event | category | flops | bytes accessed | tf_op | source)
XLA Modules:
  0.0 161.6 jit_solution(4082173662459106516)
XLA Ops:
  0.0 1.0 fusion.1
  1.1 4.9 %collective-permute-start.2 = (bf16[3,4,64,128]{3,2,1,0:T(8,128)(2,1)S(1)}, bf16[3,4,64,128]{3,2,1,0:T(8,128)(2,1)S(1)}, u32[]{:S(2)}, u32[]{:S(2)}) collective-permute-start(bf16[3,4,64,128]{3,2,1,0:T(8,128)(2,1)S(1)} %get-tuple-element.23), channel_id=1, source_target_pairs={{0,1},{1,2},{2,3},{3,4},{4,5},{5,6},{6,7},{8,9},{9,10},{10,11},{11... | collective-permute-start | bytes 589832 | tf_op jit(solution)/shard_map/ppermute | solution.py:291
  5.9 1.3 collective-permute-start.3
  7.3 0.8 copy.32.weights_ref
  8.1 0.0 copy-start.1
  8.1 0.8 copy.33.offsets_ref
  8.9 0.0 copy-start
  8.9 1.4 copy-done
  10.4 3.4 %shard_map.46 = bf16[3,32,64,128]{3,2,1,0:T(8,128)(2,1)S(1)} custom-call(f32[3,64,8]{2,1,0:T(8,128)S(1)} %copy.32.weights_ref, s32[3,64,1]{2,1,0:T(8,128)S(1)} %copy.33.offsets_ref, bf16[3,32,64,128]{3,2,1,0:T(8,128)(2,1)S(1)} %copy-done), custom_call_target="tpu_custom_call" | custom-call | bytes 12582912 | tf_op jit(solution)/shard_map/pallas_call | solution.py:55
  13.8 0.0 copy-done.1
  13.8 0.0 copy-done.3
  13.8 0.0 collective-permute-done.2
  13.8 0.4 collective-permute-done.3
  14.2 0.0 copy-start.8
  14.2 1.6 constant_dynamic-slice_fusion.1
  15.8 1.5 collective-permute-start.4
  17.3 0.0 copy-done.8
  17.3 0.5 collective-permute-start
  17.9 21.2 %collective-permute-done = f32[3,3,9]{2,1,0:T(4,128)S(1)} collective-permute-done((f32[3,3,9]{2,1,0:T(4,128)S(1)}, f32[3,3,9]{2,1,0:T(4,128)S(1)}, u32[]{:S(2)}, u32[]{:S(2)}) %collective-permute-start) | collective-permute-done | bytes 356 | tf_op jit(solution)/shard_map/ppermute | solution.py:257
  39.1 0.0 collective-permute-start.1
  39.1 1.2 collective-permute-done.1
  40.3 0.1 fusion
  40.4 0.1 bitcast_divide_fusion.taps_ref
  40.5 0.0 copy-start.5
  40.5 0.0 copy-start.2
  40.5 0.0 copy-start.4
  40.5 2.4 %shard_map.47.bands_ref = bf16[12,2,256,256]{3,2,1,0:T(8,128)(2,1)S(1)} custom-call(f32[12,3,9]{2,1,0:T(4,128)S(1)} %bitcast_divide_fusion.taps_ref), custom_call_target="tpu_custom_call" | custom-call | tf_op jit(solution)/shard_map/pallas_call | solution.py:90
  42.9 0.0 copy-done.5
  42.9 0.0 copy-done.2
  42.9 0.0 copy-done.4
  42.9 1.6 %shard_map.48 = bf16[3,8,64,128]{3,2,1,0:T(8,128)(2,1)S(1)} custom-call(f32[3,64,8]{2,1,0:T(8,128)S(1)} %copy-done.2, s32[3,64,1]{2,1,0:T(8,128)S(1)} %copy-done.4, bf16[3,8,64,128]{3,2,1,0:T(8,128)(2,1)S(1)} %pad_maximum_fusion.1.raw_ref), custom_call_target="tpu_custom_call" | custom-call | bytes 3145728 | tf_op jit(solution)/shard_map/pallas_call | solution.py:55
  44.6 0.2 collective-permute-start.5
  44.8 0.0 collective-permute-done.4.refs_2_
  44.9 0.4 collective-permute-start.6
  45.3 1.5 collective-permute-start.8
  46.8 5.5 %collective-permute-done.8.refs_6_ = bf16[3,4,64,128]{3,2,1,0:T(8,128)(2,1)S(1)} collective-permute-done((bf16[3,4,64,128]{3,2,1,0:T(8,128)(2,1)S(1)}, bf16[3,4,64,128]{3,2,1,0:T(8,128)(2,1)S(1)}, u32[]{:S(2)}, u32[]{:S(2)}) %collective-permute-start.8) | collective-permute-done | bytes 196640 | tf_op jit(solution)/shard_map/ppermute | solution.py:257
  52.2 0.0 collective-permute-start.9
  52.2 0.5 collective-permute-start.7
  52.7 0.1 pad_add_fusion.place_ref
  52.8 1.0 collective-permute-done.9.refs_7_
  53.8 0.0 collective-permute-done.5.refs_1_
  53.8 0.3 collective-permute-done.7.refs_5_
  54.1 0.0 collective-permute-done.6.refs_3_
  54.1 5.1 %shard_map.49 = (bf16[4,3,16,64,128]{4,3,2,1,0:T(8,128)(2,1)}, f32[8,64,128]{2,1,0:T(8,128)S(1)}) custom-call(s32[2]{0:T(128)S(1)} %pad_add_fusion.place_ref, bf16[3,20,64,128]{3,2,1,0:T(8,128)(2,1)} %get-tuple-element.21.refs_0_, bf16[3,20,64,128]{3,2,1,0:T(8,128)(2,1)} %collective-permute-done.5.refs_1_, ...), custom_call_target="tpu_custom_call" | custom-call | tf_op jit(solution)/shard_map/pallas_call | solution.py:131
  59.2 2.1 %collective-permute-start.10 = (f32[8,64,128]{2,1,0:T(8,128)S(1)}, f32[8,64,128]{2,1,0:T(8,128)S(1)}, u32[]{:S(2)}, u32[]{:S(2)}) collective-permute-start(f32[8,64,128]{2,1,0:T(8,128)S(1)} %get-tuple-element.18.own_ref), channel_id=1, source_target_pairs={{0,8},{8,16},{16,24},{24,1},{1,9},{9,17},{17,25},{25,2},{2,10},{10... | collective-permute-start | bytes 786440 | tf_op jit(solution)/shard_map/ppermute | solution.py:270
  61.3 1.3 collective-permute-start.11
  62.6 0.0 collective-permute-done.10.before_ref
  62.6 3.0 %collective-permute-done.11.after_ref = f32[8,64,128]{2,1,0:T(8,128)S(1)} collective-permute-done((f32[8,64,128]{2,1,0:T(8,128)S(1)}, f32[8,64,128]{2,1,0:T(8,128)S(1)}, u32[]{:S(2)}, u32[]{:S(2)}) %collective-permute-start.11) | collective-permute-done | bytes 262176 | tf_op jit(solution)/shard_map/ppermute | solution.py:274
  65.6 25.5 %shard_map.50.own_ref = f32[8,64,128]{2,1,0:T(8,128)S(1)} custom-call(f32[12,3,9]{2,1,0:T(4,128)S(1)} %copy-done.6, bf16[12,2,256,256]{3,2,1,0:T(8,128)(2,1)S(1)} %shard_map.47.bands_ref, bf16[12,16,64,128]{3,2,1,0:T(8,128)(2,1)} %bitcast.29, f32[8,64,128]{2,1,0:T(8,128)S(1)} %collective-permute-done.10.before_ref, ...), custom_call_target="tpu_custom_call" | custom-call | tf_op jit(solution)/shard_map/pallas_call | solution.py:232
  91.1 7.6 %collective-permute-start.12 = (f32[8,64,128]{2,1,0:T(8,128)S(1)}, f32[8,64,128]{2,1,0:T(8,128)S(1)}, u32[]{:S(2)}, u32[]{:S(2)}) collective-permute-start(f32[8,64,128]{2,1,0:T(8,128)S(1)} %shard_map.50.own_ref), channel_id=1, source_target_pairs={{0,8},{8,16},{16,24},{24,1},{1,9},{9,17},{17,25},{25,2},{2,10},{10... | collective-permute-start | bytes 786440 | tf_op jit(solution)/shard_map/ppermute | solution.py:270
  98.7 1.3 collective-permute-start.13
  100.0 0.0 collective-permute-done.12.before_ref
  100.0 2.1 %collective-permute-done.13.after_ref = f32[8,64,128]{2,1,0:T(8,128)S(1)} collective-permute-done((f32[8,64,128]{2,1,0:T(8,128)S(1)}, f32[8,64,128]{2,1,0:T(8,128)S(1)}, u32[]{:S(2)}, u32[]{:S(2)}) %collective-permute-start.13) | collective-permute-done | bytes 262176 | tf_op jit(solution)/shard_map/ppermute | solution.py:274
  102.1 25.5 %shard_map.51 = f32[8,64,128]{2,1,0:T(8,128)S(1)} custom-call(f32[12,3,9]{2,1,0:T(4,128)S(1)} %copy-done.6, bf16[12,2,256,256]{3,2,1,0:T(8,128)(2,1)S(1)} %shard_map.47.bands_ref, bf16[12,16,64,128]{3,2,1,0:T(8,128)(2,1)} %bitcast.30, f32[8,64,128]{2,1,0:T(8,128)S(1)} %collective-permute-done.12.before_ref, f32[8,64,128]{2,1,0:T(8,128)S(1)} %shard_map.50.own_ref, ...), custom_call_target="tpu_custom_call" | custom-call | tf_op jit(solution)/shard_map/pallas_call | solution.py:232
  127.6 0.2 copy.36
  127.8 22.5 %all_to_all.18 = f32[8,64,128]{2,0,1:T(8,128)S(1)} all-to-all(f32[8,64,128]{2,0,1:T(8,128)S(1)} %copy.36), channel_id=1, replica_groups=mesh['view'=4,'vol'=8] {'vol'}, dimensions={1} | all-to-all | bytes 524288 | tf_op jit(solution)/shard_map/all_to_all | solution.py:322
  150.4 0.1 collective-permute-start.14
  150.4 8.0 %collective-permute-done.14 = f32[64,8,128]{2,1,0:T(8,128)S(1)} collective-permute-done((f32[64,8,128]{2,1,0:T(8,128)S(1)}, f32[64,8,128]{2,1,0:T(8,128)S(1)}, u32[]{:S(2)}, u32[]{:S(2)}) %collective-permute-start.14) | collective-permute-done | bytes 262176 | tf_op jit(solution)/shard_map/ppermute | solution.py:257
  158.5 0.1 collective-permute-start.15
  158.6 0.1 broadcast_in_dim.8
  158.7 0.1 copy_dynamic-update-slice_fusion
  158.8 1.7 %collective-permute-done.15 = f32[2,64,8,128]{3,2,1,0:T(8,128)S(1)} collective-permute-done((f32[2,64,8,128]{3,2,1,0:T(8,128)S(1)}, f32[2,64,8,128]{3,2,1,0:T(8,128)S(1)}, u32[]{:S(2)}, u32[]{:S(2)}) %collective-permute-start.15) | collective-permute-done | bytes 524320 | tf_op jit(solution)/shard_map/ppermute | solution.py:257
  160.6 0.0 copy-start.7
  160.6 1.0 copy-done.7
  (14 shorter events, 0.3 us)
Async XLA Ops:
  1.1 12.8 %collective-permute-start.2 = (bf16[3,4,64,128]{3,2,1,0:T(8,128)(2,1)S(1)}, bf16[3,4,64,128]{3,2,1,0:T(8,128)(2,1)S(1)}, u32[]{:S(2)}, u32[]{:S(2)}) collective-permute-start(bf16[3,4,64,128]{3,2,1,0:T(8,128)(2,1)S(1)} %get-tuple-element.23), channel_id=1, source_target_pairs={{0,1},{1,2},{2,3},{3,4},{4,5},{5,6},{6,7},{8,9},{9,10},{10,11},{11... | collective-permute-start | bytes 589832 | tf_op jit(solution)/shard_map/ppermute | solution.py:291
  5.9 8.3 %collective-permute-start.3 = (bf16[3,4,64,128]{3,2,1,0:T(8,128)(2,1)S(1)}, bf16[3,4,64,128]{3,2,1,0:T(8,128)(2,1)S(1)}, u32[]{:S(2)}, u32[]{:S(2)}) collective-permute-start(bf16[3,4,64,128]{3,2,1,0:T(8,128)(2,1)S(1)} %get-tuple-element.24), channel_id=1, source_target_pairs={{1,0},{2,1},{3,2},{4,3},{5,4},{6,5},{7,6},{9,8},{10,9},{11,10},{12... | collective-permute-start | bytes 589832 | tf_op jit(solution)/shard_map/ppermute | solution.py:292
  8.1 5.7 %copy-start.1 = (f32[3,64,8]{2,1,0:T(8,128)}, f32[3,64,8]{2,1,0:T(8,128)S(1)}, u32[]{:S(2)}) copy-start(f32[3,64,8]{2,1,0:T(8,128)S(1)} %copy.32.weights_ref) | copy-start | bytes 18436
  8.9 4.9 %copy-start.3 = (s32[3,64,1]{2,1,0:T(8,128)}, s32[3,64,1]{2,1,0:T(8,128)S(1)}, u32[]{:S(2)}) copy-start(s32[3,64,1]{2,1,0:T(8,128)S(1)} %copy.33.offsets_ref) | copy-start | bytes 2308
  8.9 1.4 copy-start
  14.2 3.1 %copy-start.8 = (f32[3,3,9]{2,1,0:T(4,128)S(1)}, f32[3,3,9]{2,1,0:T(4,128)}, u32[]{:S(2)}) copy-start(f32[3,3,9]{2,1,0:T(4,128)} %param.7) | copy-start | bytes 976
  15.8 29.0 %collective-permute-start.4 = (bf16[3,20,64,128]{3,2,1,0:T(8,128)(2,1)}, bf16[3,20,64,128]{3,2,1,0:T(8,128)(2,1)}, u32[]{:S(2)}, u32[]{:S(2)}) collective-permute-start(bf16[3,20,64,128]{3,2,1,0:T(8,128)(2,1)} %get-tuple-element.22), channel_id=1, source_target_pairs={{0,16},{8,24},{16,0},{24,8},{1,17},{9,25},{17,1},{25,9},{2,18},{10... | collective-permute-start | bytes 2949128 | tf_op jit(solution)/shard_map/ppermute | solution.py:257
  17.3 21.7 %collective-permute-start = (f32[3,3,9]{2,1,0:T(4,128)S(1)}, f32[3,3,9]{2,1,0:T(4,128)S(1)}, u32[]{:S(2)}, u32[]{:S(2)}) collective-permute-start(f32[3,3,9]{2,1,0:T(4,128)S(1)} %copy-done.8), channel_id=1, source_target_pairs={{0,16},{8,24},{16,0},{24,8},{1,17},{9,25},{17,1},{25,9},{2,18},{10... | collective-permute-start | bytes 980 | tf_op jit(solution)/shard_map/ppermute | solution.py:257
  39.1 1.2 collective-permute-start.1
  40.5 2.4 %copy-start.5 = (f32[12,3,9]{2,1,0:T(4,128)}, f32[12,3,9]{2,1,0:T(4,128)S(1)}, u32[]{:S(2)}) copy-start(f32[12,3,9]{2,1,0:T(4,128)S(1)} %bitcast_divide_fusion.taps_ref) | copy-start | bytes 3892
  40.5 2.4 %copy-start.2 = (f32[3,64,8]{2,1,0:T(8,128)S(1)}, f32[3,64,8]{2,1,0:T(8,128)}, u32[]{:S(2)}) copy-start(f32[3,64,8]{2,1,0:T(8,128)} %copy-done.1) | copy-start | bytes 18436
  40.5 2.4 %copy-start.4 = (s32[3,64,1]{2,1,0:T(8,128)S(1)}, s32[3,64,1]{2,1,0:T(8,128)}, u32[]{:S(2)}) copy-start(s32[3,64,1]{2,1,0:T(8,128)} %copy-done.3) | copy-start | bytes 2308
  44.6 9.2 %collective-permute-start.5 = (bf16[3,20,64,128]{3,2,1,0:T(8,128)(2,1)}, bf16[3,20,64,128]{3,2,1,0:T(8,128)(2,1)}, u32[]{:S(2)}, u32[]{:S(2)}) collective-permute-start(bf16[3,20,64,128]{3,2,1,0:T(8,128)(2,1)} %get-tuple-element.21.refs_0_), channel_id=1, source_target_pairs={{0,8},{8,0},{16,24},{24,16},{1,9},{9,1},{17,25},{25,17},{2,10},{10... | collective-permute-start | bytes 2949128 | tf_op jit(solution)/shard_map/ppermute | solution.py:257
  44.9 9.2 %collective-permute-start.6 = (bf16[3,20,64,128]{3,2,1,0:T(8,128)(2,1)}, bf16[3,20,64,128]{3,2,1,0:T(8,128)(2,1)}, u32[]{:S(2)}, u32[]{:S(2)}) collective-permute-start(bf16[3,20,64,128]{3,2,1,0:T(8,128)(2,1)} %collective-permute-done.4.refs_2_), channel_id=1, source_target_pairs={{0,8},{8,0},{16,24},{24,16},{1,9},{9,1},{17,25},{25,17},{2,10},{10... | collective-permute-start | bytes 2949128 | tf_op jit(solution)/shard_map/ppermute | solution.py:257
  45.3 7.0 %collective-permute-start.8 = (bf16[3,4,64,128]{3,2,1,0:T(8,128)(2,1)S(1)}, bf16[3,4,64,128]{3,2,1,0:T(8,128)(2,1)S(1)}, u32[]{:S(2)}, u32[]{:S(2)}) collective-permute-start(bf16[3,4,64,128]{3,2,1,0:T(8,128)(2,1)S(1)} %get-tuple-element.27), channel_id=1, source_target_pairs={{0,16},{8,24},{16,0},{24,8},{1,17},{9,25},{17,1},{25,9},{2,18},{10... | collective-permute-start | bytes 589832 | tf_op jit(solution)/shard_map/ppermute | solution.py:257
  52.2 1.6 collective-permute-start.9
  52.2 1.9 %collective-permute-start.7 = (bf16[3,4,64,128]{3,2,1,0:T(8,128)(2,1)S(1)}, bf16[3,4,64,128]{3,2,1,0:T(8,128)(2,1)}, u32[]{:S(2)}, u32[]{:S(2)}) collective-permute-start(bf16[3,4,64,128]{3,2,1,0:T(8,128)(2,1)S(1)} %get-tuple-element.16.refs_4_), channel_id=1, source_target_pairs={{0,8},{8,0},{16,24},{24,16},{1,9},{9,1},{17,25},{25,17},{2,10},{10... | collective-permute-start | bytes 589832 | tf_op jit(solution)/shard_map/ppermute | solution.py:257
  52.8 12.8 %copy-start.6 = (f32[12,3,9]{2,1,0:T(4,128)S(1)}, f32[12,3,9]{2,1,0:T(4,128)}, u32[]{:S(2)}) copy-start(f32[12,3,9]{2,1,0:T(4,128)} %copy-done.5) | copy-start | bytes 3892
  59.2 3.4 %collective-permute-start.10 = (f32[8,64,128]{2,1,0:T(8,128)S(1)}, f32[8,64,128]{2,1,0:T(8,128)S(1)}, u32[]{:S(2)}, u32[]{:S(2)}) collective-permute-start(f32[8,64,128]{2,1,0:T(8,128)S(1)} %get-tuple-element.18.own_ref), channel_id=1, source_target_pairs={{0,8},{8,16},{16,24},{24,1},{1,9},{9,17},{17,25},{25,2},{2,10},{10... | collective-permute-start | bytes 786440 | tf_op jit(solution)/shard_map/ppermute | solution.py:270
  61.3 4.3 %collective-permute-start.11 = (f32[8,64,128]{2,1,0:T(8,128)S(1)}, f32[8,64,128]{2,1,0:T(8,128)S(1)}, u32[]{:S(2)}, u32[]{:S(2)}) collective-permute-start(f32[8,64,128]{2,1,0:T(8,128)S(1)} %get-tuple-element.18.own_ref), channel_id=1, source_target_pairs={{8,0},{16,8},{24,16},{1,24},{9,1},{17,9},{25,17},{2,25},{10,2},{18... | collective-permute-start | bytes 786440 | tf_op jit(solution)/shard_map/ppermute | solution.py:274
  91.1 8.9 %collective-permute-start.12 = (f32[8,64,128]{2,1,0:T(8,128)S(1)}, f32[8,64,128]{2,1,0:T(8,128)S(1)}, u32[]{:S(2)}, u32[]{:S(2)}) collective-permute-start(f32[8,64,128]{2,1,0:T(8,128)S(1)} %shard_map.50.own_ref), channel_id=1, source_target_pairs={{0,8},{8,16},{16,24},{24,1},{1,9},{9,17},{17,25},{25,2},{2,10},{10... | collective-permute-start | bytes 786440 | tf_op jit(solution)/shard_map/ppermute | solution.py:270
  98.7 3.4 %collective-permute-start.13 = (f32[8,64,128]{2,1,0:T(8,128)S(1)}, f32[8,64,128]{2,1,0:T(8,128)S(1)}, u32[]{:S(2)}, u32[]{:S(2)}) collective-permute-start(f32[8,64,128]{2,1,0:T(8,128)S(1)} %shard_map.50.own_ref), channel_id=1, source_target_pairs={{8,0},{16,8},{24,16},{1,24},{9,1},{17,9},{25,17},{2,25},{10,2},{18... | collective-permute-start | bytes 786440 | tf_op jit(solution)/shard_map/ppermute | solution.py:274
  150.4 8.1 %collective-permute-start.14 = (f32[64,8,128]{2,1,0:T(8,128)S(1)}, f32[64,8,128]{2,1,0:T(8,128)S(1)}, u32[]{:S(2)}, u32[]{:S(2)}) collective-permute-start(f32[64,8,128]{2,1,0:T(8,128)S(1)} %bitcast.36), channel_id=1, source_target_pairs={{0,16},{8,24},{16,0},{24,8},{1,17},{9,25},{17,1},{25,9},{2,18},{10... | collective-permute-start | bytes 786440 | tf_op jit(solution)/shard_map/ppermute | solution.py:257
  158.5 2.0 %collective-permute-start.15 = (f32[2,64,8,128]{3,2,1,0:T(8,128)S(1)}, f32[2,64,8,128]{3,2,1,0:T(8,128)S(1)}, u32[]{:S(2)}, u32[]{:S(2)}) collective-permute-start(f32[2,64,8,128]{3,2,1,0:T(8,128)S(1)} %pad_maximum_fusion), channel_id=1, source_target_pairs={{0,8},{8,0},{16,24},{24,16},{1,9},{9,1},{17,25},{25,17},{2,10},{10... | collective-permute-start | bytes 1572872 | tf_op jit(solution)/shard_map/ppermute | solution.py:257
  160.6 1.0 copy-start.7

commit v3 on v1

v3 whole, which is shorter than its diff:
```python
import functools

import jax
import jax.numpy as jnp
from jax import lax
from jax.experimental import pallas as pl
from jax.experimental.pallas import tpu as pltpu
from jax.sharding import PartitionSpec as P

ITERS = 2
CORES = 2
VMEM = pl.BlockSpec(memory_space=pltpu.VMEM)
SMEM = pl.BlockSpec(memory_space=pltpu.SMEM)
PARAMS = pltpu.CompilerParams(vmem_limit_bytes=48 * 1024 * 1024)


def halves(value):
    high = value.astype(jnp.bfloat16)
    low = (value - high.astype(jnp.float32)).astype(jnp.bfloat16)
    return high, low


def resample_kernel(place_ref, weights_ref, offsets_ref, before_ref, raw_ref, after_ref, own_ref, far_ref, wide):
    weights = weights_ref[0]
    band, rows = weights.shape
    width = raw_ref.shape[3]
    weights = weights / jnp.sum(weights, axis=0, keepdims=True)
    first = offsets_ref[0]
    source = lax.broadcasted_iota(jnp.int32, (rows, rows), 0)
    matrix = jnp.zeros((rows, rows), jnp.float32)
    for k in range(band):
        matrix = jnp.where(source == first + k, weights[k : k + 1, :], matrix)
    matrix = matrix.T
    high = matrix.astype(jnp.bfloat16)
    rest = matrix - high.astype(jnp.float32)
    middle = rest.astype(jnp.bfloat16)
    low = (rest - middle.astype(jnp.float32)).astype(jnp.bfloat16)
    left = jnp.concatenate([high, middle, low], axis=1)

    def four_planes(ref, base, first_z):
        for pair in range(2):
            z = first_z + pair * 2
            planes = jnp.concatenate([ref[0, z], ref[0, z + 1]], axis=1)
            planes = jnp.concatenate([planes, planes, planes], axis=0)
            total = jnp.dot(left, planes, preferred_element_type=jnp.float32).astype(jnp.bfloat16)
            wide[base + z] = total[:, :width]
            wide[base + z + 1] = total[:, width:]

    rim, depth = before_ref.shape[1], raw_ref.shape[1]
    four_planes(before_ref, 0, 0)
    four_planes(after_ref, rim + depth, 0)

    def eight_planes(step, carry):
        four_planes(raw_ref, rim, step * 8)
        four_planes(raw_ref, rim, step * 8 + 4)
        return carry

    lax.fori_loop(0, depth // 8, eight_planes, 0)
    chip = place_ref[0]
    half = depth // 2
    for z in range(own_ref.shape[1]):
        own_ref[0, z] = wide[half * chip + z]
        far_ref[0, z] = wide[half * (1 - chip) + z]


def resample(place, weights, offsets, before, raw, after):
    views, depth, rows, width = raw.shape
    rim, band = before.shape[1], weights.shape[2]
    window = depth // 2 + 2 * rim
    block = lambda planes: pl.BlockSpec((1, planes, rows, width), lambda v: (v, 0, 0, 0))
    shape = jax.ShapeDtypeStruct((views, window, rows, width), jnp.bfloat16)
    return pl.pallas_call(
        resample_kernel,
        grid=(views,),
        out_shape=(shape, shape),
        in_specs=[
            SMEM,
            pl.BlockSpec((1, band, rows), lambda v: (v, 0, 0)),
            pl.BlockSpec((1, 1, rows), lambda v: (v, 0, 0)),
            block(rim),
            block(depth),
            block(rim),
        ],
        out_specs=(block(window), block(window)),
        scratch_shapes=[pltpu.VMEM((depth + 2 * rim, rows, width), jnp.bfloat16)],
        compiler_params=PARAMS,
    )(place, weights.transpose(0, 2, 1), offsets[:, None, :], before, raw, after)


def bands_kernel(taps_ref, out_ref):
    view = pl.program_id(0)
    count = taps_ref.shape[2]
    width = out_ref.shape[2] // 2
    shape = (width, width)
    shift = lax.broadcasted_iota(jnp.int32, shape, 0) - lax.broadcasted_iota(jnp.int32, shape, 1)
    for way in range(2):
        band = jnp.zeros(shape, jnp.float32)
        for t in range(count):
            at = t - count // 2
            band = jnp.where(shift == (-at if way else at), taps_ref[view, 2, t], band)
        high, low = halves(band)
        out_ref[0, way, :width, :width] = high
        out_ref[0, way, width:, :width] = high
        out_ref[0, way, :width, width:] = low
        out_ref[0, way, width:, width:] = jnp.zeros_like(low)


def bands(taps, width):
    views = taps.shape[0]
    return pl.pallas_call(
        bands_kernel,
        grid=(views,),
        out_shape=jax.ShapeDtypeStruct((views, 2, 2 * width, 2 * width), jnp.bfloat16),
        in_specs=[SMEM],
        out_specs=pl.BlockSpec((1, 2, 2 * width, 2 * width), lambda v: (v, 0, 0, 0)),
        compiler_params=PARAMS,
    )(taps)


def start_kernel(views, planes, place_ref, *refs):
    windows, start_ref = refs[:-1], refs[-1]
    step = pl.program_id(0)
    core = place_ref[1]
    for z in range(start_ref.shape[0]):
        total = windows[0][0, planes * core + z].astype(jnp.float32)
        for window in windows[1:]:
            total = total + window[0, planes * core + z].astype(jnp.float32)

        @pl.when(step == 0)
        def _():
            start_ref[z] = total

        @pl.when(step > 0)
        def _():
            start_ref[z] += total

    @pl.when(step == pl.num_programs(0) - 1)
    def _():
        start_ref[...] = start_ref[...] / views


def sum_views(place, windows, planes, rim):
    count, window, rows, width = windows[0].shape
    return pl.pallas_call(
        functools.partial(start_kernel, len(windows) * count, planes),
        grid=(count,),
        out_shape=jax.ShapeDtypeStruct((planes + 2 * rim, rows, width), jnp.float32),
        in_specs=[SMEM] + [pl.BlockSpec((1, window, rows, width), lambda v: (v, 0, 0, 0))] * len(windows),
        out_specs=VMEM,
        compiler_params=PARAMS,
    )(place, *windows)


def update_kernel(count, place_ref, taps_ref, *refs):
    bands_ref, windows, parts = refs[0], refs[1 : 1 + count], refs[1 + count : 4 + count]
    out_ref, wide, left, ratio, back, logs = refs[4 + count :]
    step = pl.program_id(0)
    taps = taps_ref.shape[2]
    rim = taps // 2
    planes, rows, width = out_ref.shape
    outer = planes + 2 * rim
    edge = 8
    volume = [(ref, z) for ref in parts for z in range(ref.shape[0])]

    @pl.when(step == 0)
    def _():
        logs[...] = jnp.zeros_like(logs)
        for scratch in (wide, back):
            depth = scratch.shape[0]
            scratch[:, :edge, :] = jnp.zeros((depth, edge, width), jnp.float32)
            scratch[:, edge + rows :, :] = jnp.zeros((depth, edge, width), jnp.float32)

    def correlate(gains, terms):
        total = gains[0] * terms[0]
        for t in range(1, taps):
            total = total + gains[t] * terms[t]
        return total

    def along_x(source, gains, z):
        for k in range(rows // 16):
            halved = []
            for half in range(2):
                first = edge - rim + 16 * k + 8 * half
                halved.append(correlate(gains, [source[z, pl.ds(first + t, 8), :] for t in range(taps)]))
            high, low = halves(jnp.concatenate(halved, axis=0))
            at = pl.ds(pl.multiple_of(z * rows + 16 * k, 16), 16)
            left[at, :width] = high
            left[at, width:] = low

    for group in range(count):
        view = group * pl.num_programs(0) + step
        gain_z = [taps_ref[view, 0, t] for t in range(taps)]
        gain_x = [taps_ref[view, 1, t] for t in range(taps)]

        def along_z(k, carry):
            row = pl.multiple_of(k * 8, 8)
            column = [ref[z, pl.ds(row, 8), :] for ref, z in volume]
            for z in range(outer):
                wide[z, pl.ds(row + edge, 8), :] = correlate(gain_z, column[z : z + taps])
            return carry

        lax.fori_loop(0, rows // 8, along_z, 0)

        def forward_x(z, carry):
            along_x(wide, gain_x, z)
            return carry

        lax.fori_loop(0, outer, forward_x, 0)

        product = jnp.dot(left[...], bands_ref[group, 0, 0], preferred_element_type=jnp.float32)
        blurred = (product[:, :width] + product[:, width:]).reshape(outer, rows, width)
        for z in range(outer):
            ratio[z] = windows[group][0, planes * place_ref[1] + z].astype(jnp.float32) / blurred[z]

        def back_z(k, carry):
            row = pl.multiple_of(k * 8, 8)
            column = [ratio[z, pl.ds(row, 8), :] for z in range(outer)]
            for z in range(planes):
                back[z, pl.ds(row + edge, 8), :] = correlate(gain_z[::-1], column[z : z + taps])
            return carry

        lax.fori_loop(0, rows // 8, back_z, 0)

        def back_x(z, carry):
            along_x(back, gain_x[::-1], z)
            return carry

        lax.fori_loop(0, planes, back_x, 0)

        product = jnp.dot(left[: planes * rows, :], bands_ref[group, 0, 1], preferred_element_type=jnp.float32)
        logs[...] += jnp.log(product[:, :width] + product[:, width:]).reshape(logs.shape)

    @pl.when(step == pl.num_programs(0) - 1)
    def _():
        for z in range(planes):
            ref, at = volume[2 * rim + z]
            out_ref[z] = ref[at] * jnp.exp(logs[z] / (count * pl.num_programs(0)))


def update(place, taps, band, windows, volume, planes):
    groups = len(windows)
    count, window, rows, width = windows[0].shape
    outer = planes + taps.shape[2] - 1
    band = band.reshape((groups, count) + band.shape[1:])
    return pl.pallas_call(
        functools.partial(update_kernel, groups),
        grid=(count,),
        out_shape=jax.ShapeDtypeStruct((planes, rows, width), jnp.float32),
        in_specs=[SMEM, SMEM, pl.BlockSpec((groups, 1) + band.shape[2:], lambda v: (0, v, 0, 0, 0))]
        + [pl.BlockSpec((1, window, rows, width), lambda v: (v, 0, 0, 0))] * groups
        + [VMEM] * 3,
        out_specs=VMEM,
        scratch_shapes=[
            pltpu.VMEM((outer, rows + 16, width), jnp.float32),
            pltpu.VMEM((outer * rows, 2 * width), jnp.bfloat16),
            pltpu.VMEM((outer, rows, width), jnp.float32),
            pltpu.VMEM((planes, rows + 16, width), jnp.float32),
            pltpu.VMEM((planes, rows, width), jnp.float32),
        ],
        compiler_params=PARAMS,
    )(place, taps, band, *windows, *volume)


def partner(value, bit, members):
    return lax.ppermute(value, "view", [(i, i ^ bit) for i in range(members)])


def z_rims(own, inner, outer, members, blocks):
    planes = own.shape[0]
    axes = ("view", "vol")
    at = lambda line: (line % members) * blocks + line // members
    total = members * blocks
    before, after = [], []
    for hop in range(inner // planes + 1, -(-outer // planes) + 1):
        near, far = max((hop - 1) * planes, inner), min(hop * planes, outer)
        up = [(at(i), at(i + hop)) for i in range(total - hop)]
        down = [(at(i + hop), at(i)) for i in range(total - hop)]
        before.append(lax.ppermute(own[hop * planes - far : hop * planes - near], axes, up))
        after.append(lax.ppermute(own[near - (hop - 1) * planes : far - (hop - 1) * planes], axes, down))
    join = lambda parts: parts[0] if len(parts) == 1 else jnp.concatenate(parts)
    return join(before[::-1]), join(after)


def per_device(raw_views, weights, offsets, psf_taps):
    views, depth, rows, width = raw_views.shape
    members, blocks = lax.axis_size("view"), lax.axis_size("vol")
    rim = (psf_taps.shape[2] - 1) // 2
    planes = depth // members
    me = lax.axis_index("view")
    place = jnp.stack([me // CORES, me % CORES]).astype(jnp.int32)

    up = [(i, i + 1) for i in range(blocks - 1)]
    down = [(i + 1, i) for i in range(blocks - 1)]
    raw_before = lax.ppermute(raw_views[:, depth - rim :], "vol", up)
    raw_after = lax.ppermute(raw_views[:, :rim], "vol", down)
    all_taps = [psf_taps] + [partner(psf_taps, bit, members) for bit in range(1, members)]
    own, far = resample(place, weights, offsets, raw_before, raw_views, raw_after)
    own, far, all_taps = lax.optimization_barrier((own, far, all_taps))
    far = partner(far, 2, members)
    near = partner(own, 1, members)
    all_taps = jnp.concatenate(all_taps)
    all_taps = all_taps / jnp.sum(all_taps, axis=-1, keepdims=True)
    far, band = lax.optimization_barrier((far, bands(all_taps, width)))
    windows = [own, near, far, partner(far, 1, members)]
    start = sum_views(place, windows, planes, rim)
    before, after = z_rims(start[rim : rim + planes], rim, 2 * rim, members, blocks)
    joined = update(place, all_taps, band, windows, (before, start, after), planes)
    for turn in range(1, ITERS):
        before, after = z_rims(joined, 0, 2 * rim, members, blocks)
        joined = update(place, all_taps, band, windows, (before, joined, after), planes)

    columns = lax.all_to_all(joined, "vol", split_axis=1, concat_axis=0, tiled=True)
    far = partner(columns, 2, members)
    near = partner(columns, 1, members)
    parts = [columns, near, far, partner(far, 1, members)]
    width_x = columns.shape[1]
    result = jnp.zeros((blocks, members, planes, width_x, width), jnp.float32)
    for k in range(members):
        piece = parts[k].reshape(blocks, 1, planes, width_x, width)
        result = lax.dynamic_update_slice(result, piece, (0, me ^ k, 0, 0, 0))
    return result.reshape(blocks * depth, width_x, width)


def solution(mesh):
    placed = (
        P("view", "vol", None, None),
        P("view", None, None),
        P("view", None),
        P("view", None, None),
    )
    return jax.shard_map(
        per_device, mesh=mesh, in_specs=placed, out_specs=P(None, "vol", None), check_vma=False
    )
```

time: 174 us -> 153 us (0.88)
  Pallas kernels: 68.7 us -> 60 us
  blocking collectives: 31.9 us -> 23.6 us
  waiting for transfers between devices: 46.2 us -> 41 us
  starting transfers between devices: 16.8 us -> 20.3 us
    all_gather x1 -> x0, blocking collectives: 9.78 us -> none  [per_device(): all_taps = lax.all_gather(psf_taps, 'view')]
    pallas_call x5 -> x4, Pallas kernels: 66.3 us -> 57.6 us  [the longest x2 52.2 us: update(): pl.pallas_call(functools.partial(update_kernel, groups), grid=(count,), o...]
    ppermute x8 -> x9, waiting for transfers between devices: 36 us -> 31.7 us  [partner(): return lax.ppermute(value, 'view', [(i, i ^ bit) for i in range(members)])]
    ppermute x6, starting transfers between devices: 12.1 us -> 16.3 us  [the longest x2 7.51 us: z_rims(): lax.ppermute(own[hop * planes - far:hop * planes - near], axes, up)]
    unnamed x15 -> x13, local copies, waits for them, and re-layouts: 6.38 us -> 4.75 us
    ppermute x8 -> x9, starting transfers between devices: 4.71 us -> 4.07 us  [partner(): return lax.ppermute(value, 'view', [(i, i ^ bit) for i in range(members)])]
  transfers between devices with their start and end apart: 14 -> 15, of which waited for: 7 -> 8; matrix products, arithmetic and copies ran while one was open for 1% -> 1% of each run, Pallas kernels for 3% -> 4%
where the time goes in v3:
time: 153 us; the launch traced here: 152 us
  Pallas kernels  60 us (39%)
  waiting for transfers between devices  41 us (27%)
  blocking collectives  23.6 us (15%)
  starting transfers between devices  20.3 us (13%)
  local copies, waits for them, and re-layouts  6.96 us (5%)
    pallas_call x2, Pallas kernels, update(): pl.pallas_call(functools.partial(update_kernel, groups), grid=(count,), o...  52.2 us
    ppermute x9, waiting for transfers between devices, partner(): return lax.ppermute(value, 'view', [(i, i ^ bit) for i in range(members)])  31.7 us
    all_to_all x1, blocking collectives, per_device(): lax.all_to_all(joined, 'vol', split_axis=1, concat_axis=0, tiled=True)  23.6 us
    ppermute x2, starting transfers between devices, z_rims(): lax.ppermute(own[hop * planes - far:hop * planes - near], axes, up)  7.51 us
    ppermute x2, waiting for transfers between devices, z_rims(): lax.ppermute(own[near - (hop - 1) * planes:far - (hop - 1) * planes], axe...  5.02 us
    ppermute x1, starting transfers between devices, per_device(): raw_before = lax.ppermute(raw_views[:, depth - rim:], 'vol', up)  4.88 us
    unnamed x13, local copies, waits for them, and re-layouts  4.75 us
    ppermute x1, waiting for transfers between devices, per_device(): raw_after = lax.ppermute(raw_views[:, :rim], 'vol', down)  4.07 us
  transfers between devices with their start and end apart: 15, of which 8 were waited for; matrix products, arithmetic and copies ran while one was open for 1% of the time, Pallas kernels for 4%

profile of v3, /device:TPU:0, one launch (start us, length us, event | category | flops | bytes accessed | tf_op | source)
XLA Modules:
  0.0 152.3 jit_solution(14497644015643216995)
XLA Ops:
  0.0 1.0 fusion.2
  1.1 0.0 copy-start.4
  1.1 4.9 %collective-permute-start = (bf16[3,4,64,128]{3,2,1,0:T(8,128)(2,1)S(1)}, bf16[3,4,64,128]{3,2,1,0:T(8,128)(2,1)S(1)}, u32[]{:S(2)}, u32[]{:S(2)}) collective-permute-start(bf16[3,4,64,128]{3,2,1,0:T(8,128)(2,1)S(1)} %get-tuple-element.26), channel_id=1, source_target_pairs={{0,1},{1,2},{2,3},{3,4},{4,5},{5,6},{6,7},{8,9},{9,10},{10,11},{11... | collective-permute-start | bytes 589832 | tf_op jit(solution)/shard_map/ppermute | solution.py:294
  6.0 1.3 collective-permute-start.1
  7.3 0.1 collective-permute-start.2
  7.3 1.6 %collective-permute-start.3 = (f32[3,3,9]{2,1,0:T(4,128)}, f32[3,3,9]{2,1,0:T(4,128)S(1)}, u32[]{:S(2)}, u32[]{:S(2)}) collective-permute-start(f32[3,3,9]{2,1,0:T(4,128)} %param.7), channel_id=1, source_target_pairs={{0,16},{8,24},{16,0},{24,8},{1,17},{9,25},{17,1},{25,9},{2,18},{10... | collective-permute-start | bytes 980 | tf_op jit(solution)/shard_map/ppermute | solution.py:265
  8.9 0.3 collective-permute-start.4
  9.2 0.1 pad_add_fusion.place_ref
  9.3 0.7 broadcast_in_dim.8.offsets_ref
  10.0 0.2 collective-permute-done.before_ref
  10.1 4.1 %collective-permute-done.1.after_ref = bf16[3,4,64,128]{3,2,1,0:T(8,128)(2,1)S(1)} collective-permute-done((bf16[3,4,64,128]{3,2,1,0:T(8,128)(2,1)S(1)}, bf16[3,4,64,128]{3,2,1,0:T(8,128)(2,1)S(1)}, u32[]{:S(2)}, u32[]{:S(2)}) %collective-permute-start.1) | collective-permute-done | bytes 196640 | tf_op jit(solution)/shard_map/ppermute | solution.py:295
  14.2 0.0 copy-start.1
  14.2 1.4 copy-done.1
  15.6 0.0 copy-start.2
  15.6 0.7 copy-done.2
  16.3 4.1 %shard_map.46 = (bf16[3,24,64,128]{3,2,1,0:T(8,128)(2,1)S(1)}, bf16[3,24,64,128]{3,2,1,0:T(8,128)(2,1)S(1)}) custom-call(s32[2]{0:T(128)S(1)} %pad_add_fusion.place_ref, f32[3,8,64]{2,1,0:T(8,128)S(1)} %bitcast.26, s32[3,1,64]{2,1,0:T(1,128)S(1)} %broadcast_in_dim.8.offsets_ref, bf16[3,4,64,128]{3,2,1,0:T(8,128)(2,1)S(1)} %collective-permute-done.before_ref, ...), custom_call_target="tpu_custom_call" | custom-call | tf_op jit(solution)/shard_map/pallas_call | solution.py:72
  20.4 0.0 collective-permute-done.2
  20.4 0.0 collective-permute-done.3
  20.4 0.0 collective-permute-done.4
  20.4 1.6 %collective-permute-start.5 = (bf16[3,24,64,128]{3,2,1,0:T(8,128)(2,1)S(1)}, bf16[3,24,64,128]{3,2,1,0:T(8,128)(2,1)S(1)}, u32[]{:S(2)}, u32[]{:S(2)}) collective-permute-start(bf16[3,24,64,128]{3,2,1,0:T(8,128)(2,1)S(1)} %get-tuple-element.21), channel_id=1, source_target_pairs={{0,16},{8,24},{16,0},{24,8},{1,17},{9,25},{17,1},{25,9},{2,18},{10... | collective-permute-start | bytes 3538952 | tf_op jit(solution)/shard_map/ppermute | solution.py:265
  22.0 0.0 copy-done.4
  22.0 0.1 fusion.1.taps_ref
  22.1 2.4 %shard_map.47 = bf16[12,2,256,256]{3,2,1,0:T(8,128)(2,1)S(1)} custom-call(f32[12,3,9]{2,1,0:T(4,128)S(1)} %fusion.1.taps_ref), custom_call_target="tpu_custom_call" | custom-call | tf_op jit(solution)/shard_map/pallas_call | solution.py:110
  24.5 0.0 copy-start
  24.5 1.6 %copy-done = bf16[12,2,256,256]{3,2,1,0:T(8,128)(2,1)} copy-done((bf16[12,2,256,256]{3,2,1,0:T(8,128)(2,1)}, bf16[12,2,256,256]{3,2,1,0:T(8,128)(2,1)S(1)}, u32[]{:S(2)}) %copy-start) | copy-done | bytes 3145752
  26.2 0.0 collective-permute-start.6
  26.2 20.8 %collective-permute-done.5.refs_2_.refs_3_ = bf16[3,24,64,128]{3,2,1,0:T(8,128)(2,1)S(1)} collective-permute-done((bf16[3,24,64,128]{3,2,1,0:T(8,128)(2,1)S(1)}, bf16[3,24,64,128]{3,2,1,0:T(8,128)(2,1)S(1)}, u32[]{:S(2)}, u32[]{:S(2)}) %collective-permute-start.5) | collective-permute-done | bytes 1179680 | tf_op jit(solution)/shard_map/ppermute | solution.py:265
  47.0 0.0 collective-permute-start.7
  47.0 0.0 collective-permute-done.6.refs_1_.refs_2_
  47.0 2.8 %collective-permute-done.7.refs_3_.refs_4_ = bf16[3,24,64,128]{3,2,1,0:T(8,128)(2,1)S(1)} collective-permute-done((bf16[3,24,64,128]{3,2,1,0:T(8,128)(2,1)S(1)}, bf16[3,24,64,128]{3,2,1,0:T(8,128)(2,1)S(1)}, u32[]{:S(2)}, u32[]{:S(2)}) %collective-permute-start.7) | collective-permute-done | bytes 1179680 | tf_op jit(solution)/shard_map/ppermute | solution.py:265
  49.9 1.3 shard_map.48.refs_6_
  51.2 2.0 %collective-permute-start.8 = (f32[4,64,128]{2,1,0:T(8,128)S(1)}, f32[4,64,128]{2,1,0:T(8,128)S(1)}, u32[]{:S(2)}, u32[]{:S(2)}) collective-permute-start(f32[4,64,128]{2,1,0:T(8,128)S(1)} %get-tuple-element.28), channel_id=1, source_target_pairs={{0,8},{8,16},{16,24},{24,1},{1,9},{9,17},{17,25},{25,2},{2,10},{10... | collective-permute-start | bytes 393224 | tf_op jit(solution)/shard_map/ppermute | solution.py:278
  53.3 1.3 collective-permute-start.9
  54.6 0.0 collective-permute-done.8.refs_5_
  54.6 2.9 %collective-permute-done.9.refs_7_ = f32[4,64,128]{2,1,0:T(8,128)S(1)} collective-permute-done((f32[4,64,128]{2,1,0:T(8,128)S(1)}, f32[4,64,128]{2,1,0:T(8,128)S(1)}, u32[]{:S(2)}, u32[]{:S(2)}) %collective-permute-start.9) | collective-permute-done | bytes 131104 | tf_op jit(solution)/shard_map/ppermute | solution.py:279
  57.5 26.1 %shard_map.49.refs_6_ = f32[8,64,128]{2,1,0:T(8,128)S(1)} custom-call(s32[2]{0:T(128)S(1)} %pad_add_fusion.place_ref, f32[12,3,9]{2,1,0:T(4,128)S(1)} %fusion.1.taps_ref, bf16[4,3,2,256,256]{4,3,2,1,0:T(8,128)(2,1)} %bitcast.24, bf16[3,24,64,128]{3,2,1,0:T(8,128)(2,1)S(1)} %get-tuple-element.23.refs_0_.refs_1_, ...), custom_call_target="tpu_custom_call" | custom-call | tf_op jit(solution)/shard_map/pallas_call | solution.py:245
  83.6 5.5 %collective-permute-start.10 = (f32[8,64,128]{2,1,0:T(8,128)S(1)}, f32[8,64,128]{2,1,0:T(8,128)S(1)}, u32[]{:S(2)}, u32[]{:S(2)}) collective-permute-start(f32[8,64,128]{2,1,0:T(8,128)S(1)} %shard_map.49.refs_6_), channel_id=1, source_target_pairs={{0,8},{8,16},{16,24},{24,1},{1,9},{9,17},{17,25},{25,2},{2,10},{10... | collective-permute-start | bytes 786440 | tf_op jit(solution)/shard_map/ppermute | solution.py:278
  89.1 1.3 collective-permute-start.11
  90.4 0.0 collective-permute-done.10.refs_5_
  90.4 2.1 %collective-permute-done.11.refs_7_ = f32[8,64,128]{2,1,0:T(8,128)S(1)} collective-permute-done((f32[8,64,128]{2,1,0:T(8,128)S(1)}, f32[8,64,128]{2,1,0:T(8,128)S(1)}, u32[]{:S(2)}, u32[]{:S(2)}) %collective-permute-start.11) | collective-permute-done | bytes 262176 | tf_op jit(solution)/shard_map/ppermute | solution.py:279
  92.5 26.1 %shard_map.50 = f32[8,64,128]{2,1,0:T(8,128)S(1)} custom-call(s32[2]{0:T(128)S(1)} %pad_add_fusion.place_ref, f32[12,3,9]{2,1,0:T(4,128)S(1)} %fusion.1.taps_ref, bf16[4,3,2,256,256]{4,3,2,1,0:T(8,128)(2,1)} %bitcast.25, bf16[3,24,64,128]{3,2,1,0:T(8,128)(2,1)S(1)} %get-tuple-element.23.refs_0_.refs_1_, ...), custom_call_target="tpu_custom_call" | custom-call | tf_op jit(solution)/shard_map/pallas_call | solution.py:245
  118.6 0.2 copy.16
  118.8 23.6 %all_to_all.18 = f32[8,64,128]{2,0,1:T(8,128)S(1)} all-to-all(f32[8,64,128]{2,0,1:T(8,128)S(1)} %copy.16), channel_id=1, replica_groups=mesh['view'=4,'vol'=8] {'vol'}, dimensions={1} | all-to-all | bytes 524288 | tf_op jit(solution)/shard_map/all_to_all | solution.py:312
  142.5 0.1 collective-permute-start.13
  142.5 0.5 collective-permute-start.12
  143.0 6.8 %collective-permute-done.13 = f32[64,8,128]{2,1,0:T(8,128)S(1)} collective-permute-done((f32[64,8,128]{2,1,0:T(8,128)S(1)}, f32[64,8,128]{2,1,0:T(8,128)S(1)}, u32[]{:S(2)}, u32[]{:S(2)}) %collective-permute-start.13) | collective-permute-done | bytes 262176 | tf_op jit(solution)/shard_map/ppermute | solution.py:265
  149.8 0.0 collective-permute-start.14
  149.8 0.1 broadcast_in_dim.7
  149.9 0.1 copy_dynamic-update-slice_fusion
  150.0 0.0 collective-permute-done.12
  150.1 1.3 collective-permute-done.14
  151.3 0.0 copy-start.3
  151.4 1.0 copy-done.3
  (9 shorter events, 0.2 us)
Async XLA Ops:
  1.1 20.9 %copy-start.4 = (f32[3,3,9]{2,1,0:T(4,128)S(1)}, f32[3,3,9]{2,1,0:T(4,128)}, u32[]{:S(2)}) copy-start(f32[3,3,9]{2,1,0:T(4,128)} %param.7) | copy-start | bytes 976
  1.1 9.1 %collective-permute-start = (bf16[3,4,64,128]{3,2,1,0:T(8,128)(2,1)S(1)}, bf16[3,4,64,128]{3,2,1,0:T(8,128)(2,1)S(1)}, u32[]{:S(2)}, u32[]{:S(2)}) collective-permute-start(bf16[3,4,64,128]{3,2,1,0:T(8,128)(2,1)S(1)} %get-tuple-element.26), channel_id=1, source_target_pairs={{0,1},{1,2},{2,3},{3,4},{4,5},{5,6},{6,7},{8,9},{9,10},{10,11},{11... | collective-permute-start | bytes 589832 | tf_op jit(solution)/shard_map/ppermute | solution.py:294
  6.0 8.3 %collective-permute-start.1 = (bf16[3,4,64,128]{3,2,1,0:T(8,128)(2,1)S(1)}, bf16[3,4,64,128]{3,2,1,0:T(8,128)(2,1)S(1)}, u32[]{:S(2)}, u32[]{:S(2)}) collective-permute-start(bf16[3,4,64,128]{3,2,1,0:T(8,128)(2,1)S(1)} %get-tuple-element.25), channel_id=1, source_target_pairs={{1,0},{2,1},{3,2},{4,3},{5,4},{6,5},{7,6},{9,8},{10,9},{11,10},{12... | collective-permute-start | bytes 589832 | tf_op jit(solution)/shard_map/ppermute | solution.py:295
  7.3 13.1 %collective-permute-start.2 = (f32[3,3,9]{2,1,0:T(4,128)}, f32[3,3,9]{2,1,0:T(4,128)S(1)}, u32[]{:S(2)}, u32[]{:S(2)}) collective-permute-start(f32[3,3,9]{2,1,0:T(4,128)} %param.7), channel_id=1, source_target_pairs={{0,8},{8,0},{16,24},{24,16},{1,9},{9,1},{17,25},{25,17},{2,10},{10... | collective-permute-start | bytes 980 | tf_op jit(solution)/shard_map/ppermute | solution.py:265
  7.3 13.1 %collective-permute-start.3 = (f32[3,3,9]{2,1,0:T(4,128)}, f32[3,3,9]{2,1,0:T(4,128)S(1)}, u32[]{:S(2)}, u32[]{:S(2)}) collective-permute-start(f32[3,3,9]{2,1,0:T(4,128)} %param.7), channel_id=1, source_target_pairs={{0,16},{8,24},{16,0},{24,8},{1,17},{9,25},{17,1},{25,9},{2,18},{10... | collective-permute-start | bytes 980 | tf_op jit(solution)/shard_map/ppermute | solution.py:265
  8.9 11.5 %collective-permute-start.4 = (f32[3,3,9]{2,1,0:T(4,128)}, f32[3,3,9]{2,1,0:T(4,128)S(1)}, u32[]{:S(2)}, u32[]{:S(2)}) collective-permute-start(f32[3,3,9]{2,1,0:T(4,128)} %param.7), channel_id=1, source_target_pairs={{0,24},{8,16},{16,8},{24,0},{1,25},{9,17},{17,9},{25,1},{2,26},{10... | collective-permute-start | bytes 980 | tf_op jit(solution)/shard_map/ppermute | solution.py:265
  14.2 1.4 copy-start.1
  15.6 0.7 copy-start.2
  20.4 26.6 %collective-permute-start.5 = (bf16[3,24,64,128]{3,2,1,0:T(8,128)(2,1)S(1)}, bf16[3,24,64,128]{3,2,1,0:T(8,128)(2,1)S(1)}, u32[]{:S(2)}, u32[]{:S(2)}) collective-permute-start(bf16[3,24,64,128]{3,2,1,0:T(8,128)(2,1)S(1)} %get-tuple-element.21), channel_id=1, source_target_pairs={{0,16},{8,24},{16,0},{24,8},{1,17},{9,25},{17,1},{25,9},{2,18},{10... | collective-permute-start | bytes 3538952 | tf_op jit(solution)/shard_map/ppermute | solution.py:265
  24.5 1.7 %copy-start = (bf16[12,2,256,256]{3,2,1,0:T(8,128)(2,1)}, bf16[12,2,256,256]{3,2,1,0:T(8,128)(2,1)S(1)}, u32[]{:S(2)}) copy-start(bf16[12,2,256,256]{3,2,1,0:T(8,128)(2,1)S(1)} %shard_map.47) | copy-start | bytes 9437188
  26.2 20.8 %collective-permute-start.6 = (bf16[3,24,64,128]{3,2,1,0:T(8,128)(2,1)S(1)}, bf16[3,24,64,128]{3,2,1,0:T(8,128)(2,1)S(1)}, u32[]{:S(2)}, u32[]{:S(2)}) collective-permute-start(bf16[3,24,64,128]{3,2,1,0:T(8,128)(2,1)S(1)} %get-tuple-element.23.refs_0_.refs_1_), channel_id=1, source_target_pairs={{0,8},{8,0},{16,24},{24,16},{1,9},{9,1},{17,25},{25,17},{2,10},{10... | collective-permute-start | bytes 3538952 | tf_op jit(solution)/shard_map/ppermute | solution.py:265
  47.0 2.8 %collective-permute-start.7 = (bf16[3,24,64,128]{3,2,1,0:T(8,128)(2,1)S(1)}, bf16[3,24,64,128]{3,2,1,0:T(8,128)(2,1)S(1)}, u32[]{:S(2)}, u32[]{:S(2)}) collective-permute-start(bf16[3,24,64,128]{3,2,1,0:T(8,128)(2,1)S(1)} %collective-permute-done.5.refs_2_.refs_3_), channel_id=1, source_target_pairs={{0,8},{8,0},{16,24},{24,16},{1,9},{9,1},{17,25},{25,17},{2,10},{10... | collective-permute-start | bytes 3538952 | tf_op jit(solution)/shard_map/ppermute | solution.py:265
  51.2 3.4 %collective-permute-start.8 = (f32[4,64,128]{2,1,0:T(8,128)S(1)}, f32[4,64,128]{2,1,0:T(8,128)S(1)}, u32[]{:S(2)}, u32[]{:S(2)}) collective-permute-start(f32[4,64,128]{2,1,0:T(8,128)S(1)} %get-tuple-element.28), channel_id=1, source_target_pairs={{0,8},{8,16},{16,24},{24,1},{1,9},{9,17},{17,25},{25,2},{2,10},{10... | collective-permute-start | bytes 393224 | tf_op jit(solution)/shard_map/ppermute | solution.py:278
  53.3 4.2 %collective-permute-start.9 = (f32[4,64,128]{2,1,0:T(8,128)S(1)}, f32[4,64,128]{2,1,0:T(8,128)S(1)}, u32[]{:S(2)}, u32[]{:S(2)}) collective-permute-start(f32[4,64,128]{2,1,0:T(8,128)S(1)} %get-tuple-element.27), channel_id=1, source_target_pairs={{8,0},{16,8},{24,16},{1,24},{9,1},{17,9},{25,17},{2,25},{10,2},{18... | collective-permute-start | bytes 393224 | tf_op jit(solution)/shard_map/ppermute | solution.py:279
  83.6 6.8 %collective-permute-start.10 = (f32[8,64,128]{2,1,0:T(8,128)S(1)}, f32[8,64,128]{2,1,0:T(8,128)S(1)}, u32[]{:S(2)}, u32[]{:S(2)}) collective-permute-start(f32[8,64,128]{2,1,0:T(8,128)S(1)} %shard_map.49.refs_6_), channel_id=1, source_target_pairs={{0,8},{8,16},{16,24},{24,1},{1,9},{9,17},{17,25},{25,2},{2,10},{10... | collective-permute-start | bytes 786440 | tf_op jit(solution)/shard_map/ppermute | solution.py:278
  89.1 3.4 %collective-permute-start.11 = (f32[8,64,128]{2,1,0:T(8,128)S(1)}, f32[8,64,128]{2,1,0:T(8,128)S(1)}, u32[]{:S(2)}, u32[]{:S(2)}) collective-permute-start(f32[8,64,128]{2,1,0:T(8,128)S(1)} %shard_map.49.refs_6_), channel_id=1, source_target_pairs={{8,0},{16,8},{24,16},{1,24},{9,1},{17,9},{25,17},{2,25},{10,2},{18... | collective-permute-start | bytes 786440 | tf_op jit(solution)/shard_map/ppermute | solution.py:279
  142.5 7.3 %collective-permute-start.13 = (f32[64,8,128]{2,1,0:T(8,128)S(1)}, f32[64,8,128]{2,1,0:T(8,128)S(1)}, u32[]{:S(2)}, u32[]{:S(2)}) collective-permute-start(f32[64,8,128]{2,1,0:T(8,128)S(1)} %bitcast.31), channel_id=1, source_target_pairs={{0,16},{8,24},{16,0},{24,8},{1,17},{9,25},{17,1},{25,9},{2,18},{10... | collective-permute-start | bytes 786440 | tf_op jit(solution)/shard_map/ppermute | solution.py:265
  142.5 7.4 %collective-permute-start.12 = (f32[64,8,128]{2,1,0:T(8,128)S(1)}, f32[64,8,128]{2,1,0:T(8,128)S(1)}, u32[]{:S(2)}, u32[]{:S(2)}) collective-permute-start(f32[64,8,128]{2,1,0:T(8,128)S(1)} %bitcast.32), channel_id=1, source_target_pairs={{0,8},{8,0},{16,24},{24,16},{1,9},{9,1},{17,25},{25,17},{2,10},{10... | collective-permute-start | bytes 786440 | tf_op jit(solution)/shard_map/ppermute | solution.py:265
  149.8 1.5 %collective-permute-start.14 = (f32[64,8,128]{2,1,0:T(8,128)S(1)}, f32[64,8,128]{2,1,0:T(8,128)S(1)}, u32[]{:S(2)}, u32[]{:S(2)}) collective-permute-start(f32[64,8,128]{2,1,0:T(8,128)S(1)} %collective-permute-done.13), channel_id=1, source_target_pairs={{0,8},{8,0},{16,24},{24,16},{1,9},{9,1},{17,25},{25,17},{2,10},{10... | collective-permute-start | bytes 786440 | tf_op jit(solution)/shard_map/ppermute | solution.py:265
  151.3 1.0 copy-start.3

commit v4 on v3

--- a/solution.py
+++ b/solution.py
@@ -20,10 +20,11 @@
     return high, low
 
 
-def resample_kernel(place_ref, weights_ref, offsets_ref, before_ref, raw_ref, after_ref, own_ref, far_ref, wide):
+def resample_kernel(place_ref, weights_ref, offsets_ref, *refs):
+    sources, (own_ref, far_ref, wide) = refs[:-3], refs[-3:]
     weights = weights_ref[0]
     band, rows = weights.shape
-    width = raw_ref.shape[3]
+    width = wide.shape[2]
     weights = weights / jnp.sum(weights, axis=0, keepdims=True)
     first = offsets_ref[0]
     source = lax.broadcasted_iota(jnp.int32, (rows, rows), 0)
@@ -46,29 +47,35 @@
             wide[base + z] = total[:, :width]
             wide[base + z + 1] = total[:, width:]
 
-    rim, depth = before_ref.shape[1], raw_ref.shape[1]
-    four_planes(before_ref, 0, 0)
-    four_planes(after_ref, rim + depth, 0)
-
-    def eight_planes(step, carry):
-        four_planes(raw_ref, rim, step * 8)
-        four_planes(raw_ref, rim, step * 8 + 4)
-        return carry
-
-    lax.fori_loop(0, depth // 8, eight_planes, 0)
+    base = 0
+    for ref in sources:
+        depth = ref.shape[1]
+        if depth % 8:
+            for z in range(0, depth, 4):
+                four_planes(ref, base, z)
+        else:
+
+            def eight_planes(step, carry, ref=ref, base=base):
+                four_planes(ref, base, step * 8)
+                four_planes(ref, base, step * 8 + 4)
+                return carry
+
+            lax.fori_loop(0, depth // 8, eight_planes, 0)
+        base += depth
     chip = place_ref[0]
-    half = depth // 2
-    for z in range(own_ref.shape[1]):
-        own_ref[0, z] = wide[half * chip + z]
-        far_ref[0, z] = wide[half * (1 - chip) + z]
-
-
-def resample(place, weights, offsets, before, raw, after):
-    views, depth, rows, width = raw.shape
-    rim, band = before.shape[1], weights.shape[2]
-    window = depth // 2 + 2 * rim
+    count = own_ref.shape[1]
+    step = base - count
+    for z in range(count):
+        own_ref[0, z] = wide[step * chip + z]
+        far_ref[0, z] = wide[step * (1 - chip) + z]
+
+
+def resample(place, weights, offsets, sources, count):
+    views, _, rows, width = sources[0].shape
+    band = weights.shape[2]
+    depths = [source.shape[1] for source in sources]
     block = lambda planes: pl.BlockSpec((1, planes, rows, width), lambda v: (v, 0, 0, 0))
-    shape = jax.ShapeDtypeStruct((views, window, rows, width), jnp.bfloat16)
+    shape = jax.ShapeDtypeStruct((views, count, rows, width), jnp.bfloat16)
     return pl.pallas_call(
         resample_kernel,
         grid=(views,),
@@ -77,14 +84,12 @@
             SMEM,
             pl.BlockSpec((1, band, rows), lambda v: (v, 0, 0)),
             pl.BlockSpec((1, 1, rows), lambda v: (v, 0, 0)),
-            block(rim),
-            block(depth),
-            block(rim),
-        ],
-        out_specs=(block(window), block(window)),
-        scratch_shapes=[pltpu.VMEM((depth + 2 * rim, rows, width), jnp.bfloat16)],
+        ]
+        + [block(depth) for depth in depths],
+        out_specs=(block(count), block(count)),
+        scratch_shapes=[pltpu.VMEM((sum(depths), rows, width), jnp.bfloat16)],
         compiler_params=PARAMS,
-    )(place, weights.transpose(0, 2, 1), offsets[:, None, :], before, raw, after)
+    )(place, weights.transpose(0, 2, 1), offsets[:, None, :], *sources)
 
 
 def bands_kernel(taps_ref, out_ref):
@@ -117,14 +122,28 @@
     )(taps)
 
 
+def window_plane(place_ref, main_ref, rim_ref, planes, z):
+    chip, core = place_ref[0], place_ref[1]
+    rim, main = rim_ref.shape[1], main_ref.shape[1]
+    at = planes * core + z
+    inside = jnp.clip(at - rim * (1 - chip), 0, main - 1)
+    value = main_ref[0, inside].astype(jnp.float32)
+    if rim <= z < rim + planes:
+        return value
+    edge = at - main * chip
+    outside = (edge >= 0) & (edge < rim)
+    other = rim_ref[0, jnp.clip(edge, 0, rim - 1)].astype(jnp.float32)
+    return jnp.where(outside, other, value)
+
+
 def start_kernel(views, planes, place_ref, *refs):
-    windows, start_ref = refs[:-1], refs[-1]
+    count = len(refs) // 2
+    windows, start_ref = list(zip(refs[:count], refs[count:-1])), refs[-1]
     step = pl.program_id(0)
-    core = place_ref[1]
     for z in range(start_ref.shape[0]):
-        total = windows[0][0, planes * core + z].astype(jnp.float32)
+        total = window_plane(place_ref, *windows[0], planes, z)
         for window in windows[1:]:
-            total = total + window[0, planes * core + z].astype(jnp.float32)
+            total = total + window_plane(place_ref, *window, planes, z)
 
         @pl.when(step == 0)
         def _():
@@ -139,21 +158,27 @@
         start_ref[...] = start_ref[...] / views
 
 
-def sum_views(place, windows, planes, rim):
-    count, window, rows, width = windows[0].shape
+def window_specs(mains, rims):
+    return [pl.BlockSpec((1,) + part.shape[1:], lambda v: (v, 0, 0, 0)) for part in mains + rims]
+
+
+def sum_views(place, mains, rims, planes):
+    count, _, rows, width = mains[0].shape
+    rim = rims[0].shape[1]
     return pl.pallas_call(
-        functools.partial(start_kernel, len(windows) * count, planes),
+        functools.partial(start_kernel, len(mains) * count, planes),
         grid=(count,),
         out_shape=jax.ShapeDtypeStruct((planes + 2 * rim, rows, width), jnp.float32),
-        in_specs=[SMEM] + [pl.BlockSpec((1, window, rows, width), lambda v: (v, 0, 0, 0))] * len(windows),
+        in_specs=[SMEM] + window_specs(mains, rims),
         out_specs=VMEM,
         compiler_params=PARAMS,
-    )(place, *windows)
+    )(place, *mains, *rims)
 
 
 def update_kernel(count, place_ref, taps_ref, *refs):
-    bands_ref, windows, parts = refs[0], refs[1 : 1 + count], refs[1 + count : 4 + count]
-    out_ref, wide, left, ratio, back, logs = refs[4 + count :]
+    bands_ref, windows = refs[0], list(zip(refs[1 : 1 + count], refs[1 + count : 1 + 2 * count]))
+    parts = refs[1 + 2 * count : 4 + 2 * count]
+    out_ref, wide, left, ratio, back, logs = refs[4 + 2 * count :]
     step = pl.program_id(0)
     taps = taps_ref.shape[2]
     rim = taps // 2
@@ -210,7 +235,7 @@
         product = jnp.dot(left[...], bands_ref[group, 0, 0], preferred_element_type=jnp.float32)
         blurred = (product[:, :width] + product[:, width:]).reshape(outer, rows, width)
         for z in range(outer):
-            ratio[z] = windows[group][0, planes * place_ref[1] + z].astype(jnp.float32) / blurred[z]
+            ratio[z] = window_plane(place_ref, *windows[group], planes, z) / blurred[z]
 
         def back_z(k, carry):
             row = pl.multiple_of(k * 8, 8)
@@ -237,9 +262,9 @@
             out_ref[z] = ref[at] * jnp.exp(logs[z] / (count * pl.num_programs(0)))
 
 
-def update(place, taps, band, windows, volume, planes):
-    groups = len(windows)
-    count, window, rows, width = windows[0].shape
+def update(place, taps, band, mains, rims, volume, planes):
+    groups = len(mains)
+    count, _, rows, width = mains[0].shape
     outer = planes + taps.shape[2] - 1
     band = band.reshape((groups, count) + band.shape[1:])
     return pl.pallas_call(
@@ -247,7 +272,7 @@
         grid=(count,),
         out_shape=jax.ShapeDtypeStruct((planes, rows, width), jnp.float32),
         in_specs=[SMEM, SMEM, pl.BlockSpec((groups, 1) + band.shape[2:], lambda v: (0, v, 0, 0, 0))]
-        + [pl.BlockSpec((1, window, rows, width), lambda v: (v, 0, 0, 0))] * groups
+        + window_specs(mains, rims)
         + [VMEM] * 3,
         out_specs=VMEM,
         scratch_shapes=[
@@ -258,7 +283,7 @@
             pltpu.VMEM((planes, rows, width), jnp.float32),
         ],
         compiler_params=PARAMS,
-    )(place, taps, band, *windows, *volume)
+    )(place, taps, band, *mains, *rims, *volume)
 
 
 def partner(value, bit, members):
@@ -289,30 +314,38 @@
     me = lax.axis_index("view")
     place = jnp.stack([me // CORES, me % CORES]).astype(jnp.int32)
 
+    near_bit, far_bit = 1, CORES
+    own_main, far_main = resample(place, weights, offsets, [raw_views], 2 * planes + rim)
+    own_main, far_main, raw_later, taps_later = lax.optimization_barrier((own_main, far_main, raw_views, psf_taps))
+    far_main = partner(far_main, far_bit, members)
     up = [(i, i + 1) for i in range(blocks - 1)]
     down = [(i + 1, i) for i in range(blocks - 1)]
-    raw_before = lax.ppermute(raw_views[:, depth - rim :], "vol", up)
-    raw_after = lax.ppermute(raw_views[:, :rim], "vol", down)
-    all_taps = [psf_taps] + [partner(psf_taps, bit, members) for bit in range(1, members)]
-    own, far = resample(place, weights, offsets, raw_before, raw_views, raw_after)
-    own, far, all_taps = lax.optimization_barrier((own, far, all_taps))
-    far = partner(far, 2, members)
-    near = partner(own, 1, members)
-    all_taps = jnp.concatenate(all_taps)
+    raw_before = lax.ppermute(raw_later[:, depth - rim :], "vol", up)
+    raw_after = lax.ppermute(raw_later[:, :rim], "vol", down)
+    near_main = partner(own_main, near_bit, members)
+    cross_taps = partner(taps_later, near_bit + far_bit, members)
+    pair_taps = partner(jnp.stack([psf_taps, cross_taps]), near_bit, members)
+    all_taps = jnp.concatenate([psf_taps, pair_taps[0], pair_taps[1], cross_taps])
     all_taps = all_taps / jnp.sum(all_taps, axis=-1, keepdims=True)
-    far, band = lax.optimization_barrier((far, bands(all_taps, width)))
-    windows = [own, near, far, partner(far, 1, members)]
-    start = sum_views(place, windows, planes, rim)
+    band = bands(all_taps, width)
+    own_rim, far_rim = resample(place, weights, offsets, [raw_before, raw_after], rim)
+    cross_rim = partner(far_rim, near_bit + far_bit, members)
+    near_rim = partner(own_rim, near_bit, members)
+    far_main, band, own_rim = lax.optimization_barrier((far_main, band, own_rim))
+    far_rim = partner(cross_rim, near_bit, members)
+    mains = [own_main, near_main, far_main, partner(far_main, near_bit, members)]
+    rims = [own_rim, near_rim, far_rim, cross_rim]
+    start = sum_views(place, mains, rims, planes)
     before, after = z_rims(start[rim : rim + planes], rim, 2 * rim, members, blocks)
-    joined = update(place, all_taps, band, windows, (before, start, after), planes)
+    joined = update(place, all_taps, band, mains, rims, (before, start, after), planes)
     for turn in range(1, ITERS):
         before, after = z_rims(joined, 0, 2 * rim, members, blocks)
-        joined = update(place, all_taps, band, windows, (before, joined, after), planes)
+        joined = update(place, all_taps, band, mains, rims, (before, joined, after), planes)
 
     columns = lax.all_to_all(joined, "vol", split_axis=1, concat_axis=0, tiled=True)
-    far = partner(columns, 2, members)
-    near = partner(columns, 1, members)
-    parts = [columns, near, far, partner(far, 1, members)]
+    far = partner(columns, far_bit, members)
+    near = partner(columns, near_bit, members)
+    parts = [columns, near, far, partner(far, near_bit, members)]
     width_x = columns.shape[1]
     result = jnp.zeros((blocks, members, planes, width_x, width), jnp.float32)
     for k in range(members):

time: 153 us -> 156 us (1.020)
  waiting for transfers between devices: 41 us -> 42.9 us
  Pallas kernels: 60 us -> 61.7 us
  starting transfers between devices: 20.3 us -> 21.9 us
    ppermute x9 -> x11, waiting for transfers between devices: 31.7 us -> 35.3 us  [partner(): return lax.ppermute(value, 'view', [(i, i ^ bit) for i in range(members)])]
    ppermute x9 -> x11, starting transfers between devices: 4.07 us -> 6.58 us  [partner(): return lax.ppermute(value, 'view', [(i, i ^ bit) for i in range(members)])]
    pallas_call x1 -> x2, Pallas kernels: 4.06 us -> 5.18 us  [resample(): pl.pallas_call(resample_kernel, grid=(views,), out_shape=(shape, shape),...]
    unnamed x13 -> x10, local copies, waits for them, and re-layouts: 4.75 us -> 4.71 us
  transfers between devices with their start and end apart: 15 -> 17, of which waited for: 8 -> 8; matrix products, arithmetic and copies ran while one was open for 1% -> 0% of each run, Pallas kernels for 4% -> 3%
where the time goes in v4:
time: 156 us; the launch traced here: 155 us
  Pallas kernels  61.7 us (40%)
  waiting for transfers between devices  42.9 us (28%)
  blocking collectives  22.3 us (14%)
  starting transfers between devices  21.9 us (14%)
  local copies, waits for them, and re-layouts  5.91 us (4%)
    pallas_call x2, Pallas kernels, update(): pl.pallas_call(functools.partial(update_kernel, groups), grid=(count,), o...  52.2 us
    ppermute x11, waiting for transfers between devices, partner(): return lax.ppermute(value, 'view', [(i, i ^ bit) for i in range(members)])  35.3 us
    all_to_all x1, blocking collectives, per_device(): lax.all_to_all(joined, 'vol', split_axis=1, concat_axis=0, tiled=True)  22.3 us
    ppermute x2, starting transfers between devices, z_rims(): lax.ppermute(own[hop * planes - far:hop * planes - near], axes, up)  7.74 us
    ppermute x11, starting transfers between devices, partner(): return lax.ppermute(value, 'view', [(i, i ^ bit) for i in range(members)])  6.58 us
    pallas_call x2, Pallas kernels, resample(): pl.pallas_call(resample_kernel, grid=(views,), out_shape=(shape, shape),...  5.18 us
    ppermute x2, waiting for transfers between devices, z_rims(): lax.ppermute(own[near - (hop - 1) * planes:far - (hop - 1) * planes], axe...  4.79 us
    unnamed x10, local copies, waits for them, and re-layouts  4.71 us
  transfers between devices with their start and end apart: 17, of which 8 were waited for; matrix products, arithmetic and copies ran while one was open for 0% of the time, Pallas kernels for 3%

profile of v4, /device:TPU:0, one launch (start us, length us, event | category | flops | bytes accessed | tf_op | source)
XLA Modules:
  0.0 155.1 jit_solution(6549199605093880728)
XLA Ops:
  0.0 0.0 copy-start.4
  0.0 0.7 broadcast_in_dim.9.offsets_ref
  0.7 0.1 pad_add_fusion.place_ref
  0.8 0.0 copy-start.1
  0.8 1.4 copy-done.1
  2.2 0.0 copy-start.2
  2.2 0.7 copy-done.2
  2.9 3.6 %shard_map.46 = (bf16[3,20,64,128]{3,2,1,0:T(8,128)(2,1)S(1)}, bf16[3,20,64,128]{3,2,1,0:T(8,128)(2,1)S(1)}) custom-call(s32[2]{0:T(128)S(1)} %pad_add_fusion.place_ref, f32[3,8,64]{2,1,0:T(8,128)S(1)} %bitcast.31, s32[3,1,64]{2,1,0:T(1,128)S(1)} %broadcast_in_dim.9.offsets_ref, bf16[3,32,64,128]{3,2,1,0:T(8,128)(2,1)S(1)} %copy-done.1), custom_call_target="tpu_custom_call" | custom-call | tf_op jit(solution)/shard_map/pallas_call | solution.py:79
  6.5 3.0 %collective-permute-start.2 = (bf16[3,20,64,128]{3,2,1,0:T(8,128)(2,1)S(1)}, bf16[3,20,64,128]{3,2,1,0:T(8,128)(2,1)S(1)}, u32[]{:S(2)}, u32[]{:S(2)}) collective-permute-start(bf16[3,20,64,128]{3,2,1,0:T(8,128)(2,1)S(1)} %get-tuple-element.19), channel_id=1, source_target_pairs={{0,16},{8,24},{16,0},{24,8},{1,17},{9,25},{17,1},{25,9},{2,18},{10... | collective-permute-start | bytes 2949128 | tf_op jit(solution)/shard_map/ppermute | solution.py:290
  9.5 0.0 copy-done.4
  9.5 0.0 collective-permute-start
  9.5 21.1 %collective-permute-done = f32[3,3,9]{2,1,0:T(4,128)S(1)} collective-permute-done((f32[3,3,9]{2,1,0:T(4,128)S(1)}, f32[3,3,9]{2,1,0:T(4,128)S(1)}, u32[]{:S(2)}, u32[]{:S(2)}) %collective-permute-start) | collective-permute-done | bytes 356 | tf_op jit(solution)/shard_map/ppermute | solution.py:290
  30.6 0.8 collective-permute-start.1
  31.4 3.7 %collective-permute-start.3 = (bf16[3,4,64,128]{3,2,1,0:T(8,128)(2,1)S(1)}, bf16[3,4,64,128]{3,2,1,0:T(8,128)(2,1)S(1)}, u32[]{:S(2)}, u32[]{:S(2)}) collective-permute-start(bf16[3,4,64,128]{3,2,1,0:T(8,128)(2,1)S(1)} %get-tuple-element.28), channel_id=1, source_target_pairs={{0,1},{1,2},{2,3},{3,4},{4,5},{5,6},{6,7},{8,9},{9,10},{10,11},{11... | collective-permute-start | bytes 589832 | tf_op jit(solution)/shard_map/ppermute | solution.py:323
  35.1 1.3 collective-permute-start.4
  36.4 0.1 collective-permute-start.5
  36.5 0.0 collective-permute-done.1
  36.5 0.1 fusion.1.taps_ref
  36.6 2.4 %shard_map.47 = bf16[12,2,256,256]{3,2,1,0:T(8,128)(2,1)S(1)} custom-call(f32[12,3,9]{2,1,0:T(4,128)S(1)} %fusion.1.taps_ref), custom_call_target="tpu_custom_call" | custom-call | tf_op jit(solution)/shard_map/pallas_call | solution.py:115
  39.0 0.0 copy-start
  39.0 1.6 %copy-done = bf16[12,2,256,256]{3,2,1,0:T(8,128)(2,1)} copy-done((bf16[12,2,256,256]{3,2,1,0:T(8,128)(2,1)}, bf16[12,2,256,256]{3,2,1,0:T(8,128)(2,1)S(1)}, u32[]{:S(2)}) %copy-start) | copy-done | bytes 3145752
  40.7 0.0 collective-permute-done.3.refs_0_
  40.7 2.9 %collective-permute-done.4.refs_1_ = bf16[3,4,64,128]{3,2,1,0:T(8,128)(2,1)S(1)} collective-permute-done((bf16[3,4,64,128]{3,2,1,0:T(8,128)(2,1)S(1)}, bf16[3,4,64,128]{3,2,1,0:T(8,128)(2,1)S(1)}, u32[]{:S(2)}, u32[]{:S(2)}) %collective-permute-start.4) | collective-permute-done | bytes 196640 | tf_op jit(solution)/shard_map/ppermute | solution.py:324
  43.6 1.6 %shard_map.48 = (bf16[3,4,64,128]{3,2,1,0:T(8,128)(2,1)S(1)}, bf16[3,4,64,128]{3,2,1,0:T(8,128)(2,1)S(1)}) custom-call(s32[2]{0:T(128)S(1)} %pad_add_fusion.place_ref, f32[3,8,64]{2,1,0:T(8,128)S(1)} %bitcast.32, s32[3,1,64]{2,1,0:T(1,128)S(1)} %broadcast_in_dim.9.offsets_ref, bf16[3,4,64,128]{3,2,1,0:T(8,128)(2,1)S(1)} %collective-permute-done.3.refs_0_, ...), custom_call_target="tpu_custom_call" | custom-call | tf_op jit(solution)/shard_map/pallas_call | solution.py:79
  45.2 0.0 collective-permute-done.2.refs_2_.refs_3_
  45.2 0.1 collective-permute-start.6
  45.3 1.6 %collective-permute-start.8 = (bf16[3,4,64,128]{3,2,1,0:T(8,128)(2,1)S(1)}, bf16[3,4,64,128]{3,2,1,0:T(8,128)(2,1)S(1)}, u32[]{:S(2)}, u32[]{:S(2)}) collective-permute-start(bf16[3,4,64,128]{3,2,1,0:T(8,128)(2,1)S(1)} %get-tuple-element.26), channel_id=1, source_target_pairs={{0,24},{8,16},{16,8},{24,0},{1,25},{9,17},{17,9},{25,1},{2,26},{10... | collective-permute-start | bytes 589832 | tf_op jit(solution)/shard_map/ppermute | solution.py:290
  46.9 0.1 collective-permute-start.7
  46.9 5.0 %collective-permute-done.8.refs_7_.refs_8_ = bf16[3,4,64,128]{3,2,1,0:T(8,128)(2,1)S(1)} collective-permute-done((bf16[3,4,64,128]{3,2,1,0:T(8,128)(2,1)S(1)}, bf16[3,4,64,128]{3,2,1,0:T(8,128)(2,1)S(1)}, u32[]{:S(2)}, u32[]{:S(2)}) %collective-permute-start.8) | collective-permute-done | bytes 196640 | tf_op jit(solution)/shard_map/ppermute | solution.py:290
  52.0 0.4 collective-permute-start.9
  52.4 0.0 collective-permute-done.7.refs_5_.refs_6_
  52.4 1.1 collective-permute-done.9.refs_6_.refs_7_
  53.4 0.0 collective-permute-done.5.refs_1_.refs_2_
  53.4 0.0 collective-permute-done.6.refs_3_.refs_4_
  53.4 1.9 %shard_map.49.refs_10_ = f32[16,64,128]{2,1,0:T(8,128)S(1)} custom-call(s32[2]{0:T(128)S(1)} %pad_add_fusion.place_ref, bf16[3,20,64,128]{3,2,1,0:T(8,128)(2,1)S(1)} %get-tuple-element.23.refs_0_.refs_1_, bf16[3,20,64,128]{3,2,1,0:T(8,128)(2,1)S(1)} %collective-permute-done.5.refs_1_.refs_2_, ...), custom_call_target="tpu_custom_call" | custom-call | tf_op jit(solution)/shard_map/pallas_call | solution.py:168
  55.4 2.3 %collective-permute-start.10 = (f32[4,64,128]{2,1,0:T(8,128)S(1)}, f32[4,64,128]{2,1,0:T(8,128)S(1)}, u32[]{:S(2)}, u32[]{:S(2)}) collective-permute-start(f32[4,64,128]{2,1,0:T(8,128)S(1)} %get-tuple-element.30), channel_id=1, source_target_pairs={{0,8},{8,16},{16,24},{24,1},{1,9},{9,17},{17,25},{25,2},{2,10},{10... | collective-permute-start | bytes 393224 | tf_op jit(solution)/shard_map/ppermute | solution.py:303
  57.7 1.3 collective-permute-start.11
  59.0 0.0 collective-permute-done.10.refs_9_
  59.0 2.7 %collective-permute-done.11.refs_11_ = f32[4,64,128]{2,1,0:T(8,128)S(1)} collective-permute-done((f32[4,64,128]{2,1,0:T(8,128)S(1)}, f32[4,64,128]{2,1,0:T(8,128)S(1)}, u32[]{:S(2)}, u32[]{:S(2)}) %collective-permute-start.11) | collective-permute-done | bytes 131104 | tf_op jit(solution)/shard_map/ppermute | solution.py:304
  61.7 26.1 %shard_map.50.refs_10_ = f32[8,64,128]{2,1,0:T(8,128)S(1)} custom-call(s32[2]{0:T(128)S(1)} %pad_add_fusion.place_ref, f32[12,3,9]{2,1,0:T(4,128)S(1)} %fusion.1.taps_ref, bf16[4,3,2,256,256]{4,3,2,1,0:T(8,128)(2,1)} %bitcast.29, bf16[3,20,64,128]{3,2,1,0:T(8,128)(2,1)S(1)} %get-tuple-element.23.refs_0_.refs_1_, ...), custom_call_target="tpu_custom_call" | custom-call | tf_op jit(solution)/shard_map/pallas_call | solution.py:270
  87.8 5.5 %collective-permute-start.12 = (f32[8,64,128]{2,1,0:T(8,128)S(1)}, f32[8,64,128]{2,1,0:T(8,128)S(1)}, u32[]{:S(2)}, u32[]{:S(2)}) collective-permute-start(f32[8,64,128]{2,1,0:T(8,128)S(1)} %shard_map.50.refs_10_), channel_id=1, source_target_pairs={{0,8},{8,16},{16,24},{24,1},{1,9},{9,17},{17,25},{25,2},{2,10},{10... | collective-permute-start | bytes 786440 | tf_op jit(solution)/shard_map/ppermute | solution.py:303
  93.2 1.3 collective-permute-start.13
  94.5 0.0 collective-permute-done.12.refs_9_
  94.6 2.1 %collective-permute-done.13.refs_11_ = f32[8,64,128]{2,1,0:T(8,128)S(1)} collective-permute-done((f32[8,64,128]{2,1,0:T(8,128)S(1)}, f32[8,64,128]{2,1,0:T(8,128)S(1)}, u32[]{:S(2)}, u32[]{:S(2)}) %collective-permute-start.13) | collective-permute-done | bytes 262176 | tf_op jit(solution)/shard_map/ppermute | solution.py:304
  96.7 26.1 %shard_map.51 = f32[8,64,128]{2,1,0:T(8,128)S(1)} custom-call(s32[2]{0:T(128)S(1)} %pad_add_fusion.place_ref, f32[12,3,9]{2,1,0:T(4,128)S(1)} %fusion.1.taps_ref, bf16[4,3,2,256,256]{4,3,2,1,0:T(8,128)(2,1)} %bitcast.30, bf16[3,20,64,128]{3,2,1,0:T(8,128)(2,1)S(1)} %get-tuple-element.23.refs_0_.refs_1_, ...), custom_call_target="tpu_custom_call" | custom-call | tf_op jit(solution)/shard_map/pallas_call | solution.py:270
  122.8 0.2 copy.16
  122.9 22.3 %all_to_all.18 = f32[8,64,128]{2,0,1:T(8,128)S(1)} all-to-all(f32[8,64,128]{2,0,1:T(8,128)S(1)} %copy.16), channel_id=1, replica_groups=mesh['view'=4,'vol'=8] {'vol'}, dimensions={1} | all-to-all | bytes 524288 | tf_op jit(solution)/shard_map/all_to_all | solution.py:345
  145.3 0.1 collective-permute-start.15
  145.4 0.5 collective-permute-start.14
  145.9 6.8 %collective-permute-done.15 = f32[64,8,128]{2,1,0:T(8,128)S(1)} collective-permute-done((f32[64,8,128]{2,1,0:T(8,128)S(1)}, f32[64,8,128]{2,1,0:T(8,128)S(1)}, u32[]{:S(2)}, u32[]{:S(2)}) %collective-permute-start.15) | collective-permute-done | bytes 262176 | tf_op jit(solution)/shard_map/ppermute | solution.py:290
  152.6 0.0 collective-permute-start.16
  152.6 0.1 broadcast_in_dim.8
  152.7 0.1 copy_dynamic-update-slice_fusion
  152.8 0.0 collective-permute-done.14
  152.9 1.3 collective-permute-done.16
  154.2 0.0 copy-start.3
  154.2 1.0 copy-done.3
  (8 shorter events, 0.2 us)
Async XLA Ops:
  0.0 9.5 %copy-start.4 = (f32[3,3,9]{2,1,0:T(4,128)S(1)}, f32[3,3,9]{2,1,0:T(4,128)}, u32[]{:S(2)}) copy-start(f32[3,3,9]{2,1,0:T(4,128)} %param.7) | copy-start | bytes 976
  0.8 1.4 copy-start.1
  2.2 0.7 copy-start.2
  6.5 38.7 %collective-permute-start.2 = (bf16[3,20,64,128]{3,2,1,0:T(8,128)(2,1)S(1)}, bf16[3,20,64,128]{3,2,1,0:T(8,128)(2,1)S(1)}, u32[]{:S(2)}, u32[]{:S(2)}) collective-permute-start(bf16[3,20,64,128]{3,2,1,0:T(8,128)(2,1)S(1)} %get-tuple-element.19), channel_id=1, source_target_pairs={{0,16},{8,24},{16,0},{24,8},{1,17},{9,25},{17,1},{25,9},{2,18},{10... | collective-permute-start | bytes 2949128 | tf_op jit(solution)/shard_map/ppermute | solution.py:290
  9.5 21.1 %collective-permute-start = (f32[3,3,9]{2,1,0:T(4,128)S(1)}, f32[3,3,9]{2,1,0:T(4,128)S(1)}, u32[]{:S(2)}, u32[]{:S(2)}) collective-permute-start(f32[3,3,9]{2,1,0:T(4,128)S(1)} %copy-done.4), channel_id=1, source_target_pairs={{0,24},{8,16},{16,8},{24,0},{1,25},{9,17},{17,9},{25,1},{2,26},{10... | collective-permute-start | bytes 980 | tf_op jit(solution)/shard_map/ppermute | solution.py:290
  30.6 5.9 %collective-permute-start.1 = (f32[2,3,3,9]{3,2,1,0:T(4,128)S(1)}, f32[2,3,3,9]{3,2,1,0:T(4,128)S(1)}, u32[]{:S(2)}, u32[]{:S(2)}) collective-permute-start(f32[2,3,3,9]{3,2,1,0:T(4,128)S(1)} %pad_maximum_fusion.1), channel_id=1, source_target_pairs={{0,8},{8,0},{16,24},{24,16},{1,9},{9,1},{17,25},{25,17},{2,10},{10... | collective-permute-start | bytes 1952 | tf_op jit(solution)/shard_map/ppermute | solution.py:290
  31.4 9.2 %collective-permute-start.3 = (bf16[3,4,64,128]{3,2,1,0:T(8,128)(2,1)S(1)}, bf16[3,4,64,128]{3,2,1,0:T(8,128)(2,1)S(1)}, u32[]{:S(2)}, u32[]{:S(2)}) collective-permute-start(bf16[3,4,64,128]{3,2,1,0:T(8,128)(2,1)S(1)} %get-tuple-element.28), channel_id=1, source_target_pairs={{0,1},{1,2},{2,3},{3,4},{4,5},{5,6},{6,7},{8,9},{9,10},{10,11},{11... | collective-permute-start | bytes 589832 | tf_op jit(solution)/shard_map/ppermute | solution.py:323
  35.1 8.4 %collective-permute-start.4 = (bf16[3,4,64,128]{3,2,1,0:T(8,128)(2,1)S(1)}, bf16[3,4,64,128]{3,2,1,0:T(8,128)(2,1)S(1)}, u32[]{:S(2)}, u32[]{:S(2)}) collective-permute-start(bf16[3,4,64,128]{3,2,1,0:T(8,128)(2,1)S(1)} %get-tuple-element.27), channel_id=1, source_target_pairs={{1,0},{2,1},{3,2},{4,3},{5,4},{6,5},{7,6},{9,8},{10,9},{11,10},{12... | collective-permute-start | bytes 589832 | tf_op jit(solution)/shard_map/ppermute | solution.py:324
  36.4 17.0 %collective-permute-start.5 = (bf16[3,20,64,128]{3,2,1,0:T(8,128)(2,1)S(1)}, bf16[3,20,64,128]{3,2,1,0:T(8,128)(2,1)S(1)}, u32[]{:S(2)}, u32[]{:S(2)}) collective-permute-start(bf16[3,20,64,128]{3,2,1,0:T(8,128)(2,1)S(1)} %get-tuple-element.23.refs_0_.refs_1_), channel_id=1, source_target_pairs={{0,8},{8,0},{16,24},{24,16},{1,9},{9,1},{17,25},{25,17},{2,10},{10... | collective-permute-start | bytes 2949128 | tf_op jit(solution)/shard_map/ppermute | solution.py:290
  39.0 1.6 %copy-start = (bf16[12,2,256,256]{3,2,1,0:T(8,128)(2,1)}, bf16[12,2,256,256]{3,2,1,0:T(8,128)(2,1)S(1)}, u32[]{:S(2)}) copy-start(bf16[12,2,256,256]{3,2,1,0:T(8,128)(2,1)S(1)} %shard_map.47) | copy-start | bytes 9437188
  45.2 8.2 %collective-permute-start.6 = (bf16[3,20,64,128]{3,2,1,0:T(8,128)(2,1)S(1)}, bf16[3,20,64,128]{3,2,1,0:T(8,128)(2,1)S(1)}, u32[]{:S(2)}, u32[]{:S(2)}) collective-permute-start(bf16[3,20,64,128]{3,2,1,0:T(8,128)(2,1)S(1)} %collective-permute-done.2.refs_2_.refs_3_), channel_id=1, source_target_pairs={{0,8},{8,0},{16,24},{24,16},{1,9},{9,1},{17,25},{25,17},{2,10},{10... | collective-permute-start | bytes 2949128 | tf_op jit(solution)/shard_map/ppermute | solution.py:290
  45.3 6.7 %collective-permute-start.8 = (bf16[3,4,64,128]{3,2,1,0:T(8,128)(2,1)S(1)}, bf16[3,4,64,128]{3,2,1,0:T(8,128)(2,1)S(1)}, u32[]{:S(2)}, u32[]{:S(2)}) collective-permute-start(bf16[3,4,64,128]{3,2,1,0:T(8,128)(2,1)S(1)} %get-tuple-element.26), channel_id=1, source_target_pairs={{0,24},{8,16},{16,8},{24,0},{1,25},{9,17},{17,9},{25,1},{2,26},{10... | collective-permute-start | bytes 589832 | tf_op jit(solution)/shard_map/ppermute | solution.py:290
  46.9 5.5 %collective-permute-start.7 = (bf16[3,4,64,128]{3,2,1,0:T(8,128)(2,1)S(1)}, bf16[3,4,64,128]{3,2,1,0:T(8,128)(2,1)S(1)}, u32[]{:S(2)}, u32[]{:S(2)}) collective-permute-start(bf16[3,4,64,128]{3,2,1,0:T(8,128)(2,1)S(1)} %get-tuple-element.25.refs_4_.refs_5_), channel_id=1, source_target_pairs={{0,8},{8,0},{16,24},{24,16},{1,9},{9,1},{17,25},{25,17},{2,10},{10... | collective-permute-start | bytes 589832 | tf_op jit(solution)/shard_map/ppermute | solution.py:290
  52.0 1.5 collective-permute-start.9
  55.4 3.6 %collective-permute-start.10 = (f32[4,64,128]{2,1,0:T(8,128)S(1)}, f32[4,64,128]{2,1,0:T(8,128)S(1)}, u32[]{:S(2)}, u32[]{:S(2)}) collective-permute-start(f32[4,64,128]{2,1,0:T(8,128)S(1)} %get-tuple-element.30), channel_id=1, source_target_pairs={{0,8},{8,16},{16,24},{24,1},{1,9},{9,17},{17,25},{25,2},{2,10},{10... | collective-permute-start | bytes 393224 | tf_op jit(solution)/shard_map/ppermute | solution.py:303
  57.7 4.0 %collective-permute-start.11 = (f32[4,64,128]{2,1,0:T(8,128)S(1)}, f32[4,64,128]{2,1,0:T(8,128)S(1)}, u32[]{:S(2)}, u32[]{:S(2)}) collective-permute-start(f32[4,64,128]{2,1,0:T(8,128)S(1)} %get-tuple-element.29), channel_id=1, source_target_pairs={{8,0},{16,8},{24,16},{1,24},{9,1},{17,9},{25,17},{2,25},{10,2},{18... | collective-permute-start | bytes 393224 | tf_op jit(solution)/shard_map/ppermute | solution.py:304
  87.8 6.8 %collective-permute-start.12 = (f32[8,64,128]{2,1,0:T(8,128)S(1)}, f32[8,64,128]{2,1,0:T(8,128)S(1)}, u32[]{:S(2)}, u32[]{:S(2)}) collective-permute-start(f32[8,64,128]{2,1,0:T(8,128)S(1)} %shard_map.50.refs_10_), channel_id=1, source_target_pairs={{0,8},{8,16},{16,24},{24,1},{1,9},{9,17},{17,25},{25,2},{2,10},{10... | collective-permute-start | bytes 786440 | tf_op jit(solution)/shard_map/ppermute | solution.py:303
  93.2 3.4 %collective-permute-start.13 = (f32[8,64,128]{2,1,0:T(8,128)S(1)}, f32[8,64,128]{2,1,0:T(8,128)S(1)}, u32[]{:S(2)}, u32[]{:S(2)}) collective-permute-start(f32[8,64,128]{2,1,0:T(8,128)S(1)} %shard_map.50.refs_10_), channel_id=1, source_target_pairs={{8,0},{16,8},{24,16},{1,24},{9,1},{17,9},{25,17},{2,25},{10,2},{18... | collective-permute-start | bytes 786440 | tf_op jit(solution)/shard_map/ppermute | solution.py:304
  145.3 7.3 %collective-permute-start.15 = (f32[64,8,128]{2,1,0:T(8,128)S(1)}, f32[64,8,128]{2,1,0:T(8,128)S(1)}, u32[]{:S(2)}, u32[]{:S(2)}) collective-permute-start(f32[64,8,128]{2,1,0:T(8,128)S(1)} %bitcast.37), channel_id=1, source_target_pairs={{0,16},{8,24},{16,0},{24,8},{1,17},{9,25},{17,1},{25,9},{2,18},{10... | collective-permute-start | bytes 786440 | tf_op jit(solution)/shard_map/ppermute | solution.py:290
  145.4 7.4 %collective-permute-start.14 = (f32[64,8,128]{2,1,0:T(8,128)S(1)}, f32[64,8,128]{2,1,0:T(8,128)S(1)}, u32[]{:S(2)}, u32[]{:S(2)}) collective-permute-start(f32[64,8,128]{2,1,0:T(8,128)S(1)} %bitcast.38), channel_id=1, source_target_pairs={{0,8},{8,0},{16,24},{24,16},{1,9},{9,1},{17,25},{25,17},{2,10},{10... | collective-permute-start | bytes 786440 | tf_op jit(solution)/shard_map/ppermute | solution.py:290
  152.6 1.5 collective-permute-start.16
  154.2 1.0 copy-start.3

commit v5 on v4

--- a/solution.py
+++ b/solution.py
@@ -315,15 +315,17 @@
     place = jnp.stack([me // CORES, me % CORES]).astype(jnp.int32)
 
     near_bit, far_bit = 1, CORES
+    cross_taps = partner(psf_taps, near_bit + far_bit, members)
     own_main, far_main = resample(place, weights, offsets, [raw_views], 2 * planes + rim)
-    own_main, far_main, raw_later, taps_later = lax.optimization_barrier((own_main, far_main, raw_views, psf_taps))
+    own_main, far_main, raw_later, cross_taps = lax.optimization_barrier(
+        (own_main, far_main, raw_views, cross_taps)
+    )
     far_main = partner(far_main, far_bit, members)
     up = [(i, i + 1) for i in range(blocks - 1)]
     down = [(i + 1, i) for i in range(blocks - 1)]
     raw_before = lax.ppermute(raw_later[:, depth - rim :], "vol", up)
     raw_after = lax.ppermute(raw_later[:, :rim], "vol", down)
     near_main = partner(own_main, near_bit, members)
-    cross_taps = partner(taps_later, near_bit + far_bit, members)
     pair_taps = partner(jnp.stack([psf_taps, cross_taps]), near_bit, members)
     all_taps = jnp.concatenate([psf_taps, pair_taps[0], pair_taps[1], cross_taps])
     all_taps = all_taps / jnp.sum(all_taps, axis=-1, keepdims=True)

time: 156 us -> 143 us (0.917)
  waiting for transfers between devices: 42.9 us -> 32.6 us
  starting transfers between devices: 21.9 us -> 19.8 us
    ppermute x11, waiting for transfers between devices: 35.3 us -> 25.5 us  [partner(): return lax.ppermute(value, 'view', [(i, i ^ bit) for i in range(members)])]
    ppermute x11, starting transfers between devices: 6.58 us -> 4.88 us  [partner(): return lax.ppermute(value, 'view', [(i, i ^ bit) for i in range(members)])]
  transfers between devices with their start and end apart: 17 -> 17, of which waited for: 8 -> 8; matrix products, arithmetic and copies ran while one was open for 0% -> 1% of each run, Pallas kernels for 3% -> 5%
where the time goes in v5:
time: 143 us; the launch traced here: 142 us
  Pallas kernels  61.7 us (43%)
  waiting for transfers between devices  32.6 us (23%)
  blocking collectives  21.7 us (15%)
  starting transfers between devices  19.8 us (14%)
  local copies, waits for them, and re-layouts  5.89 us (4%)
    pallas_call x2, Pallas kernels, update(): pl.pallas_call(functools.partial(update_kernel, groups), grid=(count,), o...  52.2 us
    ppermute x11, waiting for transfers between devices, partner(): return lax.ppermute(value, 'view', [(i, i ^ bit) for i in range(members)])  25.5 us
    all_to_all x1, blocking collectives, per_device(): lax.all_to_all(joined, 'vol', split_axis=1, concat_axis=0, tiled=True)  21.7 us
    ppermute x2, starting transfers between devices, z_rims(): lax.ppermute(own[hop * planes - far:hop * planes - near], axes, up)  7.42 us
    pallas_call x2, Pallas kernels, resample(): pl.pallas_call(resample_kernel, grid=(views,), out_shape=(shape, shape),...  5.17 us
    ppermute x11, starting transfers between devices, partner(): return lax.ppermute(value, 'view', [(i, i ^ bit) for i in range(members)])  4.88 us
    unnamed x10, local copies, waits for them, and re-layouts  4.71 us
    ppermute x2, waiting for transfers between devices, z_rims(): lax.ppermute(own[near - (hop - 1) * planes:far - (hop - 1) * planes], axe...  4.05 us
  transfers between devices with their start and end apart: 17, of which 8 were waited for; matrix products, arithmetic and copies ran while one was open for 1% of the time, Pallas kernels for 5%

profile of v5, /device:TPU:0, one launch (start us, length us, event | category | flops | bytes accessed | tf_op | source)
XLA Modules:
  0.0 142.2 jit_solution(6158542579380922803)
XLA Ops:
  0.0 0.0 copy-start.4
  0.0 2.4 %collective-permute-start = (f32[3,3,9]{2,1,0:T(4,128)}, f32[3,3,9]{2,1,0:T(4,128)S(1)}, u32[]{:S(2)}, u32[]{:S(2)}) collective-permute-start(f32[3,3,9]{2,1,0:T(4,128)} %param.7), channel_id=1, source_target_pairs={{0,24},{8,16},{16,8},{24,0},{1,25},{9,17},{17,9},{25,1},{2,26},{10... | collective-permute-start | bytes 980 | tf_op jit(solution)/shard_map/ppermute | solution.py:290
  2.4 0.1 pad_add_fusion.place_ref
  2.5 0.7 broadcast_in_dim.9.offsets_ref
  3.1 0.0 copy-start.1
  3.1 1.4 copy-done.1
  4.5 0.0 copy-start.2
  4.5 0.7 copy-done.2
  5.3 3.6 %shard_map.46 = (bf16[3,20,64,128]{3,2,1,0:T(8,128)(2,1)S(1)}, bf16[3,20,64,128]{3,2,1,0:T(8,128)(2,1)S(1)}) custom-call(s32[2]{0:T(128)S(1)} %pad_add_fusion.place_ref, f32[3,8,64]{2,1,0:T(8,128)S(1)} %bitcast.31, s32[3,1,64]{2,1,0:T(1,128)S(1)} %broadcast_in_dim.9.offsets_ref, bf16[3,32,64,128]{3,2,1,0:T(8,128)(2,1)S(1)} %copy-done.1), custom_call_target="tpu_custom_call" | custom-call | tf_op jit(solution)/shard_map/pallas_call | solution.py:79
  8.8 0.0 collective-permute-done
  8.8 0.6 collective-permute-start.2
  9.5 0.0 copy-done.4
  9.5 0.2 collective-permute-start.1
  9.7 3.7 %collective-permute-start.3 = (bf16[3,4,64,128]{3,2,1,0:T(8,128)(2,1)S(1)}, bf16[3,4,64,128]{3,2,1,0:T(8,128)(2,1)S(1)}, u32[]{:S(2)}, u32[]{:S(2)}) collective-permute-start(bf16[3,4,64,128]{3,2,1,0:T(8,128)(2,1)S(1)} %get-tuple-element.28), channel_id=1, source_target_pairs={{0,1},{1,2},{2,3},{3,4},{4,5},{5,6},{6,7},{8,9},{9,10},{10,11},{11... | collective-permute-start | bytes 589832 | tf_op jit(solution)/shard_map/ppermute | solution.py:326
  13.4 1.3 collective-permute-start.4
  14.7 0.1 collective-permute-start.5
  14.8 0.0 collective-permute-done.1
  14.8 0.1 fusion.1.taps_ref
  14.9 2.4 %shard_map.47 = bf16[12,2,256,256]{3,2,1,0:T(8,128)(2,1)S(1)} custom-call(f32[12,3,9]{2,1,0:T(4,128)S(1)} %fusion.1.taps_ref), custom_call_target="tpu_custom_call" | custom-call | tf_op jit(solution)/shard_map/pallas_call | solution.py:115
  17.3 0.0 copy-start
  17.3 1.6 %copy-done = bf16[12,2,256,256]{3,2,1,0:T(8,128)(2,1)} copy-done((bf16[12,2,256,256]{3,2,1,0:T(8,128)(2,1)}, bf16[12,2,256,256]{3,2,1,0:T(8,128)(2,1)S(1)}, u32[]{:S(2)}) %copy-start) | copy-done | bytes 3145752
  18.9 0.0 collective-permute-done.3.refs_0_
  18.9 3.0 %collective-permute-done.4.refs_1_ = bf16[3,4,64,128]{3,2,1,0:T(8,128)(2,1)S(1)} collective-permute-done((bf16[3,4,64,128]{3,2,1,0:T(8,128)(2,1)S(1)}, bf16[3,4,64,128]{3,2,1,0:T(8,128)(2,1)S(1)}, u32[]{:S(2)}, u32[]{:S(2)}) %collective-permute-start.4) | collective-permute-done | bytes 196640 | tf_op jit(solution)/shard_map/ppermute | solution.py:327
  22.0 1.6 %shard_map.48 = (bf16[3,4,64,128]{3,2,1,0:T(8,128)(2,1)S(1)}, bf16[3,4,64,128]{3,2,1,0:T(8,128)(2,1)S(1)}) custom-call(s32[2]{0:T(128)S(1)} %pad_add_fusion.place_ref, f32[3,8,64]{2,1,0:T(8,128)S(1)} %bitcast.32, s32[3,1,64]{2,1,0:T(1,128)S(1)} %broadcast_in_dim.9.offsets_ref, bf16[3,4,64,128]{3,2,1,0:T(8,128)(2,1)S(1)} %collective-permute-done.3.refs_0_, ...), custom_call_target="tpu_custom_call" | custom-call | tf_op jit(solution)/shard_map/pallas_call | solution.py:79
  23.6 9.7 %collective-permute-done.2.refs_2_.refs_3_ = bf16[3,20,64,128]{3,2,1,0:T(8,128)(2,1)S(1)} collective-permute-done((bf16[3,20,64,128]{3,2,1,0:T(8,128)(2,1)S(1)}, bf16[3,20,64,128]{3,2,1,0:T(8,128)(2,1)S(1)}, u32[]{:S(2)}, u32[]{:S(2)}) %collective-permute-start.2) | collective-permute-done | bytes 983072 | tf_op jit(solution)/shard_map/ppermute | solution.py:290
  33.2 0.0 collective-permute-start.6
  33.3 0.4 collective-permute-start.8
  33.6 0.1 collective-permute-start.7
  33.8 6.0 %collective-permute-done.8.refs_7_.refs_8_ = bf16[3,4,64,128]{3,2,1,0:T(8,128)(2,1)S(1)} collective-permute-done((bf16[3,4,64,128]{3,2,1,0:T(8,128)(2,1)S(1)}, bf16[3,4,64,128]{3,2,1,0:T(8,128)(2,1)S(1)}, u32[]{:S(2)}, u32[]{:S(2)}) %collective-permute-start.8) | collective-permute-done | bytes 196640 | tf_op jit(solution)/shard_map/ppermute | solution.py:290
  39.8 0.5 collective-permute-start.9
  40.3 0.0 collective-permute-done.7.refs_5_.refs_6_
  40.3 1.1 collective-permute-done.9.refs_6_.refs_7_
  41.3 0.0 collective-permute-done.5.refs_1_.refs_2_
  41.3 0.0 collective-permute-done.6.refs_3_.refs_4_
  41.4 1.9 %shard_map.49.refs_10_ = f32[16,64,128]{2,1,0:T(8,128)S(1)} custom-call(s32[2]{0:T(128)S(1)} %pad_add_fusion.place_ref, bf16[3,20,64,128]{3,2,1,0:T(8,128)(2,1)S(1)} %get-tuple-element.23.refs_0_.refs_1_, bf16[3,20,64,128]{3,2,1,0:T(8,128)(2,1)S(1)} %collective-permute-done.5.refs_1_.refs_2_, ...), custom_call_target="tpu_custom_call" | custom-call | tf_op jit(solution)/shard_map/pallas_call | solution.py:168
  43.3 2.3 %collective-permute-start.10 = (f32[4,64,128]{2,1,0:T(8,128)S(1)}, f32[4,64,128]{2,1,0:T(8,128)S(1)}, u32[]{:S(2)}, u32[]{:S(2)}) collective-permute-start(f32[4,64,128]{2,1,0:T(8,128)S(1)} %get-tuple-element.30), channel_id=1, source_target_pairs={{0,8},{8,16},{16,24},{24,1},{1,9},{9,17},{17,25},{25,2},{2,10},{10... | collective-permute-start | bytes 393224 | tf_op jit(solution)/shard_map/ppermute | solution.py:303
  45.6 1.3 collective-permute-start.11
  46.9 0.0 collective-permute-done.10.refs_9_
  46.9 1.9 %collective-permute-done.11.refs_11_ = f32[4,64,128]{2,1,0:T(8,128)S(1)} collective-permute-done((f32[4,64,128]{2,1,0:T(8,128)S(1)}, f32[4,64,128]{2,1,0:T(8,128)S(1)}, u32[]{:S(2)}, u32[]{:S(2)}) %collective-permute-start.11) | collective-permute-done | bytes 131104 | tf_op jit(solution)/shard_map/ppermute | solution.py:304
  48.8 26.1 %shard_map.50.refs_10_ = f32[8,64,128]{2,1,0:T(8,128)S(1)} custom-call(s32[2]{0:T(128)S(1)} %pad_add_fusion.place_ref, f32[12,3,9]{2,1,0:T(4,128)S(1)} %fusion.1.taps_ref, bf16[4,3,2,256,256]{4,3,2,1,0:T(8,128)(2,1)} %bitcast.29, bf16[3,20,64,128]{3,2,1,0:T(8,128)(2,1)S(1)} %get-tuple-element.23.refs_0_.refs_1_, ...), custom_call_target="tpu_custom_call" | custom-call | tf_op jit(solution)/shard_map/pallas_call | solution.py:270
  75.0 5.1 %collective-permute-start.12 = (f32[8,64,128]{2,1,0:T(8,128)S(1)}, f32[8,64,128]{2,1,0:T(8,128)S(1)}, u32[]{:S(2)}, u32[]{:S(2)}) collective-permute-start(f32[8,64,128]{2,1,0:T(8,128)S(1)} %shard_map.50.refs_10_), channel_id=1, source_target_pairs={{0,8},{8,16},{16,24},{24,1},{1,9},{9,17},{17,25},{25,2},{2,10},{10... | collective-permute-start | bytes 786440 | tf_op jit(solution)/shard_map/ppermute | solution.py:303
  80.1 1.3 collective-permute-start.13
  81.4 0.0 collective-permute-done.12.refs_9_
  81.4 2.1 %collective-permute-done.13.refs_11_ = f32[8,64,128]{2,1,0:T(8,128)S(1)} collective-permute-done((f32[8,64,128]{2,1,0:T(8,128)S(1)}, f32[8,64,128]{2,1,0:T(8,128)S(1)}, u32[]{:S(2)}, u32[]{:S(2)}) %collective-permute-start.13) | collective-permute-done | bytes 262176 | tf_op jit(solution)/shard_map/ppermute | solution.py:304
  83.5 26.1 %shard_map.51 = f32[8,64,128]{2,1,0:T(8,128)S(1)} custom-call(s32[2]{0:T(128)S(1)} %pad_add_fusion.place_ref, f32[12,3,9]{2,1,0:T(4,128)S(1)} %fusion.1.taps_ref, bf16[4,3,2,256,256]{4,3,2,1,0:T(8,128)(2,1)} %bitcast.30, bf16[3,20,64,128]{3,2,1,0:T(8,128)(2,1)S(1)} %get-tuple-element.23.refs_0_.refs_1_, ...), custom_call_target="tpu_custom_call" | custom-call | tf_op jit(solution)/shard_map/pallas_call | solution.py:270
  109.6 0.2 copy.16
  109.8 21.7 %all_to_all.18 = f32[8,64,128]{2,0,1:T(8,128)S(1)} all-to-all(f32[8,64,128]{2,0,1:T(8,128)S(1)} %copy.16), channel_id=1, replica_groups=mesh['view'=4,'vol'=8] {'vol'}, dimensions={1} | all-to-all | bytes 524288 | tf_op jit(solution)/shard_map/all_to_all | solution.py:347
  131.6 0.1 collective-permute-start.15
  131.7 0.5 collective-permute-start.14
  132.2 7.5 %collective-permute-done.15 = f32[64,8,128]{2,1,0:T(8,128)S(1)} collective-permute-done((f32[64,8,128]{2,1,0:T(8,128)S(1)}, f32[64,8,128]{2,1,0:T(8,128)S(1)}, u32[]{:S(2)}, u32[]{:S(2)}) %collective-permute-start.15) | collective-permute-done | bytes 262176 | tf_op jit(solution)/shard_map/ppermute | solution.py:290
  139.7 0.0 collective-permute-start.16
  139.7 0.1 broadcast_in_dim.8
  139.8 0.1 copy_dynamic-update-slice_fusion
  139.9 0.0 collective-permute-done.14
  140.0 1.3 collective-permute-done.16
  141.3 0.0 copy-start.3
  141.3 1.0 copy-done.3
  (8 shorter events, 0.2 us)
Async XLA Ops:
  0.0 9.5 %copy-start.4 = (f32[3,3,9]{2,1,0:T(4,128)S(1)}, f32[3,3,9]{2,1,0:T(4,128)}, u32[]{:S(2)}) copy-start(f32[3,3,9]{2,1,0:T(4,128)} %param.7) | copy-start | bytes 976
  0.0 8.8 %collective-permute-start = (f32[3,3,9]{2,1,0:T(4,128)}, f32[3,3,9]{2,1,0:T(4,128)S(1)}, u32[]{:S(2)}, u32[]{:S(2)}) collective-permute-start(f32[3,3,9]{2,1,0:T(4,128)} %param.7), channel_id=1, source_target_pairs={{0,24},{8,16},{16,8},{24,0},{1,25},{9,17},{17,9},{25,1},{2,26},{10... | collective-permute-start | bytes 980 | tf_op jit(solution)/shard_map/ppermute | solution.py:290
  3.1 1.4 copy-start.1
  4.5 0.7 copy-start.2
  8.8 24.4 %collective-permute-start.2 = (bf16[3,20,64,128]{3,2,1,0:T(8,128)(2,1)S(1)}, bf16[3,20,64,128]{3,2,1,0:T(8,128)(2,1)S(1)}, u32[]{:S(2)}, u32[]{:S(2)}) collective-permute-start(bf16[3,20,64,128]{3,2,1,0:T(8,128)(2,1)S(1)} %get-tuple-element.19), channel_id=1, source_target_pairs={{0,16},{8,24},{16,0},{24,8},{1,17},{9,25},{17,1},{25,9},{2,18},{10... | collective-permute-start | bytes 2949128 | tf_op jit(solution)/shard_map/ppermute | solution.py:290
  9.5 5.3 %collective-permute-start.1 = (f32[2,3,3,9]{3,2,1,0:T(4,128)S(1)}, f32[2,3,3,9]{3,2,1,0:T(4,128)S(1)}, u32[]{:S(2)}, u32[]{:S(2)}) collective-permute-start(f32[2,3,3,9]{3,2,1,0:T(4,128)S(1)} %pad_maximum_fusion.1), channel_id=1, source_target_pairs={{0,8},{8,0},{16,24},{24,16},{1,9},{9,1},{17,25},{25,17},{2,10},{10... | collective-permute-start | bytes 1952 | tf_op jit(solution)/shard_map/ppermute | solution.py:290
  9.7 9.2 %collective-permute-start.3 = (bf16[3,4,64,128]{3,2,1,0:T(8,128)(2,1)S(1)}, bf16[3,4,64,128]{3,2,1,0:T(8,128)(2,1)S(1)}, u32[]{:S(2)}, u32[]{:S(2)}) collective-permute-start(bf16[3,4,64,128]{3,2,1,0:T(8,128)(2,1)S(1)} %get-tuple-element.28), channel_id=1, source_target_pairs={{0,1},{1,2},{2,3},{3,4},{4,5},{5,6},{6,7},{8,9},{9,10},{10,11},{11... | collective-permute-start | bytes 589832 | tf_op jit(solution)/shard_map/ppermute | solution.py:326
  13.4 8.6 %collective-permute-start.4 = (bf16[3,4,64,128]{3,2,1,0:T(8,128)(2,1)S(1)}, bf16[3,4,64,128]{3,2,1,0:T(8,128)(2,1)S(1)}, u32[]{:S(2)}, u32[]{:S(2)}) collective-permute-start(bf16[3,4,64,128]{3,2,1,0:T(8,128)(2,1)S(1)} %get-tuple-element.27), channel_id=1, source_target_pairs={{1,0},{2,1},{3,2},{4,3},{5,4},{6,5},{7,6},{9,8},{10,9},{11,10},{12... | collective-permute-start | bytes 589832 | tf_op jit(solution)/shard_map/ppermute | solution.py:327
  14.7 26.7 %collective-permute-start.5 = (bf16[3,20,64,128]{3,2,1,0:T(8,128)(2,1)S(1)}, bf16[3,20,64,128]{3,2,1,0:T(8,128)(2,1)S(1)}, u32[]{:S(2)}, u32[]{:S(2)}) collective-permute-start(bf16[3,20,64,128]{3,2,1,0:T(8,128)(2,1)S(1)} %get-tuple-element.23.refs_0_.refs_1_), channel_id=1, source_target_pairs={{0,8},{8,0},{16,24},{24,16},{1,9},{9,1},{17,25},{25,17},{2,10},{10... | collective-permute-start | bytes 2949128 | tf_op jit(solution)/shard_map/ppermute | solution.py:290
  17.3 1.6 %copy-start = (bf16[12,2,256,256]{3,2,1,0:T(8,128)(2,1)}, bf16[12,2,256,256]{3,2,1,0:T(8,128)(2,1)S(1)}, u32[]{:S(2)}) copy-start(bf16[12,2,256,256]{3,2,1,0:T(8,128)(2,1)S(1)} %shard_map.47) | copy-start | bytes 9437188
  33.2 8.1 %collective-permute-start.6 = (bf16[3,20,64,128]{3,2,1,0:T(8,128)(2,1)S(1)}, bf16[3,20,64,128]{3,2,1,0:T(8,128)(2,1)S(1)}, u32[]{:S(2)}, u32[]{:S(2)}) collective-permute-start(bf16[3,20,64,128]{3,2,1,0:T(8,128)(2,1)S(1)} %collective-permute-done.2.refs_2_.refs_3_), channel_id=1, source_target_pairs={{0,8},{8,0},{16,24},{24,16},{1,9},{9,1},{17,25},{25,17},{2,10},{10... | collective-permute-start | bytes 2949128 | tf_op jit(solution)/shard_map/ppermute | solution.py:290
  33.3 6.6 %collective-permute-start.8 = (bf16[3,4,64,128]{3,2,1,0:T(8,128)(2,1)S(1)}, bf16[3,4,64,128]{3,2,1,0:T(8,128)(2,1)S(1)}, u32[]{:S(2)}, u32[]{:S(2)}) collective-permute-start(bf16[3,4,64,128]{3,2,1,0:T(8,128)(2,1)S(1)} %get-tuple-element.26), channel_id=1, source_target_pairs={{0,24},{8,16},{16,8},{24,0},{1,25},{9,17},{17,9},{25,1},{2,26},{10... | collective-permute-start | bytes 589832 | tf_op jit(solution)/shard_map/ppermute | solution.py:290
  33.6 6.6 %collective-permute-start.7 = (bf16[3,4,64,128]{3,2,1,0:T(8,128)(2,1)S(1)}, bf16[3,4,64,128]{3,2,1,0:T(8,128)(2,1)S(1)}, u32[]{:S(2)}, u32[]{:S(2)}) collective-permute-start(bf16[3,4,64,128]{3,2,1,0:T(8,128)(2,1)S(1)} %get-tuple-element.25.refs_4_.refs_5_), channel_id=1, source_target_pairs={{0,8},{8,0},{16,24},{24,16},{1,9},{9,1},{17,25},{25,17},{2,10},{10... | collective-permute-start | bytes 589832 | tf_op jit(solution)/shard_map/ppermute | solution.py:290
  39.8 1.5 %collective-permute-start.9 = (bf16[3,4,64,128]{3,2,1,0:T(8,128)(2,1)S(1)}, bf16[3,4,64,128]{3,2,1,0:T(8,128)(2,1)S(1)}, u32[]{:S(2)}, u32[]{:S(2)}) collective-permute-start(bf16[3,4,64,128]{3,2,1,0:T(8,128)(2,1)S(1)} %collective-permute-done.8.refs_7_.refs_8_), channel_id=1, source_target_pairs={{0,8},{8,0},{16,24},{24,16},{1,9},{9,1},{17,25},{25,17},{2,10},{10... | collective-permute-start | bytes 589832 | tf_op jit(solution)/shard_map/ppermute | solution.py:290
  43.3 3.6 %collective-permute-start.10 = (f32[4,64,128]{2,1,0:T(8,128)S(1)}, f32[4,64,128]{2,1,0:T(8,128)S(1)}, u32[]{:S(2)}, u32[]{:S(2)}) collective-permute-start(f32[4,64,128]{2,1,0:T(8,128)S(1)} %get-tuple-element.30), channel_id=1, source_target_pairs={{0,8},{8,16},{16,24},{24,1},{1,9},{9,17},{17,25},{25,2},{2,10},{10... | collective-permute-start | bytes 393224 | tf_op jit(solution)/shard_map/ppermute | solution.py:303
  45.6 3.2 %collective-permute-start.11 = (f32[4,64,128]{2,1,0:T(8,128)S(1)}, f32[4,64,128]{2,1,0:T(8,128)S(1)}, u32[]{:S(2)}, u32[]{:S(2)}) collective-permute-start(f32[4,64,128]{2,1,0:T(8,128)S(1)} %get-tuple-element.29), channel_id=1, source_target_pairs={{8,0},{16,8},{24,16},{1,24},{9,1},{17,9},{25,17},{2,25},{10,2},{18... | collective-permute-start | bytes 393224 | tf_op jit(solution)/shard_map/ppermute | solution.py:304
  75.0 6.4 %collective-permute-start.12 = (f32[8,64,128]{2,1,0:T(8,128)S(1)}, f32[8,64,128]{2,1,0:T(8,128)S(1)}, u32[]{:S(2)}, u32[]{:S(2)}) collective-permute-start(f32[8,64,128]{2,1,0:T(8,128)S(1)} %shard_map.50.refs_10_), channel_id=1, source_target_pairs={{0,8},{8,16},{16,24},{24,1},{1,9},{9,17},{17,25},{25,2},{2,10},{10... | collective-permute-start | bytes 786440 | tf_op jit(solution)/shard_map/ppermute | solution.py:303
  80.1 3.4 %collective-permute-start.13 = (f32[8,64,128]{2,1,0:T(8,128)S(1)}, f32[8,64,128]{2,1,0:T(8,128)S(1)}, u32[]{:S(2)}, u32[]{:S(2)}) collective-permute-start(f32[8,64,128]{2,1,0:T(8,128)S(1)} %shard_map.50.refs_10_), channel_id=1, source_target_pairs={{8,0},{16,8},{24,16},{1,24},{9,1},{17,9},{25,17},{2,25},{10,2},{18... | collective-permute-start | bytes 786440 | tf_op jit(solution)/shard_map/ppermute | solution.py:304
  131.6 8.1 %collective-permute-start.15 = (f32[64,8,128]{2,1,0:T(8,128)S(1)}, f32[64,8,128]{2,1,0:T(8,128)S(1)}, u32[]{:S(2)}, u32[]{:S(2)}) collective-permute-start(f32[64,8,128]{2,1,0:T(8,128)S(1)} %bitcast.37), channel_id=1, source_target_pairs={{0,16},{8,24},{16,0},{24,8},{1,17},{9,25},{17,1},{25,9},{2,18},{10... | collective-permute-start | bytes 786440 | tf_op jit(solution)/shard_map/ppermute | solution.py:290
  131.7 8.2 %collective-permute-start.14 = (f32[64,8,128]{2,1,0:T(8,128)S(1)}, f32[64,8,128]{2,1,0:T(8,128)S(1)}, u32[]{:S(2)}, u32[]{:S(2)}) collective-permute-start(f32[64,8,128]{2,1,0:T(8,128)S(1)} %bitcast.38), channel_id=1, source_target_pairs={{0,8},{8,0},{16,24},{24,16},{1,9},{9,1},{17,25},{25,17},{2,10},{10... | collective-permute-start | bytes 786440 | tf_op jit(solution)/shard_map/ppermute | solution.py:290
  139.7 1.5 %collective-permute-start.16 = (f32[64,8,128]{2,1,0:T(8,128)S(1)}, f32[64,8,128]{2,1,0:T(8,128)S(1)}, u32[]{:S(2)}, u32[]{:S(2)}) collective-permute-start(f32[64,8,128]{2,1,0:T(8,128)S(1)} %collective-permute-done.15), channel_id=1, source_target_pairs={{0,8},{8,0},{16,24},{24,16},{1,9},{9,1},{17,25},{25,17},{2,10},{10... | collective-permute-start | bytes 786440 | tf_op jit(solution)/shard_map/ppermute | solution.py:290
  141.3 1.0 copy-start.3

commit v6 on v5

--- a/solution.py
+++ b/solution.py
@@ -178,7 +178,7 @@
 def update_kernel(count, place_ref, taps_ref, *refs):
     bands_ref, windows = refs[0], list(zip(refs[1 : 1 + count], refs[1 + count : 1 + 2 * count]))
     parts = refs[1 + 2 * count : 4 + 2 * count]
-    out_ref, wide, left, ratio, back, logs = refs[4 + 2 * count :]
+    out_ref, wides, lefts, ratios, backs, logs = refs[4 + 2 * count :]
     step = pl.program_id(0)
     taps = taps_ref.shape[2]
     rim = taps // 2
@@ -190,10 +190,10 @@
     @pl.when(step == 0)
     def _():
         logs[...] = jnp.zeros_like(logs)
-        for scratch in (wide, back):
-            depth = scratch.shape[0]
-            scratch[:, :edge, :] = jnp.zeros((depth, edge, width), jnp.float32)
-            scratch[:, edge + rows :, :] = jnp.zeros((depth, edge, width), jnp.float32)
+        for scratch in (wides, backs):
+            zeros = jnp.zeros(scratch.shape[:2] + (edge, width), jnp.float32)
+            scratch[:, :, :edge, :] = zeros
+            scratch[:, :, edge + rows :, :] = zeros
 
     def correlate(gains, terms):
         total = gains[0] * terms[0]
@@ -201,59 +201,45 @@
             total = total + gains[t] * terms[t]
         return total
 
-    def along_x(source, gains, z):
+    def along_x(source, left, gains, z):
         for k in range(rows // 16):
             halved = []
             for half in range(2):
                 first = edge - rim + 16 * k + 8 * half
                 halved.append(correlate(gains, [source[z, pl.ds(first + t, 8), :] for t in range(taps)]))
             high, low = halves(jnp.concatenate(halved, axis=0))
-            at = pl.ds(pl.multiple_of(z * rows + 16 * k, 16), 16)
+            at = pl.ds(z * rows + 16 * k, 16)
             left[at, :width] = high
             left[at, width:] = low
 
+    held = None
     for group in range(count):
         view = group * pl.num_programs(0) + step
+        wide, left, ratio, back = (scratch.at[group % 2] for scratch in (wides, lefts, ratios, backs))
         gain_z = [taps_ref[view, 0, t] for t in range(taps)]
         gain_x = [taps_ref[view, 1, t] for t in range(taps)]
-
-        def along_z(k, carry):
-            row = pl.multiple_of(k * 8, 8)
-            column = [ref[z, pl.ds(row, 8), :] for ref, z in volume]
+        for k in range(rows // 8):
+            column = [ref[z, pl.ds(k * 8, 8), :] for ref, z in volume]
             for z in range(outer):
-                wide[z, pl.ds(row + edge, 8), :] = correlate(gain_z, column[z : z + taps])
-            return carry
-
-        lax.fori_loop(0, rows // 8, along_z, 0)
-
-        def forward_x(z, carry):
-            along_x(wide, gain_x, z)
-            return carry
-
-        lax.fori_loop(0, outer, forward_x, 0)
-
+                wide[z, pl.ds(k * 8 + edge, 8), :] = correlate(gain_z, column[z : z + taps])
+        for z in range(outer):
+            along_x(wide, left, gain_x, z)
         product = jnp.dot(left[...], bands_ref[group, 0, 0], preferred_element_type=jnp.float32)
         blurred = (product[:, :width] + product[:, width:]).reshape(outer, rows, width)
         for z in range(outer):
             ratio[z] = window_plane(place_ref, *windows[group], planes, z) / blurred[z]
-
-        def back_z(k, carry):
-            row = pl.multiple_of(k * 8, 8)
-            column = [ratio[z, pl.ds(row, 8), :] for z in range(outer)]
+        for k in range(rows // 8):
+            column = [ratio[z, pl.ds(k * 8, 8), :] for z in range(outer)]
             for z in range(planes):
-                back[z, pl.ds(row + edge, 8), :] = correlate(gain_z[::-1], column[z : z + taps])
-            return carry
-
-        lax.fori_loop(0, rows // 8, back_z, 0)
-
-        def back_x(z, carry):
-            along_x(back, gain_x[::-1], z)
-            return carry
-
-        lax.fori_loop(0, planes, back_x, 0)
-
+                back[z, pl.ds(k * 8 + edge, 8), :] = correlate(gain_z[::-1], column[z : z + taps])
+        for z in range(planes):
+            along_x(back, left, gain_x[::-1], z)
         product = jnp.dot(left[: planes * rows, :], bands_ref[group, 0, 1], preferred_element_type=jnp.float32)
-        logs[...] += jnp.log(product[:, :width] + product[:, width:]).reshape(logs.shape)
+        total = (product[:, :width] + product[:, width:]).reshape(logs.shape)
+        if group % 2 == 0:
+            held = total
+        else:
+            logs[...] += jnp.log(held * total)
 
     @pl.when(step == pl.num_programs(0) - 1)
     def _():
@@ -276,10 +262,10 @@
         + [VMEM] * 3,
         out_specs=VMEM,
         scratch_shapes=[
-            pltpu.VMEM((outer, rows + 16, width), jnp.float32),
-            pltpu.VMEM((outer * rows, 2 * width), jnp.bfloat16),
-            pltpu.VMEM((outer, rows, width), jnp.float32),
-            pltpu.VMEM((planes, rows + 16, width), jnp.float32),
+            pltpu.VMEM((2, outer, rows + 16, width), jnp.float32),
+            pltpu.VMEM((2, outer * rows, 2 * width), jnp.bfloat16),
+            pltpu.VMEM((2, outer, rows, width), jnp.float32),
+            pltpu.VMEM((2, planes, rows + 16, width), jnp.float32),
             pltpu.VMEM((planes, rows, width), jnp.float32),
         ],
         compiler_params=PARAMS,

time: 143 us -> 127 us (0.89)
  Pallas kernels: 61.7 us -> 46.1 us
    pallas_call x2, Pallas kernels: 52.2 us -> 36.6 us  [update(): pl.pallas_call(functools.partial(update_kernel, groups), grid=(count,), o...]
  transfers between devices with their start and end apart: 17 -> 17, of which waited for: 8 -> 8; matrix products, arithmetic and copies ran while one was open for 1% -> 1% of each run, Pallas kernels for 5% -> 6%
where the time goes in v6:
time: 127 us
  Pallas kernels  46.1 us (36%)
  waiting for transfers between devices  32.4 us (26%)
  blocking collectives  21.7 us (17%)
  starting transfers between devices  20 us (16%)
  local copies, waits for them, and re-layouts  5.89 us (5%)
    pallas_call x2, Pallas kernels, update(): pl.pallas_call(functools.partial(update_kernel, groups), grid=(count,), o...  36.6 us
    ppermute x11, waiting for transfers between devices, partner(): return lax.ppermute(value, 'view', [(i, i ^ bit) for i in range(members)])  25.5 us
    all_to_all x1, blocking collectives, per_device(): lax.all_to_all(joined, 'vol', split_axis=1, concat_axis=0, tiled=True)  21.7 us
    ppermute x2, starting transfers between devices, z_rims(): lax.ppermute(own[hop * planes - far:hop * planes - near], axes, up)  7.41 us
    pallas_call x2, Pallas kernels, resample(): pl.pallas_call(resample_kernel, grid=(views,), out_shape=(shape, shape),...  5.18 us
    ppermute x11, starting transfers between devices, partner(): return lax.ppermute(value, 'view', [(i, i ^ bit) for i in range(members)])  4.88 us
    unnamed x10, local copies, waits for them, and re-layouts  4.71 us
    ppermute x2, waiting for transfers between devices, z_rims(): lax.ppermute(own[near - (hop - 1) * planes:far - (hop - 1) * planes], axe...  3.87 us
  transfers between devices with their start and end apart: 17, of which 8 were waited for; matrix products, arithmetic and copies ran while one was open for 1% of the time, Pallas kernels for 6%

profile of v6, /device:TPU:0, one launch (start us, length us, event | category | flops | bytes accessed | tf_op | source)
XLA Modules:
  0.0 126.6 jit_solution(9238394174333724764)
XLA Ops:
  0.0 0.0 copy-start.4
  0.0 2.4 %collective-permute-start = (f32[3,3,9]{2,1,0:T(4,128)}, f32[3,3,9]{2,1,0:T(4,128)S(1)}, u32[]{:S(2)}, u32[]{:S(2)}) collective-permute-start(f32[3,3,9]{2,1,0:T(4,128)} %param.7), channel_id=1, source_target_pairs={{0,24},{8,16},{16,8},{24,0},{1,25},{9,17},{17,9},{25,1},{2,26},{10... | collective-permute-start | bytes 980 | tf_op jit(solution)/shard_map/ppermute | solution.py:276
  2.4 0.1 pad_add_fusion.place_ref
  2.5 0.7 broadcast_in_dim.9.offsets_ref
  3.1 0.0 copy-start.1
  3.1 1.4 %copy-done.1 = bf16[3,32,64,128]{3,2,1,0:T(8,128)(2,1)S(1)} copy-done((bf16[3,32,64,128]{3,2,1,0:T(8,128)(2,1)S(1)}, bf16[3,32,64,128]{3,2,1,0:T(8,128)(2,1)}, u32[]{:S(2)}) %copy-start.1) | copy-done | bytes 1572888
  4.5 0.0 copy-start.2
  4.5 0.7 copy-done.2
  5.3 3.6 %shard_map.46 = (bf16[3,20,64,128]{3,2,1,0:T(8,128)(2,1)S(1)}, bf16[3,20,64,128]{3,2,1,0:T(8,128)(2,1)S(1)}) custom-call(s32[2]{0:T(128)S(1)} %pad_add_fusion.place_ref, f32[3,8,64]{2,1,0:T(8,128)S(1)} %bitcast.31, s32[3,1,64]{2,1,0:T(1,128)S(1)} %broadcast_in_dim.9.offsets_ref, bf16[3,32,64,128]{3,2,1,0:T(8,128)(2,1)S(1)} %copy-done.1), custom_call_target="tpu_custom_call" | custom-call | tf_op jit(solution)/shard_map/pallas_call | solution.py:79
  8.8 0.0 collective-permute-done
  8.8 0.6 collective-permute-start.2
  9.5 0.0 copy-done.4
  9.5 0.2 collective-permute-start.1
  9.7 3.7 %collective-permute-start.3 = (bf16[3,4,64,128]{3,2,1,0:T(8,128)(2,1)S(1)}, bf16[3,4,64,128]{3,2,1,0:T(8,128)(2,1)S(1)}, u32[]{:S(2)}, u32[]{:S(2)}) collective-permute-start(bf16[3,4,64,128]{3,2,1,0:T(8,128)(2,1)S(1)} %get-tuple-element.28), channel_id=1, source_target_pairs={{0,1},{1,2},{2,3},{3,4},{4,5},{5,6},{6,7},{8,9},{9,10},{10,11},{11... | collective-permute-start | bytes 589832 | tf_op jit(solution)/shard_map/ppermute | solution.py:312
  13.4 1.3 %collective-permute-start.4 = (bf16[3,4,64,128]{3,2,1,0:T(8,128)(2,1)S(1)}, bf16[3,4,64,128]{3,2,1,0:T(8,128)(2,1)S(1)}, u32[]{:S(2)}, u32[]{:S(2)}) collective-permute-start(bf16[3,4,64,128]{3,2,1,0:T(8,128)(2,1)S(1)} %get-tuple-element.27), channel_id=1, source_target_pairs={{1,0},{2,1},{3,2},{4,3},{5,4},{6,5},{7,6},{9,8},{10,9},{11,10},{12... | collective-permute-start | bytes 589832 | tf_op jit(solution)/shard_map/ppermute | solution.py:313
  14.7 0.1 collective-permute-start.5
  14.8 0.0 collective-permute-done.1
  14.8 0.1 fusion.1.taps_ref
  14.9 2.4 %shard_map.47 = bf16[12,2,256,256]{3,2,1,0:T(8,128)(2,1)S(1)} custom-call(f32[12,3,9]{2,1,0:T(4,128)S(1)} %fusion.1.taps_ref), custom_call_target="tpu_custom_call" | custom-call | tf_op jit(solution)/shard_map/pallas_call | solution.py:115
  17.3 0.0 copy-start
  17.3 1.6 %copy-done = bf16[12,2,256,256]{3,2,1,0:T(8,128)(2,1)} copy-done((bf16[12,2,256,256]{3,2,1,0:T(8,128)(2,1)}, bf16[12,2,256,256]{3,2,1,0:T(8,128)(2,1)S(1)}, u32[]{:S(2)}) %copy-start) | copy-done | bytes 3145752
  18.9 0.0 collective-permute-done.3.refs_0_
  18.9 3.0 %collective-permute-done.4.refs_1_ = bf16[3,4,64,128]{3,2,1,0:T(8,128)(2,1)S(1)} collective-permute-done((bf16[3,4,64,128]{3,2,1,0:T(8,128)(2,1)S(1)}, bf16[3,4,64,128]{3,2,1,0:T(8,128)(2,1)S(1)}, u32[]{:S(2)}, u32[]{:S(2)}) %collective-permute-start.4) | collective-permute-done | bytes 196640 | tf_op jit(solution)/shard_map/ppermute | solution.py:313
  22.0 1.6 %shard_map.48 = (bf16[3,4,64,128]{3,2,1,0:T(8,128)(2,1)S(1)}, bf16[3,4,64,128]{3,2,1,0:T(8,128)(2,1)S(1)}) custom-call(s32[2]{0:T(128)S(1)} %pad_add_fusion.place_ref, f32[3,8,64]{2,1,0:T(8,128)S(1)} %bitcast.32, s32[3,1,64]{2,1,0:T(1,128)S(1)} %broadcast_in_dim.9.offsets_ref, bf16[3,4,64,128]{3,2,1,0:T(8,128)(2,1)S(1)} %collective-permute-done.3.refs_0_, ...), custom_call_target="tpu_custom_call" | custom-call | tf_op jit(solution)/shard_map/pallas_call | solution.py:79
  23.6 9.7 %collective-permute-done.2.refs_2_.refs_3_ = bf16[3,20,64,128]{3,2,1,0:T(8,128)(2,1)S(1)} collective-permute-done((bf16[3,20,64,128]{3,2,1,0:T(8,128)(2,1)S(1)}, bf16[3,20,64,128]{3,2,1,0:T(8,128)(2,1)S(1)}, u32[]{:S(2)}, u32[]{:S(2)}) %collective-permute-start.2) | collective-permute-done | bytes 983072 | tf_op jit(solution)/shard_map/ppermute | solution.py:276
  33.2 0.0 collective-permute-start.6
  33.2 0.4 collective-permute-start.8
  33.6 0.1 collective-permute-start.7
  33.8 6.0 %collective-permute-done.8.refs_7_.refs_8_ = bf16[3,4,64,128]{3,2,1,0:T(8,128)(2,1)S(1)} collective-permute-done((bf16[3,4,64,128]{3,2,1,0:T(8,128)(2,1)S(1)}, bf16[3,4,64,128]{3,2,1,0:T(8,128)(2,1)S(1)}, u32[]{:S(2)}, u32[]{:S(2)}) %collective-permute-start.8) | collective-permute-done | bytes 196640 | tf_op jit(solution)/shard_map/ppermute | solution.py:276
  39.8 0.5 collective-permute-start.9
  40.3 0.0 collective-permute-done.7.refs_5_.refs_6_
  40.3 1.1 collective-permute-done.9.refs_6_.refs_7_
  41.3 0.0 collective-permute-done.5.refs_1_.refs_2_
  41.3 0.0 collective-permute-done.6.refs_3_.refs_4_
  41.4 1.9 %shard_map.49.refs_10_ = f32[16,64,128]{2,1,0:T(8,128)S(1)} custom-call(s32[2]{0:T(128)S(1)} %pad_add_fusion.place_ref, bf16[3,20,64,128]{3,2,1,0:T(8,128)(2,1)S(1)} %get-tuple-element.23.refs_0_.refs_1_, bf16[3,20,64,128]{3,2,1,0:T(8,128)(2,1)S(1)} %collective-permute-done.5.refs_1_.refs_2_, ...), custom_call_target="tpu_custom_call" | custom-call | tf_op jit(solution)/shard_map/pallas_call | solution.py:168
  43.3 2.3 %collective-permute-start.10 = (f32[4,64,128]{2,1,0:T(8,128)S(1)}, f32[4,64,128]{2,1,0:T(8,128)S(1)}, u32[]{:S(2)}, u32[]{:S(2)}) collective-permute-start(f32[4,64,128]{2,1,0:T(8,128)S(1)} %get-tuple-element.30), channel_id=1, source_target_pairs={{0,8},{8,16},{16,24},{24,1},{1,9},{9,17},{17,25},{25,2},{2,10},{10... | collective-permute-start | bytes 393224 | tf_op jit(solution)/shard_map/ppermute | solution.py:289
  45.6 1.3 %collective-permute-start.11 = (f32[4,64,128]{2,1,0:T(8,128)S(1)}, f32[4,64,128]{2,1,0:T(8,128)S(1)}, u32[]{:S(2)}, u32[]{:S(2)}) collective-permute-start(f32[4,64,128]{2,1,0:T(8,128)S(1)} %get-tuple-element.29), channel_id=1, source_target_pairs={{8,0},{16,8},{24,16},{1,24},{9,1},{17,9},{25,17},{2,25},{10,2},{18... | collective-permute-start | bytes 393224 | tf_op jit(solution)/shard_map/ppermute | solution.py:290
  46.9 0.0 collective-permute-done.10.refs_9_
  46.9 1.9 %collective-permute-done.11.refs_11_ = f32[4,64,128]{2,1,0:T(8,128)S(1)} collective-permute-done((f32[4,64,128]{2,1,0:T(8,128)S(1)}, f32[4,64,128]{2,1,0:T(8,128)S(1)}, u32[]{:S(2)}, u32[]{:S(2)}) %collective-permute-start.11) | collective-permute-done | bytes 131104 | tf_op jit(solution)/shard_map/ppermute | solution.py:290
  48.8 18.3 %shard_map.50.refs_10_ = f32[8,64,128]{2,1,0:T(8,128)S(1)} custom-call(s32[2]{0:T(128)S(1)} %pad_add_fusion.place_ref, f32[12,3,9]{2,1,0:T(4,128)S(1)} %fusion.1.taps_ref, bf16[4,3,2,256,256]{4,3,2,1,0:T(8,128)(2,1)} %bitcast.29, bf16[3,20,64,128]{3,2,1,0:T(8,128)(2,1)S(1)} %get-tuple-element.23.refs_0_.refs_1_, ...), custom_call_target="tpu_custom_call" | custom-call | tf_op jit(solution)/shard_map/pallas_call | solution.py:256
  67.2 5.1 %collective-permute-start.12 = (f32[8,64,128]{2,1,0:T(8,128)S(1)}, f32[8,64,128]{2,1,0:T(8,128)S(1)}, u32[]{:S(2)}, u32[]{:S(2)}) collective-permute-start(f32[8,64,128]{2,1,0:T(8,128)S(1)} %shard_map.50.refs_10_), channel_id=1, source_target_pairs={{0,8},{8,16},{16,24},{24,1},{1,9},{9,17},{17,25},{25,2},{2,10},{10... | collective-permute-start | bytes 786440 | tf_op jit(solution)/shard_map/ppermute | solution.py:289
  72.3 1.5 %collective-permute-start.13 = (f32[8,64,128]{2,1,0:T(8,128)S(1)}, f32[8,64,128]{2,1,0:T(8,128)S(1)}, u32[]{:S(2)}, u32[]{:S(2)}) collective-permute-start(f32[8,64,128]{2,1,0:T(8,128)S(1)} %shard_map.50.refs_10_), channel_id=1, source_target_pairs={{8,0},{16,8},{24,16},{1,24},{9,1},{17,9},{25,17},{2,25},{10,2},{18... | collective-permute-start | bytes 786440 | tf_op jit(solution)/shard_map/ppermute | solution.py:290
  73.8 0.0 collective-permute-done.12.refs_9_
  73.8 1.9 %collective-permute-done.13.refs_11_ = f32[8,64,128]{2,1,0:T(8,128)S(1)} collective-permute-done((f32[8,64,128]{2,1,0:T(8,128)S(1)}, f32[8,64,128]{2,1,0:T(8,128)S(1)}, u32[]{:S(2)}, u32[]{:S(2)}) %collective-permute-start.13) | collective-permute-done | bytes 262176 | tf_op jit(solution)/shard_map/ppermute | solution.py:290
  75.7 18.3 %shard_map.51 = f32[8,64,128]{2,1,0:T(8,128)S(1)} custom-call(s32[2]{0:T(128)S(1)} %pad_add_fusion.place_ref, f32[12,3,9]{2,1,0:T(4,128)S(1)} %fusion.1.taps_ref, bf16[4,3,2,256,256]{4,3,2,1,0:T(8,128)(2,1)} %bitcast.30, bf16[3,20,64,128]{3,2,1,0:T(8,128)(2,1)S(1)} %get-tuple-element.23.refs_0_.refs_1_, ...), custom_call_target="tpu_custom_call" | custom-call | tf_op jit(solution)/shard_map/pallas_call | solution.py:256
  94.0 0.2 copy.16
  94.2 21.7 %all_to_all.18 = f32[8,64,128]{2,0,1:T(8,128)S(1)} all-to-all(f32[8,64,128]{2,0,1:T(8,128)S(1)} %copy.16), channel_id=1, replica_groups=mesh['view'=4,'vol'=8] {'vol'}, dimensions={1} | all-to-all | bytes 524288 | tf_op jit(solution)/shard_map/all_to_all | solution.py:333
  116.0 0.1 collective-permute-start.15
  116.1 0.6 collective-permute-start.14
  116.6 7.5 %collective-permute-done.15 = f32[64,8,128]{2,1,0:T(8,128)S(1)} collective-permute-done((f32[64,8,128]{2,1,0:T(8,128)S(1)}, f32[64,8,128]{2,1,0:T(8,128)S(1)}, u32[]{:S(2)}, u32[]{:S(2)}) %collective-permute-start.15) | collective-permute-done | bytes 262176 | tf_op jit(solution)/shard_map/ppermute | solution.py:276
  124.1 0.0 collective-permute-start.16
  124.1 0.1 broadcast_in_dim.8
  124.2 0.1 copy_dynamic-update-slice_fusion
  124.3 0.0 collective-permute-done.14
  124.4 1.3 collective-permute-done.16
  125.7 0.0 copy-start.3
  125.7 1.0 copy-done.3
  (8 shorter events, 0.2 us)
Async XLA Ops:
  0.0 9.5 %copy-start.4 = (f32[3,3,9]{2,1,0:T(4,128)S(1)}, f32[3,3,9]{2,1,0:T(4,128)}, u32[]{:S(2)}) copy-start(f32[3,3,9]{2,1,0:T(4,128)} %param.7) | copy-start | bytes 976
  0.0 8.8 %collective-permute-start = (f32[3,3,9]{2,1,0:T(4,128)}, f32[3,3,9]{2,1,0:T(4,128)S(1)}, u32[]{:S(2)}, u32[]{:S(2)}) collective-permute-start(f32[3,3,9]{2,1,0:T(4,128)} %param.7), channel_id=1, source_target_pairs={{0,24},{8,16},{16,8},{24,0},{1,25},{9,17},{17,9},{25,1},{2,26},{10... | collective-permute-start | bytes 980 | tf_op jit(solution)/shard_map/ppermute | solution.py:276
  3.1 1.4 %copy-start.1 = (bf16[3,32,64,128]{3,2,1,0:T(8,128)(2,1)S(1)}, bf16[3,32,64,128]{3,2,1,0:T(8,128)(2,1)}, u32[]{:S(2)}) copy-start(bf16[3,32,64,128]{3,2,1,0:T(8,128)(2,1)} %refs_0_.1) | copy-start | bytes 4718596
  4.5 0.7 copy-start.2
  8.8 24.4 %collective-permute-start.2 = (bf16[3,20,64,128]{3,2,1,0:T(8,128)(2,1)S(1)}, bf16[3,20,64,128]{3,2,1,0:T(8,128)(2,1)S(1)}, u32[]{:S(2)}, u32[]{:S(2)}) collective-permute-start(bf16[3,20,64,128]{3,2,1,0:T(8,128)(2,1)S(1)} %get-tuple-element.19), channel_id=1, source_target_pairs={{0,16},{8,24},{16,0},{24,8},{1,17},{9,25},{17,1},{25,9},{2,18},{10... | collective-permute-start | bytes 2949128 | tf_op jit(solution)/shard_map/ppermute | solution.py:276
  9.5 5.3 %collective-permute-start.1 = (f32[2,3,3,9]{3,2,1,0:T(4,128)S(1)}, f32[2,3,3,9]{3,2,1,0:T(4,128)S(1)}, u32[]{:S(2)}, u32[]{:S(2)}) collective-permute-start(f32[2,3,3,9]{3,2,1,0:T(4,128)S(1)} %pad_maximum_fusion.1), channel_id=1, source_target_pairs={{0,8},{8,0},{16,24},{24,16},{1,9},{9,1},{17,25},{25,17},{2,10},{10... | collective-permute-start | bytes 1952 | tf_op jit(solution)/shard_map/ppermute | solution.py:276
  9.7 9.2 %collective-permute-start.3 = (bf16[3,4,64,128]{3,2,1,0:T(8,128)(2,1)S(1)}, bf16[3,4,64,128]{3,2,1,0:T(8,128)(2,1)S(1)}, u32[]{:S(2)}, u32[]{:S(2)}) collective-permute-start(bf16[3,4,64,128]{3,2,1,0:T(8,128)(2,1)S(1)} %get-tuple-element.28), channel_id=1, source_target_pairs={{0,1},{1,2},{2,3},{3,4},{4,5},{5,6},{6,7},{8,9},{9,10},{10,11},{11... | collective-permute-start | bytes 589832 | tf_op jit(solution)/shard_map/ppermute | solution.py:312
  13.4 8.6 %collective-permute-start.4 = (bf16[3,4,64,128]{3,2,1,0:T(8,128)(2,1)S(1)}, bf16[3,4,64,128]{3,2,1,0:T(8,128)(2,1)S(1)}, u32[]{:S(2)}, u32[]{:S(2)}) collective-permute-start(bf16[3,4,64,128]{3,2,1,0:T(8,128)(2,1)S(1)} %get-tuple-element.27), channel_id=1, source_target_pairs={{1,0},{2,1},{3,2},{4,3},{5,4},{6,5},{7,6},{9,8},{10,9},{11,10},{12... | collective-permute-start | bytes 589832 | tf_op jit(solution)/shard_map/ppermute | solution.py:313
  14.7 26.7 %collective-permute-start.5 = (bf16[3,20,64,128]{3,2,1,0:T(8,128)(2,1)S(1)}, bf16[3,20,64,128]{3,2,1,0:T(8,128)(2,1)S(1)}, u32[]{:S(2)}, u32[]{:S(2)}) collective-permute-start(bf16[3,20,64,128]{3,2,1,0:T(8,128)(2,1)S(1)} %get-tuple-element.23.refs_0_.refs_1_), channel_id=1, source_target_pairs={{0,8},{8,0},{16,24},{24,16},{1,9},{9,1},{17,25},{25,17},{2,10},{10... | collective-permute-start | bytes 2949128 | tf_op jit(solution)/shard_map/ppermute | solution.py:276
  17.3 1.6 %copy-start = (bf16[12,2,256,256]{3,2,1,0:T(8,128)(2,1)}, bf16[12,2,256,256]{3,2,1,0:T(8,128)(2,1)S(1)}, u32[]{:S(2)}) copy-start(bf16[12,2,256,256]{3,2,1,0:T(8,128)(2,1)S(1)} %shard_map.47) | copy-start | bytes 9437188
  33.2 8.1 %collective-permute-start.6 = (bf16[3,20,64,128]{3,2,1,0:T(8,128)(2,1)S(1)}, bf16[3,20,64,128]{3,2,1,0:T(8,128)(2,1)S(1)}, u32[]{:S(2)}, u32[]{:S(2)}) collective-permute-start(bf16[3,20,64,128]{3,2,1,0:T(8,128)(2,1)S(1)} %collective-permute-done.2.refs_2_.refs_3_), channel_id=1, source_target_pairs={{0,8},{8,0},{16,24},{24,16},{1,9},{9,1},{17,25},{25,17},{2,10},{10... | collective-permute-start | bytes 2949128 | tf_op jit(solution)/shard_map/ppermute | solution.py:276
  33.2 6.6 %collective-permute-start.8 = (bf16[3,4,64,128]{3,2,1,0:T(8,128)(2,1)S(1)}, bf16[3,4,64,128]{3,2,1,0:T(8,128)(2,1)S(1)}, u32[]{:S(2)}, u32[]{:S(2)}) collective-permute-start(bf16[3,4,64,128]{3,2,1,0:T(8,128)(2,1)S(1)} %get-tuple-element.26), channel_id=1, source_target_pairs={{0,24},{8,16},{16,8},{24,0},{1,25},{9,17},{17,9},{25,1},{2,26},{10... | collective-permute-start | bytes 589832 | tf_op jit(solution)/shard_map/ppermute | solution.py:276
  33.6 6.6 %collective-permute-start.7 = (bf16[3,4,64,128]{3,2,1,0:T(8,128)(2,1)S(1)}, bf16[3,4,64,128]{3,2,1,0:T(8,128)(2,1)S(1)}, u32[]{:S(2)}, u32[]{:S(2)}) collective-permute-start(bf16[3,4,64,128]{3,2,1,0:T(8,128)(2,1)S(1)} %get-tuple-element.25.refs_4_.refs_5_), channel_id=1, source_target_pairs={{0,8},{8,0},{16,24},{24,16},{1,9},{9,1},{17,25},{25,17},{2,10},{10... | collective-permute-start | bytes 589832 | tf_op jit(solution)/shard_map/ppermute | solution.py:276
  39.8 1.5 %collective-permute-start.9 = (bf16[3,4,64,128]{3,2,1,0:T(8,128)(2,1)S(1)}, bf16[3,4,64,128]{3,2,1,0:T(8,128)(2,1)S(1)}, u32[]{:S(2)}, u32[]{:S(2)}) collective-permute-start(bf16[3,4,64,128]{3,2,1,0:T(8,128)(2,1)S(1)} %collective-permute-done.8.refs_7_.refs_8_), channel_id=1, source_target_pairs={{0,8},{8,0},{16,24},{24,16},{1,9},{9,1},{17,25},{25,17},{2,10},{10... | collective-permute-start | bytes 589832 | tf_op jit(solution)/shard_map/ppermute | solution.py:276
  43.3 3.6 %collective-permute-start.10 = (f32[4,64,128]{2,1,0:T(8,128)S(1)}, f32[4,64,128]{2,1,0:T(8,128)S(1)}, u32[]{:S(2)}, u32[]{:S(2)}) collective-permute-start(f32[4,64,128]{2,1,0:T(8,128)S(1)} %get-tuple-element.30), channel_id=1, source_target_pairs={{0,8},{8,16},{16,24},{24,1},{1,9},{9,17},{17,25},{25,2},{2,10},{10... | collective-permute-start | bytes 393224 | tf_op jit(solution)/shard_map/ppermute | solution.py:289
  45.6 3.2 %collective-permute-start.11 = (f32[4,64,128]{2,1,0:T(8,128)S(1)}, f32[4,64,128]{2,1,0:T(8,128)S(1)}, u32[]{:S(2)}, u32[]{:S(2)}) collective-permute-start(f32[4,64,128]{2,1,0:T(8,128)S(1)} %get-tuple-element.29), channel_id=1, source_target_pairs={{8,0},{16,8},{24,16},{1,24},{9,1},{17,9},{25,17},{2,25},{10,2},{18... | collective-permute-start | bytes 393224 | tf_op jit(solution)/shard_map/ppermute | solution.py:290
  67.2 6.6 %collective-permute-start.12 = (f32[8,64,128]{2,1,0:T(8,128)S(1)}, f32[8,64,128]{2,1,0:T(8,128)S(1)}, u32[]{:S(2)}, u32[]{:S(2)}) collective-permute-start(f32[8,64,128]{2,1,0:T(8,128)S(1)} %shard_map.50.refs_10_), channel_id=1, source_target_pairs={{0,8},{8,16},{16,24},{24,1},{1,9},{9,17},{17,25},{25,2},{2,10},{10... | collective-permute-start | bytes 786440 | tf_op jit(solution)/shard_map/ppermute | solution.py:289
  72.3 3.4 %collective-permute-start.13 = (f32[8,64,128]{2,1,0:T(8,128)S(1)}, f32[8,64,128]{2,1,0:T(8,128)S(1)}, u32[]{:S(2)}, u32[]{:S(2)}) collective-permute-start(f32[8,64,128]{2,1,0:T(8,128)S(1)} %shard_map.50.refs_10_), channel_id=1, source_target_pairs={{8,0},{16,8},{24,16},{1,24},{9,1},{17,9},{25,17},{2,25},{10,2},{18... | collective-permute-start | bytes 786440 | tf_op jit(solution)/shard_map/ppermute | solution.py:290
  116.0 8.1 %collective-permute-start.15 = (f32[64,8,128]{2,1,0:T(8,128)S(1)}, f32[64,8,128]{2,1,0:T(8,128)S(1)}, u32[]{:S(2)}, u32[]{:S(2)}) collective-permute-start(f32[64,8,128]{2,1,0:T(8,128)S(1)} %bitcast.37), channel_id=1, source_target_pairs={{0,16},{8,24},{16,0},{24,8},{1,17},{9,25},{17,1},{25,9},{2,18},{10... | collective-permute-start | bytes 786440 | tf_op jit(solution)/shard_map/ppermute | solution.py:276
  116.1 8.2 %collective-permute-start.14 = (f32[64,8,128]{2,1,0:T(8,128)S(1)}, f32[64,8,128]{2,1,0:T(8,128)S(1)}, u32[]{:S(2)}, u32[]{:S(2)}) collective-permute-start(f32[64,8,128]{2,1,0:T(8,128)S(1)} %bitcast.38), channel_id=1, source_target_pairs={{0,8},{8,0},{16,24},{24,16},{1,9},{9,1},{17,25},{25,17},{2,10},{10... | collective-permute-start | bytes 786440 | tf_op jit(solution)/shard_map/ppermute | solution.py:276
  124.1 1.5 %collective-permute-start.16 = (f32[64,8,128]{2,1,0:T(8,128)S(1)}, f32[64,8,128]{2,1,0:T(8,128)S(1)}, u32[]{:S(2)}, u32[]{:S(2)}) collective-permute-start(f32[64,8,128]{2,1,0:T(8,128)S(1)} %collective-permute-done.15), channel_id=1, source_target_pairs={{0,8},{8,0},{16,24},{24,16},{1,9},{9,1},{17,25},{25,17},{2,10},{10... | collective-permute-start | bytes 786440 | tf_op jit(solution)/shard_map/ppermute | solution.py:276
  125.7 1.0 copy-start.3

commit v7 on v6

--- a/solution.py
+++ b/solution.py
@@ -9,6 +9,7 @@
 
 ITERS = 2
 CORES = 2
+SUBLANES = 8
 VMEM = pl.BlockSpec(memory_space=pltpu.VMEM)
 SMEM = pl.BlockSpec(memory_space=pltpu.SMEM)
 PARAMS = pltpu.CompilerParams(vmem_limit_bytes=48 * 1024 * 1024)
@@ -37,6 +38,10 @@
     middle = rest.astype(jnp.bfloat16)
     low = (rest - middle.astype(jnp.float32)).astype(jnp.bfloat16)
     left = jnp.concatenate([high, middle, low], axis=1)
+    place = lax.broadcasted_iota(jnp.int32, (rows, rows), 0)
+    natural = (place % SUBLANES) * (rows // SUBLANES) + place // SUBLANES
+    order = (lax.broadcasted_iota(jnp.int32, (rows, rows), 1) == natural).astype(jnp.bfloat16)
+    left = jnp.dot(order, left, preferred_element_type=jnp.float32).astype(jnp.bfloat16)
 
     def four_planes(ref, base, first_z):
         for pair in range(2):
@@ -175,7 +180,7 @@
     )(place, *mains, *rims)
 
 
-def update_kernel(count, place_ref, taps_ref, *refs):
+def update_kernel(count, last, place_ref, taps_ref, *refs):
     bands_ref, windows = refs[0], list(zip(refs[1 : 1 + count], refs[1 + count : 1 + 2 * count]))
     parts = refs[1 + 2 * count : 4 + 2 * count]
     out_ref, wides, lefts, ratios, backs, logs = refs[4 + 2 * count :]
@@ -184,16 +189,14 @@
     rim = taps // 2
     planes, rows, width = out_ref.shape
     outer = planes + 2 * rim
-    edge = 8
+    tiles = rows // SUBLANES
     volume = [(ref, z) for ref in parts for z in range(ref.shape[0])]
+    tile = lambda k: pl.ds(k * SUBLANES, SUBLANES)
+    sublane = lax.broadcasted_iota(jnp.int32, (SUBLANES, width), 0)
 
     @pl.when(step == 0)
     def _():
         logs[...] = jnp.zeros_like(logs)
-        for scratch in (wides, backs):
-            zeros = jnp.zeros(scratch.shape[:2] + (edge, width), jnp.float32)
-            scratch[:, :, :edge, :] = zeros
-            scratch[:, :, edge + rows :, :] = zeros
 
     def correlate(gains, terms):
         total = gains[0] * terms[0]
@@ -201,14 +204,18 @@
             total = total + gains[t] * terms[t]
         return total
 
+    def along_z(column, gains, length):
+        return [correlate(gains, column[z : z + taps]) for z in range(length)]
+
     def along_x(source, left, gains, z):
-        for k in range(rows // 16):
-            halved = []
-            for half in range(2):
-                first = edge - rim + 16 * k + 8 * half
-                halved.append(correlate(gains, [source[z, pl.ds(first + t, 8), :] for t in range(taps)]))
-            high, low = halves(jnp.concatenate(halved, axis=0))
-            at = pl.ds(z * rows + 16 * k, 16)
+        row = [source[z, tile(k), :] for k in range(tiles)]
+        below = [jnp.where(sublane == 0, 0.0, pltpu.roll(part, 1, 0)) for part in row[tiles - rim :]]
+        above = [jnp.where(sublane == SUBLANES - 1, 0.0, pltpu.roll(part, SUBLANES - 1, 0)) for part in row[:rim]]
+        row = below + row + above
+        for k in range(0, tiles, 2):
+            pair = [correlate(gains, row[k : k + taps]), correlate(gains, row[k + 1 : k + 1 + taps])]
+            high, low = halves(jnp.concatenate(pair, axis=0))
+            at = pl.ds(z * rows + k * SUBLANES, 2 * SUBLANES)
             left[at, :width] = high
             left[at, width:] = low
 
@@ -218,20 +225,20 @@
         wide, left, ratio, back = (scratch.at[group % 2] for scratch in (wides, lefts, ratios, backs))
         gain_z = [taps_ref[view, 0, t] for t in range(taps)]
         gain_x = [taps_ref[view, 1, t] for t in range(taps)]
-        for k in range(rows // 8):
-            column = [ref[z, pl.ds(k * 8, 8), :] for ref, z in volume]
+        for k in range(tiles):
+            column = along_z([ref[z, tile(k), :] for ref, z in volume], gain_z, outer)
             for z in range(outer):
-                wide[z, pl.ds(k * 8 + edge, 8), :] = correlate(gain_z, column[z : z + taps])
+                wide[z, tile(k), :] = column[z]
         for z in range(outer):
             along_x(wide, left, gain_x, z)
         product = jnp.dot(left[...], bands_ref[group, 0, 0], preferred_element_type=jnp.float32)
         blurred = (product[:, :width] + product[:, width:]).reshape(outer, rows, width)
         for z in range(outer):
             ratio[z] = window_plane(place_ref, *windows[group], planes, z) / blurred[z]
-        for k in range(rows // 8):
-            column = [ratio[z, pl.ds(k * 8, 8), :] for z in range(outer)]
+        for k in range(tiles):
+            column = along_z([ratio[z, tile(k), :] for z in range(outer)], gain_z[::-1], planes)
             for z in range(planes):
-                back[z, pl.ds(k * 8 + edge, 8), :] = correlate(gain_z[::-1], column[z : z + taps])
+                back[z, tile(k), :] = column[z]
         for z in range(planes):
             along_x(back, left, gain_x[::-1], z)
         product = jnp.dot(left[: planes * rows, :], bands_ref[group, 0, 1], preferred_element_type=jnp.float32)
@@ -245,16 +252,21 @@
     def _():
         for z in range(planes):
             ref, at = volume[2 * rim + z]
-            out_ref[z] = ref[at] * jnp.exp(logs[z] / (count * pl.num_programs(0)))
-
-
-def update(place, taps, band, mains, rims, volume, planes):
+            for k in range(tiles):
+                value = ref[at, tile(k), :] * jnp.exp(logs[z, tile(k), :] / (count * pl.num_programs(0)))
+                if last:
+                    out_ref[z, pl.ds(k, SUBLANES, tiles), :] = value
+                else:
+                    out_ref[z, tile(k), :] = value
+
+
+def update(place, taps, band, mains, rims, volume, planes, last):
     groups = len(mains)
     count, _, rows, width = mains[0].shape
     outer = planes + taps.shape[2] - 1
     band = band.reshape((groups, count) + band.shape[1:])
     return pl.pallas_call(
-        functools.partial(update_kernel, groups),
+        functools.partial(update_kernel, groups, last),
         grid=(count,),
         out_shape=jax.ShapeDtypeStruct((planes, rows, width), jnp.float32),
         in_specs=[SMEM, SMEM, pl.BlockSpec((groups, 1) + band.shape[2:], lambda v: (0, v, 0, 0, 0))]
@@ -262,10 +274,10 @@
         + [VMEM] * 3,
         out_specs=VMEM,
         scratch_shapes=[
-            pltpu.VMEM((2, outer, rows + 16, width), jnp.float32),
+            pltpu.VMEM((2, outer, rows, width), jnp.float32),
             pltpu.VMEM((2, outer * rows, 2 * width), jnp.bfloat16),
             pltpu.VMEM((2, outer, rows, width), jnp.float32),
-            pltpu.VMEM((2, planes, rows + 16, width), jnp.float32),
+            pltpu.VMEM((2, planes, rows, width), jnp.float32),
             pltpu.VMEM((planes, rows, width), jnp.float32),
         ],
         compiler_params=PARAMS,
@@ -325,10 +337,10 @@
     rims = [own_rim, near_rim, far_rim, cross_rim]
     start = sum_views(place, mains, rims, planes)
     before, after = z_rims(start[rim : rim + planes], rim, 2 * rim, members, blocks)
-    joined = update(place, all_taps, band, mains, rims, (before, start, after), planes)
+    joined = update(place, all_taps, band, mains, rims, (before, start, after), planes, ITERS == 1)
     for turn in range(1, ITERS):
         before, after = z_rims(joined, 0, 2 * rim, members, blocks)
-        joined = update(place, all_taps, band, mains, rims, (before, joined, after), planes)
+        joined = update(place, all_taps, band, mains, rims, (before, joined, after), planes, turn == ITERS - 1)
 
     columns = lax.all_to_all(joined, "vol", split_axis=1, concat_axis=0, tiled=True)
     far = partner(columns, far_bit, members)

time: 127 us -> 124 us (0.976)
  Pallas kernels: 46.1 us -> 43.4 us
    pallas_call x2, Pallas kernels: 36.6 us -> 33.1 us  [update(): pl.pallas_call(functools.partial(update_kernel, groups, last), grid=(coun...]
  transfers between devices with their start and end apart: 17 -> 17, of which waited for: 8 -> 8; matrix products, arithmetic and copies ran while one was open for 1% -> 1% of each run, Pallas kernels for 6% -> 7%
where the time goes in v7:
time: 124 us
  Pallas kernels  43.4 us (35%)
  waiting for transfers between devices  32.1 us (26%)
  blocking collectives  21.7 us (18%)
  starting transfers between devices  20 us (16%)
  local copies, waits for them, and re-layouts  5.89 us (5%)
    pallas_call x2, Pallas kernels, update(): pl.pallas_call(functools.partial(update_kernel, groups, last), grid=(coun...  33.1 us
    ppermute x11, waiting for transfers between devices, partner(): return lax.ppermute(value, 'view', [(i, i ^ bit) for i in range(members)])  25.1 us
    all_to_all x1, blocking collectives, per_device(): lax.all_to_all(joined, 'vol', split_axis=1, concat_axis=0, tiled=True)  21.7 us
    ppermute x2, starting transfers between devices, z_rims(): lax.ppermute(own[hop * planes - far:hop * planes - near], axes, up)  7.41 us
    pallas_call x2, Pallas kernels, resample(): pl.pallas_call(resample_kernel, grid=(views,), out_shape=(shape, shape),...  5.93 us
    ppermute x11, starting transfers between devices, partner(): return lax.ppermute(value, 'view', [(i, i ^ bit) for i in range(members)])  4.88 us
    unnamed x10, local copies, waits for them, and re-layouts  4.71 us
    ppermute x2, waiting for transfers between devices, z_rims(): lax.ppermute(own[near - (hop - 1) * planes:far - (hop - 1) * planes], axe...  3.87 us
  transfers between devices with their start and end apart: 17, of which 8 were waited for; matrix products, arithmetic and copies ran while one was open for 1% of the time, Pallas kernels for 7%

profile of v7, /device:TPU:0, one launch (start us, length us, event | category | flops | bytes accessed | tf_op | source)
XLA Modules:
  0.0 123.5 jit_solution(10731973804283662089)
XLA Ops:
  0.0 0.0 copy-start.4
  0.0 2.4 %collective-permute-start = (f32[3,3,9]{2,1,0:T(4,128)}, f32[3,3,9]{2,1,0:T(4,128)S(1)}, u32[]{:S(2)}, u32[]{:S(2)}) collective-permute-start(f32[3,3,9]{2,1,0:T(4,128)} %param.7), channel_id=1, source_target_pairs={{0,24},{8,16},{16,8},{24,0},{1,25},{9,17},{17,9},{25,1},{2,26},{10... | collective-permute-start | bytes 980 | tf_op jit(solution)/shard_map/ppermute | solution.py:288
  2.4 0.1 pad_add_fusion.place_ref
  2.5 0.7 broadcast_in_dim.9.offsets_ref
  3.1 0.0 copy-start.1
  3.1 1.4 %copy-done.1 = bf16[3,32,64,128]{3,2,1,0:T(8,128)(2,1)S(1)} copy-done((bf16[3,32,64,128]{3,2,1,0:T(8,128)(2,1)S(1)}, bf16[3,32,64,128]{3,2,1,0:T(8,128)(2,1)}, u32[]{:S(2)}) %copy-start.1) | copy-done | bytes 1572888
  4.5 0.0 copy-start.2
  4.5 0.7 copy-done.2
  5.3 3.9 %shard_map.46 = (bf16[3,20,64,128]{3,2,1,0:T(8,128)(2,1)S(1)}, bf16[3,20,64,128]{3,2,1,0:T(8,128)(2,1)S(1)}) custom-call(s32[2]{0:T(128)S(1)} %pad_add_fusion.place_ref, f32[3,8,64]{2,1,0:T(8,128)S(1)} %bitcast.31, s32[3,1,64]{2,1,0:T(1,128)S(1)} %broadcast_in_dim.9.offsets_ref, bf16[3,32,64,128]{3,2,1,0:T(8,128)(2,1)S(1)} %copy-done.1), custom_call_target="tpu_custom_call" | custom-call | tf_op jit(solution)/shard_map/pallas_call | solution.py:84
  9.2 0.0 collective-permute-done
  9.2 0.6 collective-permute-start.2
  9.8 0.0 copy-done.4
  9.9 0.2 collective-permute-start.1
  10.1 3.7 %collective-permute-start.3 = (bf16[3,4,64,128]{3,2,1,0:T(8,128)(2,1)S(1)}, bf16[3,4,64,128]{3,2,1,0:T(8,128)(2,1)S(1)}, u32[]{:S(2)}, u32[]{:S(2)}) collective-permute-start(bf16[3,4,64,128]{3,2,1,0:T(8,128)(2,1)S(1)} %get-tuple-element.28), channel_id=1, source_target_pairs={{0,1},{1,2},{2,3},{3,4},{4,5},{5,6},{6,7},{8,9},{9,10},{10,11},{11... | collective-permute-start | bytes 589832 | tf_op jit(solution)/shard_map/ppermute | solution.py:324
  13.8 1.3 %collective-permute-start.4 = (bf16[3,4,64,128]{3,2,1,0:T(8,128)(2,1)S(1)}, bf16[3,4,64,128]{3,2,1,0:T(8,128)(2,1)S(1)}, u32[]{:S(2)}, u32[]{:S(2)}) collective-permute-start(bf16[3,4,64,128]{3,2,1,0:T(8,128)(2,1)S(1)} %get-tuple-element.27), channel_id=1, source_target_pairs={{1,0},{2,1},{3,2},{4,3},{5,4},{6,5},{7,6},{9,8},{10,9},{11,10},{12... | collective-permute-start | bytes 589832 | tf_op jit(solution)/shard_map/ppermute | solution.py:325
  15.1 0.1 collective-permute-start.5
  15.1 0.0 collective-permute-done.1
  15.2 0.1 fusion.1.taps_ref
  15.3 2.4 %shard_map.47 = bf16[12,2,256,256]{3,2,1,0:T(8,128)(2,1)S(1)} custom-call(f32[12,3,9]{2,1,0:T(4,128)S(1)} %fusion.1.taps_ref), custom_call_target="tpu_custom_call" | custom-call | tf_op jit(solution)/shard_map/pallas_call | solution.py:120
  17.7 0.0 copy-start
  17.7 1.6 %copy-done = bf16[12,2,256,256]{3,2,1,0:T(8,128)(2,1)} copy-done((bf16[12,2,256,256]{3,2,1,0:T(8,128)(2,1)}, bf16[12,2,256,256]{3,2,1,0:T(8,128)(2,1)S(1)}, u32[]{:S(2)}) %copy-start) | copy-done | bytes 3145752
  19.3 0.0 collective-permute-done.3.refs_0_
  19.3 3.0 %collective-permute-done.4.refs_1_ = bf16[3,4,64,128]{3,2,1,0:T(8,128)(2,1)S(1)} collective-permute-done((bf16[3,4,64,128]{3,2,1,0:T(8,128)(2,1)S(1)}, bf16[3,4,64,128]{3,2,1,0:T(8,128)(2,1)S(1)}, u32[]{:S(2)}, u32[]{:S(2)}) %collective-permute-start.4) | collective-permute-done | bytes 196640 | tf_op jit(solution)/shard_map/ppermute | solution.py:325
  22.3 2.0 %shard_map.48 = (bf16[3,4,64,128]{3,2,1,0:T(8,128)(2,1)S(1)}, bf16[3,4,64,128]{3,2,1,0:T(8,128)(2,1)S(1)}) custom-call(s32[2]{0:T(128)S(1)} %pad_add_fusion.place_ref, f32[3,8,64]{2,1,0:T(8,128)S(1)} %bitcast.32, s32[3,1,64]{2,1,0:T(1,128)S(1)} %broadcast_in_dim.9.offsets_ref, bf16[3,4,64,128]{3,2,1,0:T(8,128)(2,1)S(1)} %collective-permute-done.3.refs_0_, ...), custom_call_target="tpu_custom_call" | custom-call | tf_op jit(solution)/shard_map/pallas_call | solution.py:84
  24.3 9.3 %collective-permute-done.2.refs_2_.refs_3_ = bf16[3,20,64,128]{3,2,1,0:T(8,128)(2,1)S(1)} collective-permute-done((bf16[3,20,64,128]{3,2,1,0:T(8,128)(2,1)S(1)}, bf16[3,20,64,128]{3,2,1,0:T(8,128)(2,1)S(1)}, u32[]{:S(2)}, u32[]{:S(2)}) %collective-permute-start.2) | collective-permute-done | bytes 983072 | tf_op jit(solution)/shard_map/ppermute | solution.py:288
  33.6 0.0 collective-permute-start.6
  33.6 0.4 collective-permute-start.8
  34.0 0.1 collective-permute-start.7
  34.1 6.0 %collective-permute-done.8.refs_7_.refs_8_ = bf16[3,4,64,128]{3,2,1,0:T(8,128)(2,1)S(1)} collective-permute-done((bf16[3,4,64,128]{3,2,1,0:T(8,128)(2,1)S(1)}, bf16[3,4,64,128]{3,2,1,0:T(8,128)(2,1)S(1)}, u32[]{:S(2)}, u32[]{:S(2)}) %collective-permute-start.8) | collective-permute-done | bytes 196640 | tf_op jit(solution)/shard_map/ppermute | solution.py:288
  40.2 0.5 collective-permute-start.9
  40.6 0.0 collective-permute-done.7.refs_5_.refs_6_
  40.6 1.1 collective-permute-done.9.refs_6_.refs_7_
  41.7 0.0 collective-permute-done.5.refs_1_.refs_2_
  41.7 0.0 collective-permute-done.6.refs_3_.refs_4_
  41.7 1.9 %shard_map.49.refs_10_ = f32[16,64,128]{2,1,0:T(8,128)S(1)} custom-call(s32[2]{0:T(128)S(1)} %pad_add_fusion.place_ref, bf16[3,20,64,128]{3,2,1,0:T(8,128)(2,1)S(1)} %get-tuple-element.23.refs_0_.refs_1_, bf16[3,20,64,128]{3,2,1,0:T(8,128)(2,1)S(1)} %collective-permute-done.5.refs_1_.refs_2_, ...), custom_call_target="tpu_custom_call" | custom-call | tf_op jit(solution)/shard_map/pallas_call | solution.py:173
  43.7 2.3 %collective-permute-start.10 = (f32[4,64,128]{2,1,0:T(8,128)S(1)}, f32[4,64,128]{2,1,0:T(8,128)S(1)}, u32[]{:S(2)}, u32[]{:S(2)}) collective-permute-start(f32[4,64,128]{2,1,0:T(8,128)S(1)} %get-tuple-element.30), channel_id=1, source_target_pairs={{0,8},{8,16},{16,24},{24,1},{1,9},{9,17},{17,25},{25,2},{2,10},{10... | collective-permute-start | bytes 393224 | tf_op jit(solution)/shard_map/ppermute | solution.py:301
  46.0 1.3 %collective-permute-start.11 = (f32[4,64,128]{2,1,0:T(8,128)S(1)}, f32[4,64,128]{2,1,0:T(8,128)S(1)}, u32[]{:S(2)}, u32[]{:S(2)}) collective-permute-start(f32[4,64,128]{2,1,0:T(8,128)S(1)} %get-tuple-element.29), channel_id=1, source_target_pairs={{8,0},{16,8},{24,16},{1,24},{9,1},{17,9},{25,17},{2,25},{10,2},{18... | collective-permute-start | bytes 393224 | tf_op jit(solution)/shard_map/ppermute | solution.py:302
  47.3 0.0 collective-permute-done.10.refs_9_
  47.3 1.9 %collective-permute-done.11.refs_11_ = f32[4,64,128]{2,1,0:T(8,128)S(1)} collective-permute-done((f32[4,64,128]{2,1,0:T(8,128)S(1)}, f32[4,64,128]{2,1,0:T(8,128)S(1)}, u32[]{:S(2)}, u32[]{:S(2)}) %collective-permute-start.11) | collective-permute-done | bytes 131104 | tf_op jit(solution)/shard_map/ppermute | solution.py:302
  49.2 16.6 %shard_map.50.refs_10_ = f32[8,64,128]{2,1,0:T(8,128)S(1)} custom-call(s32[2]{0:T(128)S(1)} %pad_add_fusion.place_ref, f32[12,3,9]{2,1,0:T(4,128)S(1)} %fusion.1.taps_ref, bf16[4,3,2,256,256]{4,3,2,1,0:T(8,128)(2,1)} %bitcast.29, bf16[3,20,64,128]{3,2,1,0:T(8,128)(2,1)S(1)} %get-tuple-element.23.refs_0_.refs_1_, ...), custom_call_target="tpu_custom_call" | custom-call | tf_op jit(solution)/shard_map/pallas_call | solution.py:268
  65.8 5.1 %collective-permute-start.12 = (f32[8,64,128]{2,1,0:T(8,128)S(1)}, f32[8,64,128]{2,1,0:T(8,128)S(1)}, u32[]{:S(2)}, u32[]{:S(2)}) collective-permute-start(f32[8,64,128]{2,1,0:T(8,128)S(1)} %shard_map.50.refs_10_), channel_id=1, source_target_pairs={{0,8},{8,16},{16,24},{24,1},{1,9},{9,17},{17,25},{25,2},{2,10},{10... | collective-permute-start | bytes 786440 | tf_op jit(solution)/shard_map/ppermute | solution.py:301
  70.9 1.5 %collective-permute-start.13 = (f32[8,64,128]{2,1,0:T(8,128)S(1)}, f32[8,64,128]{2,1,0:T(8,128)S(1)}, u32[]{:S(2)}, u32[]{:S(2)}) collective-permute-start(f32[8,64,128]{2,1,0:T(8,128)S(1)} %shard_map.50.refs_10_), channel_id=1, source_target_pairs={{8,0},{16,8},{24,16},{1,24},{9,1},{17,9},{25,17},{2,25},{10,2},{18... | collective-permute-start | bytes 786440 | tf_op jit(solution)/shard_map/ppermute | solution.py:302
  72.4 0.0 collective-permute-done.12.refs_9_
  72.4 1.9 %collective-permute-done.13.refs_11_ = f32[8,64,128]{2,1,0:T(8,128)S(1)} collective-permute-done((f32[8,64,128]{2,1,0:T(8,128)S(1)}, f32[8,64,128]{2,1,0:T(8,128)S(1)}, u32[]{:S(2)}, u32[]{:S(2)}) %collective-permute-start.13) | collective-permute-done | bytes 262176 | tf_op jit(solution)/shard_map/ppermute | solution.py:302
  74.3 16.6 %shard_map.51 = f32[8,64,128]{2,1,0:T(8,128)S(1)} custom-call(s32[2]{0:T(128)S(1)} %pad_add_fusion.place_ref, f32[12,3,9]{2,1,0:T(4,128)S(1)} %fusion.1.taps_ref, bf16[4,3,2,256,256]{4,3,2,1,0:T(8,128)(2,1)} %bitcast.30, bf16[3,20,64,128]{3,2,1,0:T(8,128)(2,1)S(1)} %get-tuple-element.23.refs_0_.refs_1_, ...), custom_call_target="tpu_custom_call" | custom-call | tf_op jit(solution)/shard_map/pallas_call | solution.py:268
  90.9 0.2 copy.16
  91.1 21.7 %all_to_all.18 = f32[8,64,128]{2,0,1:T(8,128)S(1)} all-to-all(f32[8,64,128]{2,0,1:T(8,128)S(1)} %copy.16), channel_id=1, replica_groups=mesh['view'=4,'vol'=8] {'vol'}, dimensions={1} | all-to-all | bytes 524288 | tf_op jit(solution)/shard_map/all_to_all | solution.py:345
  112.9 0.1 collective-permute-start.15
  113.0 0.5 collective-permute-start.14
  113.5 7.5 %collective-permute-done.15 = f32[64,8,128]{2,1,0:T(8,128)S(1)} collective-permute-done((f32[64,8,128]{2,1,0:T(8,128)S(1)}, f32[64,8,128]{2,1,0:T(8,128)S(1)}, u32[]{:S(2)}, u32[]{:S(2)}) %collective-permute-start.15) | collective-permute-done | bytes 262176 | tf_op jit(solution)/shard_map/ppermute | solution.py:288
  121.0 0.0 collective-permute-start.16
  121.0 0.1 broadcast_in_dim.8
  121.1 0.1 copy_dynamic-update-slice_fusion
  121.2 0.0 collective-permute-done.14
  121.2 1.3 %collective-permute-done.16 = f32[64,8,128]{2,1,0:T(8,128)S(1)} collective-permute-done((f32[64,8,128]{2,1,0:T(8,128)S(1)}, f32[64,8,128]{2,1,0:T(8,128)S(1)}, u32[]{:S(2)}, u32[]{:S(2)}) %collective-permute-start.16) | collective-permute-done | bytes 262176 | tf_op jit(solution)/shard_map/ppermute | solution.py:288
  122.5 0.0 copy-start.3
  122.5 1.0 copy-done.3
  (8 shorter events, 0.2 us)
Async XLA Ops:
  0.0 9.8 %copy-start.4 = (f32[3,3,9]{2,1,0:T(4,128)S(1)}, f32[3,3,9]{2,1,0:T(4,128)}, u32[]{:S(2)}) copy-start(f32[3,3,9]{2,1,0:T(4,128)} %param.7) | copy-start | bytes 976
  0.0 9.2 %collective-permute-start = (f32[3,3,9]{2,1,0:T(4,128)}, f32[3,3,9]{2,1,0:T(4,128)S(1)}, u32[]{:S(2)}, u32[]{:S(2)}) collective-permute-start(f32[3,3,9]{2,1,0:T(4,128)} %param.7), channel_id=1, source_target_pairs={{0,24},{8,16},{16,8},{24,0},{1,25},{9,17},{17,9},{25,1},{2,26},{10... | collective-permute-start | bytes 980 | tf_op jit(solution)/shard_map/ppermute | solution.py:288
  3.1 1.4 %copy-start.1 = (bf16[3,32,64,128]{3,2,1,0:T(8,128)(2,1)S(1)}, bf16[3,32,64,128]{3,2,1,0:T(8,128)(2,1)}, u32[]{:S(2)}) copy-start(bf16[3,32,64,128]{3,2,1,0:T(8,128)(2,1)} %refs_0_.1) | copy-start | bytes 4718596
  4.5 0.7 copy-start.2
  9.2 24.4 %collective-permute-start.2 = (bf16[3,20,64,128]{3,2,1,0:T(8,128)(2,1)S(1)}, bf16[3,20,64,128]{3,2,1,0:T(8,128)(2,1)S(1)}, u32[]{:S(2)}, u32[]{:S(2)}) collective-permute-start(bf16[3,20,64,128]{3,2,1,0:T(8,128)(2,1)S(1)} %get-tuple-element.19), channel_id=1, source_target_pairs={{0,16},{8,24},{16,0},{24,8},{1,17},{9,25},{17,1},{25,9},{2,18},{10... | collective-permute-start | bytes 2949128 | tf_op jit(solution)/shard_map/ppermute | solution.py:288
  9.9 5.3 %collective-permute-start.1 = (f32[2,3,3,9]{3,2,1,0:T(4,128)S(1)}, f32[2,3,3,9]{3,2,1,0:T(4,128)S(1)}, u32[]{:S(2)}, u32[]{:S(2)}) collective-permute-start(f32[2,3,3,9]{3,2,1,0:T(4,128)S(1)} %pad_maximum_fusion.1), channel_id=1, source_target_pairs={{0,8},{8,0},{16,24},{24,16},{1,9},{9,1},{17,25},{25,17},{2,10},{10... | collective-permute-start | bytes 1952 | tf_op jit(solution)/shard_map/ppermute | solution.py:288
  10.1 9.2 %collective-permute-start.3 = (bf16[3,4,64,128]{3,2,1,0:T(8,128)(2,1)S(1)}, bf16[3,4,64,128]{3,2,1,0:T(8,128)(2,1)S(1)}, u32[]{:S(2)}, u32[]{:S(2)}) collective-permute-start(bf16[3,4,64,128]{3,2,1,0:T(8,128)(2,1)S(1)} %get-tuple-element.28), channel_id=1, source_target_pairs={{0,1},{1,2},{2,3},{3,4},{4,5},{5,6},{6,7},{8,9},{9,10},{10,11},{11... | collective-permute-start | bytes 589832 | tf_op jit(solution)/shard_map/ppermute | solution.py:324
  13.8 8.6 %collective-permute-start.4 = (bf16[3,4,64,128]{3,2,1,0:T(8,128)(2,1)S(1)}, bf16[3,4,64,128]{3,2,1,0:T(8,128)(2,1)S(1)}, u32[]{:S(2)}, u32[]{:S(2)}) collective-permute-start(bf16[3,4,64,128]{3,2,1,0:T(8,128)(2,1)S(1)} %get-tuple-element.27), channel_id=1, source_target_pairs={{1,0},{2,1},{3,2},{4,3},{5,4},{6,5},{7,6},{9,8},{10,9},{11,10},{12... | collective-permute-start | bytes 589832 | tf_op jit(solution)/shard_map/ppermute | solution.py:325
  15.1 26.7 %collective-permute-start.5 = (bf16[3,20,64,128]{3,2,1,0:T(8,128)(2,1)S(1)}, bf16[3,20,64,128]{3,2,1,0:T(8,128)(2,1)S(1)}, u32[]{:S(2)}, u32[]{:S(2)}) collective-permute-start(bf16[3,20,64,128]{3,2,1,0:T(8,128)(2,1)S(1)} %get-tuple-element.23.refs_0_.refs_1_), channel_id=1, source_target_pairs={{0,8},{8,0},{16,24},{24,16},{1,9},{9,1},{17,25},{25,17},{2,10},{10... | collective-permute-start | bytes 2949128 | tf_op jit(solution)/shard_map/ppermute | solution.py:288
  17.7 1.6 %copy-start = (bf16[12,2,256,256]{3,2,1,0:T(8,128)(2,1)}, bf16[12,2,256,256]{3,2,1,0:T(8,128)(2,1)S(1)}, u32[]{:S(2)}) copy-start(bf16[12,2,256,256]{3,2,1,0:T(8,128)(2,1)S(1)} %shard_map.47) | copy-start | bytes 9437188
  33.6 8.1 %collective-permute-start.6 = (bf16[3,20,64,128]{3,2,1,0:T(8,128)(2,1)S(1)}, bf16[3,20,64,128]{3,2,1,0:T(8,128)(2,1)S(1)}, u32[]{:S(2)}, u32[]{:S(2)}) collective-permute-start(bf16[3,20,64,128]{3,2,1,0:T(8,128)(2,1)S(1)} %collective-permute-done.2.refs_2_.refs_3_), channel_id=1, source_target_pairs={{0,8},{8,0},{16,24},{24,16},{1,9},{9,1},{17,25},{25,17},{2,10},{10... | collective-permute-start | bytes 2949128 | tf_op jit(solution)/shard_map/ppermute | solution.py:288
  33.6 6.6 %collective-permute-start.8 = (bf16[3,4,64,128]{3,2,1,0:T(8,128)(2,1)S(1)}, bf16[3,4,64,128]{3,2,1,0:T(8,128)(2,1)S(1)}, u32[]{:S(2)}, u32[]{:S(2)}) collective-permute-start(bf16[3,4,64,128]{3,2,1,0:T(8,128)(2,1)S(1)} %get-tuple-element.26), channel_id=1, source_target_pairs={{0,24},{8,16},{16,8},{24,0},{1,25},{9,17},{17,9},{25,1},{2,26},{10... | collective-permute-start | bytes 589832 | tf_op jit(solution)/shard_map/ppermute | solution.py:288
  34.0 6.6 %collective-permute-start.7 = (bf16[3,4,64,128]{3,2,1,0:T(8,128)(2,1)S(1)}, bf16[3,4,64,128]{3,2,1,0:T(8,128)(2,1)S(1)}, u32[]{:S(2)}, u32[]{:S(2)}) collective-permute-start(bf16[3,4,64,128]{3,2,1,0:T(8,128)(2,1)S(1)} %get-tuple-element.25.refs_4_.refs_5_), channel_id=1, source_target_pairs={{0,8},{8,0},{16,24},{24,16},{1,9},{9,1},{17,25},{25,17},{2,10},{10... | collective-permute-start | bytes 589832 | tf_op jit(solution)/shard_map/ppermute | solution.py:288
  40.2 1.5 %collective-permute-start.9 = (bf16[3,4,64,128]{3,2,1,0:T(8,128)(2,1)S(1)}, bf16[3,4,64,128]{3,2,1,0:T(8,128)(2,1)S(1)}, u32[]{:S(2)}, u32[]{:S(2)}) collective-permute-start(bf16[3,4,64,128]{3,2,1,0:T(8,128)(2,1)S(1)} %collective-permute-done.8.refs_7_.refs_8_), channel_id=1, source_target_pairs={{0,8},{8,0},{16,24},{24,16},{1,9},{9,1},{17,25},{25,17},{2,10},{10... | collective-permute-start | bytes 589832 | tf_op jit(solution)/shard_map/ppermute | solution.py:288
  43.7 3.6 %collective-permute-start.10 = (f32[4,64,128]{2,1,0:T(8,128)S(1)}, f32[4,64,128]{2,1,0:T(8,128)S(1)}, u32[]{:S(2)}, u32[]{:S(2)}) collective-permute-start(f32[4,64,128]{2,1,0:T(8,128)S(1)} %get-tuple-element.30), channel_id=1, source_target_pairs={{0,8},{8,16},{16,24},{24,1},{1,9},{9,17},{17,25},{25,2},{2,10},{10... | collective-permute-start | bytes 393224 | tf_op jit(solution)/shard_map/ppermute | solution.py:301
  46.0 3.2 %collective-permute-start.11 = (f32[4,64,128]{2,1,0:T(8,128)S(1)}, f32[4,64,128]{2,1,0:T(8,128)S(1)}, u32[]{:S(2)}, u32[]{:S(2)}) collective-permute-start(f32[4,64,128]{2,1,0:T(8,128)S(1)} %get-tuple-element.29), channel_id=1, source_target_pairs={{8,0},{16,8},{24,16},{1,24},{9,1},{17,9},{25,17},{2,25},{10,2},{18... | collective-permute-start | bytes 393224 | tf_op jit(solution)/shard_map/ppermute | solution.py:302
  65.8 6.6 %collective-permute-start.12 = (f32[8,64,128]{2,1,0:T(8,128)S(1)}, f32[8,64,128]{2,1,0:T(8,128)S(1)}, u32[]{:S(2)}, u32[]{:S(2)}) collective-permute-start(f32[8,64,128]{2,1,0:T(8,128)S(1)} %shard_map.50.refs_10_), channel_id=1, source_target_pairs={{0,8},{8,16},{16,24},{24,1},{1,9},{9,17},{17,25},{25,2},{2,10},{10... | collective-permute-start | bytes 786440 | tf_op jit(solution)/shard_map/ppermute | solution.py:301
  70.9 3.4 %collective-permute-start.13 = (f32[8,64,128]{2,1,0:T(8,128)S(1)}, f32[8,64,128]{2,1,0:T(8,128)S(1)}, u32[]{:S(2)}, u32[]{:S(2)}) collective-permute-start(f32[8,64,128]{2,1,0:T(8,128)S(1)} %shard_map.50.refs_10_), channel_id=1, source_target_pairs={{8,0},{16,8},{24,16},{1,24},{9,1},{17,9},{25,17},{2,25},{10,2},{18... | collective-permute-start | bytes 786440 | tf_op jit(solution)/shard_map/ppermute | solution.py:302
  112.9 8.1 %collective-permute-start.15 = (f32[64,8,128]{2,1,0:T(8,128)S(1)}, f32[64,8,128]{2,1,0:T(8,128)S(1)}, u32[]{:S(2)}, u32[]{:S(2)}) collective-permute-start(f32[64,8,128]{2,1,0:T(8,128)S(1)} %bitcast.37), channel_id=1, source_target_pairs={{0,16},{8,24},{16,0},{24,8},{1,17},{9,25},{17,1},{25,9},{2,18},{10... | collective-permute-start | bytes 786440 | tf_op jit(solution)/shard_map/ppermute | solution.py:288
  113.0 8.2 %collective-permute-start.14 = (f32[64,8,128]{2,1,0:T(8,128)S(1)}, f32[64,8,128]{2,1,0:T(8,128)S(1)}, u32[]{:S(2)}, u32[]{:S(2)}) collective-permute-start(f32[64,8,128]{2,1,0:T(8,128)S(1)} %bitcast.38), channel_id=1, source_target_pairs={{0,8},{8,0},{16,24},{24,16},{1,9},{9,1},{17,25},{25,17},{2,10},{10... | collective-permute-start | bytes 786440 | tf_op jit(solution)/shard_map/ppermute | solution.py:288
  121.0 1.5 %collective-permute-start.16 = (f32[64,8,128]{2,1,0:T(8,128)S(1)}, f32[64,8,128]{2,1,0:T(8,128)S(1)}, u32[]{:S(2)}, u32[]{:S(2)}) collective-permute-start(f32[64,8,128]{2,1,0:T(8,128)S(1)} %collective-permute-done.15), channel_id=1, source_target_pairs={{0,8},{8,0},{16,24},{24,16},{1,9},{9,1},{17,25},{25,17},{2,10},{10... | collective-permute-start | bytes 786440 | tf_op jit(solution)/shard_map/ppermute | solution.py:288
  122.5 1.0 copy-start.3

commit v8 on v7

v8 whole, which is shorter than its diff:
```python
import functools

import jax
import jax.numpy as jnp
from jax import lax
from jax.experimental import pallas as pl
from jax.experimental.pallas import tpu as pltpu
from jax.sharding import PartitionSpec as P

ITERS = 2
CORES = 2
SUBLANES = 8
VMEM = pl.BlockSpec(memory_space=pltpu.VMEM)
SMEM = pl.BlockSpec(memory_space=pltpu.SMEM)
PARAMS = pltpu.CompilerParams(vmem_limit_bytes=48 * 1024 * 1024)


def halves(value):
    high = value.astype(jnp.bfloat16)
    low = (value - high.astype(jnp.float32)).astype(jnp.bfloat16)
    return high, low


def resample_kernel(plan, place_ref, weights_ref, offsets_ref, *refs):
    count = 1 + max(segment[0] for parts in plan for segment in parts[1])
    sources, outs = refs[:count], refs[count:]
    weights = weights_ref[0]
    band, rows = weights.shape
    width = sources[0].shape[3]
    weights = weights / jnp.sum(weights, axis=0, keepdims=True)
    first = offsets_ref[0]
    source = lax.broadcasted_iota(jnp.int32, (rows, rows), 0)
    matrix = jnp.zeros((rows, rows), jnp.float32)
    for k in range(band):
        matrix = jnp.where(source == first + k, weights[k : k + 1, :], matrix)
    matrix = matrix.T
    high = matrix.astype(jnp.bfloat16)
    rest = matrix - high.astype(jnp.float32)
    middle = rest.astype(jnp.bfloat16)
    low = (rest - middle.astype(jnp.float32)).astype(jnp.bfloat16)
    left = jnp.concatenate([high, middle, low], axis=1)
    place = lax.broadcasted_iota(jnp.int32, (rows, rows), 0)
    natural = (place % SUBLANES) * (rows // SUBLANES) + place // SUBLANES
    order = (lax.broadcasted_iota(jnp.int32, (rows, rows), 1) == natural).astype(jnp.bfloat16)
    left = jnp.dot(order, left, preferred_element_type=jnp.float32).astype(jnp.bfloat16)

    for out_ref, (other, segments) in zip(outs, plan):
        half = 1 - place_ref[0] if other else place_ref[0]
        for index, start, target, length in segments:
            start = start[0] + (start[1] - start[0]) * half
            target = target[0] + (target[1] - target[0]) * half
            for z in range(0, length, 2):
                planes = [sources[index][0, start + z + i] for i in range(2)]
                planes = jnp.concatenate(planes, axis=1)
                planes = jnp.concatenate([planes, planes, planes], axis=0)
                total = jnp.dot(left, planes, preferred_element_type=jnp.float32).astype(jnp.bfloat16)
                for i in range(2):
                    out_ref[0, target + z + i] = total[:, i * width : (i + 1) * width]


def resample(place, weights, offsets, sources, plan):
    views, _, rows, width = sources[0].shape
    band = weights.shape[2]
    block = lambda planes: pl.BlockSpec((1, planes, rows, width), lambda v: (v, 0, 0, 0))
    counts = [sum(segment[3] for segment in segments) for _, segments in plan]
    return pl.pallas_call(
        functools.partial(resample_kernel, plan),
        grid=(views,),
        out_shape=[jax.ShapeDtypeStruct((views, count, rows, width), jnp.bfloat16) for count in counts],
        in_specs=[
            SMEM,
            pl.BlockSpec((1, band, rows), lambda v: (v, 0, 0)),
            pl.BlockSpec((1, 1, rows), lambda v: (v, 0, 0)),
        ]
        + [block(source.shape[1]) for source in sources],
        out_specs=[block(count) for count in counts],
        compiler_params=PARAMS,
    )(place, weights.transpose(0, 2, 1), offsets[:, None, :], *sources)


def bands_kernel(taps_ref, out_ref):
    view = pl.program_id(0)
    count = taps_ref.shape[2]
    width = out_ref.shape[2] // 2
    shape = (width, width)
    shift = lax.broadcasted_iota(jnp.int32, shape, 0) - lax.broadcasted_iota(jnp.int32, shape, 1)
    for way in range(2):
        band = jnp.zeros(shape, jnp.float32)
        for t in range(count):
            at = t - count // 2
            band = jnp.where(shift == (-at if way else at), taps_ref[view, 2, t], band)
        high, low = halves(band)
        out_ref[0, way, :width, :width] = high
        out_ref[0, way, width:, :width] = high
        out_ref[0, way, :width, width:] = low
        out_ref[0, way, width:, width:] = jnp.zeros_like(low)


def bands(taps, width):
    views = taps.shape[0]
    return pl.pallas_call(
        bands_kernel,
        grid=(views,),
        out_shape=jax.ShapeDtypeStruct((views, 2, 2 * width, 2 * width), jnp.bfloat16),
        in_specs=[SMEM],
        out_specs=pl.BlockSpec((1, 2, 2 * width, 2 * width), lambda v: (v, 0, 0, 0)),
        compiler_params=PARAMS,
    )(taps)


def gather_kernel(views, planes, rim, place_ref, *refs):
    count = (len(refs) - 3) // 2
    inner, edges = refs[:count], refs[count : 2 * count]
    bricks_ref, start_ref, window = refs[2 * count :]
    step = pl.program_id(0)
    half, core = place_ref[0], place_ref[1]
    main, side = inner[0].shape[1], edges[0].shape[1]

    @pl.when(step == 0)
    def _():
        start_ref[...] = jnp.zeros_like(start_ref)

    for group in range(count):
        for z in range(main):
            window[group, side * (1 - half) + z] = inner[group][0, z]
        for z in range(side):
            window[group, main * half + z] = edges[group][0, z]
    for z in range(planes + 2 * rim):
        total = start_ref[z]
        for group in range(count):
            plane = window[group, planes * core + z]
            bricks_ref[group, 0, z] = plane
            total = total + plane.astype(jnp.float32)
        start_ref[z] = total

    @pl.when(step == pl.num_programs(0) - 1)
    def _():
        start_ref[...] = start_ref[...] / views


def gather_views(place, inner, edges, planes, rim):
    groups = len(inner)
    count, main, rows, width = inner[0].shape
    outer, side = planes + 2 * rim, edges[0].shape[1]
    return pl.pallas_call(
        functools.partial(gather_kernel, groups * count, planes, rim),
        grid=(count,),
        out_shape=[
            jax.ShapeDtypeStruct((groups, count, outer, rows, width), jnp.bfloat16),
            jax.ShapeDtypeStruct((outer, rows, width), jnp.float32),
        ],
        in_specs=[SMEM] + [pl.BlockSpec((1,) + part.shape[1:], lambda v: (v, 0, 0, 0)) for part in inner + edges],
        out_specs=[pl.BlockSpec((groups, 1, outer, rows, width), lambda v: (0, v, 0, 0, 0)), VMEM],
        scratch_shapes=[pltpu.VMEM((groups, main + side, rows, width), jnp.bfloat16)],
        compiler_params=PARAMS,
    )(place, *inner, *edges)


def update_kernel(last, taps_ref, bands_ref, bricks_ref, before_ref, own_ref, after_ref, out_ref, *scratches):
    wides, lefts, ratios, backs, logs = scratches
    parts = (before_ref, own_ref, after_ref)
    count = bricks_ref.shape[0]
    step = pl.program_id(0)
    taps = taps_ref.shape[2]
    rim = taps // 2
    planes, rows, width = out_ref.shape
    outer = planes + 2 * rim
    tiles = rows // SUBLANES
    volume = [(ref, z) for ref in parts for z in range(ref.shape[0])]
    tile = lambda k: pl.ds(k * SUBLANES, SUBLANES)
    sublane = lax.broadcasted_iota(jnp.int32, (SUBLANES, width), 0)

    @pl.when(step == 0)
    def _():
        logs[...] = jnp.zeros_like(logs)

    def correlate(gains, terms):
        total = gains[0] * terms[0]
        for t in range(1, taps):
            total = total + gains[t] * terms[t]
        return total

    def along_z(column, gains, length):
        return [correlate(gains, column[z : z + taps]) for z in range(length)]

    def along_x(source, left, gains, z):
        row = [source[z, tile(k), :] for k in range(tiles)]
        below = [jnp.where(sublane == 0, 0.0, pltpu.roll(part, 1, 0)) for part in row[tiles - rim :]]
        above = [jnp.where(sublane == SUBLANES - 1, 0.0, pltpu.roll(part, SUBLANES - 1, 0)) for part in row[:rim]]
        row = below + row + above
        for k in range(0, tiles, 2):
            pair = [correlate(gains, row[k : k + taps]), correlate(gains, row[k + 1 : k + 1 + taps])]
            high, low = halves(jnp.concatenate(pair, axis=0))
            at = pl.ds(z * rows + k * SUBLANES, 2 * SUBLANES)
            left[at, :width] = high
            left[at, width:] = low

    held = None
    for group in range(count):
        view = group * pl.num_programs(0) + step
        wide, left, ratio, back = (scratch.at[group % 2] for scratch in (wides, lefts, ratios, backs))
        gain_z = [taps_ref[view, 0, t] for t in range(taps)]
        gain_x = [taps_ref[view, 1, t] for t in range(taps)]
        for k in range(tiles):
            column = along_z([ref[z, tile(k), :] for ref, z in volume], gain_z, outer)
            for z in range(outer):
                wide[z, tile(k), :] = column[z]
        for z in range(outer):
            along_x(wide, left, gain_x, z)
        product = jnp.dot(left[...], bands_ref[group, 0, 0], preferred_element_type=jnp.float32)
        blurred = (product[:, :width] + product[:, width:]).reshape(outer, rows, width)
        for z in range(outer):
            guess = pl.reciprocal(blurred[z], approx=True)
            guess = guess * (2.0 - blurred[z] * guess)
            ratio[z] = bricks_ref[group, 0, z].astype(jnp.float32) * guess
        for k in range(tiles):
            column = along_z([ratio[z, tile(k), :] for z in range(outer)], gain_z[::-1], planes)
            for z in range(planes):
                back[z, tile(k), :] = column[z]
        for z in range(planes):
            along_x(back, left, gain_x[::-1], z)
        product = jnp.dot(left[: planes * rows, :], bands_ref[group, 0, 1], preferred_element_type=jnp.float32)
        total = (product[:, :width] + product[:, width:]).reshape(logs.shape)
        if group % 2 == 0:
            held = total
        else:
            logs[...] += jnp.log(held * total)

    @pl.when(step == pl.num_programs(0) - 1)
    def _():
        for z in range(planes):
            ref, at = volume[2 * rim + z]
            for k in range(tiles):
                value = ref[at, tile(k), :] * jnp.exp(logs[z, tile(k), :] / (count * pl.num_programs(0)))
                if last:
                    out_ref[z, pl.ds(k, SUBLANES, tiles), :] = value
                else:
                    out_ref[z, tile(k), :] = value


def update(taps, band, bricks, volume, planes, last):
    groups, count, outer, rows, width = bricks.shape
    band = band.reshape((groups, count) + band.shape[1:])
    step = lambda v: (0, v, 0, 0, 0)
    return pl.pallas_call(
        functools.partial(update_kernel, last),
        grid=(count,),
        out_shape=jax.ShapeDtypeStruct((planes, rows, width), jnp.float32),
        in_specs=[
            SMEM,
            pl.BlockSpec((groups, 1) + band.shape[2:], step),
            pl.BlockSpec((groups, 1, outer, rows, width), step),
            VMEM,
            VMEM,
            VMEM,
        ],
        out_specs=VMEM,
        scratch_shapes=[
            pltpu.VMEM((2, outer, rows, width), jnp.float32),
            pltpu.VMEM((2, outer * rows, 2 * width), jnp.bfloat16),
            pltpu.VMEM((2, outer, rows, width), jnp.float32),
            pltpu.VMEM((2, planes, rows, width), jnp.float32),
            pltpu.VMEM((planes, rows, width), jnp.float32),
        ],
        compiler_params=PARAMS,
    )(taps, band, bricks, *volume)


def place_kernel(planes, place_ref, *refs):
    parts, out_ref = refs[:-1], refs[-1]
    blocks, members = out_ref.shape[:2]
    slot = place_ref[0]
    for index, part in enumerate(parts):
        for block in range(blocks):
            at = slot ^ index
            at = members - 1 - at if block % 2 else at
            out_ref[block, at] = part[block * planes : (block + 1) * planes]


def place_parts(slot, parts, planes):
    depth, rows, width = parts[0].shape
    return pl.pallas_call(
        functools.partial(place_kernel, planes),
        out_shape=jax.ShapeDtypeStruct((depth // planes, len(parts), planes, rows, width), jnp.float32),
        in_specs=[SMEM] + [VMEM] * len(parts),
        out_specs=VMEM,
        compiler_params=PARAMS,
    )(slot, *parts)


def partner(value, bit, members):
    return lax.ppermute(value, "view", [(i, i ^ bit) for i in range(members)])


def z_rims(own, inner, outer, members, blocks):
    planes = own.shape[0]
    axes = ("view", "vol")
    def at(line):
        block, slab = divmod(line, members)
        return (members - 1 - slab if block % 2 else slab) * blocks + block

    total = members * blocks
    before, after = [], []
    for hop in range(inner // planes + 1, -(-outer // planes) + 1):
        near, far = max((hop - 1) * planes, inner), min(hop * planes, outer)
        up = [(at(i), at(i + hop)) for i in range(total - hop)]
        down = [(at(i + hop), at(i)) for i in range(total - hop)]
        before.append(lax.ppermute(own[hop * planes - far : hop * planes - near], axes, up))
        after.append(lax.ppermute(own[near - (hop - 1) * planes : far - (hop - 1) * planes], axes, down))
    join = lambda parts: parts[0] if len(parts) == 1 else jnp.concatenate(parts)
    return join(before[::-1]), join(after)


def per_device(raw_views, weights, offsets, psf_taps):
    views, depth, rows, width = raw_views.shape
    members, blocks = lax.axis_size("view"), lax.axis_size("vol")
    rim = (psf_taps.shape[2] - 1) // 2
    planes = depth // members
    me = lax.axis_index("view")
    odd = lax.axis_index("vol") % 2
    slab = jnp.where(odd == 1, members - 1 - me, me)
    place = jnp.stack([slab // CORES, slab % CORES]).astype(jnp.int32)

    near_bit, far_bit = 1, CORES
    inner = (0, (rim, 2 * planes - rim), (0, 0), 2 * planes)
    first_edge = (0, (0, depth - rim), (rim, 0), rim)
    second_edge = (1, (0, rim), (0, rim), rim)
    cross_taps = partner(psf_taps, near_bit + far_bit, members)
    (far_inner,) = resample(place, weights, offsets, [raw_views], [(True, [inner])])
    far_inner, raw_later, cross_taps = lax.optimization_barrier((far_inner, raw_views, cross_taps))
    far_inner = partner(far_inner, far_bit, members)
    up = [(i, i + 1) for i in range(blocks - 1)]
    down = [(i + 1, i) for i in range(blocks - 1)]
    raw_before = lax.ppermute(raw_later[:, depth - rim :], "vol", up)
    raw_after = lax.ppermute(raw_later[:, :rim], "vol", down)
    (own_inner,) = resample(place, weights, offsets, [raw_later], [(False, [inner])])
    near_inner = partner(own_inner, near_bit, members)
    pair_taps = partner(jnp.stack([psf_taps, cross_taps]), near_bit, members)
    all_taps = jnp.concatenate([psf_taps, pair_taps[0], pair_taps[1], cross_taps])
    all_taps = all_taps / jnp.sum(all_taps, axis=-1, keepdims=True)
    band = bands(all_taps, width)
    raw_rims = jnp.concatenate([raw_before, raw_after], axis=1)
    edge = [first_edge, second_edge]
    far_edge, own_edge = resample(place, weights, offsets, [raw_later, raw_rims], [(True, edge), (False, edge)])
    far_edge = partner(far_edge, far_bit, members)
    near_edge = partner(own_edge, near_bit, members)
    far_edge, band, own_edge = lax.optimization_barrier((far_edge, band, own_edge))
    inners = [own_inner, near_inner, far_inner, partner(far_inner, near_bit, members)]
    edges = [own_edge, near_edge, far_edge, partner(far_edge, near_bit, members)]
    bricks, start = gather_views(place, inners, edges, planes, rim)
    before, after = z_rims(start[rim : rim + planes], rim, 2 * rim, members, blocks)
    joined = update(all_taps, band, bricks, (before, start, after), planes, ITERS == 1)
    for turn in range(1, ITERS):
        before, after = z_rims(joined, 0, 2 * rim, members, blocks)
        joined = update(all_taps, band, bricks, (before, joined, after), planes, turn == ITERS - 1)

    columns = lax.all_to_all(joined, "vol", split_axis=1, concat_axis=0, tiled=True)
    far = partner(columns, far_bit, members)
    near = partner(columns, near_bit, members)
    parts = [columns, near, far, partner(far, near_bit, members)]
    result = place_parts(me.reshape(1).astype(jnp.int32), parts, planes)
    return result.reshape((blocks * depth,) + columns.shape[1:])


def solution(mesh):
    placed = (
        P("view", "vol", None, None),
        P("view", None, None),
        P("view", None),
        P("view", None, None),
    )
    return jax.shard_map(
        per_device, mesh=mesh, in_specs=placed, out_specs=P(None, "vol", None), check_vma=False
    )
```

time: 124 us -> 120 us (0.968)
  waiting for transfers between devices: 32.1 us -> 25.2 us
  Pallas kernels: 43.4 us -> 47 us
  local copies, waits for them, and re-layouts: 5.89 us -> 3.06 us
    ppermute x11, waiting for transfers between devices: 25.1 us -> 18.1 us  [partner(): return lax.ppermute(value, 'view', [(i, i ^ bit) for i in range(members)])]
    ppermute x2, waiting for transfers between devices: 3.87 us -> 0.01 us  [z_rims(): lax.ppermute(own[near - (hop - 1) * planes:far - (hop - 1) * planes], axe...]
    pallas_call x5 -> x7, Pallas kernels: 41 us -> 44.7 us  [the longest x2 33.7 us: update(): pl.pallas_call(functools.partial(update_kernel, last), grid=(count,), out...]
    unnamed x10 -> x6, local copies, waits for them, and re-layouts: 4.71 us -> 2.12 us
    ppermute x2, waiting for transfers between devices: 0.01 us -> 1.89 us  [z_rims(): lax.ppermute(own[hop * planes - far:hop * planes - near], axes, up)]
  transfers between devices with their start and end apart: 17 -> 17, of which waited for: 8 -> 10; matrix products, arithmetic and copies ran while one was open for 1% -> 1% of each run, Pallas kernels for 7% -> 7%
where the time goes in v8:
time: 120 us; the launch traced here: 119 us
  Pallas kernels  47 us (39%)
  waiting for transfers between devices  25.2 us (21%)
  blocking collectives  22.4 us (19%)
  starting transfers between devices  21.1 us (18%)
  local copies, waits for them, and re-layouts  3.06 us (3%)
    pallas_call x2, Pallas kernels, update(): pl.pallas_call(functools.partial(update_kernel, last), grid=(count,), out...  33.7 us
    all_to_all x1, blocking collectives, per_device(): lax.all_to_all(joined, 'vol', split_axis=1, concat_axis=0, tiled=True)  22.4 us
    ppermute x11, waiting for transfers between devices, partner(): return lax.ppermute(value, 'view', [(i, i ^ bit) for i in range(members)])  18.1 us
    ppermute x2, starting transfers between devices, z_rims(): lax.ppermute(own[hop * planes - far:hop * planes - near], axes, up)  8.1 us
    pallas_call x3, Pallas kernels, resample(): pl.pallas_call(functools.partial(resample_kernel, plan), grid=(views,), o...  6.54 us
    ppermute x11, starting transfers between devices, partner(): return lax.ppermute(value, 'view', [(i, i ^ bit) for i in range(members)])  5.65 us
    ppermute x1, waiting for transfers between devices, per_device(): raw_after = lax.ppermute(raw_later[:, :rim], 'vol', down)  4.08 us
    ppermute x1, starting transfers between devices, per_device(): raw_before = lax.ppermute(raw_later[:, depth - rim:], 'vol', up)  3.45 us
  transfers between devices with their start and end apart: 17, of which 10 were waited for; matrix products, arithmetic and copies ran while one was open for 1% of the time, Pallas kernels for 7%

profile of v8, /device:TPU:0, one launch (start us, length us, event | category | flops | bytes accessed | tf_op | source)
XLA Modules:
  0.0 119.2 jit_solution(2771118082829762716)
XLA Ops:
  0.0 2.4 %collective-permute-start = (f32[3,3,9]{2,1,0:T(4,128)}, f32[3,3,9]{2,1,0:T(4,128)S(1)}, u32[]{:S(2)}, u32[]{:S(2)}) collective-permute-start(f32[3,3,9]{2,1,0:T(4,128)} %param.7), channel_id=1, source_target_pairs={{0,24},{8,16},{16,8},{24,0},{1,25},{9,17},{17,9},{25,1},{2,26},{10... | collective-permute-start | bytes 980 | tf_op jit(solution)/shard_map/ppermute | solution.py:292
  2.4 0.1 pad_add_fusion.place_ref
  2.5 0.7 broadcast_in_dim.2.offsets_ref
  3.1 0.0 copy-start
  3.1 1.4 %copy-done = bf16[3,32,64,128]{3,2,1,0:T(8,128)(2,1)S(1)} copy-done((bf16[3,32,64,128]{3,2,1,0:T(8,128)(2,1)S(1)}, bf16[3,32,64,128]{3,2,1,0:T(8,128)(2,1)}, u32[]{:S(2)}) %copy-start) | copy-done | bytes 1572888
  4.5 0.0 copy-start.1
  4.5 0.7 copy-done.1
  5.3 2.2 %shard_map.46 = bf16[3,16,64,128]{3,2,1,0:T(8,128)(2,1)S(1)} custom-call(s32[2]{0:T(128)S(1)} %pad_add_fusion.place_ref, f32[3,8,64]{2,1,0:T(8,128)S(1)} %bitcast.21, s32[3,1,64]{2,1,0:T(1,128)S(1)} %broadcast_in_dim.2.offsets_ref, bf16[3,32,64,128]{3,2,1,0:T(8,128)(2,1)S(1)} %copy-done), custom_call_target="tpu_custom_call" | custom-call | tf_op jit(solution)/shard_map/pallas_call | solution.py:66
  7.4 0.0 copy-start.2
  7.4 0.0 collective-permute-done
  7.5 0.6 collective-permute-start.6
  8.1 3.4 %collective-permute-start.2 = (bf16[3,4,64,128]{3,2,1,0:T(8,128)(2,1)S(1)}, bf16[3,4,64,128]{3,2,1,0:T(8,128)(2,1)S(1)}, u32[]{:S(2)}, u32[]{:S(2)}) collective-permute-start(bf16[3,4,64,128]{3,2,1,0:T(8,128)(2,1)S(1)} %get-tuple-element.25), channel_id=1, source_target_pairs={{0,1},{1,2},{2,3},{3,4},{4,5},{5,6},{6,7},{8,9},{9,10},{10,11},{11... | collective-permute-start | bytes 589832 | tf_op jit(solution)/shard_map/ppermute | solution.py:334
  11.6 1.3 %collective-permute-start.3 = (bf16[3,4,64,128]{3,2,1,0:T(8,128)(2,1)S(1)}, bf16[3,4,64,128]{3,2,1,0:T(8,128)(2,1)S(1)}, u32[]{:S(2)}, u32[]{:S(2)}) collective-permute-start(bf16[3,4,64,128]{3,2,1,0:T(8,128)(2,1)S(1)} %get-tuple-element.26), channel_id=1, source_target_pairs={{1,0},{2,1},{3,2},{4,3},{5,4},{6,5},{7,6},{9,8},{10,9},{11,10},{12... | collective-permute-start | bytes 589832 | tf_op jit(solution)/shard_map/ppermute | solution.py:335
  12.9 2.2 %shard_map.49.refs_0_ = bf16[3,16,64,128]{3,2,1,0:T(8,128)(2,1)S(1)} custom-call(s32[2]{0:T(128)S(1)} %pad_add_fusion.place_ref, f32[3,8,64]{2,1,0:T(8,128)S(1)} %bitcast.22, s32[3,1,64]{2,1,0:T(1,128)S(1)} %broadcast_in_dim.2.offsets_ref, bf16[3,32,64,128]{3,2,1,0:T(8,128)(2,1)S(1)} %copy-done), custom_call_target="tpu_custom_call" | custom-call | tf_op jit(solution)/shard_map/pallas_call | solution.py:66
  15.1 0.1 collective-permute-start.5
  15.2 1.1 collective-permute-done.2
  16.3 4.1 %collective-permute-done.3 = bf16[3,4,64,128]{3,2,1,0:T(8,128)(2,1)S(1)} collective-permute-done((bf16[3,4,64,128]{3,2,1,0:T(8,128)(2,1)S(1)}, bf16[3,4,64,128]{3,2,1,0:T(8,128)(2,1)S(1)}, u32[]{:S(2)}, u32[]{:S(2)}) %collective-permute-start.3) | collective-permute-done | bytes 196640 | tf_op jit(solution)/shard_map/ppermute | solution.py:335
  20.4 2.2 %shard_map.47 = (bf16[3,8,64,128]{3,2,1,0:T(8,128)(2,1)S(1)}, bf16[3,8,64,128]{3,2,1,0:T(8,128)(2,1)S(1)}) custom-call(s32[2]{0:T(128)S(1)} %pad_add_fusion.place_ref, f32[3,8,64]{2,1,0:T(8,128)S(1)} %bitcast.23, s32[3,1,64]{2,1,0:T(1,128)S(1)} %broadcast_in_dim.2.offsets_ref, bf16[3,32,64,128]{3,2,1,0:T(8,128)(2,1)S(1)} %copy-done, ...), custom_call_target="tpu_custom_call" | custom-call | tf_op jit(solution)/shard_map/pallas_call | solution.py:66
  22.6 1.6 %collective-permute-start.4 = (bf16[3,8,64,128]{3,2,1,0:T(8,128)(2,1)S(1)}, bf16[3,8,64,128]{3,2,1,0:T(8,128)(2,1)S(1)}, u32[]{:S(2)}, u32[]{:S(2)}) collective-permute-start(bf16[3,8,64,128]{3,2,1,0:T(8,128)(2,1)S(1)} %get-tuple-element.17), channel_id=1, source_target_pairs={{0,16},{8,24},{16,0},{24,8},{1,17},{9,25},{17,1},{25,9},{2,18},{10... | collective-permute-start | bytes 1179656 | tf_op jit(solution)/shard_map/ppermute | solution.py:292
  24.2 3.8 %collective-permute-done.6.refs_2_ = bf16[3,16,64,128]{3,2,1,0:T(8,128)(2,1)S(1)} collective-permute-done((bf16[3,16,64,128]{3,2,1,0:T(8,128)(2,1)S(1)}, bf16[3,16,64,128]{3,2,1,0:T(8,128)(2,1)S(1)}, u32[]{:S(2)}, u32[]{:S(2)}) %collective-permute-start.6) | collective-permute-done | bytes 786464 | tf_op jit(solution)/shard_map/ppermute | solution.py:292
  27.9 0.0 collective-permute-start.7
  27.9 0.0 copy-done.2
  27.9 0.6 collective-permute-start.1
  28.5 1.7 %collective-permute-done.1 = f32[2,3,3,9]{3,2,1,0:T(4,128)S(1)} collective-permute-done((f32[2,3,3,9]{3,2,1,0:T(4,128)S(1)}, f32[2,3,3,9]{3,2,1,0:T(4,128)S(1)}, u32[]{:S(2)}, u32[]{:S(2)}) %collective-permute-start.1) | collective-permute-done | bytes 680 | tf_op jit(solution)/shard_map/ppermute | solution.py:292
  30.2 0.1 fusion.1.taps_ref
  30.3 2.4 %shard_map.48 = bf16[12,2,256,256]{3,2,1,0:T(8,128)(2,1)S(1)} custom-call(f32[12,3,9]{2,1,0:T(4,128)S(1)} %fusion.1.taps_ref), custom_call_target="tpu_custom_call" | custom-call | tf_op jit(solution)/shard_map/pallas_call | solution.py:101
  32.7 0.2 collective-permute-start.8
  32.9 3.1 %collective-permute-done.4.refs_6_ = bf16[3,8,64,128]{3,2,1,0:T(8,128)(2,1)S(1)} collective-permute-done((bf16[3,8,64,128]{3,2,1,0:T(8,128)(2,1)S(1)}, bf16[3,8,64,128]{3,2,1,0:T(8,128)(2,1)S(1)}, u32[]{:S(2)}, u32[]{:S(2)}) %collective-permute-start.4) | collective-permute-done | bytes 393248 | tf_op jit(solution)/shard_map/ppermute | solution.py:292
  36.1 0.0 collective-permute-start.9
  36.1 0.0 collective-permute-done.8.refs_5_
  36.1 0.0 collective-permute-done.5.refs_1_
  36.1 1.7 %collective-permute-done.9.refs_7_ = bf16[3,8,64,128]{3,2,1,0:T(8,128)(2,1)S(1)} collective-permute-done((bf16[3,8,64,128]{3,2,1,0:T(8,128)(2,1)S(1)}, bf16[3,8,64,128]{3,2,1,0:T(8,128)(2,1)S(1)}, u32[]{:S(2)}, u32[]{:S(2)}) %collective-permute-start.9) | collective-permute-done | bytes 393248 | tf_op jit(solution)/shard_map/ppermute | solution.py:292
  37.8 0.0 collective-permute-done.7.refs_3_
  37.8 3.4 %shard_map.50 = (bf16[4,3,16,64,128]{4,3,2,1,0:T(8,128)(2,1)}, f32[16,64,128]{2,1,0:T(8,128)S(1)}) custom-call(s32[2]{0:T(128)S(1)} %pad_add_fusion.place_ref, bf16[3,16,64,128]{3,2,1,0:T(8,128)(2,1)S(1)} %shard_map.49.refs_0_, bf16[3,16,64,128]{3,2,1,0:T(8,128)(2,1)S(1)} %collective-permute-done.5.refs_1_, ...), custom_call_target="tpu_custom_call" | custom-call | tf_op jit(solution)/shard_map/pallas_call | solution.py:145
  41.2 1.3 %collective-permute-start.11 = (f32[4,64,128]{2,1,0:T(8,128)S(1)}, f32[4,64,128]{2,1,0:T(8,128)S(1)}, u32[]{:S(2)}, u32[]{:S(2)}) collective-permute-start(f32[4,64,128]{2,1,0:T(8,128)S(1)} %get-tuple-element.27), channel_id=1, source_target_pairs={{8,0},{16,8},{24,16},{25,24},{17,25},{9,17},{1,9},{2,1},{10,2},{18... | collective-permute-start | bytes 393224 | tf_op jit(solution)/shard_map/ppermute | solution.py:309
  42.5 3.0 %collective-permute-start.10 = (f32[4,64,128]{2,1,0:T(8,128)S(1)}, f32[4,64,128]{2,1,0:T(8,128)S(1)}, u32[]{:S(2)}, u32[]{:S(2)}) collective-permute-start(f32[4,64,128]{2,1,0:T(8,128)S(1)} %get-tuple-element.28), channel_id=1, source_target_pairs={{0,8},{8,16},{16,24},{24,25},{25,17},{17,9},{9,1},{1,2},{2,10},{10... | collective-permute-start | bytes 393224 | tf_op jit(solution)/shard_map/ppermute | solution.py:308
  45.5 0.0 collective-permute-done.11.after_ref
  45.5 1.0 collective-permute-done.10.before_ref
  46.5 16.9 %shard_map.51.own_ref = f32[8,64,128]{2,1,0:T(8,128)S(1)} custom-call(f32[12,3,9]{2,1,0:T(4,128)S(1)} %fusion.1.taps_ref, bf16[4,3,2,256,256]{4,3,2,1,0:T(8,128)(2,1)S(1)} %bitcast.16, bf16[4,3,16,64,128]{4,3,2,1,0:T(8,128)(2,1)} %get-tuple-element.23.bricks_ref, f32[4,64,128]{2,1,0:T(8,128)S(1)} %collective-permute-done.10.before_ref, ...), custom_call_target="tpu_custom_call" | custom-call | tf_op jit(solution)/shard_map/pallas_call | solution.py:245
  63.4 1.3 %collective-permute-start.13 = (f32[8,64,128]{2,1,0:T(8,128)S(1)}, f32[8,64,128]{2,1,0:T(8,128)S(1)}, u32[]{:S(2)}, u32[]{:S(2)}) collective-permute-start(f32[8,64,128]{2,1,0:T(8,128)S(1)} %shard_map.51.own_ref), channel_id=1, source_target_pairs={{8,0},{16,8},{24,16},{25,24},{17,25},{9,17},{1,9},{2,1},{10,2},{18... | collective-permute-start | bytes 786440 | tf_op jit(solution)/shard_map/ppermute | solution.py:309
  64.7 5.1 %collective-permute-start.12 = (f32[8,64,128]{2,1,0:T(8,128)S(1)}, f32[8,64,128]{2,1,0:T(8,128)S(1)}, u32[]{:S(2)}, u32[]{:S(2)}) collective-permute-start(f32[8,64,128]{2,1,0:T(8,128)S(1)} %shard_map.51.own_ref), channel_id=1, source_target_pairs={{0,8},{8,16},{16,24},{24,25},{25,17},{17,9},{9,1},{1,2},{2,10},{10... | collective-permute-start | bytes 786440 | tf_op jit(solution)/shard_map/ppermute | solution.py:308
  69.7 0.0 collective-permute-done.13.after_ref
  69.7 0.9 collective-permute-done.12.before_ref
  70.7 16.8 %shard_map.52 = f32[8,64,128]{2,1,0:T(8,128)S(1)} custom-call(f32[12,3,9]{2,1,0:T(4,128)S(1)} %fusion.1.taps_ref, bf16[4,3,2,256,256]{4,3,2,1,0:T(8,128)(2,1)S(1)} %bitcast.17, bf16[4,3,16,64,128]{4,3,2,1,0:T(8,128)(2,1)} %get-tuple-element.23.bricks_ref, f32[8,64,128]{2,1,0:T(8,128)S(1)} %collective-permute-done.12.before_ref, ...), custom_call_target="tpu_custom_call" | custom-call | tf_op jit(solution)/shard_map/pallas_call | solution.py:245
  87.5 0.2 copy.6
  87.7 22.4 %all_to_all.18 = f32[8,64,128]{2,0,1:T(8,128)S(1)} all-to-all(f32[8,64,128]{2,0,1:T(8,128)S(1)} %copy.6), channel_id=1, replica_groups=mesh['view'=4,'vol'=8] {'vol'}, dimensions={1} | all-to-all | bytes 524288 | tf_op jit(solution)/shard_map/all_to_all | solution.py:357
  110.2 0.1 collective-permute-start.15
  110.3 0.1 collective-permute-start.14
  110.4 6.3 %collective-permute-done.15.refs_2_ = f32[64,8,128]{2,1,0:T(8,128)S(1)} collective-permute-done((f32[64,8,128]{2,1,0:T(8,128)S(1)}, f32[64,8,128]{2,1,0:T(8,128)S(1)}, u32[]{:S(2)}, u32[]{:S(2)}) %collective-permute-start.15) | collective-permute-done | bytes 262176 | tf_op jit(solution)/shard_map/ppermute | solution.py:292
  116.6 0.0 collective-permute-start.16
  116.6 0.0 collective-permute-done.14.refs_1_
  116.6 1.5 %collective-permute-done.16.refs_3_ = f32[64,8,128]{2,1,0:T(8,128)S(1)} collective-permute-done((f32[64,8,128]{2,1,0:T(8,128)S(1)}, f32[64,8,128]{2,1,0:T(8,128)S(1)}, u32[]{:S(2)}, u32[]{:S(2)}) %collective-permute-start.16) | collective-permute-done | bytes 262176 | tf_op jit(solution)/shard_map/ppermute | solution.py:292
  118.2 1.0 shard_map.53
  (6 shorter events, 0.1 us)
Async XLA Ops:
  0.0 7.4 %collective-permute-start = (f32[3,3,9]{2,1,0:T(4,128)}, f32[3,3,9]{2,1,0:T(4,128)S(1)}, u32[]{:S(2)}, u32[]{:S(2)}) collective-permute-start(f32[3,3,9]{2,1,0:T(4,128)} %param.7), channel_id=1, source_target_pairs={{0,24},{8,16},{16,8},{24,0},{1,25},{9,17},{17,9},{25,1},{2,26},{10... | collective-permute-start | bytes 980 | tf_op jit(solution)/shard_map/ppermute | solution.py:292
  3.1 1.4 %copy-start = (bf16[3,32,64,128]{3,2,1,0:T(8,128)(2,1)S(1)}, bf16[3,32,64,128]{3,2,1,0:T(8,128)(2,1)}, u32[]{:S(2)}) copy-start(bf16[3,32,64,128]{3,2,1,0:T(8,128)(2,1)} %refs_0_.3) | copy-start | bytes 4718596
  4.5 0.7 copy-start.1
  7.4 20.5 %copy-start.2 = (f32[3,3,9]{2,1,0:T(4,128)S(1)}, f32[3,3,9]{2,1,0:T(4,128)}, u32[]{:S(2)}) copy-start(f32[3,3,9]{2,1,0:T(4,128)} %param.7) | copy-start | bytes 976
  7.5 20.5 %collective-permute-start.6 = (bf16[3,16,64,128]{3,2,1,0:T(8,128)(2,1)S(1)}, bf16[3,16,64,128]{3,2,1,0:T(8,128)(2,1)S(1)}, u32[]{:S(2)}, u32[]{:S(2)}) collective-permute-start(bf16[3,16,64,128]{3,2,1,0:T(8,128)(2,1)S(1)} %shard_map.46), channel_id=1, source_target_pairs={{0,16},{8,24},{16,0},{24,8},{1,17},{9,25},{17,1},{25,9},{2,18},{10... | collective-permute-start | bytes 2359304 | tf_op jit(solution)/shard_map/ppermute | solution.py:292
  8.1 8.2 %collective-permute-start.2 = (bf16[3,4,64,128]{3,2,1,0:T(8,128)(2,1)S(1)}, bf16[3,4,64,128]{3,2,1,0:T(8,128)(2,1)S(1)}, u32[]{:S(2)}, u32[]{:S(2)}) collective-permute-start(bf16[3,4,64,128]{3,2,1,0:T(8,128)(2,1)S(1)} %get-tuple-element.25), channel_id=1, source_target_pairs={{0,1},{1,2},{2,3},{3,4},{4,5},{5,6},{6,7},{8,9},{9,10},{10,11},{11... | collective-permute-start | bytes 589832 | tf_op jit(solution)/shard_map/ppermute | solution.py:334
  11.6 8.8 %collective-permute-start.3 = (bf16[3,4,64,128]{3,2,1,0:T(8,128)(2,1)S(1)}, bf16[3,4,64,128]{3,2,1,0:T(8,128)(2,1)S(1)}, u32[]{:S(2)}, u32[]{:S(2)}) collective-permute-start(bf16[3,4,64,128]{3,2,1,0:T(8,128)(2,1)S(1)} %get-tuple-element.26), channel_id=1, source_target_pairs={{1,0},{2,1},{3,2},{4,3},{5,4},{6,5},{7,6},{9,8},{10,9},{11,10},{12... | collective-permute-start | bytes 589832 | tf_op jit(solution)/shard_map/ppermute | solution.py:335
  15.1 21.0 %collective-permute-start.5 = (bf16[3,16,64,128]{3,2,1,0:T(8,128)(2,1)S(1)}, bf16[3,16,64,128]{3,2,1,0:T(8,128)(2,1)S(1)}, u32[]{:S(2)}, u32[]{:S(2)}) collective-permute-start(bf16[3,16,64,128]{3,2,1,0:T(8,128)(2,1)S(1)} %shard_map.49.refs_0_), channel_id=1, source_target_pairs={{0,8},{8,0},{16,24},{24,16},{1,9},{9,1},{17,25},{25,17},{2,10},{10... | collective-permute-start | bytes 2359304 | tf_op jit(solution)/shard_map/ppermute | solution.py:292
  22.6 13.5 %collective-permute-start.4 = (bf16[3,8,64,128]{3,2,1,0:T(8,128)(2,1)S(1)}, bf16[3,8,64,128]{3,2,1,0:T(8,128)(2,1)S(1)}, u32[]{:S(2)}, u32[]{:S(2)}) collective-permute-start(bf16[3,8,64,128]{3,2,1,0:T(8,128)(2,1)S(1)} %get-tuple-element.17), channel_id=1, source_target_pairs={{0,16},{8,24},{16,0},{24,8},{1,17},{9,25},{17,1},{25,9},{2,18},{10... | collective-permute-start | bytes 1179656 | tf_op jit(solution)/shard_map/ppermute | solution.py:292
  27.9 9.9 %collective-permute-start.7 = (bf16[3,16,64,128]{3,2,1,0:T(8,128)(2,1)S(1)}, bf16[3,16,64,128]{3,2,1,0:T(8,128)(2,1)S(1)}, u32[]{:S(2)}, u32[]{:S(2)}) collective-permute-start(bf16[3,16,64,128]{3,2,1,0:T(8,128)(2,1)S(1)} %collective-permute-done.6.refs_2_), channel_id=1, source_target_pairs={{0,8},{8,0},{16,24},{24,16},{1,9},{9,1},{17,25},{25,17},{2,10},{10... | collective-permute-start | bytes 2359304 | tf_op jit(solution)/shard_map/ppermute | solution.py:292
  27.9 2.3 %collective-permute-start.1 = (f32[2,3,3,9]{3,2,1,0:T(4,128)S(1)}, f32[2,3,3,9]{3,2,1,0:T(4,128)S(1)}, u32[]{:S(2)}, u32[]{:S(2)}) collective-permute-start(f32[2,3,3,9]{3,2,1,0:T(4,128)S(1)} %pad_maximum_fusion.2), channel_id=1, source_target_pairs={{0,8},{8,0},{16,24},{24,16},{1,9},{9,1},{17,25},{25,17},{2,10},{10... | collective-permute-start | bytes 1952 | tf_op jit(solution)/shard_map/ppermute | solution.py:292
  32.7 3.3 %collective-permute-start.8 = (bf16[3,8,64,128]{3,2,1,0:T(8,128)(2,1)S(1)}, bf16[3,8,64,128]{3,2,1,0:T(8,128)(2,1)S(1)}, u32[]{:S(2)}, u32[]{:S(2)}) collective-permute-start(bf16[3,8,64,128]{3,2,1,0:T(8,128)(2,1)S(1)} %get-tuple-element.21.refs_4_), channel_id=1, source_target_pairs={{0,8},{8,0},{16,24},{24,16},{1,9},{9,1},{17,25},{25,17},{2,10},{10... | collective-permute-start | bytes 1179656 | tf_op jit(solution)/shard_map/ppermute | solution.py:292
  36.1 1.7 %collective-permute-start.9 = (bf16[3,8,64,128]{3,2,1,0:T(8,128)(2,1)S(1)}, bf16[3,8,64,128]{3,2,1,0:T(8,128)(2,1)S(1)}, u32[]{:S(2)}, u32[]{:S(2)}) collective-permute-start(bf16[3,8,64,128]{3,2,1,0:T(8,128)(2,1)S(1)} %collective-permute-done.4.refs_6_), channel_id=1, source_target_pairs={{0,8},{8,0},{16,24},{24,16},{1,9},{9,1},{17,25},{25,17},{2,10},{10... | collective-permute-start | bytes 1179656 | tf_op jit(solution)/shard_map/ppermute | solution.py:292
  41.2 4.3 %collective-permute-start.11 = (f32[4,64,128]{2,1,0:T(8,128)S(1)}, f32[4,64,128]{2,1,0:T(8,128)S(1)}, u32[]{:S(2)}, u32[]{:S(2)}) collective-permute-start(f32[4,64,128]{2,1,0:T(8,128)S(1)} %get-tuple-element.27), channel_id=1, source_target_pairs={{8,0},{16,8},{24,16},{25,24},{17,25},{9,17},{1,9},{2,1},{10,2},{18... | collective-permute-start | bytes 393224 | tf_op jit(solution)/shard_map/ppermute | solution.py:309
  42.5 4.0 %collective-permute-start.10 = (f32[4,64,128]{2,1,0:T(8,128)S(1)}, f32[4,64,128]{2,1,0:T(8,128)S(1)}, u32[]{:S(2)}, u32[]{:S(2)}) collective-permute-start(f32[4,64,128]{2,1,0:T(8,128)S(1)} %get-tuple-element.28), channel_id=1, source_target_pairs={{0,8},{8,16},{16,24},{24,25},{25,17},{17,9},{9,1},{1,2},{2,10},{10... | collective-permute-start | bytes 393224 | tf_op jit(solution)/shard_map/ppermute | solution.py:308
  63.4 6.4 %collective-permute-start.13 = (f32[8,64,128]{2,1,0:T(8,128)S(1)}, f32[8,64,128]{2,1,0:T(8,128)S(1)}, u32[]{:S(2)}, u32[]{:S(2)}) collective-permute-start(f32[8,64,128]{2,1,0:T(8,128)S(1)} %shard_map.51.own_ref), channel_id=1, source_target_pairs={{8,0},{16,8},{24,16},{25,24},{17,25},{9,17},{1,9},{2,1},{10,2},{18... | collective-permute-start | bytes 786440 | tf_op jit(solution)/shard_map/ppermute | solution.py:309
  64.7 6.0 %collective-permute-start.12 = (f32[8,64,128]{2,1,0:T(8,128)S(1)}, f32[8,64,128]{2,1,0:T(8,128)S(1)}, u32[]{:S(2)}, u32[]{:S(2)}) collective-permute-start(f32[8,64,128]{2,1,0:T(8,128)S(1)} %shard_map.51.own_ref), channel_id=1, source_target_pairs={{0,8},{8,16},{16,24},{24,25},{25,17},{17,9},{9,1},{1,2},{2,10},{10... | collective-permute-start | bytes 786440 | tf_op jit(solution)/shard_map/ppermute | solution.py:308
  110.2 6.4 %collective-permute-start.15 = (f32[64,8,128]{2,1,0:T(8,128)S(1)}, f32[64,8,128]{2,1,0:T(8,128)S(1)}, u32[]{:S(2)}, u32[]{:S(2)}) collective-permute-start(f32[64,8,128]{2,1,0:T(8,128)S(1)} %bitcast.18), channel_id=1, source_target_pairs={{0,16},{8,24},{16,0},{24,8},{1,17},{9,25},{17,1},{25,9},{2,18},{10... | collective-permute-start | bytes 786440 | tf_op jit(solution)/shard_map/ppermute | solution.py:292
  110.3 6.4 %collective-permute-start.14 = (f32[64,8,128]{2,1,0:T(8,128)S(1)}, f32[64,8,128]{2,1,0:T(8,128)S(1)}, u32[]{:S(2)}, u32[]{:S(2)}) collective-permute-start(f32[64,8,128]{2,1,0:T(8,128)S(1)} %bitcast.19), channel_id=1, source_target_pairs={{0,8},{8,0},{16,24},{24,16},{1,9},{9,1},{17,25},{25,17},{2,10},{10... | collective-permute-start | bytes 786440 | tf_op jit(solution)/shard_map/ppermute | solution.py:292
  116.6 1.5 %collective-permute-start.16 = (f32[64,8,128]{2,1,0:T(8,128)S(1)}, f32[64,8,128]{2,1,0:T(8,128)S(1)}, u32[]{:S(2)}, u32[]{:S(2)}) collective-permute-start(f32[64,8,128]{2,1,0:T(8,128)S(1)} %collective-permute-done.15.refs_2_), channel_id=1, source_target_pairs={{0,8},{8,0},{16,24},{24,16},{1,9},{9,1},{17,25},{25,17},{2,10},{10... | collective-permute-start | bytes 786440 | tf_op jit(solution)/shard_map/ppermute | solution.py:292

commit v9 on v8

--- a/solution.py
+++ b/solution.py
@@ -109,70 +109,93 @@
 
 
 def gather_kernel(views, planes, rim, place_ref, *refs):
-    count = (len(refs) - 3) // 2
-    inner, edges = refs[:count], refs[count : 2 * count]
-    bricks_ref, start_ref, window = refs[2 * count :]
+    partial_ref = None
+    if views is not None:
+        partial_ref, refs = refs[0], refs[1:]
+    groups = 2
+    inner, bound, edge = refs[:groups], refs[groups : 2 * groups], refs[2 * groups : 3 * groups]
+    bricks_ref, start_ref = refs[3 * groups : 3 * groups + 2]
+    window = refs[-1]
     step = pl.program_id(0)
     half, core = place_ref[0], place_ref[1]
-    main, side = inner[0].shape[1], edges[0].shape[1]
+    main = inner[0].shape[1]
 
     @pl.when(step == 0)
     def _():
-        start_ref[...] = jnp.zeros_like(start_ref)
-
-    for group in range(count):
+        start_ref[...] = jnp.zeros_like(start_ref) if partial_ref is None else partial_ref[...]
+
+    for group in range(groups):
         for z in range(main):
-            window[group, side * (1 - half) + z] = inner[group][0, z]
-        for z in range(side):
-            window[group, main * half + z] = edges[group][0, z]
+            window[group, 2 * rim * (1 - half) + z] = inner[group][0, z]
+        for z in range(rim):
+            window[group, rim + (main - rim) * half + z] = bound[group][0, z]
+            window[group, (main + rim) * half + z] = edge[group][0, z]
     for z in range(planes + 2 * rim):
         total = start_ref[z]
-        for group in range(count):
+        for group in range(groups):
             plane = window[group, planes * core + z]
             bricks_ref[group, 0, z] = plane
             total = total + plane.astype(jnp.float32)
         start_ref[z] = total
 
-    @pl.when(step == pl.num_programs(0) - 1)
-    def _():
-        start_ref[...] = start_ref[...] / views
-
-
-def gather_views(place, inner, edges, planes, rim):
+    if views is not None:
+        near_ref, cross_ref = refs[3 * groups + 2 : 3 * groups + 4]
+
+        @pl.when(step == pl.num_programs(0) - 1)
+        def _():
+            start_ref[...] = start_ref[...] / views
+            for z in range(rim):
+                upward, downward = rim + planes - 2 * rim + z, 2 * rim + z
+                near_ref[z] = start_ref[upward + (downward - upward) * core]
+                cross_ref[z] = start_ref[downward + (upward - downward) * core]
+
+
+def gather_views(place, inner, bound, edge, planes, views=None, partial=None):
     groups = len(inner)
     count, main, rows, width = inner[0].shape
-    outer, side = planes + 2 * rim, edges[0].shape[1]
+    rim = edge[0].shape[1]
+    outer = planes + 2 * rim
+    field = lambda depth: jax.ShapeDtypeStruct((depth, rows, width), jnp.float32)
+    sends = [] if views is None else [field(rim), field(rim)]
+    parts = [*inner, *bound, *edge]
     return pl.pallas_call(
-        functools.partial(gather_kernel, groups * count, planes, rim),
+        functools.partial(gather_kernel, views, planes, rim),
         grid=(count,),
-        out_shape=[
-            jax.ShapeDtypeStruct((groups, count, outer, rows, width), jnp.bfloat16),
-            jax.ShapeDtypeStruct((outer, rows, width), jnp.float32),
-        ],
-        in_specs=[SMEM] + [pl.BlockSpec((1,) + part.shape[1:], lambda v: (v, 0, 0, 0)) for part in inner + edges],
-        out_specs=[pl.BlockSpec((groups, 1, outer, rows, width), lambda v: (0, v, 0, 0, 0)), VMEM],
-        scratch_shapes=[pltpu.VMEM((groups, main + side, rows, width), jnp.bfloat16)],
+        out_shape=[jax.ShapeDtypeStruct((groups, count, outer, rows, width), jnp.bfloat16), field(outer)] + sends,
+        in_specs=[SMEM]
+        + ([] if partial is None else [VMEM])
+        + [pl.BlockSpec((1,) + part.shape[1:], lambda v: (v, 0, 0, 0)) for part in parts],
+        out_specs=[pl.BlockSpec((groups, 1, outer, rows, width), lambda v: (0, v, 0, 0, 0))]
+        + [VMEM] * (1 + len(sends)),
+        scratch_shapes=[pltpu.VMEM((groups, main + 2 * rim, rows, width), jnp.bfloat16)],
         compiler_params=PARAMS,
-    )(place, *inner, *edges)
-
-
-def update_kernel(last, taps_ref, bands_ref, bricks_ref, before_ref, own_ref, after_ref, out_ref, *scratches):
-    wides, lefts, ratios, backs, logs = scratches
-    parts = (before_ref, own_ref, after_ref)
-    count = bricks_ref.shape[0]
+    )(place, *([] if partial is None else [partial]), *parts)
+
+
+def update_kernel(last, paired, place_ref, taps_ref, bands_ref, *refs):
+    bricks_refs, (first_ref, own_ref, second_ref, out_ref) = refs[:2], refs[2:6]
+    volume, wides, lefts, ratios, backs, logs = refs[6:]
+    bricks = [ref.at[group] for ref in bricks_refs for group in range(ref.shape[0])]
+    count = len(bricks)
     step = pl.program_id(0)
     taps = taps_ref.shape[2]
     rim = taps // 2
     planes, rows, width = out_ref.shape
     outer = planes + 2 * rim
     tiles = rows // SUBLANES
-    volume = [(ref, z) for ref in parts for z in range(ref.shape[0])]
     tile = lambda k: pl.ds(k * SUBLANES, SUBLANES)
     sublane = lax.broadcasted_iota(jnp.int32, (SUBLANES, width), 0)
 
     @pl.when(step == 0)
     def _():
         logs[...] = jnp.zeros_like(logs)
+        side, middle = first_ref.shape[0], own_ref.shape[0]
+        flip = 1 - place_ref[1] if paired else 0
+        for z in range(side):
+            volume[(side + middle) * flip + z] = first_ref[z]
+            volume[(side + middle) * (1 - flip) + z] = second_ref[z]
+        for z in range(middle):
+            volume[side + z] = own_ref[z]
 
     def correlate(gains, terms):
         total = gains[0] * terms[0]
@@ -202,7 +225,7 @@
         gain_z = [taps_ref[view, 0, t] for t in range(taps)]
         gain_x = [taps_ref[view, 1, t] for t in range(taps)]
         for k in range(tiles):
-            column = along_z([ref[z, tile(k), :] for ref, z in volume], gain_z, outer)
+            column = along_z([volume[z, tile(k), :] for z in range(outer + 2 * rim)], gain_z, outer)
             for z in range(outer):
                 wide[z, tile(k), :] = column[z]
         for z in range(outer):
@@ -212,7 +235,7 @@
         for z in range(outer):
             guess = pl.reciprocal(blurred[z], approx=True)
             guess = guess * (2.0 - blurred[z] * guess)
-            ratio[z] = bricks_ref[group, 0, z].astype(jnp.float32) * guess
+            ratio[z] = bricks[group][0, z].astype(jnp.float32) * guess
         for k in range(tiles):
             column = along_z([ratio[z, tile(k), :] for z in range(outer)], gain_z[::-1], planes)
             for z in range(planes):
@@ -229,33 +252,29 @@
     @pl.when(step == pl.num_programs(0) - 1)
     def _():
         for z in range(planes):
-            ref, at = volume[2 * rim + z]
             for k in range(tiles):
-                value = ref[at, tile(k), :] * jnp.exp(logs[z, tile(k), :] / (count * pl.num_programs(0)))
+                value = volume[2 * rim + z, tile(k), :] * jnp.exp(logs[z, tile(k), :] / (count * pl.num_programs(0)))
                 if last:
                     out_ref[z, pl.ds(k, SUBLANES, tiles), :] = value
                 else:
                     out_ref[z, tile(k), :] = value
 
 
-def update(taps, band, bricks, volume, planes, last):
-    groups, count, outer, rows, width = bricks.shape
+def update(place, taps, band, bricks, halo, own, planes, paired, last):
+    _, count, outer, rows, width = bricks[0].shape
+    groups = sum(part.shape[0] for part in bricks)
     band = band.reshape((groups, count) + band.shape[1:])
     step = lambda v: (0, v, 0, 0, 0)
     return pl.pallas_call(
-        functools.partial(update_kernel, last),
+        functools.partial(update_kernel, last, paired),
         grid=(count,),
         out_shape=jax.ShapeDtypeStruct((planes, rows, width), jnp.float32),
-        in_specs=[
-            SMEM,
-            pl.BlockSpec((groups, 1) + band.shape[2:], step),
-            pl.BlockSpec((groups, 1, outer, rows, width), step),
-            VMEM,
-            VMEM,
-            VMEM,
-        ],
+        in_specs=[SMEM, SMEM, pl.BlockSpec((groups, 1) + band.shape[2:], step)]
+        + [pl.BlockSpec((part.shape[0], 1, outer, rows, width), step) for part in bricks]
+        + [VMEM] * 3,
         out_specs=VMEM,
         scratch_shapes=[
+            pltpu.VMEM((2 * outer - planes, rows, width), jnp.float32),
             pltpu.VMEM((2, outer, rows, width), jnp.float32),
             pltpu.VMEM((2, outer * rows, 2 * width), jnp.bfloat16),
             pltpu.VMEM((2, outer, rows, width), jnp.float32),
@@ -263,7 +282,7 @@
             pltpu.VMEM((planes, rows, width), jnp.float32),
         ],
         compiler_params=PARAMS,
-    )(taps, band, bricks, *volume)
+    )(place, taps, band, *bricks, halo[0], own, halo[1])
 
 
 def place_kernel(planes, place_ref, *refs):
@@ -292,21 +311,28 @@
     return lax.ppermute(value, "view", [(i, i ^ bit) for i in range(members)])
 
 
+def line_device(line, members, blocks):
+    block, slab = divmod(line, members)
+    return (members - 1 - slab if block % 2 else slab) * blocks + block
+
+
+def swap(value, pairs, members, blocks):
+    at = lambda line: line_device(line, members, blocks)
+    perm = [(at(i), at(j)) for i, j in pairs] + [(at(j), at(i)) for i, j in pairs]
+    return lax.ppermute(value, ("view", "vol"), perm)
+
+
 def z_rims(own, inner, outer, members, blocks):
     planes = own.shape[0]
-    axes = ("view", "vol")
-    def at(line):
-        block, slab = divmod(line, members)
-        return (members - 1 - slab if block % 2 else slab) * blocks + block
-
+    at = lambda line: line_device(line, members, blocks)
     total = members * blocks
     before, after = [], []
     for hop in range(inner // planes + 1, -(-outer // planes) + 1):
         near, far = max((hop - 1) * planes, inner), min(hop * planes, outer)
         up = [(at(i), at(i + hop)) for i in range(total - hop)]
         down = [(at(i + hop), at(i)) for i in range(total - hop)]
-        before.append(lax.ppermute(own[hop * planes - far : hop * planes - near], axes, up))
-        after.append(lax.ppermute(own[near - (hop - 1) * planes : far - (hop - 1) * planes], axes, down))
+        before.append(lax.ppermute(own[hop * planes - far : hop * planes - near], ("view", "vol"), up))
+        after.append(lax.ppermute(own[near - (hop - 1) * planes : far - (hop - 1) * planes], ("view", "vol"), down))
     join = lambda parts: parts[0] if len(parts) == 1 else jnp.concatenate(parts)
     return join(before[::-1]), join(after)
 
@@ -322,42 +348,57 @@
     place = jnp.stack([slab // CORES, slab % CORES]).astype(jnp.int32)
 
     near_bit, far_bit = 1, CORES
-    inner = (0, (rim, 2 * planes - rim), (0, 0), 2 * planes)
-    first_edge = (0, (0, depth - rim), (rim, 0), rim)
-    second_edge = (1, (0, rim), (0, rim), rim)
+    near = lambda value: partner(value, near_bit, members)
+    far = lambda value: partner(value, far_bit, members)
+    seams = [(members * block + members - 1 - i, members * (block + 1) + i) for block in range(blocks - 1) for i in range(CORES)]
+    across = lambda value: swap(value, seams, members, blocks)
+    bound = [(0, (0, depth - rim), (0, 0), rim)]
+    inner = [(0, (rim, 2 * planes - rim), (0, 0), 2 * planes)]
+
     cross_taps = partner(psf_taps, near_bit + far_bit, members)
-    (far_inner,) = resample(place, weights, offsets, [raw_views], [(True, [inner])])
-    far_inner, raw_later, cross_taps = lax.optimization_barrier((far_inner, raw_views, cross_taps))
-    far_inner = partner(far_inner, far_bit, members)
-    up = [(i, i + 1) for i in range(blocks - 1)]
-    down = [(i + 1, i) for i in range(blocks - 1)]
-    raw_before = lax.ppermute(raw_later[:, depth - rim :], "vol", up)
-    raw_after = lax.ppermute(raw_later[:, :rim], "vol", down)
-    (own_inner,) = resample(place, weights, offsets, [raw_later], [(False, [inner])])
-    near_inner = partner(own_inner, near_bit, members)
-    pair_taps = partner(jnp.stack([psf_taps, cross_taps]), near_bit, members)
+    (far_bound,) = resample(place, weights, offsets, [raw_views], [(True, bound)])
+    far_bound, raw_later, cross_taps = lax.optimization_barrier((far_bound, raw_views, cross_taps))
+    far_bound = far(far_bound)
+    (far_inner,) = resample(place, weights, offsets, [raw_later], [(True, inner)])
+    own_bound, own_inner = resample(place, weights, offsets, [raw_later], [(False, bound), (False, inner)])
+    far_inner, far_bound, own_bound, own_inner = lax.optimization_barrier(
+        (far_inner, far_bound, own_bound, own_inner)
+    )
+    far_inner = far(far_inner)
+    own_edge, far_edge = across(own_bound), across(far_bound)
+    pair_taps = near(jnp.stack([psf_taps, cross_taps]))
     all_taps = jnp.concatenate([psf_taps, pair_taps[0], pair_taps[1], cross_taps])
     all_taps = all_taps / jnp.sum(all_taps, axis=-1, keepdims=True)
     band = bands(all_taps, width)
-    raw_rims = jnp.concatenate([raw_before, raw_after], axis=1)
-    edge = [first_edge, second_edge]
-    far_edge, own_edge = resample(place, weights, offsets, [raw_later, raw_rims], [(True, edge), (False, edge)])
-    far_edge = partner(far_edge, far_bit, members)
-    near_edge = partner(own_edge, near_bit, members)
-    far_edge, band, own_edge = lax.optimization_barrier((far_edge, band, own_edge))
-    inners = [own_inner, near_inner, far_inner, partner(far_inner, near_bit, members)]
-    edges = [own_edge, near_edge, far_edge, partner(far_edge, near_bit, members)]
-    bricks, start = gather_views(place, inners, edges, planes, rim)
-    before, after = z_rims(start[rim : rim + planes], rim, 2 * rim, members, blocks)
-    joined = update(all_taps, band, bricks, (before, start, after), planes, ITERS == 1)
+    home, partial = gather_views(
+        place, [own_inner, near(own_inner)], [own_bound, near(own_bound)], [own_edge, near(own_edge)], planes
+    )
+    far_bounds, far_edges = [far_bound, near(far_bound)], [far_edge, near(far_edge)]
+    far_inner, band, home, partial, far_bounds, far_edges = lax.optimization_barrier(
+        (far_inner, band, home, partial, far_bounds, far_edges)
+    )
+    away, start, near_send, cross_send = gather_views(
+        place, [far_inner, near(far_inner)], far_bounds, far_edges, planes, members * views, partial
+    )
+    bricks = [home, away]
+    lines = members * blocks
+    gaps = [(i, i + 1) for i in range(1, lines - 1, 2)]
+    paired = planes == 2 * rim
+    if paired:
+        halo = (near(near_send), swap(cross_send, gaps, members, blocks))
+    else:
+        halo = z_rims(start[rim : rim + planes], rim, 2 * rim, members, blocks)
+    joined = update(place, all_taps, band, bricks, halo, start, planes, paired, ITERS == 1)
     for turn in range(1, ITERS):
-        before, after = z_rims(joined, 0, 2 * rim, members, blocks)
-        joined = update(all_taps, band, bricks, (before, joined, after), planes, turn == ITERS - 1)
+        if paired:
+            halo = (near(joined), swap(joined, gaps, members, blocks))
+        else:
+            halo = z_rims(joined, 0, 2 * rim, members, blocks)
+        joined = update(place, all_taps, band, bricks, halo, joined, planes, paired, turn == ITERS - 1)
 
     columns = lax.all_to_all(joined, "vol", split_axis=1, concat_axis=0, tiled=True)
-    far = partner(columns, far_bit, members)
-    near = partner(columns, near_bit, members)
-    parts = [columns, near, far, partner(far, near_bit, members)]
+    far_columns = far(columns)
+    parts = [columns, near(columns), far_columns, near(far_columns)]
     result = place_parts(me.reshape(1).astype(jnp.int32), parts, planes)
     return result.reshape((blocks * depth,) + columns.shape[1:])
 

time: 120 us -> 111 us (0.925)
  starting transfers between devices: 21.1 us -> 15.7 us
  blocking collectives: 22.4 us -> 19.5 us
  Pallas kernels: 47 us -> 44.5 us
  local copies, waits for them, and re-layouts: 3.06 us -> 4.64 us
    ppermute x6 -> x4, starting transfers between devices: 15.4 us -> 2.84 us  [swap(): return lax.ppermute(value, ('view', 'vol'), perm)]
    ppermute x11 -> x15, waiting for transfers between devices: 18.1 us -> 25.8 us  [partner(): return lax.ppermute(value, 'view', [(i, i ^ bit) for i in range(members)])]
    ppermute x11 -> x15, starting transfers between devices: 5.65 us -> 12.9 us  [partner(): return lax.ppermute(value, 'view', [(i, i ^ bit) for i in range(members)])]
    ppermute x6 -> x4, waiting for transfers between devices: 7.04 us -> 0.01 us  [swap(): return lax.ppermute(value, ('view', 'vol'), perm)]
    all_to_all x1, blocking collectives: 22.4 us -> 19.5 us  [per_device(): lax.all_to_all(joined, 'vol', split_axis=1, concat_axis=0, tiled=True)]
    pallas_call x3 -> x4, Pallas kernels: 37.1 us -> 34.8 us  [the longest x2 32.2 us: update(): pl.pallas_call(functools.partial(update_kernel, last, paired), grid=(coun...]
    unnamed x6 -> x8, local copies, waits for them, and re-layouts: 2.12 us -> 3.75 us
  transfers between devices with their start and end apart: 17 -> 19, of which waited for: 10 -> 8; matrix products, arithmetic and copies ran while one was open for 1% -> 1% of each run, Pallas kernels for 7% -> 9%
where the time goes in v9:
time: 111 us
  Pallas kernels  44.5 us (40%)
  waiting for transfers between devices  25.8 us (23%)
  blocking collectives  19.5 us (18%)
  starting transfers between devices  15.7 us (14%)
  local copies, waits for them, and re-layouts  4.64 us (4%)
    pallas_call x2, Pallas kernels, update(): pl.pallas_call(functools.partial(update_kernel, last, paired), grid=(coun...  32.2 us
    ppermute x15, waiting for transfers between devices, partner(): return lax.ppermute(value, 'view', [(i, i ^ bit) for i in range(members)])  25.8 us
    all_to_all x1, blocking collectives, per_device(): lax.all_to_all(joined, 'vol', split_axis=1, concat_axis=0, tiled=True)  19.5 us
    ppermute x15, starting transfers between devices, partner(): return lax.ppermute(value, 'view', [(i, i ^ bit) for i in range(members)])  12.9 us
    pallas_call x3, Pallas kernels, resample(): pl.pallas_call(functools.partial(resample_kernel, plan), grid=(views,), o...  6.32 us
    unnamed x8, local copies, waits for them, and re-layouts  3.75 us
    ppermute x4, starting transfers between devices, swap(): return lax.ppermute(value, ('view', 'vol'), perm)  2.84 us
    pallas_call x2, Pallas kernels, gather_views(): pl.pallas_call(functools.partial(gather_kernel, views, planes, rim), grid...  2.6 us
  transfers between devices with their start and end apart: 19, of which 8 were waited for; matrix products, arithmetic and copies ran while one was open for 1% of the time, Pallas kernels for 9%

profile of v9, /device:TPU:0, one launch (start us, length us, event | category | flops | bytes accessed | tf_op | source)
XLA Modules:
  0.0 110.6 jit_solution(8754617292542005098)
XLA Ops:
  0.0 2.4 %collective-permute-start = (f32[3,3,9]{2,1,0:T(4,128)}, f32[3,3,9]{2,1,0:T(4,128)S(1)}, u32[]{:S(2)}, u32[]{:S(2)}) collective-permute-start(f32[3,3,9]{2,1,0:T(4,128)} %param.7), channel_id=1, source_target_pairs={{0,24},{8,16},{16,8},{24,0},{1,25},{9,17},{17,9},{25,1},{2,26},{10... | collective-permute-start | bytes 980 | tf_op jit(solution)/shard_map/ppermute | solution.py:311
  2.4 0.1 pad_add_fusion.place_ref
  2.5 0.7 broadcast_in_dim.2.offsets_ref
  3.1 0.0 copy-start.1
  3.1 1.4 %copy-done.1 = bf16[3,32,64,128]{3,2,1,0:T(8,128)(2,1)S(1)} copy-done((bf16[3,32,64,128]{3,2,1,0:T(8,128)(2,1)S(1)}, bf16[3,32,64,128]{3,2,1,0:T(8,128)(2,1)}, u32[]{:S(2)}) %copy-start.1) | copy-done | bytes 1572888
  4.5 0.0 copy-start.2
  4.5 0.7 copy-done.2
  5.3 1.9 %shard_map.46 = bf16[3,4,64,128]{3,2,1,0:T(8,128)(2,1)S(1)} custom-call(s32[2]{0:T(128)S(1)} %pad_add_fusion.place_ref, f32[3,8,64]{2,1,0:T(8,128)S(1)} %bitcast.21, s32[3,1,64]{2,1,0:T(1,128)S(1)} %broadcast_in_dim.2.offsets_ref, bf16[3,32,64,128]{3,2,1,0:T(8,128)(2,1)S(1)} %copy-done.1), custom_call_target="tpu_custom_call" | custom-call | tf_op jit(solution)/shard_map/pallas_call | solution.py:66
  7.1 0.0 copy-start.3
  7.1 0.0 collective-permute-done
  7.1 0.6 collective-permute-start.2
  7.8 2.2 %shard_map.47 = bf16[3,16,64,128]{3,2,1,0:T(8,128)(2,1)S(1)} custom-call(s32[2]{0:T(128)S(1)} %pad_add_fusion.place_ref, f32[3,8,64]{2,1,0:T(8,128)S(1)} %bitcast.22, s32[3,1,64]{2,1,0:T(1,128)S(1)} %broadcast_in_dim.2.offsets_ref, bf16[3,32,64,128]{3,2,1,0:T(8,128)(2,1)S(1)} %copy-done.1), custom_call_target="tpu_custom_call" | custom-call | tf_op jit(solution)/shard_map/pallas_call | solution.py:66
  9.9 2.3 %shard_map.48 = (bf16[3,4,64,128]{3,2,1,0:T(8,128)(2,1)S(1)}, bf16[3,16,64,128]{3,2,1,0:T(8,128)(2,1)S(1)}) custom-call(s32[2]{0:T(128)S(1)} %pad_add_fusion.place_ref, f32[3,8,64]{2,1,0:T(8,128)S(1)} %bitcast.23, s32[3,1,64]{2,1,0:T(1,128)S(1)} %broadcast_in_dim.2.offsets_ref, bf16[3,32,64,128]{3,2,1,0:T(8,128)(2,1)S(1)} %copy-done.1), custom_call_target="tpu_custom_call" | custom-call | tf_op jit(solution)/shard_map/pallas_call | solution.py:66
  12.2 2.4 %collective-permute-done.2.refs_3_ = bf16[3,4,64,128]{3,2,1,0:T(8,128)(2,1)S(1)} collective-permute-done((bf16[3,4,64,128]{3,2,1,0:T(8,128)(2,1)S(1)}, bf16[3,4,64,128]{3,2,1,0:T(8,128)(2,1)S(1)}, u32[]{:S(2)}, u32[]{:S(2)}) %collective-permute-start.2) | collective-permute-done | bytes 196640 | tf_op jit(solution)/shard_map/ppermute | solution.py:311
  14.7 0.0 collective-permute-start.4
  14.7 0.3 collective-permute-start.3
  15.0 0.0 copy-done.3
  15.0 0.3 collective-permute-start.1
  15.3 0.7 collective-permute-start.6
  16.0 0.3 collective-permute-start.5
  16.3 0.7 collective-permute-done.1
  17.0 0.7 collective-permute-start.9
  17.7 0.0 collective-permute-done.6.refs_4_
  17.7 0.2 collective-permute-start.8
  17.9 0.0 collective-permute-done.5.refs_3_
  17.9 0.4 collective-permute-start.7
  18.3 0.0 collective-permute-done.9.refs_5_
  18.3 0.1 collective-permute-start.10
  18.4 0.1 fusion.1.taps_ref
  18.5 2.4 %shard_map.49 = bf16[12,2,256,256]{3,2,1,0:T(8,128)(2,1)S(1)} custom-call(f32[12,3,9]{2,1,0:T(4,128)S(1)} %fusion.1.taps_ref), custom_call_target="tpu_custom_call" | custom-call | tf_op jit(solution)/shard_map/pallas_call | solution.py:101
  20.9 0.0 copy-start
  20.9 1.6 %copy-done = bf16[12,2,256,256]{3,2,1,0:T(8,128)(2,1)} copy-done((bf16[12,2,256,256]{3,2,1,0:T(8,128)(2,1)}, bf16[12,2,256,256]{3,2,1,0:T(8,128)(2,1)S(1)}, u32[]{:S(2)}) %copy-start) | copy-done | bytes 3145752
  22.5 0.0 collective-permute-done.7.refs_5_
  22.5 0.0 collective-permute-done.4.refs_1_
  22.5 1.3 %shard_map.50 = (bf16[2,3,16,64,128]{4,3,2,1,0:T(8,128)(2,1)S(1)}, f32[16,64,128]{2,1,0:T(8,128)S(1)}) custom-call(s32[2]{0:T(128)S(1)} %pad_add_fusion.place_ref, bf16[3,16,64,128]{3,2,1,0:T(8,128)(2,1)S(1)} %get-tuple-element.34.refs_0_, bf16[3,16,64,128]{3,2,1,0:T(8,128)(2,1)S(1)} %collective-permute-done.4.refs_1_, ...), custom_call_target="tpu_custom_call" | custom-call | tf_op jit(solution)/shard_map/pallas_call | solution.py:161
  23.8 0.0 collective-permute-done.8.refs_4_
  23.8 0.0 collective-permute-done.10.refs_6_
  23.8 10.8 %collective-permute-done.3.refs_1_ = bf16[3,16,64,128]{3,2,1,0:T(8,128)(2,1)S(1)} collective-permute-done((bf16[3,16,64,128]{3,2,1,0:T(8,128)(2,1)S(1)}, bf16[3,16,64,128]{3,2,1,0:T(8,128)(2,1)S(1)}, u32[]{:S(2)}, u32[]{:S(2)}) %collective-permute-start.3) | collective-permute-done | bytes 786464 | tf_op jit(solution)/shard_map/ppermute | solution.py:311
  34.7 0.0 collective-permute-start.11
  34.7 2.3 %collective-permute-done.11.refs_2_ = bf16[3,16,64,128]{3,2,1,0:T(8,128)(2,1)S(1)} collective-permute-done((bf16[3,16,64,128]{3,2,1,0:T(8,128)(2,1)S(1)}, bf16[3,16,64,128]{3,2,1,0:T(8,128)(2,1)S(1)}, u32[]{:S(2)}, u32[]{:S(2)}) %collective-permute-start.11) | collective-permute-done | bytes 786464 | tf_op jit(solution)/shard_map/ppermute | solution.py:311
  36.9 1.3 %shard_map.51 = (bf16[2,3,16,64,128]{4,3,2,1,0:T(8,128)(2,1)S(1)}, f32[16,64,128]{2,1,0:T(8,128)S(1)}, f32[4,64,128]{2,1,0:T(8,128)S(1)}, f32[4,64,128]{2,1,0:T(8,128)S(1)}) custom-call(s32[2]{0:T(128)S(1)} %pad_add_fusion.place_ref, f32[16,64,128]{2,1,0:T(8,128)S(1)} %get-tuple-element.41.refs_0_, ...), custom_call_target="tpu_custom_call" | custom-call | tf_op jit(solution)/shard_map/pallas_call | solution.py:161
  38.3 0.2 collective-permute-start.12
  38.5 0.7 collective-permute-start.13
  39.2 0.5 collective-permute-done.12.refs_2_
  39.7 0.0 collective-permute-done.13.refs_4_
  39.7 16.1 %shard_map.52.refs_3_ = f32[8,64,128]{2,1,0:T(8,128)S(1)} custom-call(s32[2]{0:T(128)S(1)} %pad_add_fusion.place_ref, f32[12,3,9]{2,1,0:T(4,128)S(1)} %fusion.1.taps_ref, bf16[4,3,2,256,256]{4,3,2,1,0:T(8,128)(2,1)} %bitcast.16, bf16[2,3,16,64,128]{4,3,2,1,0:T(8,128)(2,1)S(1)} %get-tuple-element.40.refs_0_, ...), custom_call_target="tpu_custom_call" | custom-call | tf_op jit(solution)/shard_map/pallas_call | solution.py:268
  55.8 0.9 collective-permute-start.15
  56.7 7.9 %collective-permute-start.14 = (f32[8,64,128]{2,1,0:T(8,128)S(1)}, f32[8,64,128]{2,1,0:T(8,128)S(1)}, u32[]{:S(2)}, u32[]{:S(2)}) collective-permute-start(f32[8,64,128]{2,1,0:T(8,128)S(1)} %shard_map.52.refs_3_), channel_id=1, source_target_pairs={{0,8},{8,0},{16,24},{24,16},{1,9},{9,1},{17,25},{25,17},{2,10},{10... | collective-permute-start | bytes 786440 | tf_op jit(solution)/shard_map/ppermute | solution.py:311
  64.6 0.0 collective-permute-done.15.refs_4_
  64.6 1.2 %collective-permute-done.14.refs_2_ = f32[8,64,128]{2,1,0:T(8,128)S(1)} collective-permute-done((f32[8,64,128]{2,1,0:T(8,128)S(1)}, f32[8,64,128]{2,1,0:T(8,128)S(1)}, u32[]{:S(2)}, u32[]{:S(2)}) %collective-permute-start.14) | collective-permute-done | bytes 262176 | tf_op jit(solution)/shard_map/ppermute | solution.py:311
  65.7 16.1 %shard_map.53 = f32[8,64,128]{2,1,0:T(8,128)S(1)} custom-call(s32[2]{0:T(128)S(1)} %pad_add_fusion.place_ref, f32[12,3,9]{2,1,0:T(4,128)S(1)} %fusion.1.taps_ref, bf16[4,3,2,256,256]{4,3,2,1,0:T(8,128)(2,1)} %bitcast.17, bf16[2,3,16,64,128]{4,3,2,1,0:T(8,128)(2,1)S(1)} %get-tuple-element.40.refs_0_, ...), custom_call_target="tpu_custom_call" | custom-call | tf_op jit(solution)/shard_map/pallas_call | solution.py:268
  81.9 0.2 copy.6
  82.0 19.5 %all_to_all.18 = f32[8,64,128]{2,0,1:T(8,128)S(1)} all-to-all(f32[8,64,128]{2,0,1:T(8,128)S(1)} %copy.6), channel_id=1, replica_groups=mesh['view'=4,'vol'=8] {'vol'}, dimensions={1} | all-to-all | bytes 524288 | tf_op jit(solution)/shard_map/all_to_all | solution.py:399
  101.6 0.1 collective-permute-start.17
  101.7 0.1 collective-permute-start.16
  101.7 6.3 %collective-permute-done.17.refs_2_ = f32[64,8,128]{2,1,0:T(8,128)S(1)} collective-permute-done((f32[64,8,128]{2,1,0:T(8,128)S(1)}, f32[64,8,128]{2,1,0:T(8,128)S(1)}, u32[]{:S(2)}, u32[]{:S(2)}) %collective-permute-start.17) | collective-permute-done | bytes 262176 | tf_op jit(solution)/shard_map/ppermute | solution.py:311
  108.0 0.0 collective-permute-start.18
  108.0 0.0 collective-permute-done.16.refs_1_
  108.0 1.5 %collective-permute-done.18.refs_3_ = f32[64,8,128]{2,1,0:T(8,128)S(1)} collective-permute-done((f32[64,8,128]{2,1,0:T(8,128)S(1)}, f32[64,8,128]{2,1,0:T(8,128)S(1)}, u32[]{:S(2)}, u32[]{:S(2)}) %collective-permute-start.18) | collective-permute-done | bytes 262176 | tf_op jit(solution)/shard_map/ppermute | solution.py:311
  109.6 1.0 shard_map.54
  (3 shorter events, 0.1 us)
Async XLA Ops:
  0.0 7.1 %collective-permute-start = (f32[3,3,9]{2,1,0:T(4,128)}, f32[3,3,9]{2,1,0:T(4,128)S(1)}, u32[]{:S(2)}, u32[]{:S(2)}) collective-permute-start(f32[3,3,9]{2,1,0:T(4,128)} %param.7), channel_id=1, source_target_pairs={{0,24},{8,16},{16,8},{24,0},{1,25},{9,17},{17,9},{25,1},{2,26},{10... | collective-permute-start | bytes 980 | tf_op jit(solution)/shard_map/ppermute | solution.py:311
  3.1 1.4 %copy-start.1 = (bf16[3,32,64,128]{3,2,1,0:T(8,128)(2,1)S(1)}, bf16[3,32,64,128]{3,2,1,0:T(8,128)(2,1)}, u32[]{:S(2)}) copy-start(bf16[3,32,64,128]{3,2,1,0:T(8,128)(2,1)} %refs_0_.3) | copy-start | bytes 4718596
  4.5 0.7 copy-start.2
  7.1 7.9 %copy-start.3 = (f32[3,3,9]{2,1,0:T(4,128)S(1)}, f32[3,3,9]{2,1,0:T(4,128)}, u32[]{:S(2)}) copy-start(f32[3,3,9]{2,1,0:T(4,128)} %param.7) | copy-start | bytes 976
  7.1 7.5 %collective-permute-start.2 = (bf16[3,4,64,128]{3,2,1,0:T(8,128)(2,1)S(1)}, bf16[3,4,64,128]{3,2,1,0:T(8,128)(2,1)S(1)}, u32[]{:S(2)}, u32[]{:S(2)}) collective-permute-start(bf16[3,4,64,128]{3,2,1,0:T(8,128)(2,1)S(1)} %shard_map.46), channel_id=1, source_target_pairs={{0,16},{8,24},{16,0},{24,8},{1,17},{9,25},{17,1},{25,9},{2,18},{10... | collective-permute-start | bytes 589832 | tf_op jit(solution)/shard_map/ppermute | solution.py:311
  14.7 7.8 %collective-permute-start.4 = (bf16[3,16,64,128]{3,2,1,0:T(8,128)(2,1)S(1)}, bf16[3,16,64,128]{3,2,1,0:T(8,128)(2,1)S(1)}, u32[]{:S(2)}, u32[]{:S(2)}) collective-permute-start(bf16[3,16,64,128]{3,2,1,0:T(8,128)(2,1)S(1)} %get-tuple-element.34.refs_0_), channel_id=1, source_target_pairs={{0,8},{8,0},{16,24},{24,16},{1,9},{9,1},{17,25},{25,17},{2,10},{10... | collective-permute-start | bytes 2359304 | tf_op jit(solution)/shard_map/ppermute | solution.py:311
  14.7 20.0 %collective-permute-start.3 = (bf16[3,16,64,128]{3,2,1,0:T(8,128)(2,1)S(1)}, bf16[3,16,64,128]{3,2,1,0:T(8,128)(2,1)S(1)}, u32[]{:S(2)}, u32[]{:S(2)}) collective-permute-start(bf16[3,16,64,128]{3,2,1,0:T(8,128)(2,1)S(1)} %shard_map.47), channel_id=1, source_target_pairs={{0,16},{8,24},{16,0},{24,8},{1,17},{9,25},{17,1},{25,9},{2,18},{10... | collective-permute-start | bytes 2359304 | tf_op jit(solution)/shard_map/ppermute | solution.py:311
  15.0 2.0 %collective-permute-start.1 = (f32[2,3,3,9]{3,2,1,0:T(4,128)S(1)}, f32[2,3,3,9]{3,2,1,0:T(4,128)S(1)}, u32[]{:S(2)}, u32[]{:S(2)}) collective-permute-start(f32[2,3,3,9]{3,2,1,0:T(4,128)S(1)} %pad_maximum_fusion.1), channel_id=1, source_target_pairs={{0,8},{8,0},{16,24},{24,16},{1,9},{9,1},{17,25},{25,17},{2,10},{10... | collective-permute-start | bytes 1952 | tf_op jit(solution)/shard_map/ppermute | solution.py:311
  15.3 2.4 %collective-permute-start.6 = (bf16[3,4,64,128]{3,2,1,0:T(8,128)(2,1)S(1)}, bf16[3,4,64,128]{3,2,1,0:T(8,128)(2,1)S(1)}, u32[]{:S(2)}, u32[]{:S(2)}) collective-permute-start(bf16[3,4,64,128]{3,2,1,0:T(8,128)(2,1)S(1)} %get-tuple-element.35.refs_2_), channel_id=1, source_target_pairs={{24,25},{16,17},{1,2},{9,10},{26,27},{18,19},{3,4},{11,12},{28,29}... | collective-permute-start | bytes 589832 | tf_op jit(solution)/shard_map/ppermute | solution.py:322
  16.0 1.9 %collective-permute-start.5 = (bf16[3,4,64,128]{3,2,1,0:T(8,128)(2,1)S(1)}, bf16[3,4,64,128]{3,2,1,0:T(8,128)(2,1)S(1)}, u32[]{:S(2)}, u32[]{:S(2)}) collective-permute-start(bf16[3,4,64,128]{3,2,1,0:T(8,128)(2,1)S(1)} %get-tuple-element.35.refs_2_), channel_id=1, source_target_pairs={{0,8},{8,0},{16,24},{24,16},{1,9},{9,1},{17,25},{25,17},{2,10},{10... | collective-permute-start | bytes 589832 | tf_op jit(solution)/shard_map/ppermute | solution.py:311
  17.0 1.3 %collective-permute-start.9 = (bf16[3,4,64,128]{3,2,1,0:T(8,128)(2,1)S(1)}, bf16[3,4,64,128]{3,2,1,0:T(8,128)(2,1)S(1)}, u32[]{:S(2)}, u32[]{:S(2)}) collective-permute-start(bf16[3,4,64,128]{3,2,1,0:T(8,128)(2,1)S(1)} %collective-permute-done.2.refs_3_), channel_id=1, source_target_pairs={{24,25},{16,17},{1,2},{9,10},{26,27},{18,19},{3,4},{11,12},{28,29}... | collective-permute-start | bytes 589832 | tf_op jit(solution)/shard_map/ppermute | solution.py:322
  17.7 6.1 %collective-permute-start.8 = (bf16[3,4,64,128]{3,2,1,0:T(8,128)(2,1)S(1)}, bf16[3,4,64,128]{3,2,1,0:T(8,128)(2,1)S(1)}, u32[]{:S(2)}, u32[]{:S(2)}) collective-permute-start(bf16[3,4,64,128]{3,2,1,0:T(8,128)(2,1)S(1)} %collective-permute-done.2.refs_3_), channel_id=1, source_target_pairs={{0,8},{8,0},{16,24},{24,16},{1,9},{9,1},{17,25},{25,17},{2,10},{10... | collective-permute-start | bytes 589832 | tf_op jit(solution)/shard_map/ppermute | solution.py:311
  17.9 4.7 %collective-permute-start.7 = (bf16[3,4,64,128]{3,2,1,0:T(8,128)(2,1)S(1)}, bf16[3,4,64,128]{3,2,1,0:T(8,128)(2,1)S(1)}, u32[]{:S(2)}, u32[]{:S(2)}) collective-permute-start(bf16[3,4,64,128]{3,2,1,0:T(8,128)(2,1)S(1)} %collective-permute-done.6.refs_4_), channel_id=1, source_target_pairs={{0,8},{8,0},{16,24},{24,16},{1,9},{9,1},{17,25},{25,17},{2,10},{10... | collective-permute-start | bytes 589832 | tf_op jit(solution)/shard_map/ppermute | solution.py:311
  18.3 5.6 %collective-permute-start.10 = (bf16[3,4,64,128]{3,2,1,0:T(8,128)(2,1)S(1)}, bf16[3,4,64,128]{3,2,1,0:T(8,128)(2,1)S(1)}, u32[]{:S(2)}, u32[]{:S(2)}) collective-permute-start(bf16[3,4,64,128]{3,2,1,0:T(8,128)(2,1)S(1)} %collective-permute-done.9.refs_5_), channel_id=1, source_target_pairs={{0,8},{8,0},{16,24},{24,16},{1,9},{9,1},{17,25},{25,17},{2,10},{10... | collective-permute-start | bytes 589832 | tf_op jit(solution)/shard_map/ppermute | solution.py:311
  20.9 1.6 %copy-start = (bf16[12,2,256,256]{3,2,1,0:T(8,128)(2,1)}, bf16[12,2,256,256]{3,2,1,0:T(8,128)(2,1)S(1)}, u32[]{:S(2)}) copy-start(bf16[12,2,256,256]{3,2,1,0:T(8,128)(2,1)S(1)} %shard_map.49) | copy-start | bytes 9437188
  34.7 2.3 %collective-permute-start.11 = (bf16[3,16,64,128]{3,2,1,0:T(8,128)(2,1)S(1)}, bf16[3,16,64,128]{3,2,1,0:T(8,128)(2,1)S(1)}, u32[]{:S(2)}, u32[]{:S(2)}) collective-permute-start(bf16[3,16,64,128]{3,2,1,0:T(8,128)(2,1)S(1)} %collective-permute-done.3.refs_1_), channel_id=1, source_target_pairs={{0,8},{8,0},{16,24},{24,16},{1,9},{9,1},{17,25},{25,17},{2,10},{10... | collective-permute-start | bytes 2359304 | tf_op jit(solution)/shard_map/ppermute | solution.py:311
  38.3 1.4 %collective-permute-start.12 = (f32[4,64,128]{2,1,0:T(8,128)S(1)}, f32[4,64,128]{2,1,0:T(8,128)S(1)}, u32[]{:S(2)}, u32[]{:S(2)}) collective-permute-start(f32[4,64,128]{2,1,0:T(8,128)S(1)} %get-tuple-element.48), channel_id=1, source_target_pairs={{0,8},{8,0},{16,24},{24,16},{1,9},{9,1},{17,25},{25,17},{2,10},{10... | collective-permute-start | bytes 393224 | tf_op jit(solution)/shard_map/ppermute | solution.py:311
  38.5 1.2 %collective-permute-start.13 = (f32[4,64,128]{2,1,0:T(8,128)S(1)}, f32[4,64,128]{2,1,0:T(8,128)S(1)}, u32[]{:S(2)}, u32[]{:S(2)}) collective-permute-start(f32[4,64,128]{2,1,0:T(8,128)S(1)} %get-tuple-element.50), channel_id=1, source_target_pairs={{8,16},{24,25},{17,9},{1,2},{10,18},{26,27},{19,11},{3,4},{12,20},... | collective-permute-start | bytes 393224 | tf_op jit(solution)/shard_map/ppermute | solution.py:322
  55.8 8.8 %collective-permute-start.15 = (f32[8,64,128]{2,1,0:T(8,128)S(1)}, f32[8,64,128]{2,1,0:T(8,128)S(1)}, u32[]{:S(2)}, u32[]{:S(2)}) collective-permute-start(f32[8,64,128]{2,1,0:T(8,128)S(1)} %shard_map.52.refs_3_), channel_id=1, source_target_pairs={{8,16},{24,25},{17,9},{1,2},{10,18},{26,27},{19,11},{3,4},{12,20},... | collective-permute-start | bytes 786440 | tf_op jit(solution)/shard_map/ppermute | solution.py:322
  56.7 9.1 %collective-permute-start.14 = (f32[8,64,128]{2,1,0:T(8,128)S(1)}, f32[8,64,128]{2,1,0:T(8,128)S(1)}, u32[]{:S(2)}, u32[]{:S(2)}) collective-permute-start(f32[8,64,128]{2,1,0:T(8,128)S(1)} %shard_map.52.refs_3_), channel_id=1, source_target_pairs={{0,8},{8,0},{16,24},{24,16},{1,9},{9,1},{17,25},{25,17},{2,10},{10... | collective-permute-start | bytes 786440 | tf_op jit(solution)/shard_map/ppermute | solution.py:311
  101.6 6.4 %collective-permute-start.17 = (f32[64,8,128]{2,1,0:T(8,128)S(1)}, f32[64,8,128]{2,1,0:T(8,128)S(1)}, u32[]{:S(2)}, u32[]{:S(2)}) collective-permute-start(f32[64,8,128]{2,1,0:T(8,128)S(1)} %bitcast.18), channel_id=1, source_target_pairs={{0,16},{8,24},{16,0},{24,8},{1,17},{9,25},{17,1},{25,9},{2,18},{10... | collective-permute-start | bytes 786440 | tf_op jit(solution)/shard_map/ppermute | solution.py:311
  101.7 6.4 %collective-permute-start.16 = (f32[64,8,128]{2,1,0:T(8,128)S(1)}, f32[64,8,128]{2,1,0:T(8,128)S(1)}, u32[]{:S(2)}, u32[]{:S(2)}) collective-permute-start(f32[64,8,128]{2,1,0:T(8,128)S(1)} %bitcast.19), channel_id=1, source_target_pairs={{0,8},{8,0},{16,24},{24,16},{1,9},{9,1},{17,25},{25,17},{2,10},{10... | collective-permute-start | bytes 786440 | tf_op jit(solution)/shard_map/ppermute | solution.py:311
  108.0 1.5 %collective-permute-start.18 = (f32[64,8,128]{2,1,0:T(8,128)S(1)}, f32[64,8,128]{2,1,0:T(8,128)S(1)}, u32[]{:S(2)}, u32[]{:S(2)}) collective-permute-start(f32[64,8,128]{2,1,0:T(8,128)S(1)} %collective-permute-done.17.refs_2_), channel_id=1, source_target_pairs={{0,8},{8,0},{16,24},{24,16},{1,9},{9,1},{17,25},{25,17},{2,10},{10... | collective-permute-start | bytes 786440 | tf_op jit(solution)/shard_map/ppermute | solution.py:311

commit v10 on v9

--- a/solution.py
+++ b/solution.py
@@ -9,7 +9,6 @@
 
 ITERS = 2
 CORES = 2
-SUBLANES = 8
 VMEM = pl.BlockSpec(memory_space=pltpu.VMEM)
 SMEM = pl.BlockSpec(memory_space=pltpu.SMEM)
 PARAMS = pltpu.CompilerParams(vmem_limit_bytes=48 * 1024 * 1024)
@@ -39,11 +38,6 @@
     middle = rest.astype(jnp.bfloat16)
     low = (rest - middle.astype(jnp.float32)).astype(jnp.bfloat16)
     left = jnp.concatenate([high, middle, low], axis=1)
-    place = lax.broadcasted_iota(jnp.int32, (rows, rows), 0)
-    natural = (place % SUBLANES) * (rows // SUBLANES) + place // SUBLANES
-    order = (lax.broadcasted_iota(jnp.int32, (rows, rows), 1) == natural).astype(jnp.bfloat16)
-    left = jnp.dot(order, left, preferred_element_type=jnp.float32).astype(jnp.bfloat16)
-
     for out_ref, (other, segments) in zip(outs, plan):
         half = 1 - place_ref[0] if other else place_ref[0]
         for index, start, target, length in segments:
@@ -78,32 +72,39 @@
     )(place, weights.transpose(0, 2, 1), offsets[:, None, :], *sources)
 
 
-def bands_kernel(taps_ref, out_ref):
+def bands_kernel(taps_ref, left_ref, right_ref):
     view = pl.program_id(0)
     count = taps_ref.shape[2]
-    width = out_ref.shape[2] // 2
-    shape = (width, width)
-    shift = lax.broadcasted_iota(jnp.int32, shape, 0) - lax.broadcasted_iota(jnp.int32, shape, 1)
-    for way in range(2):
-        band = jnp.zeros(shape, jnp.float32)
+    rows, width = left_ref.shape[2], right_ref.shape[2] // 2
+
+    def band(size, axis, way):
+        shape = (size, size)
+        shift = lax.broadcasted_iota(jnp.int32, shape, 0) - lax.broadcasted_iota(jnp.int32, shape, 1)
+        total = jnp.zeros(shape, jnp.float32)
         for t in range(count):
             at = t - count // 2
-            band = jnp.where(shift == (-at if way else at), taps_ref[view, 2, t], band)
-        high, low = halves(band)
-        out_ref[0, way, :width, :width] = high
-        out_ref[0, way, width:, :width] = high
-        out_ref[0, way, :width, width:] = low
-        out_ref[0, way, width:, width:] = jnp.zeros_like(low)
-
-
-def bands(taps, width):
+            total = jnp.where(shift == (-at if way else at), taps_ref[view, axis, t], total)
+        return halves(total)
+
+    for way in range(2):
+        high, low = band(rows, 1, 1 - way)
+        left_ref[0, way] = jnp.concatenate([high, high, low], axis=1)
+        high, low = band(width, 2, way)
+        right_ref[0, way, :width, :width] = high
+        right_ref[0, way, width:, :width] = high
+        right_ref[0, way, :width, width:] = low
+        right_ref[0, way, width:, width:] = jnp.zeros_like(low)
+
+
+def bands(taps, rows, width):
     views = taps.shape[0]
+    shapes = [(2, rows, 3 * rows), (2, 2 * width, 2 * width)]
     return pl.pallas_call(
         bands_kernel,
         grid=(views,),
-        out_shape=jax.ShapeDtypeStruct((views, 2, 2 * width, 2 * width), jnp.bfloat16),
+        out_shape=[jax.ShapeDtypeStruct((views,) + shape, jnp.bfloat16) for shape in shapes],
         in_specs=[SMEM],
-        out_specs=pl.BlockSpec((1, 2, 2 * width, 2 * width), lambda v: (v, 0, 0, 0)),
+        out_specs=[pl.BlockSpec((1,) + shape, lambda v: (v, 0, 0, 0)) for shape in shapes],
         compiler_params=PARAMS,
     )(taps)
 
@@ -172,9 +173,9 @@
     )(place, *([] if partial is None else [partial]), *parts)
 
 
-def update_kernel(last, paired, place_ref, taps_ref, bands_ref, *refs):
+def update_kernel(paired, place_ref, taps_ref, lefts_ref, rights_ref, *refs):
     bricks_refs, (first_ref, own_ref, second_ref, out_ref) = refs[:2], refs[2:6]
-    volume, wides, lefts, ratios, backs, logs = refs[6:]
+    volume, fields, flats, ratios, logs = refs[6:]
     bricks = [ref.at[group] for ref in bricks_refs for group in range(ref.shape[0])]
     count = len(bricks)
     step = pl.program_id(0)
@@ -182,9 +183,6 @@
     rim = taps // 2
     planes, rows, width = out_ref.shape
     outer = planes + 2 * rim
-    tiles = rows // SUBLANES
-    tile = lambda k: pl.ds(k * SUBLANES, SUBLANES)
-    sublane = lax.broadcasted_iota(jnp.int32, (SUBLANES, width), 0)
 
     @pl.when(step == 0)
     def _():
@@ -197,53 +195,53 @@
         for z in range(middle):
             volume[side + z] = own_ref[z]
 
-    def correlate(gains, terms):
-        total = gains[0] * terms[0]
-        for t in range(1, taps):
-            total = total + gains[t] * terms[t]
-        return total
-
-    def along_z(column, gains, length):
-        return [correlate(gains, column[z : z + taps]) for z in range(length)]
-
-    def along_x(source, left, gains, z):
-        row = [source[z, tile(k), :] for k in range(tiles)]
-        below = [jnp.where(sublane == 0, 0.0, pltpu.roll(part, 1, 0)) for part in row[tiles - rim :]]
-        above = [jnp.where(sublane == SUBLANES - 1, 0.0, pltpu.roll(part, SUBLANES - 1, 0)) for part in row[:rim]]
-        row = below + row + above
-        for k in range(0, tiles, 2):
-            pair = [correlate(gains, row[k : k + taps]), correlate(gains, row[k + 1 : k + 1 + taps])]
-            high, low = halves(jnp.concatenate(pair, axis=0))
-            at = pl.ds(z * rows + k * SUBLANES, 2 * SUBLANES)
-            left[at, :width] = high
-            left[at, width:] = low
+    def along_z(source, field, gains, length):
+        for k in range(0, rows, 16):
+            pair = []
+            for half in range(2):
+                column = [source[z, pl.ds(k + 8 * half, 8), :] for z in range(length + 2 * rim)]
+                sums = []
+                for z in range(length):
+                    total = column[z + rim]
+                    for t in range(taps):
+                        if t != rim:
+                            total = total + gains[t] * column[z + t]
+                    sums.append(total)
+                pair.append(sums)
+            for z in range(length):
+                high, low = halves(jnp.concatenate([pair[0][z], pair[1][z]], axis=0))
+                field[0, z, pl.ds(k, 16), :] = high
+                field[1, z, pl.ds(k, 16), :] = low
+
+    def along_x(field, flat, matrix, length):
+        for z in range(0, length, 2):
+            high, low = [jnp.concatenate([field[part, z], field[part, z + 1]], axis=1) for part in range(2)]
+            right = jnp.concatenate([high, low, high], axis=0)
+            high, low = halves(jnp.dot(matrix, right, preferred_element_type=jnp.float32))
+            for i in range(2):
+                at = pl.ds((z + i) * rows, rows)
+                flat[at, :width] = high[:, i * width : (i + 1) * width]
+                flat[at, width:] = low[:, i * width : (i + 1) * width]
+
+    def along_y(flat, matrix, length):
+        product = jnp.dot(flat[: length * rows, :], matrix, preferred_element_type=jnp.float32)
+        return (product[:, :width] + product[:, width:]).reshape(length, rows, width)
 
     held = None
     for group in range(count):
         view = group * pl.num_programs(0) + step
-        wide, left, ratio, back = (scratch.at[group % 2] for scratch in (wides, lefts, ratios, backs))
-        gain_z = [taps_ref[view, 0, t] for t in range(taps)]
-        gain_x = [taps_ref[view, 1, t] for t in range(taps)]
-        for k in range(tiles):
-            column = along_z([volume[z, tile(k), :] for z in range(outer + 2 * rim)], gain_z, outer)
-            for z in range(outer):
-                wide[z, tile(k), :] = column[z]
-        for z in range(outer):
-            along_x(wide, left, gain_x, z)
-        product = jnp.dot(left[...], bands_ref[group, 0, 0], preferred_element_type=jnp.float32)
-        blurred = (product[:, :width] + product[:, width:]).reshape(outer, rows, width)
+        field, flat, ratio = (scratch.at[group % 2] for scratch in (fields, flats, ratios))
+        gains = [taps_ref[view, 0, t] for t in range(taps)]
+        along_z(volume, field, gains, outer)
+        along_x(field, flat, lefts_ref[group, 0, 0], outer)
+        blurred = along_y(flat, rights_ref[group, 0, 0], outer)
         for z in range(outer):
             guess = pl.reciprocal(blurred[z], approx=True)
             guess = guess * (2.0 - blurred[z] * guess)
             ratio[z] = bricks[group][0, z].astype(jnp.float32) * guess
-        for k in range(tiles):
-            column = along_z([ratio[z, tile(k), :] for z in range(outer)], gain_z[::-1], planes)
-            for z in range(planes):
-                back[z, tile(k), :] = column[z]
-        for z in range(planes):
-            along_x(back, left, gain_x[::-1], z)
-        product = jnp.dot(left[: planes * rows, :], bands_ref[group, 0, 1], preferred_element_type=jnp.float32)
-        total = (product[:, :width] + product[:, width:]).reshape(logs.shape)
+        along_z(ratio, field, gains[::-1], planes)
+        along_x(field, flat, lefts_ref[group, 0, 1], planes)
+        total = along_y(flat, rights_ref[group, 0, 1], planes)
         if group % 2 == 0:
             held = total
         else:
@@ -252,37 +250,32 @@
     @pl.when(step == pl.num_programs(0) - 1)
     def _():
         for z in range(planes):
-            for k in range(tiles):
-                value = volume[2 * rim + z, tile(k), :] * jnp.exp(logs[z, tile(k), :] / (count * pl.num_programs(0)))
-                if last:
-                    out_ref[z, pl.ds(k, SUBLANES, tiles), :] = value
-                else:
-                    out_ref[z, tile(k), :] = value
-
-
-def update(place, taps, band, bricks, halo, own, planes, paired, last):
+            out_ref[z] = volume[2 * rim + z] * jnp.exp(logs[z] / (count * pl.num_programs(0)))
+
+
+def update(place, taps, band, bricks, halo, own, planes, paired):
     _, count, outer, rows, width = bricks[0].shape
     groups = sum(part.shape[0] for part in bricks)
-    band = band.reshape((groups, count) + band.shape[1:])
+    band = [part.reshape((groups, count) + part.shape[1:]) for part in band]
     step = lambda v: (0, v, 0, 0, 0)
     return pl.pallas_call(
-        functools.partial(update_kernel, last, paired),
+        functools.partial(update_kernel, paired),
         grid=(count,),
         out_shape=jax.ShapeDtypeStruct((planes, rows, width), jnp.float32),
-        in_specs=[SMEM, SMEM, pl.BlockSpec((groups, 1) + band.shape[2:], step)]
+        in_specs=[SMEM, SMEM]
+        + [pl.BlockSpec((groups, 1) + part.shape[2:], step) for part in band]
         + [pl.BlockSpec((part.shape[0], 1, outer, rows, width), step) for part in bricks]
         + [VMEM] * 3,
         out_specs=VMEM,
         scratch_shapes=[
             pltpu.VMEM((2 * outer - planes, rows, width), jnp.float32),
-            pltpu.VMEM((2, outer, rows, width), jnp.float32),
+            pltpu.VMEM((2, 2, outer, rows, width), jnp.bfloat16),
             pltpu.VMEM((2, outer * rows, 2 * width), jnp.bfloat16),
             pltpu.VMEM((2, outer, rows, width), jnp.float32),
-            pltpu.VMEM((2, planes, rows, width), jnp.float32),
             pltpu.VMEM((planes, rows, width), jnp.float32),
         ],
         compiler_params=PARAMS,
-    )(place, taps, band, *bricks, halo[0], own, halo[1])
+    )(place, taps, *band, *bricks, halo[0], own, halo[1])
 
 
 def place_kernel(planes, place_ref, *refs):
@@ -369,7 +362,9 @@
     pair_taps = near(jnp.stack([psf_taps, cross_taps]))
     all_taps = jnp.concatenate([psf_taps, pair_taps[0], pair_taps[1], cross_taps])
     all_taps = all_taps / jnp.sum(all_taps, axis=-1, keepdims=True)
-    band = bands(all_taps, width)
+    centre = all_taps[:, :1, rim : rim + 1]
+    all_taps = jnp.concatenate([all_taps[:, :1] / centre, all_taps[:, 1:2], all_taps[:, 2:] * centre], axis=1)
+    band = bands(all_taps, rows, width)
     home, partial = gather_views(
         place, [own_inner, near(own_inner)], [own_bound, near(own_bound)], [own_edge, near(own_edge)], planes
     )
@@ -388,13 +383,13 @@
         halo = (near(near_send), swap(cross_send, gaps, members, blocks))
     else:
         halo = z_rims(start[rim : rim + planes], rim, 2 * rim, members, blocks)
-    joined = update(place, all_taps, band, bricks, halo, start, planes, paired, ITERS == 1)
+    joined = update(place, all_taps, band, bricks, halo, start, planes, paired)
     for turn in range(1, ITERS):
         if paired:
             halo = (near(joined), swap(joined, gaps, members, blocks))
         else:
             halo = z_rims(joined, 0, 2 * rim, members, blocks)
-        joined = update(place, all_taps, band, bricks, halo, joined, planes, paired, turn == ITERS - 1)
+        joined = update(place, all_taps, band, bricks, halo, joined, planes, paired)
 
     columns = lax.all_to_all(joined, "vol", split_axis=1, concat_axis=0, tiled=True)
     far_columns = far(columns)

time: 111 us -> 110 us (level)
  Pallas kernels: 44.5 us -> 42.6 us
  starting transfers between devices: 15.7 us -> 17.1 us
  waiting for transfers between devices: 25.8 us -> 24.6 us
    ppermute x15, starting transfers between devices: 12.9 us -> 14.4 us  [partner(): return lax.ppermute(value, 'view', [(i, i ^ bit) for i in range(members)])]
    pallas_call x3, Pallas kernels: 6.32 us -> 5.15 us  [resample(): pl.pallas_call(functools.partial(resample_kernel, plan), grid=(views,), o...]
    ppermute x15, waiting for transfers between devices: 25.8 us -> 24.6 us  [partner(): return lax.ppermute(value, 'view', [(i, i ^ bit) for i in range(members)])]
where the time goes in v10:
time: 110 us
  Pallas kernels  42.6 us (39%)
  waiting for transfers between devices  24.6 us (22%)
  blocking collectives  19.7 us (18%)
  starting transfers between devices  17.1 us (16%)
  local copies, waits for them, and re-layouts  4.89 us (4%)
    pallas_call x2, Pallas kernels, update(): pl.pallas_call(functools.partial(update_kernel, paired), grid=(count,), o...  30.7 us
    ppermute x15, waiting for transfers between devices, partner(): return lax.ppermute(value, 'view', [(i, i ^ bit) for i in range(members)])  24.6 us
    all_to_all x1, blocking collectives, per_device(): lax.all_to_all(joined, 'vol', split_axis=1, concat_axis=0, tiled=True)  19.7 us
    ppermute x15, starting transfers between devices, partner(): return lax.ppermute(value, 'view', [(i, i ^ bit) for i in range(members)])  14.4 us
    pallas_call x3, Pallas kernels, resample(): pl.pallas_call(functools.partial(resample_kernel, plan), grid=(views,), o...  5.15 us
    unnamed x8, local copies, waits for them, and re-layouts  3.75 us
    pallas_call x1, Pallas kernels, bands(): pl.pallas_call(bands_kernel, grid=(views,), out_shape=[jax.ShapeDtypeStru...  3.13 us
    ppermute x4, starting transfers between devices, swap(): return lax.ppermute(value, ('view', 'vol'), perm)  2.67 us
  transfers between devices with their start and end apart: 19, of which 8 were waited for; matrix products, arithmetic and copies ran while one was open for 1% of the time, Pallas kernels for 9%

profile of v10, /device:TPU:0, one launch (start us, length us, event | category | flops | bytes accessed | tf_op | source)
XLA Modules:
  0.0 109.5 jit_solution(17985200024109457061)
XLA Ops:
  0.0 0.0 copy-start.3
  0.0 2.4 %collective-permute-start = (f32[3,3,9]{2,1,0:T(4,128)}, f32[3,3,9]{2,1,0:T(4,128)S(1)}, u32[]{:S(2)}, u32[]{:S(2)}) collective-permute-start(f32[3,3,9]{2,1,0:T(4,128)} %param.7), channel_id=1, source_target_pairs={{0,24},{8,16},{16,8},{24,0},{1,25},{9,17},{17,9},{25,1},{2,26},{10... | collective-permute-start | bytes 980 | tf_op jit(solution)/shard_map/ppermute | solution.py:304
  2.4 0.1 pad_add_fusion.place_ref
  2.5 0.7 broadcast_in_dim.2.offsets_ref
  3.1 0.0 copy-start
  3.1 1.4 %copy-done = bf16[3,32,64,128]{3,2,1,0:T(8,128)(2,1)S(1)} copy-done((bf16[3,32,64,128]{3,2,1,0:T(8,128)(2,1)S(1)}, bf16[3,32,64,128]{3,2,1,0:T(8,128)(2,1)}, u32[]{:S(2)}) %copy-start) | copy-done | bytes 1572888
  4.5 0.0 copy-start.2
  4.5 0.7 copy-done.2
  5.3 1.5 %shard_map.46 = bf16[3,4,64,128]{3,2,1,0:T(8,128)(2,1)S(1)} custom-call(s32[2]{0:T(128)S(1)} %pad_add_fusion.place_ref, f32[3,8,64]{2,1,0:T(8,128)S(1)} %bitcast.24, s32[3,1,64]{2,1,0:T(1,128)S(1)} %broadcast_in_dim.2.offsets_ref, bf16[3,32,64,128]{3,2,1,0:T(8,128)(2,1)S(1)} %copy-done), custom_call_target="tpu_custom_call" | custom-call | tf_op jit(solution)/shard_map/pallas_call | solution.py:60
  6.7 0.0 collective-permute-done
  6.7 0.6 collective-permute-start.2
  7.4 0.0 copy-done.3
  7.4 0.2 collective-permute-start.1
  7.6 1.8 %shard_map.47 = bf16[3,16,64,128]{3,2,1,0:T(8,128)(2,1)S(1)} custom-call(s32[2]{0:T(128)S(1)} %pad_add_fusion.place_ref, f32[3,8,64]{2,1,0:T(8,128)S(1)} %bitcast.25, s32[3,1,64]{2,1,0:T(1,128)S(1)} %broadcast_in_dim.2.offsets_ref, bf16[3,32,64,128]{3,2,1,0:T(8,128)(2,1)S(1)} %copy-done), custom_call_target="tpu_custom_call" | custom-call | tf_op jit(solution)/shard_map/pallas_call | solution.py:60
  9.4 1.9 %shard_map.48 = (bf16[3,4,64,128]{3,2,1,0:T(8,128)(2,1)S(1)}, bf16[3,16,64,128]{3,2,1,0:T(8,128)(2,1)S(1)}) custom-call(s32[2]{0:T(128)S(1)} %pad_add_fusion.place_ref, f32[3,8,64]{2,1,0:T(8,128)S(1)} %bitcast.26, s32[3,1,64]{2,1,0:T(1,128)S(1)} %broadcast_in_dim.2.offsets_ref, bf16[3,32,64,128]{3,2,1,0:T(8,128)(2,1)S(1)} %copy-done), custom_call_target="tpu_custom_call" | custom-call | tf_op jit(solution)/shard_map/pallas_call | solution.py:60
  11.3 3.0 %collective-permute-done.2.refs_3_ = bf16[3,4,64,128]{3,2,1,0:T(8,128)(2,1)S(1)} collective-permute-done((bf16[3,4,64,128]{3,2,1,0:T(8,128)(2,1)S(1)}, bf16[3,4,64,128]{3,2,1,0:T(8,128)(2,1)S(1)}, u32[]{:S(2)}, u32[]{:S(2)}) %collective-permute-start.2) | collective-permute-done | bytes 196640 | tf_op jit(solution)/shard_map/ppermute | solution.py:304
  14.3 0.3 collective-permute-start.3
  14.6 0.0 collective-permute-start.4
  14.6 0.0 collective-permute-done.1
  14.6 0.1 fusion
  14.7 0.7 collective-permute-start.6
  15.4 0.6 collective-permute-start.5
  15.9 0.7 collective-permute-start.9
  16.6 0.1 broadcast_divide_fusion
  16.7 0.3 slice_reduce_fusion
  16.9 0.0 collective-permute-done.6.refs_4_
  16.9 0.1 collective-permute-start.8
  17.0 0.1 collective-permute-done.5.refs_3_
  17.1 0.4 collective-permute-start.7
  17.5 0.0 collective-permute-done.9.refs_5_
  17.5 0.1 collective-permute-start.10
  17.7 0.1 slice_divide_fusion
  17.8 3.1 %shard_map.49 = (bf16[12,2,64,192]{3,2,1,0:T(8,128)(2,1)S(1)}, bf16[12,2,256,256]{3,2,1,0:T(8,128)(2,1)S(1)}) custom-call(f32[12,3,9]{2,1,0:T(4,128)S(1)} %pad_maximum_fusion.1.taps_ref), custom_call_target="tpu_custom_call" | custom-call | tf_op jit(solution)/shard_map/pallas_call | solution.py:102
  20.9 0.0 copy-start.1
  20.9 1.6 %copy-done.1 = bf16[12,2,256,256]{3,2,1,0:T(8,128)(2,1)} copy-done((bf16[12,2,256,256]{3,2,1,0:T(8,128)(2,1)}, bf16[12,2,256,256]{3,2,1,0:T(8,128)(2,1)S(1)}, u32[]{:S(2)}) %copy-start.1) | copy-done | bytes 3145752
  22.6 0.0 collective-permute-done.7.refs_5_
  22.6 0.0 collective-permute-done.4.refs_1_
  22.6 1.3 %shard_map.50 = (bf16[2,3,16,64,128]{4,3,2,1,0:T(8,128)(2,1)S(1)}, f32[16,64,128]{2,1,0:T(8,128)S(1)}) custom-call(s32[2]{0:T(128)S(1)} %pad_add_fusion.place_ref, bf16[3,16,64,128]{3,2,1,0:T(8,128)(2,1)S(1)} %get-tuple-element.39.refs_0_, bf16[3,16,64,128]{3,2,1,0:T(8,128)(2,1)S(1)} %collective-permute-done.4.refs_1_, ...), custom_call_target="tpu_custom_call" | custom-call | tf_op jit(solution)/shard_map/pallas_call | solution.py:162
  23.8 0.0 collective-permute-done.8.refs_4_
  23.8 0.0 collective-permute-done.10.refs_6_
  23.9 9.7 %collective-permute-done.3.refs_1_ = bf16[3,16,64,128]{3,2,1,0:T(8,128)(2,1)S(1)} collective-permute-done((bf16[3,16,64,128]{3,2,1,0:T(8,128)(2,1)S(1)}, bf16[3,16,64,128]{3,2,1,0:T(8,128)(2,1)S(1)}, u32[]{:S(2)}, u32[]{:S(2)}) %collective-permute-start.3) | collective-permute-done | bytes 786464 | tf_op jit(solution)/shard_map/ppermute | solution.py:304
  33.6 0.0 collective-permute-start.11
  33.6 2.3 %collective-permute-done.11.refs_2_ = bf16[3,16,64,128]{3,2,1,0:T(8,128)(2,1)S(1)} collective-permute-done((bf16[3,16,64,128]{3,2,1,0:T(8,128)(2,1)S(1)}, bf16[3,16,64,128]{3,2,1,0:T(8,128)(2,1)S(1)}, u32[]{:S(2)}, u32[]{:S(2)}) %collective-permute-start.11) | collective-permute-done | bytes 786464 | tf_op jit(solution)/shard_map/ppermute | solution.py:304
  35.8 1.3 %shard_map.51 = (bf16[2,3,16,64,128]{4,3,2,1,0:T(8,128)(2,1)S(1)}, f32[16,64,128]{2,1,0:T(8,128)S(1)}, f32[4,64,128]{2,1,0:T(8,128)S(1)}, f32[4,64,128]{2,1,0:T(8,128)S(1)}) custom-call(s32[2]{0:T(128)S(1)} %pad_add_fusion.place_ref, f32[16,64,128]{2,1,0:T(8,128)S(1)} %get-tuple-element.47.refs_0_, ...), custom_call_target="tpu_custom_call" | custom-call | tf_op jit(solution)/shard_map/pallas_call | solution.py:162
  37.2 0.2 collective-permute-start.12
  37.4 0.7 collective-permute-start.13
  38.1 0.5 collective-permute-done.12.refs_2_
  38.6 0.0 collective-permute-done.13.refs_4_
  38.6 15.4 %shard_map.52.refs_3_ = f32[8,64,128]{2,1,0:T(8,128)S(1)} custom-call(s32[2]{0:T(128)S(1)} %pad_add_fusion.place_ref, f32[12,3,9]{2,1,0:T(4,128)S(1)} %pad_maximum_fusion.1.taps_ref, bf16[4,3,2,64,192]{4,3,2,1,0:T(8,128)(2,1)S(1)} %bitcast.19, bf16[4,3,2,256,256]{4,3,2,1,0:T(8,128)(2,1)} %bitcast.17, ...), custom_call_target="tpu_custom_call" | custom-call | tf_op jit(solution)/shard_map/pallas_call | solution.py:261
  54.0 0.7 collective-permute-start.15
  54.7 9.4 %collective-permute-start.14 = (f32[8,64,128]{2,1,0:T(8,128)S(1)}, f32[8,64,128]{2,1,0:T(8,128)S(1)}, u32[]{:S(2)}, u32[]{:S(2)}) collective-permute-start(f32[8,64,128]{2,1,0:T(8,128)S(1)} %shard_map.52.refs_3_), channel_id=1, source_target_pairs={{0,8},{8,0},{16,24},{24,16},{1,9},{9,1},{17,25},{25,17},{2,10},{10... | collective-permute-start | bytes 786440 | tf_op jit(solution)/shard_map/ppermute | solution.py:304
  64.1 0.0 collective-permute-done.15.refs_4_
  64.1 1.2 %collective-permute-done.14.refs_2_ = f32[8,64,128]{2,1,0:T(8,128)S(1)} collective-permute-done((f32[8,64,128]{2,1,0:T(8,128)S(1)}, f32[8,64,128]{2,1,0:T(8,128)S(1)}, u32[]{:S(2)}, u32[]{:S(2)}) %collective-permute-start.14) | collective-permute-done | bytes 262176 | tf_op jit(solution)/shard_map/ppermute | solution.py:304
  65.2 15.4 %shard_map.53 = f32[8,64,128]{2,1,0:T(8,128)S(1)} custom-call(s32[2]{0:T(128)S(1)} %pad_add_fusion.place_ref, f32[12,3,9]{2,1,0:T(4,128)S(1)} %pad_maximum_fusion.1.taps_ref, bf16[4,3,2,64,192]{4,3,2,1,0:T(8,128)(2,1)S(1)} %bitcast.20, bf16[4,3,2,256,256]{4,3,2,1,0:T(8,128)(2,1)} %bitcast.18, bf16[2,3,16,64,128]{4,3,2,1,0:T(8,128)(2,1)S(1)} %get-tuple-element.46.refs_0_, ...), custom_call_target="tpu_custom_call" | custom-call | tf_op jit(solution)/shard_map/pallas_call | solution.py:261
  80.6 0.2 copy.7
  80.8 19.7 %all_to_all.18 = f32[8,64,128]{2,0,1:T(8,128)S(1)} all-to-all(f32[8,64,128]{2,0,1:T(8,128)S(1)} %copy.7), channel_id=1, replica_groups=mesh['view'=4,'vol'=8] {'vol'}, dimensions={1} | all-to-all | bytes 524288 | tf_op jit(solution)/shard_map/all_to_all | solution.py:394
  100.5 0.1 collective-permute-start.17
  100.6 0.1 collective-permute-start.16
  100.7 6.3 %collective-permute-done.17.refs_2_ = f32[64,8,128]{2,1,0:T(8,128)S(1)} collective-permute-done((f32[64,8,128]{2,1,0:T(8,128)S(1)}, f32[64,8,128]{2,1,0:T(8,128)S(1)}, u32[]{:S(2)}, u32[]{:S(2)}) %collective-permute-start.17) | collective-permute-done | bytes 262176 | tf_op jit(solution)/shard_map/ppermute | solution.py:304
  106.9 0.0 collective-permute-start.18
  106.9 0.0 collective-permute-done.16.refs_1_
  106.9 1.5 %collective-permute-done.18.refs_3_ = f32[64,8,128]{2,1,0:T(8,128)S(1)} collective-permute-done((f32[64,8,128]{2,1,0:T(8,128)S(1)}, f32[64,8,128]{2,1,0:T(8,128)S(1)}, u32[]{:S(2)}, u32[]{:S(2)}) %collective-permute-start.18) | collective-permute-done | bytes 262176 | tf_op jit(solution)/shard_map/ppermute | solution.py:304
  108.5 1.0 shard_map.54
  (4 shorter events, 0.1 us)
Async XLA Ops:
  0.0 7.4 %copy-start.3 = (f32[3,3,9]{2,1,0:T(4,128)S(1)}, f32[3,3,9]{2,1,0:T(4,128)}, u32[]{:S(2)}) copy-start(f32[3,3,9]{2,1,0:T(4,128)} %param.7) | copy-start | bytes 976
  0.0 6.7 %collective-permute-start = (f32[3,3,9]{2,1,0:T(4,128)}, f32[3,3,9]{2,1,0:T(4,128)S(1)}, u32[]{:S(2)}, u32[]{:S(2)}) collective-permute-start(f32[3,3,9]{2,1,0:T(4,128)} %param.7), channel_id=1, source_target_pairs={{0,24},{8,16},{16,8},{24,0},{1,25},{9,17},{17,9},{25,1},{2,26},{10... | collective-permute-start | bytes 980 | tf_op jit(solution)/shard_map/ppermute | solution.py:304
  3.1 1.4 %copy-start = (bf16[3,32,64,128]{3,2,1,0:T(8,128)(2,1)S(1)}, bf16[3,32,64,128]{3,2,1,0:T(8,128)(2,1)}, u32[]{:S(2)}) copy-start(bf16[3,32,64,128]{3,2,1,0:T(8,128)(2,1)} %refs_0_.3) | copy-start | bytes 4718596
  4.5 0.7 copy-start.2
  6.7 7.5 %collective-permute-start.2 = (bf16[3,4,64,128]{3,2,1,0:T(8,128)(2,1)S(1)}, bf16[3,4,64,128]{3,2,1,0:T(8,128)(2,1)S(1)}, u32[]{:S(2)}, u32[]{:S(2)}) collective-permute-start(bf16[3,4,64,128]{3,2,1,0:T(8,128)(2,1)S(1)} %shard_map.46), channel_id=1, source_target_pairs={{0,16},{8,24},{16,0},{24,8},{1,17},{9,25},{17,1},{25,9},{2,18},{10... | collective-permute-start | bytes 589832 | tf_op jit(solution)/shard_map/ppermute | solution.py:304
  7.4 7.2 %collective-permute-start.1 = (f32[2,3,3,9]{3,2,1,0:T(4,128)S(1)}, f32[2,3,3,9]{3,2,1,0:T(4,128)S(1)}, u32[]{:S(2)}, u32[]{:S(2)}) collective-permute-start(f32[2,3,3,9]{3,2,1,0:T(4,128)S(1)} %pad_maximum_fusion.2), channel_id=1, source_target_pairs={{0,8},{8,0},{16,24},{24,16},{1,9},{9,1},{17,25},{25,17},{2,10},{10... | collective-permute-start | bytes 1952 | tf_op jit(solution)/shard_map/ppermute | solution.py:304
  14.3 19.3 %collective-permute-start.3 = (bf16[3,16,64,128]{3,2,1,0:T(8,128)(2,1)S(1)}, bf16[3,16,64,128]{3,2,1,0:T(8,128)(2,1)S(1)}, u32[]{:S(2)}, u32[]{:S(2)}) collective-permute-start(bf16[3,16,64,128]{3,2,1,0:T(8,128)(2,1)S(1)} %shard_map.47), channel_id=1, source_target_pairs={{0,16},{8,24},{16,0},{24,8},{1,17},{9,25},{17,1},{25,9},{2,18},{10... | collective-permute-start | bytes 2359304 | tf_op jit(solution)/shard_map/ppermute | solution.py:304
  14.6 8.0 %collective-permute-start.4 = (bf16[3,16,64,128]{3,2,1,0:T(8,128)(2,1)S(1)}, bf16[3,16,64,128]{3,2,1,0:T(8,128)(2,1)S(1)}, u32[]{:S(2)}, u32[]{:S(2)}) collective-permute-start(bf16[3,16,64,128]{3,2,1,0:T(8,128)(2,1)S(1)} %get-tuple-element.39.refs_0_), channel_id=1, source_target_pairs={{0,8},{8,0},{16,24},{24,16},{1,9},{9,1},{17,25},{25,17},{2,10},{10... | collective-permute-start | bytes 2359304 | tf_op jit(solution)/shard_map/ppermute | solution.py:304
  14.7 2.3 %collective-permute-start.6 = (bf16[3,4,64,128]{3,2,1,0:T(8,128)(2,1)S(1)}, bf16[3,4,64,128]{3,2,1,0:T(8,128)(2,1)S(1)}, u32[]{:S(2)}, u32[]{:S(2)}) collective-permute-start(bf16[3,4,64,128]{3,2,1,0:T(8,128)(2,1)S(1)} %get-tuple-element.40.refs_2_), channel_id=1, source_target_pairs={{24,25},{16,17},{1,2},{9,10},{26,27},{18,19},{3,4},{11,12},{28,29}... | collective-permute-start | bytes 589832 | tf_op jit(solution)/shard_map/ppermute | solution.py:315
  15.4 1.8 %collective-permute-start.5 = (bf16[3,4,64,128]{3,2,1,0:T(8,128)(2,1)S(1)}, bf16[3,4,64,128]{3,2,1,0:T(8,128)(2,1)S(1)}, u32[]{:S(2)}, u32[]{:S(2)}) collective-permute-start(bf16[3,4,64,128]{3,2,1,0:T(8,128)(2,1)S(1)} %get-tuple-element.40.refs_2_), channel_id=1, source_target_pairs={{0,8},{8,0},{16,24},{24,16},{1,9},{9,1},{17,25},{25,17},{2,10},{10... | collective-permute-start | bytes 589832 | tf_op jit(solution)/shard_map/ppermute | solution.py:304
  15.9 1.6 %collective-permute-start.9 = (bf16[3,4,64,128]{3,2,1,0:T(8,128)(2,1)S(1)}, bf16[3,4,64,128]{3,2,1,0:T(8,128)(2,1)S(1)}, u32[]{:S(2)}, u32[]{:S(2)}) collective-permute-start(bf16[3,4,64,128]{3,2,1,0:T(8,128)(2,1)S(1)} %collective-permute-done.2.refs_3_), channel_id=1, source_target_pairs={{24,25},{16,17},{1,2},{9,10},{26,27},{18,19},{3,4},{11,12},{28,29}... | collective-permute-start | bytes 589832 | tf_op jit(solution)/shard_map/ppermute | solution.py:315
  16.9 6.9 %collective-permute-start.8 = (bf16[3,4,64,128]{3,2,1,0:T(8,128)(2,1)S(1)}, bf16[3,4,64,128]{3,2,1,0:T(8,128)(2,1)S(1)}, u32[]{:S(2)}, u32[]{:S(2)}) collective-permute-start(bf16[3,4,64,128]{3,2,1,0:T(8,128)(2,1)S(1)} %collective-permute-done.2.refs_3_), channel_id=1, source_target_pairs={{0,8},{8,0},{16,24},{24,16},{1,9},{9,1},{17,25},{25,17},{2,10},{10... | collective-permute-start | bytes 589832 | tf_op jit(solution)/shard_map/ppermute | solution.py:304
  17.1 5.4 %collective-permute-start.7 = (bf16[3,4,64,128]{3,2,1,0:T(8,128)(2,1)S(1)}, bf16[3,4,64,128]{3,2,1,0:T(8,128)(2,1)S(1)}, u32[]{:S(2)}, u32[]{:S(2)}) collective-permute-start(bf16[3,4,64,128]{3,2,1,0:T(8,128)(2,1)S(1)} %collective-permute-done.6.refs_4_), channel_id=1, source_target_pairs={{0,8},{8,0},{16,24},{24,16},{1,9},{9,1},{17,25},{25,17},{2,10},{10... | collective-permute-start | bytes 589832 | tf_op jit(solution)/shard_map/ppermute | solution.py:304
  17.5 6.3 %collective-permute-start.10 = (bf16[3,4,64,128]{3,2,1,0:T(8,128)(2,1)S(1)}, bf16[3,4,64,128]{3,2,1,0:T(8,128)(2,1)S(1)}, u32[]{:S(2)}, u32[]{:S(2)}) collective-permute-start(bf16[3,4,64,128]{3,2,1,0:T(8,128)(2,1)S(1)} %collective-permute-done.9.refs_5_), channel_id=1, source_target_pairs={{0,8},{8,0},{16,24},{24,16},{1,9},{9,1},{17,25},{25,17},{2,10},{10... | collective-permute-start | bytes 589832 | tf_op jit(solution)/shard_map/ppermute | solution.py:304
  20.9 1.6 %copy-start.1 = (bf16[12,2,256,256]{3,2,1,0:T(8,128)(2,1)}, bf16[12,2,256,256]{3,2,1,0:T(8,128)(2,1)S(1)}, u32[]{:S(2)}) copy-start(bf16[12,2,256,256]{3,2,1,0:T(8,128)(2,1)S(1)} %get-tuple-element.45) | copy-start | bytes 9437188
  33.6 2.3 %collective-permute-start.11 = (bf16[3,16,64,128]{3,2,1,0:T(8,128)(2,1)S(1)}, bf16[3,16,64,128]{3,2,1,0:T(8,128)(2,1)S(1)}, u32[]{:S(2)}, u32[]{:S(2)}) collective-permute-start(bf16[3,16,64,128]{3,2,1,0:T(8,128)(2,1)S(1)} %collective-permute-done.3.refs_1_), channel_id=1, source_target_pairs={{0,8},{8,0},{16,24},{24,16},{1,9},{9,1},{17,25},{25,17},{2,10},{10... | collective-permute-start | bytes 2359304 | tf_op jit(solution)/shard_map/ppermute | solution.py:304
  37.2 1.4 %collective-permute-start.12 = (f32[4,64,128]{2,1,0:T(8,128)S(1)}, f32[4,64,128]{2,1,0:T(8,128)S(1)}, u32[]{:S(2)}, u32[]{:S(2)}) collective-permute-start(f32[4,64,128]{2,1,0:T(8,128)S(1)} %get-tuple-element.54), channel_id=1, source_target_pairs={{0,8},{8,0},{16,24},{24,16},{1,9},{9,1},{17,25},{25,17},{2,10},{10... | collective-permute-start | bytes 393224 | tf_op jit(solution)/shard_map/ppermute | solution.py:304
  37.4 1.2 %collective-permute-start.13 = (f32[4,64,128]{2,1,0:T(8,128)S(1)}, f32[4,64,128]{2,1,0:T(8,128)S(1)}, u32[]{:S(2)}, u32[]{:S(2)}) collective-permute-start(f32[4,64,128]{2,1,0:T(8,128)S(1)} %get-tuple-element.56), channel_id=1, source_target_pairs={{8,16},{24,25},{17,9},{1,2},{10,18},{26,27},{19,11},{3,4},{12,20},... | collective-permute-start | bytes 393224 | tf_op jit(solution)/shard_map/ppermute | solution.py:315
  54.0 10.1 %collective-permute-start.15 = (f32[8,64,128]{2,1,0:T(8,128)S(1)}, f32[8,64,128]{2,1,0:T(8,128)S(1)}, u32[]{:S(2)}, u32[]{:S(2)}) collective-permute-start(f32[8,64,128]{2,1,0:T(8,128)S(1)} %shard_map.52.refs_3_), channel_id=1, source_target_pairs={{8,16},{24,25},{17,9},{1,2},{10,18},{26,27},{19,11},{3,4},{12,20},... | collective-permute-start | bytes 786440 | tf_op jit(solution)/shard_map/ppermute | solution.py:315
  54.7 10.6 %collective-permute-start.14 = (f32[8,64,128]{2,1,0:T(8,128)S(1)}, f32[8,64,128]{2,1,0:T(8,128)S(1)}, u32[]{:S(2)}, u32[]{:S(2)}) collective-permute-start(f32[8,64,128]{2,1,0:T(8,128)S(1)} %shard_map.52.refs_3_), channel_id=1, source_target_pairs={{0,8},{8,0},{16,24},{24,16},{1,9},{9,1},{17,25},{25,17},{2,10},{10... | collective-permute-start | bytes 786440 | tf_op jit(solution)/shard_map/ppermute | solution.py:304
  100.5 6.4 %collective-permute-start.17 = (f32[64,8,128]{2,1,0:T(8,128)S(1)}, f32[64,8,128]{2,1,0:T(8,128)S(1)}, u32[]{:S(2)}, u32[]{:S(2)}) collective-permute-start(f32[64,8,128]{2,1,0:T(8,128)S(1)} %bitcast.21), channel_id=1, source_target_pairs={{0,16},{8,24},{16,0},{24,8},{1,17},{9,25},{17,1},{25,9},{2,18},{10... | collective-permute-start | bytes 786440 | tf_op jit(solution)/shard_map/ppermute | solution.py:304
  100.6 6.4 %collective-permute-start.16 = (f32[64,8,128]{2,1,0:T(8,128)S(1)}, f32[64,8,128]{2,1,0:T(8,128)S(1)}, u32[]{:S(2)}, u32[]{:S(2)}) collective-permute-start(f32[64,8,128]{2,1,0:T(8,128)S(1)} %bitcast.22), channel_id=1, source_target_pairs={{0,8},{8,0},{16,24},{24,16},{1,9},{9,1},{17,25},{25,17},{2,10},{10... | collective-permute-start | bytes 786440 | tf_op jit(solution)/shard_map/ppermute | solution.py:304
  106.9 1.5 %collective-permute-start.18 = (f32[64,8,128]{2,1,0:T(8,128)S(1)}, f32[64,8,128]{2,1,0:T(8,128)S(1)}, u32[]{:S(2)}, u32[]{:S(2)}) collective-permute-start(f32[64,8,128]{2,1,0:T(8,128)S(1)} %collective-permute-done.17.refs_2_), channel_id=1, source_target_pairs={{0,8},{8,0},{16,24},{24,16},{1,9},{9,1},{17,25},{25,17},{2,10},{10... | collective-permute-start | bytes 786440 | tf_op jit(solution)/shard_map/ppermute | solution.py:304

commit v11 on v10

--- a/solution.py
+++ b/solution.py
@@ -175,7 +175,7 @@
 
 def update_kernel(paired, place_ref, taps_ref, lefts_ref, rights_ref, *refs):
     bricks_refs, (first_ref, own_ref, second_ref, out_ref) = refs[:2], refs[2:6]
-    volume, fields, flats, ratios, logs = refs[6:]
+    volume, ratios, held, logs = refs[6:]
     bricks = [ref.at[group] for ref in bricks_refs for group in range(ref.shape[0])]
     count = len(bricks)
     step = pl.program_id(0)
@@ -195,57 +195,45 @@
         for z in range(middle):
             volume[side + z] = own_ref[z]
 
-    def along_z(source, field, gains, length):
-        for k in range(0, rows, 16):
-            pair = []
-            for half in range(2):
-                column = [source[z, pl.ds(k + 8 * half, 8), :] for z in range(length + 2 * rim)]
-                sums = []
-                for z in range(length):
-                    total = column[z + rim]
-                    for t in range(taps):
-                        if t != rim:
-                            total = total + gains[t] * column[z + t]
-                    sums.append(total)
-                pair.append(sums)
-            for z in range(length):
-                high, low = halves(jnp.concatenate([pair[0][z], pair[1][z]], axis=0))
-                field[0, z, pl.ds(k, 16), :] = high
-                field[1, z, pl.ds(k, 16), :] = low
-
-    def along_x(field, flat, matrix, length):
-        for z in range(0, length, 2):
-            high, low = [jnp.concatenate([field[part, z], field[part, z + 1]], axis=1) for part in range(2)]
-            right = jnp.concatenate([high, low, high], axis=0)
-            high, low = halves(jnp.dot(matrix, right, preferred_element_type=jnp.float32))
-            for i in range(2):
-                at = pl.ds((z + i) * rows, rows)
-                flat[at, :width] = high[:, i * width : (i + 1) * width]
-                flat[at, width:] = low[:, i * width : (i + 1) * width]
-
-    def along_y(flat, matrix, length):
-        product = jnp.dot(flat[: length * rows, :], matrix, preferred_element_type=jnp.float32)
-        return (product[:, :width] + product[:, width:]).reshape(length, rows, width)
-
-    held = None
+    def along_z(source, gains, z):
+        tiles = []
+        for k in range(0, rows, 8):
+            column = [source[z + t, pl.ds(k, 8), :] for t in range(taps)]
+            total = column[rim]
+            for t in range(taps):
+                if t != rim:
+                    total = total + gains[t] * column[t]
+            tiles.append(total)
+        return jnp.concatenate(tiles, axis=0)
+
+    def chain(source, gains, left, right, z):
+        high, low = halves(jnp.concatenate([along_z(source, gains, z + i) for i in range(2)], axis=1))
+        stacked = jnp.concatenate([high, low, high], axis=0)
+        parts = halves(jnp.dot(left, stacked, preferred_element_type=jnp.float32))
+        flat = jnp.concatenate(
+            [jnp.concatenate([part[:, i * width : (i + 1) * width] for part in parts], axis=1) for i in range(2)], axis=0
+        )
+        product = jnp.dot(flat, right, preferred_element_type=jnp.float32)
+        total = product[:, :width] + product[:, width:]
+        return total[:rows], total[rows:]
+
     for group in range(count):
         view = group * pl.num_programs(0) + step
-        field, flat, ratio = (scratch.at[group % 2] for scratch in (fields, flats, ratios))
+        ratio = ratios.at[group % 2]
         gains = [taps_ref[view, 0, t] for t in range(taps)]
-        along_z(volume, field, gains, outer)
-        along_x(field, flat, lefts_ref[group, 0, 0], outer)
-        blurred = along_y(flat, rights_ref[group, 0, 0], outer)
-        for z in range(outer):
-            guess = pl.reciprocal(blurred[z], approx=True)
-            guess = guess * (2.0 - blurred[z] * guess)
-            ratio[z] = bricks[group][0, z].astype(jnp.float32) * guess
-        along_z(ratio, field, gains[::-1], planes)
-        along_x(field, flat, lefts_ref[group, 0, 1], planes)
-        total = along_y(flat, rights_ref[group, 0, 1], planes)
-        if group % 2 == 0:
-            held = total
-        else:
-            logs[...] += jnp.log(held * total)
+        for z in range(0, outer, 2):
+            pair = chain(volume, gains, lefts_ref[group, 0, 0], rights_ref[group, 0, 0], z)
+            for i, blurred in enumerate(pair):
+                guess = pl.reciprocal(blurred, approx=True)
+                guess = guess * (2.0 - blurred * guess)
+                ratio[z + i] = bricks[group][0, z + i].astype(jnp.float32) * guess
+        for z in range(0, planes, 2):
+            pair = chain(ratio, gains[::-1], lefts_ref[group, 0, 1], rights_ref[group, 0, 1], z)
+            for i, back in enumerate(pair):
+                if group % 2 == 0:
+                    held[z + i] = back
+                else:
+                    logs[z + i] += jnp.log(held[z + i] * back)
 
     @pl.when(step == pl.num_programs(0) - 1)
     def _():
@@ -269,9 +257,8 @@
         out_specs=VMEM,
         scratch_shapes=[
             pltpu.VMEM((2 * outer - planes, rows, width), jnp.float32),
-            pltpu.VMEM((2, 2, outer, rows, width), jnp.bfloat16),
-            pltpu.VMEM((2, outer * rows, 2 * width), jnp.bfloat16),
             pltpu.VMEM((2, outer, rows, width), jnp.float32),
+            pltpu.VMEM((planes, rows, width), jnp.float32),
             pltpu.VMEM((planes, rows, width), jnp.float32),
         ],
         compiler_params=PARAMS,
@@ -353,11 +340,9 @@
     far_bound, raw_later, cross_taps = lax.optimization_barrier((far_bound, raw_views, cross_taps))
     far_bound = far(far_bound)
     (far_inner,) = resample(place, weights, offsets, [raw_later], [(True, inner)])
+    far_inner = far(far_inner)
+    far_bound, raw_later = lax.optimization_barrier((far_bound, raw_later))
     own_bound, own_inner = resample(place, weights, offsets, [raw_later], [(False, bound), (False, inner)])
-    far_inner, far_bound, own_bound, own_inner = lax.optimization_barrier(
-        (far_inner, far_bound, own_bound, own_inner)
-    )
-    far_inner = far(far_inner)
     own_edge, far_edge = across(own_bound), across(far_bound)
     pair_taps = near(jnp.stack([psf_taps, cross_taps]))
     all_taps = jnp.concatenate([psf_taps, pair_taps[0], pair_taps[1], cross_taps])

time: 110 us -> 110 us (level)
  starting transfers between devices: 17.1 us -> 22.3 us
  waiting for transfers between devices: 24.6 us -> 20.6 us
  Pallas kernels: 42.6 us -> 40.1 us
    ppermute x15, starting transfers between devices: 14.4 us -> 19.7 us  [partner(): return lax.ppermute(value, 'view', [(i, i ^ bit) for i in range(members)])]
    ppermute x15, waiting for transfers between devices: 24.6 us -> 20.6 us  [partner(): return lax.ppermute(value, 'view', [(i, i ^ bit) for i in range(members)])]
    pallas_call x2, Pallas kernels: 30.7 us -> 28.2 us  [update(): pl.pallas_call(functools.partial(update_kernel, paired), grid=(count,), o...]
  transfers between devices with their start and end apart: 19 -> 19, of which waited for: 8 -> 7; matrix products, arithmetic and copies ran while one was open for 1% -> 1% of each run, Pallas kernels for 9% -> 9%
where the time goes in v11:
time: 110 us; the launch traced here: 109 us
  Pallas kernels  40.1 us (36%)
  starting transfers between devices  22.3 us (20%)
  blocking collectives  20.7 us (19%)
  waiting for transfers between devices  20.6 us (19%)
  local copies, waits for them, and re-layouts  4.89 us (4%)
    pallas_call x2, Pallas kernels, update(): pl.pallas_call(functools.partial(update_kernel, paired), grid=(count,), o...  28.2 us
    all_to_all x1, blocking collectives, per_device(): lax.all_to_all(joined, 'vol', split_axis=1, concat_axis=0, tiled=True)  20.7 us
    ppermute x15, waiting for transfers between devices, partner(): return lax.ppermute(value, 'view', [(i, i ^ bit) for i in range(members)])  20.6 us
    ppermute x15, starting transfers between devices, partner(): return lax.ppermute(value, 'view', [(i, i ^ bit) for i in range(members)])  19.7 us
    pallas_call x3, Pallas kernels, resample(): pl.pallas_call(functools.partial(resample_kernel, plan), grid=(views,), o...  5.13 us
    unnamed x8, local copies, waits for them, and re-layouts  3.75 us
    pallas_call x1, Pallas kernels, bands(): pl.pallas_call(bands_kernel, grid=(views,), out_shape=[jax.ShapeDtypeStru...  3.13 us
    ppermute x4, starting transfers between devices, swap(): return lax.ppermute(value, ('view', 'vol'), perm)  2.67 us
  transfers between devices with their start and end apart: 19, of which 7 were waited for; matrix products, arithmetic and copies ran while one was open for 1% of the time, Pallas kernels for 9%

profile of v11, /device:TPU:0, one launch (start us, length us, event | category | flops | bytes accessed | tf_op | source)
XLA Modules:
  0.0 109.2 jit_solution(121591009389379282)
XLA Ops:
  0.0 0.0 copy-start.3
  0.0 2.4 %collective-permute-start = (f32[3,3,9]{2,1,0:T(4,128)}, f32[3,3,9]{2,1,0:T(4,128)S(1)}, u32[]{:S(2)}, u32[]{:S(2)}) collective-permute-start(f32[3,3,9]{2,1,0:T(4,128)} %param.7), channel_id=1, source_target_pairs={{0,24},{8,16},{16,8},{24,0},{1,25},{9,17},{17,9},{25,1},{2,26},{10... | collective-permute-start | bytes 980 | tf_op jit(solution)/shard_map/ppermute | solution.py:291
  2.4 0.1 pad_add_fusion.place_ref
  2.5 0.7 broadcast_in_dim.2.offsets_ref
  3.1 0.0 copy-start
  3.1 1.4 %copy-done = bf16[3,32,64,128]{3,2,1,0:T(8,128)(2,1)S(1)} copy-done((bf16[3,32,64,128]{3,2,1,0:T(8,128)(2,1)S(1)}, bf16[3,32,64,128]{3,2,1,0:T(8,128)(2,1)}, u32[]{:S(2)}) %copy-start) | copy-done | bytes 1572888
  4.5 0.0 copy-start.2
  4.5 0.7 copy-done.2
  5.3 1.5 %shard_map.46 = bf16[3,4,64,128]{3,2,1,0:T(8,128)(2,1)S(1)} custom-call(s32[2]{0:T(128)S(1)} %pad_add_fusion.place_ref, f32[3,8,64]{2,1,0:T(8,128)S(1)} %bitcast.24, s32[3,1,64]{2,1,0:T(1,128)S(1)} %broadcast_in_dim.2.offsets_ref, bf16[3,32,64,128]{3,2,1,0:T(8,128)(2,1)S(1)} %copy-done), custom_call_target="tpu_custom_call" | custom-call | tf_op jit(solution)/shard_map/pallas_call | solution.py:60
  6.7 0.0 collective-permute-done
  6.7 0.6 collective-permute-start.3
  7.4 0.0 copy-done.3
  7.4 0.2 collective-permute-start.1
  7.6 1.8 %shard_map.47 = bf16[3,16,64,128]{3,2,1,0:T(8,128)(2,1)S(1)} custom-call(s32[2]{0:T(128)S(1)} %pad_add_fusion.place_ref, f32[3,8,64]{2,1,0:T(8,128)S(1)} %bitcast.25, s32[3,1,64]{2,1,0:T(1,128)S(1)} %broadcast_in_dim.2.offsets_ref, bf16[3,32,64,128]{3,2,1,0:T(8,128)(2,1)S(1)} %copy-done), custom_call_target="tpu_custom_call" | custom-call | tf_op jit(solution)/shard_map/pallas_call | solution.py:60
  9.4 1.8 %collective-permute-start.2 = (bf16[3,16,64,128]{3,2,1,0:T(8,128)(2,1)S(1)}, bf16[3,16,64,128]{3,2,1,0:T(8,128)(2,1)S(1)}, u32[]{:S(2)}, u32[]{:S(2)}) collective-permute-start(bf16[3,16,64,128]{3,2,1,0:T(8,128)(2,1)S(1)} %shard_map.47), channel_id=1, source_target_pairs={{0,16},{8,24},{16,0},{24,8},{1,17},{9,25},{17,1},{25,9},{2,18},{10... | collective-permute-start | bytes 2359304 | tf_op jit(solution)/shard_map/ppermute | solution.py:291
  11.2 3.4 %collective-permute-done.3.refs_3_ = bf16[3,4,64,128]{3,2,1,0:T(8,128)(2,1)S(1)} collective-permute-done((bf16[3,4,64,128]{3,2,1,0:T(8,128)(2,1)S(1)}, bf16[3,4,64,128]{3,2,1,0:T(8,128)(2,1)S(1)}, u32[]{:S(2)}, u32[]{:S(2)}) %collective-permute-start.3) | collective-permute-done | bytes 196640 | tf_op jit(solution)/shard_map/ppermute | solution.py:291
  14.6 1.9 %shard_map.49 = (bf16[3,4,64,128]{3,2,1,0:T(8,128)(2,1)S(1)}, bf16[3,16,64,128]{3,2,1,0:T(8,128)(2,1)S(1)}) custom-call(s32[2]{0:T(128)S(1)} %pad_add_fusion.place_ref, f32[3,8,64]{2,1,0:T(8,128)S(1)} %bitcast.26, s32[3,1,64]{2,1,0:T(1,128)S(1)} %broadcast_in_dim.2.offsets_ref, bf16[3,32,64,128]{3,2,1,0:T(8,128)(2,1)S(1)} %copy-done), custom_call_target="tpu_custom_call" | custom-call | tf_op jit(solution)/shard_map/pallas_call | solution.py:60
  16.5 0.1 collective-permute-start.4
  16.5 0.0 collective-permute-done.1
  16.6 0.1 fusion
  16.7 0.7 collective-permute-start.6
  17.3 0.5 collective-permute-start.5
  17.9 0.7 collective-permute-start.9
  18.6 0.1 broadcast_divide_fusion
  18.6 0.3 slice_reduce_fusion
  18.9 0.0 collective-permute-done.9.refs_5_
  18.9 0.1 collective-permute-start.8
  19.0 0.0 collective-permute-done.6.refs_4_
  19.0 0.5 collective-permute-start.10
  19.5 0.0 collective-permute-done.5.refs_3_
  19.5 0.1 collective-permute-start.7
  19.6 0.1 slice_divide_fusion
  19.7 3.1 %shard_map.48 = (bf16[12,2,64,192]{3,2,1,0:T(8,128)(2,1)S(1)}, bf16[12,2,256,256]{3,2,1,0:T(8,128)(2,1)S(1)}) custom-call(f32[12,3,9]{2,1,0:T(4,128)S(1)} %pad_maximum_fusion.1.taps_ref), custom_call_target="tpu_custom_call" | custom-call | tf_op jit(solution)/shard_map/pallas_call | solution.py:102
  22.8 0.0 copy-start.1
  22.8 1.6 %copy-done.1 = bf16[12,2,256,256]{3,2,1,0:T(8,128)(2,1)} copy-done((bf16[12,2,256,256]{3,2,1,0:T(8,128)(2,1)}, bf16[12,2,256,256]{3,2,1,0:T(8,128)(2,1)S(1)}, u32[]{:S(2)}) %copy-start.1) | copy-done | bytes 3145752
  24.5 0.0 collective-permute-done.7.refs_5_
  24.5 0.0 collective-permute-done.4.refs_1_
  24.5 1.3 %shard_map.50 = (bf16[2,3,16,64,128]{4,3,2,1,0:T(8,128)(2,1)S(1)}, f32[16,64,128]{2,1,0:T(8,128)S(1)}) custom-call(s32[2]{0:T(128)S(1)} %pad_add_fusion.place_ref, bf16[3,16,64,128]{3,2,1,0:T(8,128)(2,1)S(1)} %get-tuple-element.35.refs_0_, bf16[3,16,64,128]{3,2,1,0:T(8,128)(2,1)S(1)} %collective-permute-done.4.refs_1_, ...), custom_call_target="tpu_custom_call" | custom-call | tf_op jit(solution)/shard_map/pallas_call | solution.py:162
  25.7 0.0 collective-permute-done.8.refs_4_
  25.8 0.0 collective-permute-done.10.refs_6_
  25.8 5.4 %collective-permute-done.2.refs_1_ = bf16[3,16,64,128]{3,2,1,0:T(8,128)(2,1)S(1)} collective-permute-done((bf16[3,16,64,128]{3,2,1,0:T(8,128)(2,1)S(1)}, bf16[3,16,64,128]{3,2,1,0:T(8,128)(2,1)S(1)}, u32[]{:S(2)}, u32[]{:S(2)}) %collective-permute-start.2) | collective-permute-done | bytes 786464 | tf_op jit(solution)/shard_map/ppermute | solution.py:291
  31.1 0.0 collective-permute-start.11
  31.1 2.3 %collective-permute-done.11.refs_2_ = bf16[3,16,64,128]{3,2,1,0:T(8,128)(2,1)S(1)} collective-permute-done((bf16[3,16,64,128]{3,2,1,0:T(8,128)(2,1)S(1)}, bf16[3,16,64,128]{3,2,1,0:T(8,128)(2,1)S(1)}, u32[]{:S(2)}, u32[]{:S(2)}) %collective-permute-start.11) | collective-permute-done | bytes 786464 | tf_op jit(solution)/shard_map/ppermute | solution.py:291
  33.4 1.3 %shard_map.51 = (bf16[2,3,16,64,128]{4,3,2,1,0:T(8,128)(2,1)S(1)}, f32[16,64,128]{2,1,0:T(8,128)S(1)}, f32[4,64,128]{2,1,0:T(8,128)S(1)}, f32[4,64,128]{2,1,0:T(8,128)S(1)}) custom-call(s32[2]{0:T(128)S(1)} %pad_add_fusion.place_ref, f32[16,64,128]{2,1,0:T(8,128)S(1)} %get-tuple-element.43.refs_0_, ...), custom_call_target="tpu_custom_call" | custom-call | tf_op jit(solution)/shard_map/pallas_call | solution.py:162
  34.8 0.2 collective-permute-start.12
  35.0 0.7 collective-permute-start.13
  35.7 0.5 collective-permute-done.12.refs_2_
  36.2 0.0 collective-permute-done.13.refs_4_
  36.2 14.1 %shard_map.52.refs_3_ = f32[8,64,128]{2,1,0:T(8,128)S(1)} custom-call(s32[2]{0:T(128)S(1)} %pad_add_fusion.place_ref, f32[12,3,9]{2,1,0:T(4,128)S(1)} %pad_maximum_fusion.1.taps_ref, bf16[4,3,2,64,192]{4,3,2,1,0:T(8,128)(2,1)S(1)} %bitcast.19, bf16[4,3,2,256,256]{4,3,2,1,0:T(8,128)(2,1)} %bitcast.17, ...), custom_call_target="tpu_custom_call" | custom-call | tf_op jit(solution)/shard_map/pallas_call | solution.py:249
  50.3 0.7 collective-permute-start.15
  51.0 13.0 %collective-permute-start.14 = (f32[8,64,128]{2,1,0:T(8,128)S(1)}, f32[8,64,128]{2,1,0:T(8,128)S(1)}, u32[]{:S(2)}, u32[]{:S(2)}) collective-permute-start(f32[8,64,128]{2,1,0:T(8,128)S(1)} %shard_map.52.refs_3_), channel_id=1, source_target_pairs={{0,8},{8,0},{16,24},{24,16},{1,9},{9,1},{17,25},{25,17},{2,10},{10... | collective-permute-start | bytes 786440 | tf_op jit(solution)/shard_map/ppermute | solution.py:291
  64.0 0.0 collective-permute-done.15.refs_4_
  64.0 1.2 %collective-permute-done.14.refs_2_ = f32[8,64,128]{2,1,0:T(8,128)S(1)} collective-permute-done((f32[8,64,128]{2,1,0:T(8,128)S(1)}, f32[8,64,128]{2,1,0:T(8,128)S(1)}, u32[]{:S(2)}, u32[]{:S(2)}) %collective-permute-start.14) | collective-permute-done | bytes 262176 | tf_op jit(solution)/shard_map/ppermute | solution.py:291
  65.2 14.1 %shard_map.53 = f32[8,64,128]{2,1,0:T(8,128)S(1)} custom-call(s32[2]{0:T(128)S(1)} %pad_add_fusion.place_ref, f32[12,3,9]{2,1,0:T(4,128)S(1)} %pad_maximum_fusion.1.taps_ref, bf16[4,3,2,64,192]{4,3,2,1,0:T(8,128)(2,1)S(1)} %bitcast.20, bf16[4,3,2,256,256]{4,3,2,1,0:T(8,128)(2,1)} %bitcast.18, bf16[2,3,16,64,128]{4,3,2,1,0:T(8,128)(2,1)S(1)} %get-tuple-element.42.refs_0_, ...), custom_call_target="tpu_custom_call" | custom-call | tf_op jit(solution)/shard_map/pallas_call | solution.py:249
  79.3 0.2 copy.7
  79.5 20.7 %all_to_all.18 = f32[8,64,128]{2,0,1:T(8,128)S(1)} all-to-all(f32[8,64,128]{2,0,1:T(8,128)S(1)} %copy.7), channel_id=1, replica_groups=mesh['view'=4,'vol'=8] {'vol'}, dimensions={1} | all-to-all | bytes 524288 | tf_op jit(solution)/shard_map/all_to_all | solution.py:379
  100.2 0.1 collective-permute-start.17
  100.3 0.1 collective-permute-start.16
  100.4 6.3 %collective-permute-done.17.refs_2_ = f32[64,8,128]{2,1,0:T(8,128)S(1)} collective-permute-done((f32[64,8,128]{2,1,0:T(8,128)S(1)}, f32[64,8,128]{2,1,0:T(8,128)S(1)}, u32[]{:S(2)}, u32[]{:S(2)}) %collective-permute-start.17) | collective-permute-done | bytes 262176 | tf_op jit(solution)/shard_map/ppermute | solution.py:291
  106.6 0.0 collective-permute-start.18
  106.6 0.0 collective-permute-done.16.refs_1_
  106.6 1.5 %collective-permute-done.18.refs_3_ = f32[64,8,128]{2,1,0:T(8,128)S(1)} collective-permute-done((f32[64,8,128]{2,1,0:T(8,128)S(1)}, f32[64,8,128]{2,1,0:T(8,128)S(1)}, u32[]{:S(2)}, u32[]{:S(2)}) %collective-permute-start.18) | collective-permute-done | bytes 262176 | tf_op jit(solution)/shard_map/ppermute | solution.py:291
  108.2 1.0 shard_map.54
  (4 shorter events, 0.1 us)
Async XLA Ops:
  0.0 7.4 %copy-start.3 = (f32[3,3,9]{2,1,0:T(4,128)S(1)}, f32[3,3,9]{2,1,0:T(4,128)}, u32[]{:S(2)}) copy-start(f32[3,3,9]{2,1,0:T(4,128)} %param.7) | copy-start | bytes 976
  0.0 6.7 %collective-permute-start = (f32[3,3,9]{2,1,0:T(4,128)}, f32[3,3,9]{2,1,0:T(4,128)S(1)}, u32[]{:S(2)}, u32[]{:S(2)}) collective-permute-start(f32[3,3,9]{2,1,0:T(4,128)} %param.7), channel_id=1, source_target_pairs={{0,24},{8,16},{16,8},{24,0},{1,25},{9,17},{17,9},{25,1},{2,26},{10... | collective-permute-start | bytes 980 | tf_op jit(solution)/shard_map/ppermute | solution.py:291
  3.1 1.4 %copy-start = (bf16[3,32,64,128]{3,2,1,0:T(8,128)(2,1)S(1)}, bf16[3,32,64,128]{3,2,1,0:T(8,128)(2,1)}, u32[]{:S(2)}) copy-start(bf16[3,32,64,128]{3,2,1,0:T(8,128)(2,1)} %refs_0_.3) | copy-start | bytes 4718596
  4.5 0.7 copy-start.2
  6.7 7.8 %collective-permute-start.3 = (bf16[3,4,64,128]{3,2,1,0:T(8,128)(2,1)S(1)}, bf16[3,4,64,128]{3,2,1,0:T(8,128)(2,1)S(1)}, u32[]{:S(2)}, u32[]{:S(2)}) collective-permute-start(bf16[3,4,64,128]{3,2,1,0:T(8,128)(2,1)S(1)} %shard_map.46), channel_id=1, source_target_pairs={{0,16},{8,24},{16,0},{24,8},{1,17},{9,25},{17,1},{25,9},{2,18},{10... | collective-permute-start | bytes 589832 | tf_op jit(solution)/shard_map/ppermute | solution.py:291
  7.4 9.2 %collective-permute-start.1 = (f32[2,3,3,9]{3,2,1,0:T(4,128)S(1)}, f32[2,3,3,9]{3,2,1,0:T(4,128)S(1)}, u32[]{:S(2)}, u32[]{:S(2)}) collective-permute-start(f32[2,3,3,9]{3,2,1,0:T(4,128)S(1)} %pad_maximum_fusion.2), channel_id=1, source_target_pairs={{0,8},{8,0},{16,24},{24,16},{1,9},{9,1},{17,25},{25,17},{2,10},{10... | collective-permute-start | bytes 1952 | tf_op jit(solution)/shard_map/ppermute | solution.py:291
  9.4 21.8 %collective-permute-start.2 = (bf16[3,16,64,128]{3,2,1,0:T(8,128)(2,1)S(1)}, bf16[3,16,64,128]{3,2,1,0:T(8,128)(2,1)S(1)}, u32[]{:S(2)}, u32[]{:S(2)}) collective-permute-start(bf16[3,16,64,128]{3,2,1,0:T(8,128)(2,1)S(1)} %shard_map.47), channel_id=1, source_target_pairs={{0,16},{8,24},{16,0},{24,8},{1,17},{9,25},{17,1},{25,9},{2,18},{10... | collective-permute-start | bytes 2359304 | tf_op jit(solution)/shard_map/ppermute | solution.py:291
  16.5 8.0 %collective-permute-start.4 = (bf16[3,16,64,128]{3,2,1,0:T(8,128)(2,1)S(1)}, bf16[3,16,64,128]{3,2,1,0:T(8,128)(2,1)S(1)}, u32[]{:S(2)}, u32[]{:S(2)}) collective-permute-start(bf16[3,16,64,128]{3,2,1,0:T(8,128)(2,1)S(1)} %get-tuple-element.35.refs_0_), channel_id=1, source_target_pairs={{0,8},{8,0},{16,24},{24,16},{1,9},{9,1},{17,25},{25,17},{2,10},{10... | collective-permute-start | bytes 2359304 | tf_op jit(solution)/shard_map/ppermute | solution.py:291
  16.7 2.3 %collective-permute-start.6 = (bf16[3,4,64,128]{3,2,1,0:T(8,128)(2,1)S(1)}, bf16[3,4,64,128]{3,2,1,0:T(8,128)(2,1)S(1)}, u32[]{:S(2)}, u32[]{:S(2)}) collective-permute-start(bf16[3,4,64,128]{3,2,1,0:T(8,128)(2,1)S(1)} %get-tuple-element.36.refs_2_), channel_id=1, source_target_pairs={{24,25},{16,17},{1,2},{9,10},{26,27},{18,19},{3,4},{11,12},{28,29}... | collective-permute-start | bytes 589832 | tf_op jit(solution)/shard_map/ppermute | solution.py:302
  17.3 2.1 %collective-permute-start.5 = (bf16[3,4,64,128]{3,2,1,0:T(8,128)(2,1)S(1)}, bf16[3,4,64,128]{3,2,1,0:T(8,128)(2,1)S(1)}, u32[]{:S(2)}, u32[]{:S(2)}) collective-permute-start(bf16[3,4,64,128]{3,2,1,0:T(8,128)(2,1)S(1)} %get-tuple-element.36.refs_2_), channel_id=1, source_target_pairs={{0,8},{8,0},{16,24},{24,16},{1,9},{9,1},{17,25},{25,17},{2,10},{10... | collective-permute-start | bytes 589832 | tf_op jit(solution)/shard_map/ppermute | solution.py:291
  17.9 1.0 collective-permute-start.9
  18.9 6.8 %collective-permute-start.8 = (bf16[3,4,64,128]{3,2,1,0:T(8,128)(2,1)S(1)}, bf16[3,4,64,128]{3,2,1,0:T(8,128)(2,1)S(1)}, u32[]{:S(2)}, u32[]{:S(2)}) collective-permute-start(bf16[3,4,64,128]{3,2,1,0:T(8,128)(2,1)S(1)} %collective-permute-done.3.refs_3_), channel_id=1, source_target_pairs={{0,8},{8,0},{16,24},{24,16},{1,9},{9,1},{17,25},{25,17},{2,10},{10... | collective-permute-start | bytes 589832 | tf_op jit(solution)/shard_map/ppermute | solution.py:291
  19.0 6.8 %collective-permute-start.10 = (bf16[3,4,64,128]{3,2,1,0:T(8,128)(2,1)S(1)}, bf16[3,4,64,128]{3,2,1,0:T(8,128)(2,1)S(1)}, u32[]{:S(2)}, u32[]{:S(2)}) collective-permute-start(bf16[3,4,64,128]{3,2,1,0:T(8,128)(2,1)S(1)} %collective-permute-done.9.refs_5_), channel_id=1, source_target_pairs={{0,8},{8,0},{16,24},{24,16},{1,9},{9,1},{17,25},{25,17},{2,10},{10... | collective-permute-start | bytes 589832 | tf_op jit(solution)/shard_map/ppermute | solution.py:291
  19.5 5.0 %collective-permute-start.7 = (bf16[3,4,64,128]{3,2,1,0:T(8,128)(2,1)S(1)}, bf16[3,4,64,128]{3,2,1,0:T(8,128)(2,1)S(1)}, u32[]{:S(2)}, u32[]{:S(2)}) collective-permute-start(bf16[3,4,64,128]{3,2,1,0:T(8,128)(2,1)S(1)} %collective-permute-done.6.refs_4_), channel_id=1, source_target_pairs={{0,8},{8,0},{16,24},{24,16},{1,9},{9,1},{17,25},{25,17},{2,10},{10... | collective-permute-start | bytes 589832 | tf_op jit(solution)/shard_map/ppermute | solution.py:291
  22.8 1.6 %copy-start.1 = (bf16[12,2,256,256]{3,2,1,0:T(8,128)(2,1)}, bf16[12,2,256,256]{3,2,1,0:T(8,128)(2,1)S(1)}, u32[]{:S(2)}) copy-start(bf16[12,2,256,256]{3,2,1,0:T(8,128)(2,1)S(1)} %get-tuple-element.41) | copy-start | bytes 9437188
  31.1 2.3 %collective-permute-start.11 = (bf16[3,16,64,128]{3,2,1,0:T(8,128)(2,1)S(1)}, bf16[3,16,64,128]{3,2,1,0:T(8,128)(2,1)S(1)}, u32[]{:S(2)}, u32[]{:S(2)}) collective-permute-start(bf16[3,16,64,128]{3,2,1,0:T(8,128)(2,1)S(1)} %collective-permute-done.2.refs_1_), channel_id=1, source_target_pairs={{0,8},{8,0},{16,24},{24,16},{1,9},{9,1},{17,25},{25,17},{2,10},{10... | collective-permute-start | bytes 2359304 | tf_op jit(solution)/shard_map/ppermute | solution.py:291
  34.8 1.4 %collective-permute-start.12 = (f32[4,64,128]{2,1,0:T(8,128)S(1)}, f32[4,64,128]{2,1,0:T(8,128)S(1)}, u32[]{:S(2)}, u32[]{:S(2)}) collective-permute-start(f32[4,64,128]{2,1,0:T(8,128)S(1)} %get-tuple-element.50), channel_id=1, source_target_pairs={{0,8},{8,0},{16,24},{24,16},{1,9},{9,1},{17,25},{25,17},{2,10},{10... | collective-permute-start | bytes 393224 | tf_op jit(solution)/shard_map/ppermute | solution.py:291
  35.0 1.2 %collective-permute-start.13 = (f32[4,64,128]{2,1,0:T(8,128)S(1)}, f32[4,64,128]{2,1,0:T(8,128)S(1)}, u32[]{:S(2)}, u32[]{:S(2)}) collective-permute-start(f32[4,64,128]{2,1,0:T(8,128)S(1)} %get-tuple-element.52), channel_id=1, source_target_pairs={{8,16},{24,25},{17,9},{1,2},{10,18},{26,27},{19,11},{3,4},{12,20},... | collective-permute-start | bytes 393224 | tf_op jit(solution)/shard_map/ppermute | solution.py:302
  50.3 13.7 %collective-permute-start.15 = (f32[8,64,128]{2,1,0:T(8,128)S(1)}, f32[8,64,128]{2,1,0:T(8,128)S(1)}, u32[]{:S(2)}, u32[]{:S(2)}) collective-permute-start(f32[8,64,128]{2,1,0:T(8,128)S(1)} %shard_map.52.refs_3_), channel_id=1, source_target_pairs={{8,16},{24,25},{17,9},{1,2},{10,18},{26,27},{19,11},{3,4},{12,20},... | collective-permute-start | bytes 786440 | tf_op jit(solution)/shard_map/ppermute | solution.py:302
  51.0 14.2 %collective-permute-start.14 = (f32[8,64,128]{2,1,0:T(8,128)S(1)}, f32[8,64,128]{2,1,0:T(8,128)S(1)}, u32[]{:S(2)}, u32[]{:S(2)}) collective-permute-start(f32[8,64,128]{2,1,0:T(8,128)S(1)} %shard_map.52.refs_3_), channel_id=1, source_target_pairs={{0,8},{8,0},{16,24},{24,16},{1,9},{9,1},{17,25},{25,17},{2,10},{10... | collective-permute-start | bytes 786440 | tf_op jit(solution)/shard_map/ppermute | solution.py:291
  100.2 6.4 %collective-permute-start.17 = (f32[64,8,128]{2,1,0:T(8,128)S(1)}, f32[64,8,128]{2,1,0:T(8,128)S(1)}, u32[]{:S(2)}, u32[]{:S(2)}) collective-permute-start(f32[64,8,128]{2,1,0:T(8,128)S(1)} %bitcast.21), channel_id=1, source_target_pairs={{0,16},{8,24},{16,0},{24,8},{1,17},{9,25},{17,1},{25,9},{2,18},{10... | collective-permute-start | bytes 786440 | tf_op jit(solution)/shard_map/ppermute | solution.py:291
  100.3 6.4 %collective-permute-start.16 = (f32[64,8,128]{2,1,0:T(8,128)S(1)}, f32[64,8,128]{2,1,0:T(8,128)S(1)}, u32[]{:S(2)}, u32[]{:S(2)}) collective-permute-start(f32[64,8,128]{2,1,0:T(8,128)S(1)} %bitcast.22), channel_id=1, source_target_pairs={{0,8},{8,0},{16,24},{24,16},{1,9},{9,1},{17,25},{25,17},{2,10},{10... | collective-permute-start | bytes 786440 | tf_op jit(solution)/shard_map/ppermute | solution.py:291
  106.6 1.5 %collective-permute-start.18 = (f32[64,8,128]{2,1,0:T(8,128)S(1)}, f32[64,8,128]{2,1,0:T(8,128)S(1)}, u32[]{:S(2)}, u32[]{:S(2)}) collective-permute-start(f32[64,8,128]{2,1,0:T(8,128)S(1)} %collective-permute-done.17.refs_2_), channel_id=1, source_target_pairs={{0,8},{8,0},{16,24},{24,16},{1,9},{9,1},{17,25},{25,17},{2,10},{10... | collective-permute-start | bytes 786440 | tf_op jit(solution)/shard_map/ppermute | solution.py:291

commit v12 on v11

--- a/solution.py
+++ b/solution.py
@@ -75,7 +75,7 @@
 def bands_kernel(taps_ref, left_ref, right_ref):
     view = pl.program_id(0)
     count = taps_ref.shape[2]
-    rows, width = left_ref.shape[2], right_ref.shape[2] // 2
+    rows, width = left_ref.shape[2], right_ref.shape[2]
 
     def band(size, axis, way):
         shape = (size, size)
@@ -89,16 +89,12 @@
     for way in range(2):
         high, low = band(rows, 1, 1 - way)
         left_ref[0, way] = jnp.concatenate([high, high, low], axis=1)
-        high, low = band(width, 2, way)
-        right_ref[0, way, :width, :width] = high
-        right_ref[0, way, width:, :width] = high
-        right_ref[0, way, :width, width:] = low
-        right_ref[0, way, width:, width:] = jnp.zeros_like(low)
+        right_ref[0, way] = jnp.concatenate(band(width, 2, way), axis=1)
 
 
 def bands(taps, rows, width):
     views = taps.shape[0]
-    shapes = [(2, rows, 3 * rows), (2, 2 * width, 2 * width)]
+    shapes = [(2, rows, 3 * rows), (2, width, 2 * width)]
     return pl.pallas_call(
         bands_kernel,
         grid=(views,),
@@ -151,10 +147,11 @@
                 cross_ref[z] = start_ref[downward + (upward - downward) * core]
 
 
-def gather_views(place, inner, bound, edge, planes, views=None, partial=None):
+def gather_views(place, inner, bound, edge, planes, side, views=None, partial=None):
     groups = len(inner)
     count, main, rows, width = inner[0].shape
     rim = edge[0].shape[1]
+    take = lambda part: 0 if part.shape[0] == count else side * count
     outer = planes + 2 * rim
     field = lambda depth: jax.ShapeDtypeStruct((depth, rows, width), jnp.float32)
     sends = [] if views is None else [field(rim), field(rim)]
@@ -165,7 +162,7 @@
         out_shape=[jax.ShapeDtypeStruct((groups, count, outer, rows, width), jnp.bfloat16), field(outer)] + sends,
         in_specs=[SMEM]
         + ([] if partial is None else [VMEM])
-        + [pl.BlockSpec((1,) + part.shape[1:], lambda v: (v, 0, 0, 0)) for part in parts],
+        + [pl.BlockSpec((1,) + part.shape[1:], lambda v, base=take(part): (v + base, 0, 0, 0)) for part in parts],
         out_specs=[pl.BlockSpec((groups, 1, outer, rows, width), lambda v: (0, v, 0, 0, 0))]
         + [VMEM] * (1 + len(sends)),
         scratch_shapes=[pltpu.VMEM((groups, main + 2 * rim, rows, width), jnp.bfloat16)],
@@ -195,41 +192,51 @@
         for z in range(middle):
             volume[side + z] = own_ref[z]
 
-    def along_z(source, gains, z):
-        tiles = []
+    def along_z(source, gains, z, length):
+        sums = [[] for _ in range(length)]
         for k in range(0, rows, 8):
-            column = [source[z + t, pl.ds(k, 8), :] for t in range(taps)]
-            total = column[rim]
-            for t in range(taps):
-                if t != rim:
-                    total = total + gains[t] * column[t]
-            tiles.append(total)
-        return jnp.concatenate(tiles, axis=0)
-
-    def chain(source, gains, left, right, z):
-        high, low = halves(jnp.concatenate([along_z(source, gains, z + i) for i in range(2)], axis=1))
-        stacked = jnp.concatenate([high, low, high], axis=0)
-        parts = halves(jnp.dot(left, stacked, preferred_element_type=jnp.float32))
-        flat = jnp.concatenate(
-            [jnp.concatenate([part[:, i * width : (i + 1) * width] for part in parts], axis=1) for i in range(2)], axis=0
+            column = [source[z + t, pl.ds(k, 8), :] for t in range(length + 2 * rim)]
+            for i in range(length):
+                total = column[i + rim]
+                for t in range(taps):
+                    if t != rim:
+                        total = total + gains[t] * column[i + t]
+                sums[i].append(total)
+        return [jnp.concatenate(tiles, axis=0) for tiles in sums]
+
+    def chain(source, gains, left, right, z, length):
+        fields = along_z(source, gains, z, length)
+        flats = []
+        for i in range(0, length, 2):
+            high, low = halves(jnp.concatenate(fields[i : i + 2], axis=1))
+            stacked = jnp.concatenate([high, low, high], axis=0)
+            parts = halves(jnp.dot(left, stacked, preferred_element_type=jnp.float32))
+            for j in range(2):
+                flats.append(jnp.concatenate([part[:, j * width : (j + 1) * width] for part in parts], axis=1))
+        right = jnp.concatenate(
+            [right, jnp.concatenate([right[:, :width], jnp.zeros((width, width), jnp.bfloat16)], axis=1)], axis=0
         )
-        product = jnp.dot(flat, right, preferred_element_type=jnp.float32)
+        product = jnp.dot(jnp.concatenate(flats, axis=0), right, preferred_element_type=jnp.float32)
         total = product[:, :width] + product[:, width:]
-        return total[:rows], total[rows:]
+        return [total[i * rows : (i + 1) * rows] for i in range(length)]
+
+    def chunks(length):
+        size = 2 if length % 4 else 4
+        return [(z, size) for z in range(0, length, size)]
 
     for group in range(count):
         view = group * pl.num_programs(0) + step
         ratio = ratios.at[group % 2]
         gains = [taps_ref[view, 0, t] for t in range(taps)]
-        for z in range(0, outer, 2):
-            pair = chain(volume, gains, lefts_ref[group, 0, 0], rights_ref[group, 0, 0], z)
-            for i, blurred in enumerate(pair):
+        for z, size in chunks(outer):
+            fields = chain(volume, gains, lefts_ref[group, 0, 0], rights_ref[group, 0, 0], z, size)
+            for i, blurred in enumerate(fields):
                 guess = pl.reciprocal(blurred, approx=True)
                 guess = guess * (2.0 - blurred * guess)
                 ratio[z + i] = bricks[group][0, z + i].astype(jnp.float32) * guess
-        for z in range(0, planes, 2):
-            pair = chain(ratio, gains[::-1], lefts_ref[group, 0, 1], rights_ref[group, 0, 1], z)
-            for i, back in enumerate(pair):
+        for z, size in chunks(planes):
+            fields = chain(ratio, gains[::-1], lefts_ref[group, 0, 1], rights_ref[group, 0, 1], z, size)
+            for i, back in enumerate(fields):
                 if group % 2 == 0:
                     held[z + i] = back
                 else:
@@ -339,26 +346,25 @@
     (far_bound,) = resample(place, weights, offsets, [raw_views], [(True, bound)])
     far_bound, raw_later, cross_taps = lax.optimization_barrier((far_bound, raw_views, cross_taps))
     far_bound = far(far_bound)
-    (far_inner,) = resample(place, weights, offsets, [raw_later], [(True, inner)])
+    far_inner, own_bound, own_inner = resample(
+        place, weights, offsets, [raw_later], [(True, inner), (False, bound), (False, inner)]
+    )
     far_inner = far(far_inner)
-    far_bound, raw_later = lax.optimization_barrier((far_bound, raw_later))
-    own_bound, own_inner = resample(place, weights, offsets, [raw_later], [(False, bound), (False, inner)])
-    own_edge, far_edge = across(own_bound), across(far_bound)
+    near_inner = near(own_inner)
     pair_taps = near(jnp.stack([psf_taps, cross_taps]))
     all_taps = jnp.concatenate([psf_taps, pair_taps[0], pair_taps[1], cross_taps])
     all_taps = all_taps / jnp.sum(all_taps, axis=-1, keepdims=True)
     centre = all_taps[:, :1, rim : rim + 1]
     all_taps = jnp.concatenate([all_taps[:, :1] / centre, all_taps[:, 1:2], all_taps[:, 2:] * centre], axis=1)
     band = bands(all_taps, rows, width)
-    home, partial = gather_views(
-        place, [own_inner, near(own_inner)], [own_bound, near(own_bound)], [own_edge, near(own_edge)], planes
-    )
-    far_bounds, far_edges = [far_bound, near(far_bound)], [far_edge, near(far_edge)]
-    far_inner, band, home, partial, far_bounds, far_edges = lax.optimization_barrier(
-        (far_inner, band, home, partial, far_bounds, far_edges)
-    )
+    bounds = jnp.concatenate([own_bound, far_bound])
+    edges = across(bounds)
+    edges, band = lax.optimization_barrier((edges, band))
+    bounds, edges = [bounds, near(bounds)], [edges, near(edges)]
+    home, partial = gather_views(place, [own_inner, near_inner], bounds, edges, planes, 0)
+    far_inner, home, partial = lax.optimization_barrier((far_inner, home, partial))
     away, start, near_send, cross_send = gather_views(
-        place, [far_inner, near(far_inner)], far_bounds, far_edges, planes, members * views, partial
+        place, [far_inner, near(far_inner)], bounds, edges, planes, 1, members * views, partial
     )
     bricks = [home, away]
     lines = members * blocks

time: 110 us -> 99.8 us (0.907)
  starting transfers between devices: 22.3 us -> 14.9 us
  Pallas kernels: 40.1 us -> 35 us
  waiting for transfers between devices: 20.6 us -> 24.6 us
    ppermute x15 -> x13, starting transfers between devices: 19.7 us -> 12.9 us  [partner(): return lax.ppermute(value, 'view', [(i, i ^ bit) for i in range(members)])]
    pallas_call x2, Pallas kernels: 28.2 us -> 24.2 us  [update(): pl.pallas_call(functools.partial(update_kernel, paired), grid=(count,), o...]
    ppermute x15 -> x13, waiting for transfers between devices: 20.6 us -> 24.6 us  [partner(): return lax.ppermute(value, 'view', [(i, i ^ bit) for i in range(members)])]
    pallas_call x3 -> x2, Pallas kernels: 5.13 us -> 3.81 us  [resample(): pl.pallas_call(functools.partial(resample_kernel, plan), grid=(views,), o...]
    ppermute x4 -> x3, starting transfers between devices: 2.67 us -> 2.02 us  [swap(): return lax.ppermute(value, ('view', 'vol'), perm)]
    unnamed x8 -> x9, local copies, waits for them, and re-layouts: 3.75 us -> 3.3 us
  transfers between devices with their start and end apart: 19 -> 16, of which waited for: 7 -> 9; matrix products, arithmetic and copies ran while one was open for 1% -> 1% of each run, Pallas kernels for 9% -> 8%
where the time goes in v12:
time: 99.8 us; the launch traced here: 99.4 us
  Pallas kernels  35 us (35%)
  waiting for transfers between devices  24.6 us (25%)
  blocking collectives  19.9 us (20%)
  starting transfers between devices  14.9 us (15%)
  local copies, waits for them, and re-layouts  4.47 us (4%)
    ppermute x13, waiting for transfers between devices, partner(): return lax.ppermute(value, 'view', [(i, i ^ bit) for i in range(members)])  24.6 us
    pallas_call x2, Pallas kernels, update(): pl.pallas_call(functools.partial(update_kernel, paired), grid=(count,), o...  24.2 us
    all_to_all x1, blocking collectives, per_device(): lax.all_to_all(joined, 'vol', split_axis=1, concat_axis=0, tiled=True)  19.9 us
    ppermute x13, starting transfers between devices, partner(): return lax.ppermute(value, 'view', [(i, i ^ bit) for i in range(members)])  12.9 us
    pallas_call x2, Pallas kernels, resample(): pl.pallas_call(functools.partial(resample_kernel, plan), grid=(views,), o...  3.81 us
    pallas_call x1, Pallas kernels, bands(): pl.pallas_call(bands_kernel, grid=(views,), out_shape=[jax.ShapeDtypeStru...  3.34 us
    unnamed x9, local copies, waits for them, and re-layouts  3.3 us
    pallas_call x2, Pallas kernels, gather_views(): pl.pallas_call(functools.partial(gather_kernel, views, planes, rim), grid...  2.6 us
  transfers between devices with their start and end apart: 16, of which 9 were waited for; matrix products, arithmetic and copies ran while one was open for 1% of the time, Pallas kernels for 8%

profile of v12, /device:TPU:0, one launch (start us, length us, event | category | flops | bytes accessed | tf_op | source)
XLA Modules:
  0.0 99.4 jit_solution(96787653422935847)
XLA Ops:
  0.0 0.0 copy-start.3
  0.0 2.4 %collective-permute-start = (f32[3,3,9]{2,1,0:T(4,128)}, f32[3,3,9]{2,1,0:T(4,128)S(1)}, u32[]{:S(2)}, u32[]{:S(2)}) collective-permute-start(f32[3,3,9]{2,1,0:T(4,128)} %param.7), channel_id=1, source_target_pairs={{0,24},{8,16},{16,8},{24,0},{1,25},{9,17},{17,9},{25,1},{2,26},{10... | collective-permute-start | bytes 980 | tf_op jit(solution)/shard_map/ppermute | solution.py:298
  2.4 0.1 pad_add_fusion.place_ref
  2.5 0.7 broadcast_in_dim.2.offsets_ref
  3.1 0.0 copy-start
  3.1 1.4 %copy-done = bf16[3,32,64,128]{3,2,1,0:T(8,128)(2,1)S(1)} copy-done((bf16[3,32,64,128]{3,2,1,0:T(8,128)(2,1)S(1)}, bf16[3,32,64,128]{3,2,1,0:T(8,128)(2,1)}, u32[]{:S(2)}) %copy-start) | copy-done | bytes 1572888
  4.5 0.0 copy-start.2
  4.5 0.7 copy-done.2
  5.3 1.5 %shard_map.46 = bf16[3,4,64,128]{3,2,1,0:T(8,128)(2,1)S(1)} custom-call(s32[2]{0:T(128)S(1)} %pad_add_fusion.place_ref, f32[3,8,64]{2,1,0:T(8,128)S(1)} %bitcast.24, s32[3,1,64]{2,1,0:T(1,128)S(1)} %broadcast_in_dim.2.offsets_ref, bf16[3,32,64,128]{3,2,1,0:T(8,128)(2,1)S(1)} %copy-done), custom_call_target="tpu_custom_call" | custom-call | tf_op jit(solution)/shard_map/pallas_call | solution.py:60
  6.7 0.0 collective-permute-done
  6.7 0.0 copy-done.3
  6.8 0.7 collective-permute-start.1
  7.5 0.0 collective-permute-start.2
  7.5 2.3 %shard_map.47 = (bf16[3,16,64,128]{3,2,1,0:T(8,128)(2,1)S(1)}, bf16[3,4,64,128]{3,2,1,0:T(8,128)(2,1)S(1)}, bf16[3,16,64,128]{3,2,1,0:T(8,128)(2,1)S(1)}) custom-call(s32[2]{0:T(128)S(1)} %pad_add_fusion.place_ref, f32[3,8,64]{2,1,0:T(8,128)S(1)} %bitcast.25, s32[3,1,64]{2,1,0:T(1,128)S(1)} %broadcast_in_dim.2.offsets_ref, bf16[3,32,64,128]{3,2,1,0:T(8,128)(2,1)S(1)} %copy-done), custom_call_target="tpu_custom_call" | custom-call | tf_op jit(solution)/shard_map/pallas_call | solution.py:60
  9.9 2.1 %collective-permute-start.4 = (bf16[3,16,64,128]{3,2,1,0:T(8,128)(2,1)S(1)}, bf16[3,16,64,128]{3,2,1,0:T(8,128)(2,1)S(1)}, u32[]{:S(2)}, u32[]{:S(2)}) collective-permute-start(bf16[3,16,64,128]{3,2,1,0:T(8,128)(2,1)S(1)} %get-tuple-element.33), channel_id=1, source_target_pairs={{0,16},{8,24},{16,0},{24,8},{1,17},{9,25},{17,1},{25,9},{2,18},{10... | collective-permute-start | bytes 2359304 | tf_op jit(solution)/shard_map/ppermute | solution.py:298
  12.0 0.0 collective-permute-start.5
  12.0 0.0 collective-permute-done.1
  12.0 0.1 fusion
  12.1 0.1 broadcast_divide_fusion
  12.2 3.1 %collective-permute-done.2 = bf16[3,4,64,128]{3,2,1,0:T(8,128)(2,1)S(1)} collective-permute-done((bf16[3,4,64,128]{3,2,1,0:T(8,128)(2,1)S(1)}, bf16[3,4,64,128]{3,2,1,0:T(8,128)(2,1)S(1)}, u32[]{:S(2)}, u32[]{:S(2)}) %collective-permute-start.2) | collective-permute-done | bytes 196640 | tf_op jit(solution)/shard_map/ppermute | solution.py:298
  15.3 0.7 collective-permute-start.3
  16.0 0.3 slice_reduce_fusion
  16.2 0.1 slice_divide_fusion
  16.4 3.3 %shard_map.48 = (bf16[12,2,64,192]{3,2,1,0:T(8,128)(2,1)S(1)}, bf16[12,2,128,256]{3,2,1,0:T(8,128)(2,1)S(1)}) custom-call(f32[12,3,9]{2,1,0:T(4,128)S(1)} %pad_maximum_fusion.1.taps_ref), custom_call_target="tpu_custom_call" | custom-call | tf_op jit(solution)/shard_map/pallas_call | solution.py:98
  19.7 0.1 collective-permute-start.6
  19.8 0.0 collective-permute-done.3.refs_4_.refs_5_
  19.8 0.5 collective-permute-start.7
  20.3 1.2 %collective-permute-done.6.refs_3_.refs_4_ = bf16[6,4,64,128]{3,2,1,0:T(8,128)(2,1)S(1)} collective-permute-done((bf16[6,4,64,128]{3,2,1,0:T(8,128)(2,1)S(1)}, bf16[6,4,64,128]{3,2,1,0:T(8,128)(2,1)S(1)}, u32[]{:S(2)}, u32[]{:S(2)}) %collective-permute-start.6) | collective-permute-done | bytes 393248 | tf_op jit(solution)/shard_map/ppermute | solution.py:298
  21.5 0.0 collective-permute-done.5.refs_1_
  21.5 0.6 collective-permute-done.7.refs_5_.refs_6_
  22.1 1.3 %shard_map.49 = (bf16[2,3,16,64,128]{4,3,2,1,0:T(8,128)(2,1)S(1)}, f32[16,64,128]{2,1,0:T(8,128)S(1)}) custom-call(s32[2]{0:T(128)S(1)} %pad_add_fusion.place_ref, bf16[3,16,64,128]{3,2,1,0:T(8,128)(2,1)S(1)} %get-tuple-element.34.refs_0_, bf16[3,16,64,128]{3,2,1,0:T(8,128)(2,1)S(1)} %collective-permute-done.5.refs_1_, ...), custom_call_target="tpu_custom_call" | custom-call | tf_op jit(solution)/shard_map/pallas_call | solution.py:159
  23.4 7.9 %collective-permute-done.4.refs_1_ = bf16[3,16,64,128]{3,2,1,0:T(8,128)(2,1)S(1)} collective-permute-done((bf16[3,16,64,128]{3,2,1,0:T(8,128)(2,1)S(1)}, bf16[3,16,64,128]{3,2,1,0:T(8,128)(2,1)S(1)}, u32[]{:S(2)}, u32[]{:S(2)}) %collective-permute-start.4) | collective-permute-done | bytes 786464 | tf_op jit(solution)/shard_map/ppermute | solution.py:298
  31.2 0.0 collective-permute-start.8
  31.3 2.3 %collective-permute-done.8.refs_2_ = bf16[3,16,64,128]{3,2,1,0:T(8,128)(2,1)S(1)} collective-permute-done((bf16[3,16,64,128]{3,2,1,0:T(8,128)(2,1)S(1)}, bf16[3,16,64,128]{3,2,1,0:T(8,128)(2,1)S(1)}, u32[]{:S(2)}, u32[]{:S(2)}) %collective-permute-start.8) | collective-permute-done | bytes 786464 | tf_op jit(solution)/shard_map/ppermute | solution.py:298
  33.5 1.3 %shard_map.50 = (bf16[2,3,16,64,128]{4,3,2,1,0:T(8,128)(2,1)S(1)}, f32[16,64,128]{2,1,0:T(8,128)S(1)}, f32[4,64,128]{2,1,0:T(8,128)S(1)}, f32[4,64,128]{2,1,0:T(8,128)S(1)}) custom-call(s32[2]{0:T(128)S(1)} %pad_add_fusion.place_ref, f32[16,64,128]{2,1,0:T(8,128)S(1)} %get-tuple-element.39.refs_0_, ...), custom_call_target="tpu_custom_call" | custom-call | tf_op jit(solution)/shard_map/pallas_call | solution.py:159
  34.9 0.0 copy-start.1
  34.9 1.2 %copy-done.1 = bf16[2,3,16,64,128]{4,3,2,1,0:T(8,128)(2,1)} copy-done((bf16[2,3,16,64,128]{4,3,2,1,0:T(8,128)(2,1)}, bf16[2,3,16,64,128]{4,3,2,1,0:T(8,128)(2,1)S(1)}, u32[]{:S(2)}) %copy-start.1) | copy-done | bytes 1572888
  36.1 0.1 collective-permute-start.9
  36.2 0.7 collective-permute-start.10
  36.9 0.5 collective-permute-done.9.refs_2_
  37.4 0.0 collective-permute-done.10.refs_4_
  37.4 12.1 %shard_map.51.refs_3_ = f32[8,64,128]{2,1,0:T(8,128)S(1)} custom-call(s32[2]{0:T(128)S(1)} %pad_add_fusion.place_ref, f32[12,3,9]{2,1,0:T(4,128)S(1)} %pad_maximum_fusion.1.taps_ref, bf16[4,3,2,64,192]{4,3,2,1,0:T(8,128)(2,1)S(1)} %bitcast.19, bf16[4,3,2,128,256]{4,3,2,1,0:T(8,128)(2,1)S(1)} %bitcast.17, ...), custom_call_target="tpu_custom_call" | custom-call | tf_op jit(solution)/shard_map/pallas_call | solution.py:256
  49.5 0.7 collective-permute-start.12
  50.2 6.8 %collective-permute-start.11 = (f32[8,64,128]{2,1,0:T(8,128)S(1)}, f32[8,64,128]{2,1,0:T(8,128)S(1)}, u32[]{:S(2)}, u32[]{:S(2)}) collective-permute-start(f32[8,64,128]{2,1,0:T(8,128)S(1)} %shard_map.51.refs_3_), channel_id=1, source_target_pairs={{0,8},{8,0},{16,24},{24,16},{1,9},{9,1},{17,25},{25,17},{2,10},{10... | collective-permute-start | bytes 786440 | tf_op jit(solution)/shard_map/ppermute | solution.py:298
  57.0 0.0 collective-permute-done.12.refs_4_
  57.0 1.2 %collective-permute-done.11.refs_2_ = f32[8,64,128]{2,1,0:T(8,128)S(1)} collective-permute-done((f32[8,64,128]{2,1,0:T(8,128)S(1)}, f32[8,64,128]{2,1,0:T(8,128)S(1)}, u32[]{:S(2)}, u32[]{:S(2)}) %collective-permute-start.11) | collective-permute-done | bytes 262176 | tf_op jit(solution)/shard_map/ppermute | solution.py:298
  58.2 12.1 %shard_map.52 = f32[8,64,128]{2,1,0:T(8,128)S(1)} custom-call(s32[2]{0:T(128)S(1)} %pad_add_fusion.place_ref, f32[12,3,9]{2,1,0:T(4,128)S(1)} %pad_maximum_fusion.1.taps_ref, bf16[4,3,2,64,192]{4,3,2,1,0:T(8,128)(2,1)S(1)} %bitcast.20, bf16[4,3,2,128,256]{4,3,2,1,0:T(8,128)(2,1)S(1)} %bitcast.18, bf16[2,3,16,64,128]{4,3,2,1,0:T(8,128)(2,1)S(1)} %get-tuple-element.38.refs_0_, ...), custom_call_target="tpu_custom_call" | custom-call | tf_op jit(solution)/shard_map/pallas_call | solution.py:256
  70.3 0.2 copy.7
  70.4 19.9 %all_to_all.18 = f32[8,64,128]{2,0,1:T(8,128)S(1)} all-to-all(f32[8,64,128]{2,0,1:T(8,128)S(1)} %copy.7), channel_id=1, replica_groups=mesh['view'=4,'vol'=8] {'vol'}, dimensions={1} | all-to-all | bytes 524288 | tf_op jit(solution)/shard_map/all_to_all | solution.py:385
  90.4 0.1 collective-permute-start.14
  90.5 0.1 collective-permute-start.13
  90.6 6.3 %collective-permute-done.14.refs_2_ = f32[64,8,128]{2,1,0:T(8,128)S(1)} collective-permute-done((f32[64,8,128]{2,1,0:T(8,128)S(1)}, f32[64,8,128]{2,1,0:T(8,128)S(1)}, u32[]{:S(2)}, u32[]{:S(2)}) %collective-permute-start.14) | collective-permute-done | bytes 262176 | tf_op jit(solution)/shard_map/ppermute | solution.py:298
  96.9 0.0 collective-permute-start.15
  96.9 0.0 collective-permute-done.13.refs_1_
  96.9 1.5 %collective-permute-done.15.refs_3_ = f32[64,8,128]{2,1,0:T(8,128)S(1)} collective-permute-done((f32[64,8,128]{2,1,0:T(8,128)S(1)}, f32[64,8,128]{2,1,0:T(8,128)S(1)}, u32[]{:S(2)}, u32[]{:S(2)}) %collective-permute-start.15) | collective-permute-done | bytes 262176 | tf_op jit(solution)/shard_map/ppermute | solution.py:298
  98.4 1.0 %shard_map.53 = f32[8,4,8,8,128]{4,3,2,1,0:T(8,128)} custom-call(s32[1]{0:T(128)} %bitcast.place_ref, f32[64,8,128]{2,1,0:T(8,128)S(1)} %bitcast.23, f32[64,8,128]{2,1,0:T(8,128)S(1)} %collective-permute-done.13.refs_1_, f32[64,8,128]{2,1,0:T(8,128)S(1)} %collective-permute-done.14.refs_2_, f32[64,8,128]{2,1,0:T(8,128)S(1)} %collective-permute-done.15.refs_3_), custom_call_target="tpu_custom_call" | custom-call | tf_op jit(solution)/shard_map/pallas_call | solution.py:288
  (6 shorter events, 0.1 us)
Async XLA Ops:
  0.0 6.7 %copy-start.3 = (f32[3,3,9]{2,1,0:T(4,128)S(1)}, f32[3,3,9]{2,1,0:T(4,128)}, u32[]{:S(2)}) copy-start(f32[3,3,9]{2,1,0:T(4,128)} %param.7) | copy-start | bytes 976
  0.0 6.7 %collective-permute-start = (f32[3,3,9]{2,1,0:T(4,128)}, f32[3,3,9]{2,1,0:T(4,128)S(1)}, u32[]{:S(2)}, u32[]{:S(2)}) collective-permute-start(f32[3,3,9]{2,1,0:T(4,128)} %param.7), channel_id=1, source_target_pairs={{0,24},{8,16},{16,8},{24,0},{1,25},{9,17},{17,9},{25,1},{2,26},{10... | collective-permute-start | bytes 980 | tf_op jit(solution)/shard_map/ppermute | solution.py:298
  3.1 1.4 %copy-start = (bf16[3,32,64,128]{3,2,1,0:T(8,128)(2,1)S(1)}, bf16[3,32,64,128]{3,2,1,0:T(8,128)(2,1)}, u32[]{:S(2)}) copy-start(bf16[3,32,64,128]{3,2,1,0:T(8,128)(2,1)} %refs_0_.2) | copy-start | bytes 4718596
  4.5 0.7 copy-start.2
  6.8 5.2 %collective-permute-start.1 = (f32[2,3,3,9]{3,2,1,0:T(4,128)S(1)}, f32[2,3,3,9]{3,2,1,0:T(4,128)S(1)}, u32[]{:S(2)}, u32[]{:S(2)}) collective-permute-start(f32[2,3,3,9]{3,2,1,0:T(4,128)S(1)} %pad_maximum_fusion.2), channel_id=1, source_target_pairs={{0,8},{8,0},{16,24},{24,16},{1,9},{9,1},{17,25},{25,17},{2,10},{10... | collective-permute-start | bytes 1952 | tf_op jit(solution)/shard_map/ppermute | solution.py:298
  7.5 7.8 %collective-permute-start.2 = (bf16[3,4,64,128]{3,2,1,0:T(8,128)(2,1)S(1)}, bf16[3,4,64,128]{3,2,1,0:T(8,128)(2,1)S(1)}, u32[]{:S(2)}, u32[]{:S(2)}) collective-permute-start(bf16[3,4,64,128]{3,2,1,0:T(8,128)(2,1)S(1)} %shard_map.46), channel_id=1, source_target_pairs={{0,16},{8,24},{16,0},{24,8},{1,17},{9,25},{17,1},{25,9},{2,18},{10... | collective-permute-start | bytes 589832 | tf_op jit(solution)/shard_map/ppermute | solution.py:298
  9.9 21.4 %collective-permute-start.4 = (bf16[3,16,64,128]{3,2,1,0:T(8,128)(2,1)S(1)}, bf16[3,16,64,128]{3,2,1,0:T(8,128)(2,1)S(1)}, u32[]{:S(2)}, u32[]{:S(2)}) collective-permute-start(bf16[3,16,64,128]{3,2,1,0:T(8,128)(2,1)S(1)} %get-tuple-element.33), channel_id=1, source_target_pairs={{0,16},{8,24},{16,0},{24,8},{1,17},{9,25},{17,1},{25,9},{2,18},{10... | collective-permute-start | bytes 2359304 | tf_op jit(solution)/shard_map/ppermute | solution.py:298
  12.0 9.6 %collective-permute-start.5 = (bf16[3,16,64,128]{3,2,1,0:T(8,128)(2,1)S(1)}, bf16[3,16,64,128]{3,2,1,0:T(8,128)(2,1)S(1)}, u32[]{:S(2)}, u32[]{:S(2)}) collective-permute-start(bf16[3,16,64,128]{3,2,1,0:T(8,128)(2,1)S(1)} %get-tuple-element.34.refs_0_), channel_id=1, source_target_pairs={{0,8},{8,0},{16,24},{24,16},{1,9},{9,1},{17,25},{25,17},{2,10},{10... | collective-permute-start | bytes 2359304 | tf_op jit(solution)/shard_map/ppermute | solution.py:298
  15.3 4.5 %collective-permute-start.3 = (bf16[6,4,64,128]{3,2,1,0:T(8,128)(2,1)S(1)}, bf16[6,4,64,128]{3,2,1,0:T(8,128)(2,1)S(1)}, u32[]{:S(2)}, u32[]{:S(2)}) collective-permute-start(bf16[6,4,64,128]{3,2,1,0:T(8,128)(2,1)S(1)} %constant_dynamic-update-slice_fusion.refs_2_.refs_3_), channel_id=1, source_target_pairs={{24,25},{16,17},{1,2},{9,10},{26,27},{18,19},{3,4},{11,12},{28,29}... | collective-permute-start | bytes 1179656 | tf_op jit(solution)/shard_map/ppermute | solution.py:309
  19.7 1.8 %collective-permute-start.6 = (bf16[6,4,64,128]{3,2,1,0:T(8,128)(2,1)S(1)}, bf16[6,4,64,128]{3,2,1,0:T(8,128)(2,1)S(1)}, u32[]{:S(2)}, u32[]{:S(2)}) collective-permute-start(bf16[6,4,64,128]{3,2,1,0:T(8,128)(2,1)S(1)} %constant_dynamic-update-slice_fusion.refs_2_.refs_3_), channel_id=1, source_target_pairs={{0,8},{8,0},{16,24},{24,16},{1,9},{9,1},{17,25},{25,17},{2,10},{10... | collective-permute-start | bytes 1179656 | tf_op jit(solution)/shard_map/ppermute | solution.py:298
  19.8 2.3 %collective-permute-start.7 = (bf16[6,4,64,128]{3,2,1,0:T(8,128)(2,1)S(1)}, bf16[6,4,64,128]{3,2,1,0:T(8,128)(2,1)S(1)}, u32[]{:S(2)}, u32[]{:S(2)}) collective-permute-start(bf16[6,4,64,128]{3,2,1,0:T(8,128)(2,1)S(1)} %collective-permute-done.3.refs_4_.refs_5_), channel_id=1, source_target_pairs={{0,8},{8,0},{16,24},{24,16},{1,9},{9,1},{17,25},{25,17},{2,10},{10... | collective-permute-start | bytes 1179656 | tf_op jit(solution)/shard_map/ppermute | solution.py:298
  31.2 2.3 %collective-permute-start.8 = (bf16[3,16,64,128]{3,2,1,0:T(8,128)(2,1)S(1)}, bf16[3,16,64,128]{3,2,1,0:T(8,128)(2,1)S(1)}, u32[]{:S(2)}, u32[]{:S(2)}) collective-permute-start(bf16[3,16,64,128]{3,2,1,0:T(8,128)(2,1)S(1)} %collective-permute-done.4.refs_1_), channel_id=1, source_target_pairs={{0,8},{8,0},{16,24},{24,16},{1,9},{9,1},{17,25},{25,17},{2,10},{10... | collective-permute-start | bytes 2359304 | tf_op jit(solution)/shard_map/ppermute | solution.py:298
  34.9 1.2 %copy-start.1 = (bf16[2,3,16,64,128]{4,3,2,1,0:T(8,128)(2,1)}, bf16[2,3,16,64,128]{4,3,2,1,0:T(8,128)(2,1)S(1)}, u32[]{:S(2)}) copy-start(bf16[2,3,16,64,128]{4,3,2,1,0:T(8,128)(2,1)S(1)} %get-tuple-element.41.refs_1_) | copy-start | bytes 4718596
  36.1 1.3 %collective-permute-start.9 = (f32[4,64,128]{2,1,0:T(8,128)S(1)}, f32[4,64,128]{2,1,0:T(8,128)S(1)}, u32[]{:S(2)}, u32[]{:S(2)}) collective-permute-start(f32[4,64,128]{2,1,0:T(8,128)S(1)} %get-tuple-element.42), channel_id=1, source_target_pairs={{0,8},{8,0},{16,24},{24,16},{1,9},{9,1},{17,25},{25,17},{2,10},{10... | collective-permute-start | bytes 393224 | tf_op jit(solution)/shard_map/ppermute | solution.py:298
  36.2 1.2 %collective-permute-start.10 = (f32[4,64,128]{2,1,0:T(8,128)S(1)}, f32[4,64,128]{2,1,0:T(8,128)S(1)}, u32[]{:S(2)}, u32[]{:S(2)}) collective-permute-start(f32[4,64,128]{2,1,0:T(8,128)S(1)} %get-tuple-element.44), channel_id=1, source_target_pairs={{8,16},{24,25},{17,9},{1,2},{10,18},{26,27},{19,11},{3,4},{12,20},... | collective-permute-start | bytes 393224 | tf_op jit(solution)/shard_map/ppermute | solution.py:309
  49.5 7.5 %collective-permute-start.12 = (f32[8,64,128]{2,1,0:T(8,128)S(1)}, f32[8,64,128]{2,1,0:T(8,128)S(1)}, u32[]{:S(2)}, u32[]{:S(2)}) collective-permute-start(f32[8,64,128]{2,1,0:T(8,128)S(1)} %shard_map.51.refs_3_), channel_id=1, source_target_pairs={{8,16},{24,25},{17,9},{1,2},{10,18},{26,27},{19,11},{3,4},{12,20},... | collective-permute-start | bytes 786440 | tf_op jit(solution)/shard_map/ppermute | solution.py:309
  50.2 8.0 %collective-permute-start.11 = (f32[8,64,128]{2,1,0:T(8,128)S(1)}, f32[8,64,128]{2,1,0:T(8,128)S(1)}, u32[]{:S(2)}, u32[]{:S(2)}) collective-permute-start(f32[8,64,128]{2,1,0:T(8,128)S(1)} %shard_map.51.refs_3_), channel_id=1, source_target_pairs={{0,8},{8,0},{16,24},{24,16},{1,9},{9,1},{17,25},{25,17},{2,10},{10... | collective-permute-start | bytes 786440 | tf_op jit(solution)/shard_map/ppermute | solution.py:298
  90.4 6.4 %collective-permute-start.14 = (f32[64,8,128]{2,1,0:T(8,128)S(1)}, f32[64,8,128]{2,1,0:T(8,128)S(1)}, u32[]{:S(2)}, u32[]{:S(2)}) collective-permute-start(f32[64,8,128]{2,1,0:T(8,128)S(1)} %bitcast.21), channel_id=1, source_target_pairs={{0,16},{8,24},{16,0},{24,8},{1,17},{9,25},{17,1},{25,9},{2,18},{10... | collective-permute-start | bytes 786440 | tf_op jit(solution)/shard_map/ppermute | solution.py:298
  90.5 6.4 %collective-permute-start.13 = (f32[64,8,128]{2,1,0:T(8,128)S(1)}, f32[64,8,128]{2,1,0:T(8,128)S(1)}, u32[]{:S(2)}, u32[]{:S(2)}) collective-permute-start(f32[64,8,128]{2,1,0:T(8,128)S(1)} %bitcast.22), channel_id=1, source_target_pairs={{0,8},{8,0},{16,24},{24,16},{1,9},{9,1},{17,25},{25,17},{2,10},{10... | collective-permute-start | bytes 786440 | tf_op jit(solution)/shard_map/ppermute | solution.py:298
  96.9 1.5 %collective-permute-start.15 = (f32[64,8,128]{2,1,0:T(8,128)S(1)}, f32[64,8,128]{2,1,0:T(8,128)S(1)}, u32[]{:S(2)}, u32[]{:S(2)}) collective-permute-start(f32[64,8,128]{2,1,0:T(8,128)S(1)} %collective-permute-done.14.refs_2_), channel_id=1, source_target_pairs={{0,8},{8,0},{16,24},{24,16},{1,9},{9,1},{17,25},{25,17},{2,10},{10... | collective-permute-start | bytes 786440 | tf_op jit(solution)/shard_map/ppermute | solution.py:298

commit v13 on v12

--- a/solution.py
+++ b/solution.py
@@ -11,7 +11,7 @@
 CORES = 2
 VMEM = pl.BlockSpec(memory_space=pltpu.VMEM)
 SMEM = pl.BlockSpec(memory_space=pltpu.SMEM)
-PARAMS = pltpu.CompilerParams(vmem_limit_bytes=48 * 1024 * 1024)
+PARAMS = pltpu.CompilerParams(vmem_limit_bytes=24 * 1024 * 1024)
 
 
 def halves(value):
@@ -20,14 +20,9 @@
     return high, low
 
 
-def resample_kernel(plan, place_ref, weights_ref, offsets_ref, *refs):
-    count = 1 + max(segment[0] for parts in plan for segment in parts[1])
-    sources, outs = refs[:count], refs[count:]
-    weights = weights_ref[0]
+def row_matrix(weights, first):
     band, rows = weights.shape
-    width = sources[0].shape[3]
     weights = weights / jnp.sum(weights, axis=0, keepdims=True)
-    first = offsets_ref[0]
     source = lax.broadcasted_iota(jnp.int32, (rows, rows), 0)
     matrix = jnp.zeros((rows, rows), jnp.float32)
     for k in range(band):
@@ -37,39 +32,81 @@
     rest = matrix - high.astype(jnp.float32)
     middle = rest.astype(jnp.bfloat16)
     low = (rest - middle.astype(jnp.float32)).astype(jnp.bfloat16)
-    left = jnp.concatenate([high, middle, low], axis=1)
-    for out_ref, (other, segments) in zip(outs, plan):
+    return jnp.concatenate([high, middle, low], axis=1)
+
+
+def two_rows(left, first, second):
+    planes = jnp.concatenate([first, second], axis=1)
+    planes = jnp.concatenate([planes, planes, planes], axis=0)
+    total = jnp.dot(left, planes, preferred_element_type=jnp.float32).astype(jnp.bfloat16)
+    width = first.shape[1]
+    return total[:, :width], total[:, width:]
+
+
+def bound_kernel(place_ref, weights_hbm, offsets_hbm, raw_hbm, out_ref, weights_ref, offsets_ref, planes_ref, sems):
+    view = pl.program_id(0)
+    depth, rim = raw_hbm.shape[1], out_ref.shape[1]
+
+    @pl.when(view == 0)
+    def _():
+        start = (depth - rim) * (1 - place_ref[0])
+        pairs = [(weights_hbm, weights_ref), (offsets_hbm, offsets_ref), (raw_hbm.at[:, pl.ds(start, rim)], planes_ref)]
+        copies = [pltpu.make_async_copy(*pair, sems.at[i]) for i, pair in enumerate(pairs)]
+        for copy in copies:
+            copy.start()
+        for copy in copies:
+            copy.wait()
+
+    left = row_matrix(weights_ref[view], offsets_ref[pl.ds(view, 1), :])
+    for z in range(0, rim, 2):
+        out_ref[0, z], out_ref[0, z + 1] = two_rows(left, planes_ref[view, z], planes_ref[view, z + 1])
+
+
+def resample_bound(place, weights, offsets, raw, rim):
+    views, _, rows, width = raw.shape
+    shape = (views, rim, rows, width)
+    weights = weights.transpose(0, 2, 1)
+    return pl.pallas_call(
+        bound_kernel,
+        grid=(views,),
+        out_shape=jax.ShapeDtypeStruct(shape, jnp.bfloat16),
+        in_specs=[SMEM] + [pl.BlockSpec(memory_space=pltpu.HBM)] * 3,
+        out_specs=pl.BlockSpec((1,) + shape[1:], lambda v: (v, 0, 0, 0)),
+        scratch_shapes=[
+            pltpu.VMEM(weights.shape, jnp.float32),
+            pltpu.VMEM(offsets.shape, jnp.int32),
+            pltpu.VMEM(shape, jnp.bfloat16),
+            pltpu.SemaphoreType.DMA((3,)),
+        ],
+        compiler_params=pltpu.CompilerParams(vmem_limit_bytes=63 * 1024 * 1024),
+    )(place, weights, offsets, raw)
+
+
+def resample_kernel(plan, place_ref, weights_ref, offsets_ref, raw_ref, *outs):
+    left = row_matrix(weights_ref[0], offsets_ref[pl.ds(pl.program_id(0), 1), :])
+    for out_ref, (other, starts) in zip(outs, plan):
         half = 1 - place_ref[0] if other else place_ref[0]
-        for index, start, target, length in segments:
-            start = start[0] + (start[1] - start[0]) * half
-            target = target[0] + (target[1] - target[0]) * half
-            for z in range(0, length, 2):
-                planes = [sources[index][0, start + z + i] for i in range(2)]
-                planes = jnp.concatenate(planes, axis=1)
-                planes = jnp.concatenate([planes, planes, planes], axis=0)
-                total = jnp.dot(left, planes, preferred_element_type=jnp.float32).astype(jnp.bfloat16)
-                for i in range(2):
-                    out_ref[0, target + z + i] = total[:, i * width : (i + 1) * width]
-
-
-def resample(place, weights, offsets, sources, plan):
-    views, _, rows, width = sources[0].shape
-    band = weights.shape[2]
+        start = starts[0] + (starts[1] - starts[0]) * half
+        for z in range(0, out_ref.shape[1], 2):
+            out_ref[0, z], out_ref[0, z + 1] = two_rows(left, raw_ref[0, start + z], raw_ref[0, start + z + 1])
+
+
+def resample(place, weights, offsets, raw, counts, plan):
+    views, depth, rows, width = raw.shape
     block = lambda planes: pl.BlockSpec((1, planes, rows, width), lambda v: (v, 0, 0, 0))
-    counts = [sum(segment[3] for segment in segments) for _, segments in plan]
     return pl.pallas_call(
         functools.partial(resample_kernel, plan),
         grid=(views,),
         out_shape=[jax.ShapeDtypeStruct((views, count, rows, width), jnp.bfloat16) for count in counts],
         in_specs=[
             SMEM,
-            pl.BlockSpec((1, band, rows), lambda v: (v, 0, 0)),
-            pl.BlockSpec((1, 1, rows), lambda v: (v, 0, 0)),
-        ]
-        + [block(source.shape[1]) for source in sources],
+            pl.BlockSpec((1, weights.shape[2], rows), lambda v: (v, 0, 0)),
+            VMEM,
+            block(depth),
+        ],
         out_specs=[block(count) for count in counts],
         compiler_params=PARAMS,
-    )(place, weights.transpose(0, 2, 1), offsets[:, None, :], *sources)
+    )(place, weights.transpose(0, 2, 1), offsets, raw)
 
 
 def bands_kernel(taps_ref, left_ref, right_ref):
@@ -339,16 +376,21 @@
     far = lambda value: partner(value, far_bit, members)
     seams = [(members * block + members - 1 - i, members * (block + 1) + i) for block in range(blocks - 1) for i in range(CORES)]
     across = lambda value: swap(value, seams, members, blocks)
-    bound = [(0, (0, depth - rim), (0, 0), rim)]
-    inner = [(0, (rim, 2 * planes - rim), (0, 0), 2 * planes)]
+    bound, inner = (0, depth - rim), (rim, 2 * planes - rim)
 
     cross_taps = partner(psf_taps, near_bit + far_bit, members)
-    (far_bound,) = resample(place, weights, offsets, [raw_views], [(True, bound)])
+    far_bound = resample_bound(place, weights, offsets, raw_views, rim)
     far_bound, raw_later, cross_taps = lax.optimization_barrier((far_bound, raw_views, cross_taps))
     far_bound = far(far_bound)
     far_inner, own_bound, own_inner = resample(
-        place, weights, offsets, [raw_later], [(True, inner), (False, bound), (False, inner)]
+        place,
+        weights,
+        offsets,
+        raw_later,
+        (2 * planes, rim, 2 * planes),
+        [(True, inner), (False, bound), (False, inner)],
     )
+    far_inner, cross_taps = lax.optimization_barrier((far_inner, cross_taps))
     far_inner = far(far_inner)
     near_inner = near(own_inner)
     pair_taps = near(jnp.stack([psf_taps, cross_taps]))

time: 99.8 us -> 98.6 us (0.988)
  local copies, waits for them, and re-layouts: 4.47 us -> 1.92 us
  Pallas kernels: 35 us -> 37 us
  waiting for transfers between devices: 24.6 us -> 23.5 us
  blocking collectives: 19.9 us -> 18.9 us
    pallas_call x0 -> x1, Pallas kernels: none -> 3.66 us  [resample_bound(): pl.pallas_call(bound_kernel, grid=(views,), out_shape=jax.ShapeDtypeStruc...]
    unnamed x9 -> x11, local copies, waits for them, and re-layouts: 3.3 us -> 1.43 us
    pallas_call x2 -> x1, Pallas kernels: 3.81 us -> 2.34 us  [resample(): pl.pallas_call(functools.partial(resample_kernel, plan), grid=(views,), o...]
    ppermute x13, waiting for transfers between devices: 24.6 us -> 23.5 us  [partner(): return lax.ppermute(value, 'view', [(i, i ^ bit) for i in range(members)])]
    all_to_all x1, blocking collectives: 19.9 us -> 18.9 us  [per_device(): lax.all_to_all(joined, 'vol', split_axis=1, concat_axis=0, tiled=True)]
  transfers between devices with their start and end apart: 16 -> 16, of which waited for: 9 -> 9; matrix products, arithmetic and copies ran while one was open for 1% -> 1% of each run, Pallas kernels for 8% -> 11%
where the time goes in v13:
time: 98.6 us; the launch traced here: 98.3 us
  Pallas kernels  37 us (38%)
  waiting for transfers between devices  23.5 us (24%)
  blocking collectives  18.9 us (19%)
  starting transfers between devices  15.8 us (16%)
  local copies, waits for them, and re-layouts  1.92 us (2%)
    pallas_call x2, Pallas kernels, update(): pl.pallas_call(functools.partial(update_kernel, paired), grid=(count,), o...  24.1 us
    ppermute x13, waiting for transfers between devices, partner(): return lax.ppermute(value, 'view', [(i, i ^ bit) for i in range(members)])  23.5 us
    all_to_all x1, blocking collectives, per_device(): lax.all_to_all(joined, 'vol', split_axis=1, concat_axis=0, tiled=True)  18.9 us
    ppermute x13, starting transfers between devices, partner(): return lax.ppermute(value, 'view', [(i, i ^ bit) for i in range(members)])  13.8 us
    pallas_call x1, Pallas kernels, resample_bound(): pl.pallas_call(bound_kernel, grid=(views,), out_shape=jax.ShapeDtypeStruc...  3.66 us
    pallas_call x1, Pallas kernels, bands(): pl.pallas_call(bands_kernel, grid=(views,), out_shape=[jax.ShapeDtypeStru...  3.34 us
    pallas_call x2, Pallas kernels, gather_views(): pl.pallas_call(functools.partial(gather_kernel, views, planes, rim), grid...  2.6 us
    pallas_call x1, Pallas kernels, resample(): pl.pallas_call(functools.partial(resample_kernel, plan), grid=(views,), o...  2.34 us
  transfers between devices with their start and end apart: 16, of which 9 were waited for; matrix products, arithmetic and copies ran while one was open for 1% of the time, Pallas kernels for 11%

profile of v13, /device:TPU:0, one launch (start us, length us, event | category | flops | bytes accessed | tf_op | source)
XLA Modules:
  0.0 98.3 jit_solution(9593317677542627645)
XLA Ops:
  0.0 0.0 copy-start.3
  0.0 0.0 copy-start.1
  0.0 2.4 %collective-permute-start = (f32[3,3,9]{2,1,0:T(4,128)}, f32[3,3,9]{2,1,0:T(4,128)S(1)}, u32[]{:S(2)}, u32[]{:S(2)}) collective-permute-start(f32[3,3,9]{2,1,0:T(4,128)} %param.7), channel_id=1, source_target_pairs={{0,24},{8,16},{16,8},{24,0},{1,25},{9,17},{17,9},{25,1},{2,26},{10... | collective-permute-start | bytes 980 | tf_op jit(solution)/shard_map/ppermute | solution.py:335
  2.4 0.6 pad_add_fusion.place_ref
  3.0 0.0 copy-start.2
  3.0 0.0 copy-start.4
  3.0 3.7 %shard_map.46 = bf16[3,4,64,128]{3,2,1,0:T(8,128)(2,1)} custom-call(s32[2]{0:T(128)} %pad_add_fusion.place_ref, f32[3,8,64]{2,1,0:T(8,128)} %bitcast.24, s32[3,64]{1,0:T(4,128)} %offsets_ref.1, bf16[3,32,64,128]{3,2,1,0:T(8,128)(2,1)} %raw_ref), custom_call_target="tpu_custom_call" | custom-call | tf_op jit(solution)/shard_map/pallas_call | solution.py:69
  6.7 0.0 collective-permute-done
  6.7 0.7 collective-permute-start.2
  7.4 0.0 copy-done.3
  7.4 0.0 copy-done.1
  7.4 0.0 copy-done.2
  7.4 0.0 copy-start
  7.4 1.4 %copy-done = bf16[3,32,64,128]{3,2,1,0:T(8,128)(2,1)S(1)} copy-done((bf16[3,32,64,128]{3,2,1,0:T(8,128)(2,1)S(1)}, bf16[3,32,64,128]{3,2,1,0:T(8,128)(2,1)}, u32[]{:S(2)}) %copy-start) | copy-done | bytes 1572888
  8.8 2.3 %shard_map.47 = (bf16[3,16,64,128]{3,2,1,0:T(8,128)(2,1)S(1)}, bf16[3,4,64,128]{3,2,1,0:T(8,128)(2,1)S(1)}, bf16[3,16,64,128]{3,2,1,0:T(8,128)(2,1)S(1)}) custom-call(s32[2]{0:T(128)S(1)} %copy-done.2, f32[3,8,64]{2,1,0:T(8,128)S(1)} %bitcast.25, s32[3,64]{1,0:T(4,128)S(1)} %copy-done.3, bf16[3,32,64,128]{3,2,1,0:T(8,128)(2,1)S(1)} %copy-done), custom_call_target="tpu_custom_call" | custom-call | tf_op jit(solution)/shard_map/pallas_call | solution.py:97
  11.1 0.0 copy-done.4
  11.2 0.2 collective-permute-start.1
  11.4 1.8 %collective-permute-start.4 = (bf16[3,16,64,128]{3,2,1,0:T(8,128)(2,1)S(1)}, bf16[3,16,64,128]{3,2,1,0:T(8,128)(2,1)S(1)}, u32[]{:S(2)}, u32[]{:S(2)}) collective-permute-start(bf16[3,16,64,128]{3,2,1,0:T(8,128)(2,1)S(1)} %get-tuple-element.37), channel_id=1, source_target_pairs={{0,16},{8,24},{16,0},{24,8},{1,17},{9,25},{17,1},{25,9},{2,18},{10... | collective-permute-start | bytes 2359304 | tf_op jit(solution)/shard_map/ppermute | solution.py:335
  13.1 0.0 collective-permute-start.5
  13.1 0.0 collective-permute-done.1
  13.1 0.1 fusion
  13.2 0.1 broadcast_divide_fusion
  13.3 1.1 %collective-permute-done.2 = bf16[3,4,64,128]{3,2,1,0:T(8,128)(2,1)S(1)} collective-permute-done((bf16[3,4,64,128]{3,2,1,0:T(8,128)(2,1)}, bf16[3,4,64,128]{3,2,1,0:T(8,128)(2,1)S(1)}, u32[]{:S(2)}, u32[]{:S(2)}) %collective-permute-start.2) | collective-permute-done | bytes 196640 | tf_op jit(solution)/shard_map/ppermute | solution.py:335
  14.5 0.7 collective-permute-start.3
  15.2 0.3 slice_reduce_fusion
  15.5 0.1 slice_divide_fusion
  15.6 3.3 %shard_map.48 = (bf16[12,2,64,192]{3,2,1,0:T(8,128)(2,1)S(1)}, bf16[12,2,128,256]{3,2,1,0:T(8,128)(2,1)S(1)}) custom-call(f32[12,3,9]{2,1,0:T(4,128)S(1)} %pad_maximum_fusion.1.taps_ref), custom_call_target="tpu_custom_call" | custom-call | tf_op jit(solution)/shard_map/pallas_call | solution.py:135
  18.9 0.1 collective-permute-start.6
  19.0 0.0 collective-permute-done.3.refs_4_.refs_5_
  19.0 0.5 collective-permute-start.7
  19.5 1.2 %collective-permute-done.6.refs_3_.refs_4_ = bf16[6,4,64,128]{3,2,1,0:T(8,128)(2,1)S(1)} collective-permute-done((bf16[6,4,64,128]{3,2,1,0:T(8,128)(2,1)S(1)}, bf16[6,4,64,128]{3,2,1,0:T(8,128)(2,1)S(1)}, u32[]{:S(2)}, u32[]{:S(2)}) %collective-permute-start.6) | collective-permute-done | bytes 393248 | tf_op jit(solution)/shard_map/ppermute | solution.py:335
  20.7 0.0 collective-permute-done.5.refs_1_
  20.7 0.6 collective-permute-done.7.refs_5_.refs_6_
  21.3 1.3 %shard_map.49 = (bf16[2,3,16,64,128]{4,3,2,1,0:T(8,128)(2,1)S(1)}, f32[16,64,128]{2,1,0:T(8,128)S(1)}) custom-call(s32[2]{0:T(128)S(1)} %copy-done.2, bf16[3,16,64,128]{3,2,1,0:T(8,128)(2,1)S(1)} %get-tuple-element.38.refs_0_, bf16[3,16,64,128]{3,2,1,0:T(8,128)(2,1)S(1)} %collective-permute-done.5.refs_1_, ...), custom_call_target="tpu_custom_call" | custom-call | tf_op jit(solution)/shard_map/pallas_call | solution.py:196
  22.6 8.8 %collective-permute-done.4.refs_1_ = bf16[3,16,64,128]{3,2,1,0:T(8,128)(2,1)S(1)} collective-permute-done((bf16[3,16,64,128]{3,2,1,0:T(8,128)(2,1)S(1)}, bf16[3,16,64,128]{3,2,1,0:T(8,128)(2,1)S(1)}, u32[]{:S(2)}, u32[]{:S(2)}) %collective-permute-start.4) | collective-permute-done | bytes 786464 | tf_op jit(solution)/shard_map/ppermute | solution.py:335
  31.3 0.0 collective-permute-start.8
  31.3 2.3 %collective-permute-done.8.refs_2_ = bf16[3,16,64,128]{3,2,1,0:T(8,128)(2,1)S(1)} collective-permute-done((bf16[3,16,64,128]{3,2,1,0:T(8,128)(2,1)S(1)}, bf16[3,16,64,128]{3,2,1,0:T(8,128)(2,1)S(1)}, u32[]{:S(2)}, u32[]{:S(2)}) %collective-permute-start.8) | collective-permute-done | bytes 786464 | tf_op jit(solution)/shard_map/ppermute | solution.py:335
  33.6 1.3 %shard_map.50 = (bf16[2,3,16,64,128]{4,3,2,1,0:T(8,128)(2,1)S(1)}, f32[16,64,128]{2,1,0:T(8,128)S(1)}, f32[4,64,128]{2,1,0:T(8,128)S(1)}, f32[4,64,128]{2,1,0:T(8,128)S(1)}) custom-call(s32[2]{0:T(128)S(1)} %copy-done.2, f32[16,64,128]{2,1,0:T(8,128)S(1)} %get-tuple-element.43.refs_0_, bf16[3,16,64,128]{3,2,1,0:T(8,128)(2,1)S(1)} %collective-permute-done.4.refs_1_, ...), custom_call_target="tpu_custom_call" | custom-call | tf_op jit(solution)/shard_map/pallas_call | solution.py:196
  35.0 0.2 collective-permute-start.9
  35.2 0.7 collective-permute-start.10
  35.8 0.5 collective-permute-done.9.refs_2_
  36.4 0.0 collective-permute-done.10.refs_4_
  36.4 12.0 %shard_map.51.refs_3_ = f32[8,64,128]{2,1,0:T(8,128)S(1)} custom-call(s32[2]{0:T(128)S(1)} %copy-done.2, f32[12,3,9]{2,1,0:T(4,128)S(1)} %pad_maximum_fusion.1.taps_ref, bf16[4,3,2,64,192]{4,3,2,1,0:T(8,128)(2,1)S(1)} %bitcast.19, bf16[4,3,2,128,256]{4,3,2,1,0:T(8,128)(2,1)S(1)} %bitcast.17, bf16[2,3,16,64,128]{4,3,2,1,0:T(8,128)(2,1)S(1)} %get-tuple-element.42.refs_0_, ...), custom_call_target="tpu_custom_call" | custom-call | tf_op jit(solution)/shard_map/pallas_call | solution.py:293
  48.4 0.7 collective-permute-start.12
  49.1 7.8 %collective-permute-start.11 = (f32[8,64,128]{2,1,0:T(8,128)S(1)}, f32[8,64,128]{2,1,0:T(8,128)S(1)}, u32[]{:S(2)}, u32[]{:S(2)}) collective-permute-start(f32[8,64,128]{2,1,0:T(8,128)S(1)} %shard_map.51.refs_3_), channel_id=1, source_target_pairs={{0,8},{8,0},{16,24},{24,16},{1,9},{9,1},{17,25},{25,17},{2,10},{10... | collective-permute-start | bytes 786440 | tf_op jit(solution)/shard_map/ppermute | solution.py:335
  57.0 0.0 collective-permute-done.12.refs_4_
  57.0 1.2 %collective-permute-done.11.refs_2_ = f32[8,64,128]{2,1,0:T(8,128)S(1)} collective-permute-done((f32[8,64,128]{2,1,0:T(8,128)S(1)}, f32[8,64,128]{2,1,0:T(8,128)S(1)}, u32[]{:S(2)}, u32[]{:S(2)}) %collective-permute-start.11) | collective-permute-done | bytes 262176 | tf_op jit(solution)/shard_map/ppermute | solution.py:335
  58.1 12.0 %shard_map.52 = f32[8,64,128]{2,1,0:T(8,128)S(1)} custom-call(s32[2]{0:T(128)S(1)} %copy-done.2, f32[12,3,9]{2,1,0:T(4,128)S(1)} %pad_maximum_fusion.1.taps_ref, bf16[4,3,2,64,192]{4,3,2,1,0:T(8,128)(2,1)S(1)} %bitcast.20, bf16[4,3,2,128,256]{4,3,2,1,0:T(8,128)(2,1)S(1)} %bitcast.18, bf16[2,3,16,64,128]{4,3,2,1,0:T(8,128)(2,1)S(1)} %get-tuple-element.42.refs_0_, ...), custom_call_target="tpu_custom_call" | custom-call | tf_op jit(solution)/shard_map/pallas_call | solution.py:293
  70.2 0.2 copy.7
  70.3 18.9 %all_to_all.18 = f32[8,64,128]{2,0,1:T(8,128)S(1)} all-to-all(f32[8,64,128]{2,0,1:T(8,128)S(1)} %copy.7), channel_id=1, replica_groups=mesh['view'=4,'vol'=8] {'vol'}, dimensions={1} | all-to-all | bytes 524288 | tf_op jit(solution)/shard_map/all_to_all | solution.py:427
  89.3 0.1 collective-permute-start.14
  89.4 0.0 collective-permute-start.13
  89.4 6.3 %collective-permute-done.14.refs_2_ = f32[64,8,128]{2,1,0:T(8,128)S(1)} collective-permute-done((f32[64,8,128]{2,1,0:T(8,128)S(1)}, f32[64,8,128]{2,1,0:T(8,128)S(1)}, u32[]{:S(2)}, u32[]{:S(2)}) %collective-permute-start.14) | collective-permute-done | bytes 262176 | tf_op jit(solution)/shard_map/ppermute | solution.py:335
  95.7 0.0 collective-permute-start.15
  95.7 0.0 collective-permute-done.13.refs_1_
  95.7 1.5 %collective-permute-done.15.refs_3_ = f32[64,8,128]{2,1,0:T(8,128)S(1)} collective-permute-done((f32[64,8,128]{2,1,0:T(8,128)S(1)}, f32[64,8,128]{2,1,0:T(8,128)S(1)}, u32[]{:S(2)}, u32[]{:S(2)}) %collective-permute-start.15) | collective-permute-done | bytes 262176 | tf_op jit(solution)/shard_map/ppermute | solution.py:335
  97.3 1.0 %shard_map.53 = f32[8,4,8,8,128]{4,3,2,1,0:T(8,128)} custom-call(s32[1]{0:T(128)} %bitcast.place_ref, f32[64,8,128]{2,1,0:T(8,128)S(1)} %bitcast.23, f32[64,8,128]{2,1,0:T(8,128)S(1)} %collective-permute-done.13.refs_1_, f32[64,8,128]{2,1,0:T(8,128)S(1)} %collective-permute-done.14.refs_2_, f32[64,8,128]{2,1,0:T(8,128)S(1)} %collective-permute-done.15.refs_3_), custom_call_target="tpu_custom_call" | custom-call | tf_op jit(solution)/shard_map/pallas_call | solution.py:325
  (6 shorter events, 0.1 us)
Async XLA Ops:
  0.0 7.4 %copy-start.3 = (s32[3,64]{1,0:T(4,128)S(1)}, s32[3,64]{1,0:T(4,128)}, u32[]{:S(2)}) copy-start(s32[3,64]{1,0:T(4,128)} %offsets_ref.1) | copy-start | bytes 2308
  0.0 7.4 %copy-start.1 = (f32[3,64,8]{1,2,0:T(8,128)S(1)}, f32[3,64,8]{1,2,0:T(8,128)}, u32[]{:S(2)}) copy-start(f32[3,64,8]{1,2,0:T(8,128)} %param.5) | copy-start | bytes 18436
  0.0 6.7 %collective-permute-start = (f32[3,3,9]{2,1,0:T(4,128)}, f32[3,3,9]{2,1,0:T(4,128)S(1)}, u32[]{:S(2)}, u32[]{:S(2)}) collective-permute-start(f32[3,3,9]{2,1,0:T(4,128)} %param.7), channel_id=1, source_target_pairs={{0,24},{8,16},{16,8},{24,0},{1,25},{9,17},{17,9},{25,1},{2,26},{10... | collective-permute-start | bytes 980 | tf_op jit(solution)/shard_map/ppermute | solution.py:335
  3.0 4.4 %copy-start.2 = (s32[2]{0:T(128)S(1)}, s32[2]{0:T(128)}, u32[]{:S(2)}) copy-start(s32[2]{0:T(128)} %pad_add_fusion.place_ref) | copy-start | bytes 28
  3.0 8.1 %copy-start.4 = (f32[3,3,9]{2,1,0:T(4,128)S(1)}, f32[3,3,9]{2,1,0:T(4,128)}, u32[]{:S(2)}) copy-start(f32[3,3,9]{2,1,0:T(4,128)} %param.7) | copy-start | bytes 976
  6.7 7.8 %collective-permute-start.2 = (bf16[3,4,64,128]{3,2,1,0:T(8,128)(2,1)}, bf16[3,4,64,128]{3,2,1,0:T(8,128)(2,1)S(1)}, u32[]{:S(2)}, u32[]{:S(2)}) collective-permute-start(bf16[3,4,64,128]{3,2,1,0:T(8,128)(2,1)} %shard_map.46), channel_id=1, source_target_pairs={{0,16},{8,24},{16,0},{24,8},{1,17},{9,25},{17,1},{25,9},{2,18},{10... | collective-permute-start | bytes 589832 | tf_op jit(solution)/shard_map/ppermute | solution.py:335
  7.4 1.4 %copy-start = (bf16[3,32,64,128]{3,2,1,0:T(8,128)(2,1)S(1)}, bf16[3,32,64,128]{3,2,1,0:T(8,128)(2,1)}, u32[]{:S(2)}) copy-start(bf16[3,32,64,128]{3,2,1,0:T(8,128)(2,1)} %raw_ref) | copy-start | bytes 4718596
  11.2 2.0 %collective-permute-start.1 = (f32[2,3,3,9]{3,2,1,0:T(4,128)S(1)}, f32[2,3,3,9]{3,2,1,0:T(4,128)S(1)}, u32[]{:S(2)}, u32[]{:S(2)}) collective-permute-start(f32[2,3,3,9]{3,2,1,0:T(4,128)S(1)} %pad_maximum_fusion.2), channel_id=1, source_target_pairs={{0,8},{8,0},{16,24},{24,16},{1,9},{9,1},{17,25},{25,17},{2,10},{10... | collective-permute-start | bytes 1952 | tf_op jit(solution)/shard_map/ppermute | solution.py:335
  11.4 20.0 %collective-permute-start.4 = (bf16[3,16,64,128]{3,2,1,0:T(8,128)(2,1)S(1)}, bf16[3,16,64,128]{3,2,1,0:T(8,128)(2,1)S(1)}, u32[]{:S(2)}, u32[]{:S(2)}) collective-permute-start(bf16[3,16,64,128]{3,2,1,0:T(8,128)(2,1)S(1)} %get-tuple-element.37), channel_id=1, source_target_pairs={{0,16},{8,24},{16,0},{24,8},{1,17},{9,25},{17,1},{25,9},{2,18},{10... | collective-permute-start | bytes 2359304 | tf_op jit(solution)/shard_map/ppermute | solution.py:335
  13.1 7.6 %collective-permute-start.5 = (bf16[3,16,64,128]{3,2,1,0:T(8,128)(2,1)S(1)}, bf16[3,16,64,128]{3,2,1,0:T(8,128)(2,1)S(1)}, u32[]{:S(2)}, u32[]{:S(2)}) collective-permute-start(bf16[3,16,64,128]{3,2,1,0:T(8,128)(2,1)S(1)} %get-tuple-element.38.refs_0_), channel_id=1, source_target_pairs={{0,8},{8,0},{16,24},{24,16},{1,9},{9,1},{17,25},{25,17},{2,10},{10... | collective-permute-start | bytes 2359304 | tf_op jit(solution)/shard_map/ppermute | solution.py:335
  14.5 4.5 %collective-permute-start.3 = (bf16[6,4,64,128]{3,2,1,0:T(8,128)(2,1)S(1)}, bf16[6,4,64,128]{3,2,1,0:T(8,128)(2,1)S(1)}, u32[]{:S(2)}, u32[]{:S(2)}) collective-permute-start(bf16[6,4,64,128]{3,2,1,0:T(8,128)(2,1)S(1)} %constant_dynamic-update-slice_fusion.refs_2_.refs_3_), channel_id=1, source_target_pairs={{24,25},{16,17},{1,2},{9,10},{26,27},{18,19},{3,4},{11,12},{28,29}... | collective-permute-start | bytes 1179656 | tf_op jit(solution)/shard_map/ppermute | solution.py:346
  18.9 1.8 %collective-permute-start.6 = (bf16[6,4,64,128]{3,2,1,0:T(8,128)(2,1)S(1)}, bf16[6,4,64,128]{3,2,1,0:T(8,128)(2,1)S(1)}, u32[]{:S(2)}, u32[]{:S(2)}) collective-permute-start(bf16[6,4,64,128]{3,2,1,0:T(8,128)(2,1)S(1)} %constant_dynamic-update-slice_fusion.refs_2_.refs_3_), channel_id=1, source_target_pairs={{0,8},{8,0},{16,24},{24,16},{1,9},{9,1},{17,25},{25,17},{2,10},{10... | collective-permute-start | bytes 1179656 | tf_op jit(solution)/shard_map/ppermute | solution.py:335
  19.0 2.3 %collective-permute-start.7 = (bf16[6,4,64,128]{3,2,1,0:T(8,128)(2,1)S(1)}, bf16[6,4,64,128]{3,2,1,0:T(8,128)(2,1)S(1)}, u32[]{:S(2)}, u32[]{:S(2)}) collective-permute-start(bf16[6,4,64,128]{3,2,1,0:T(8,128)(2,1)S(1)} %collective-permute-done.3.refs_4_.refs_5_), channel_id=1, source_target_pairs={{0,8},{8,0},{16,24},{24,16},{1,9},{9,1},{17,25},{25,17},{2,10},{10... | collective-permute-start | bytes 1179656 | tf_op jit(solution)/shard_map/ppermute | solution.py:335
  31.3 2.3 %collective-permute-start.8 = (bf16[3,16,64,128]{3,2,1,0:T(8,128)(2,1)S(1)}, bf16[3,16,64,128]{3,2,1,0:T(8,128)(2,1)S(1)}, u32[]{:S(2)}, u32[]{:S(2)}) collective-permute-start(bf16[3,16,64,128]{3,2,1,0:T(8,128)(2,1)S(1)} %collective-permute-done.4.refs_1_), channel_id=1, source_target_pairs={{0,8},{8,0},{16,24},{24,16},{1,9},{9,1},{17,25},{25,17},{2,10},{10... | collective-permute-start | bytes 2359304 | tf_op jit(solution)/shard_map/ppermute | solution.py:335
  35.0 1.4 %collective-permute-start.9 = (f32[4,64,128]{2,1,0:T(8,128)S(1)}, f32[4,64,128]{2,1,0:T(8,128)S(1)}, u32[]{:S(2)}, u32[]{:S(2)}) collective-permute-start(f32[4,64,128]{2,1,0:T(8,128)S(1)} %get-tuple-element.46), channel_id=1, source_target_pairs={{0,8},{8,0},{16,24},{24,16},{1,9},{9,1},{17,25},{25,17},{2,10},{10... | collective-permute-start | bytes 393224 | tf_op jit(solution)/shard_map/ppermute | solution.py:335
  35.2 1.2 %collective-permute-start.10 = (f32[4,64,128]{2,1,0:T(8,128)S(1)}, f32[4,64,128]{2,1,0:T(8,128)S(1)}, u32[]{:S(2)}, u32[]{:S(2)}) collective-permute-start(f32[4,64,128]{2,1,0:T(8,128)S(1)} %get-tuple-element.48), channel_id=1, source_target_pairs={{8,16},{24,25},{17,9},{1,2},{10,18},{26,27},{19,11},{3,4},{12,20},... | collective-permute-start | bytes 393224 | tf_op jit(solution)/shard_map/ppermute | solution.py:346
  48.4 8.5 %collective-permute-start.12 = (f32[8,64,128]{2,1,0:T(8,128)S(1)}, f32[8,64,128]{2,1,0:T(8,128)S(1)}, u32[]{:S(2)}, u32[]{:S(2)}) collective-permute-start(f32[8,64,128]{2,1,0:T(8,128)S(1)} %shard_map.51.refs_3_), channel_id=1, source_target_pairs={{8,16},{24,25},{17,9},{1,2},{10,18},{26,27},{19,11},{3,4},{12,20},... | collective-permute-start | bytes 786440 | tf_op jit(solution)/shard_map/ppermute | solution.py:346
  49.1 9.0 %collective-permute-start.11 = (f32[8,64,128]{2,1,0:T(8,128)S(1)}, f32[8,64,128]{2,1,0:T(8,128)S(1)}, u32[]{:S(2)}, u32[]{:S(2)}) collective-permute-start(f32[8,64,128]{2,1,0:T(8,128)S(1)} %shard_map.51.refs_3_), channel_id=1, source_target_pairs={{0,8},{8,0},{16,24},{24,16},{1,9},{9,1},{17,25},{25,17},{2,10},{10... | collective-permute-start | bytes 786440 | tf_op jit(solution)/shard_map/ppermute | solution.py:335
  89.3 6.4 %collective-permute-start.14 = (f32[64,8,128]{2,1,0:T(8,128)S(1)}, f32[64,8,128]{2,1,0:T(8,128)S(1)}, u32[]{:S(2)}, u32[]{:S(2)}) collective-permute-start(f32[64,8,128]{2,1,0:T(8,128)S(1)} %bitcast.21), channel_id=1, source_target_pairs={{0,16},{8,24},{16,0},{24,8},{1,17},{9,25},{17,1},{25,9},{2,18},{10... | collective-permute-start | bytes 786440 | tf_op jit(solution)/shard_map/ppermute | solution.py:335
  89.4 6.3 %collective-permute-start.13 = (f32[64,8,128]{2,1,0:T(8,128)S(1)}, f32[64,8,128]{2,1,0:T(8,128)S(1)}, u32[]{:S(2)}, u32[]{:S(2)}) collective-permute-start(f32[64,8,128]{2,1,0:T(8,128)S(1)} %bitcast.22), channel_id=1, source_target_pairs={{0,8},{8,0},{16,24},{24,16},{1,9},{9,1},{17,25},{25,17},{2,10},{10... | collective-permute-start | bytes 786440 | tf_op jit(solution)/shard_map/ppermute | solution.py:335
  95.7 1.5 %collective-permute-start.15 = (f32[64,8,128]{2,1,0:T(8,128)S(1)}, f32[64,8,128]{2,1,0:T(8,128)S(1)}, u32[]{:S(2)}, u32[]{:S(2)}) collective-permute-start(f32[64,8,128]{2,1,0:T(8,128)S(1)} %collective-permute-done.14.refs_2_), channel_id=1, source_target_pairs={{0,8},{8,0},{16,24},{24,16},{1,9},{9,1},{17,25},{25,17},{2,10},{10... | collective-permute-start | bytes 786440 | tf_op jit(solution)/shard_map/ppermute | solution.py:335

commit v14 on v13

--- a/solution.py
+++ b/solution.py
@@ -18,6 +18,11 @@
     high = value.astype(jnp.bfloat16)
     low = (value - high.astype(jnp.float32)).astype(jnp.bfloat16)
     return high, low
+
+
+def slab_index():
+    me, odd = lax.axis_index("view"), lax.axis_index("vol") % 2
+    return me + odd * (lax.axis_size("view") - 1 - 2 * me)
 
 
 def row_matrix(weights, first):
@@ -43,13 +48,13 @@
     return total[:, :width], total[:, width:]
 
 
-def bound_kernel(place_ref, weights_hbm, offsets_hbm, raw_hbm, out_ref, weights_ref, offsets_ref, planes_ref, sems):
+def bound_kernel(weights_hbm, offsets_hbm, raw_hbm, out_ref, weights_ref, offsets_ref, planes_ref, sems):
     view = pl.program_id(0)
     depth, rim = raw_hbm.shape[1], out_ref.shape[1]
 
     @pl.when(view == 0)
     def _():
-        start = (depth - rim) * (1 - place_ref[0])
+        start = (depth - rim) * (1 - slab_index() // CORES)
         pairs = [(weights_hbm, weights_ref), (offsets_hbm, offsets_ref), (raw_hbm.at[:, pl.ds(start, rim)], planes_ref)]
         copies = [pltpu.make_async_copy(*pair, sems.at[i]) for i, pair in enumerate(pairs)]
         for copy in copies:
@@ -62,7 +67,7 @@
         out_ref[0, z], out_ref[0, z + 1] = two_rows(left, planes_ref[view, z], planes_ref[view, z + 1])
 
 
-def resample_bound(place, weights, offsets, raw, rim):
+def resample_bound(weights, offsets, raw, rim):
     views, _, rows, width = raw.shape
     shape = (views, rim, rows, width)
     weights = weights.transpose(0, 2, 1)
@@ -70,7 +75,7 @@
         bound_kernel,
         grid=(views,),
         out_shape=jax.ShapeDtypeStruct(shape, jnp.bfloat16),
-        in_specs=[SMEM] + [pl.BlockSpec(memory_space=pltpu.HBM)] * 3,
+        in_specs=[pl.BlockSpec(memory_space=pltpu.HBM)] * 3,
         out_specs=pl.BlockSpec((1,) + shape[1:], lambda v: (v, 0, 0, 0)),
         scratch_shapes=[
             pltpu.VMEM(weights.shape, jnp.float32),
@@ -79,7 +84,7 @@
             pltpu.SemaphoreType.DMA((3,)),
         ],
         compiler_params=pltpu.CompilerParams(vmem_limit_bytes=63 * 1024 * 1024),
-    )(place, weights, offsets, raw)
+    )(weights, offsets, raw)
 
 
 def resample_kernel(plan, place_ref, weights_ref, offsets_ref, raw_ref, *outs):
@@ -147,12 +152,17 @@
     if views is not None:
         partial_ref, refs = refs[0], refs[1:]
     groups = 2
-    inner, bound, edge = refs[:groups], refs[groups : 2 * groups], refs[2 * groups : 3 * groups]
-    bricks_ref, start_ref = refs[3 * groups : 3 * groups + 2]
+    extra = 2 if views is None else 4
+    inner, (bound, edge) = refs[: -2 * groups - extra - 1], [
+        refs[i - groups - extra - 1 : i - extra - 1] for i in (-groups, 0)
+    ]
+    pieces = len(inner) // groups
+    bricks_ref, start_ref = refs[-extra - 1 : 1 - extra]
     window = refs[-1]
     step = pl.program_id(0)
     half, core = place_ref[0], place_ref[1]
-    main = inner[0].shape[1]
+    piece = inner[0].shape[1]
+    main = pieces * piece
 
     @pl.when(step == 0)
     def _():
@@ -160,7 +170,7 @@
 
     for group in range(groups):
         for z in range(main):
-            window[group, 2 * rim * (1 - half) + z] = inner[group][0, z]
+            window[group, 2 * rim * (1 - half) + z] = inner[group * pieces + z // piece][0, z % piece]
         for z in range(rim):
             window[group, rim + (main - rim) * half + z] = bound[group][0, z]
             window[group, (main + rim) * half + z] = edge[group][0, z]
@@ -173,7 +183,7 @@
         start_ref[z] = total
 
     if views is not None:
-        near_ref, cross_ref = refs[3 * groups + 2 : 3 * groups + 4]
+        near_ref, cross_ref = refs[-3:-1]
 
         @pl.when(step == pl.num_programs(0) - 1)
         def _():
@@ -185,8 +195,9 @@
 
 
 def gather_views(place, inner, bound, edge, planes, side, views=None, partial=None):
-    groups = len(inner)
+    groups = len(bound)
     count, main, rows, width = inner[0].shape
+    main = main * len(inner) // groups
     rim = edge[0].shape[1]
     take = lambda part: 0 if part.shape[0] == count else side * count
     outer = planes + 2 * rim
@@ -209,7 +220,7 @@
 
 def update_kernel(paired, place_ref, taps_ref, lefts_ref, rights_ref, *refs):
     bricks_refs, (first_ref, own_ref, second_ref, out_ref) = refs[:2], refs[2:6]
-    volume, ratios, held, logs = refs[6:]
+    volume, ratios, logs = refs[6:]
     bricks = [ref.at[group] for ref in bricks_refs for group in range(ref.shape[0])]
     count = len(bricks)
     step = pl.program_id(0)
@@ -261,23 +272,23 @@
         size = 2 if length % 4 else 4
         return [(z, size) for z in range(0, length, size)]
 
-    for group in range(count):
-        view = group * pl.num_programs(0) + step
-        ratio = ratios.at[group % 2]
-        gains = [taps_ref[view, 0, t] for t in range(taps)]
+    for first in range(0, count, 2):
+        pair = (first, first + 1)
+        gains = [[taps_ref[group * pl.num_programs(0) + step, 0, t] for t in range(taps)] for group in pair]
         for z, size in chunks(outer):
-            fields = chain(volume, gains, lefts_ref[group, 0, 0], rights_ref[group, 0, 0], z, size)
-            for i, blurred in enumerate(fields):
-                guess = pl.reciprocal(blurred, approx=True)
-                guess = guess * (2.0 - blurred * guess)
-                ratio[z + i] = bricks[group][0, z + i].astype(jnp.float32) * guess
+            for group, gain in zip(pair, gains):
+                fields = chain(volume, gain, lefts_ref[group, 0, 0], rights_ref[group, 0, 0], z, size)
+                for i, blurred in enumerate(fields):
+                    guess = pl.reciprocal(blurred, approx=True)
+                    guess = guess * (2.0 - blurred * guess)
+                    ratios[group, z + i] = bricks[group][0, z + i].astype(jnp.float32) * guess
         for z, size in chunks(planes):
-            fields = chain(ratio, gains[::-1], lefts_ref[group, 0, 1], rights_ref[group, 0, 1], z, size)
-            for i, back in enumerate(fields):
-                if group % 2 == 0:
-                    held[z + i] = back
-                else:
-                    logs[z + i] += jnp.log(held[z + i] * back)
+            backs = [
+                chain(ratios.at[group], gain[::-1], lefts_ref[group, 0, 1], rights_ref[group, 0, 1], z, size)
+                for group, gain in zip(pair, gains)
+            ]
+            for i in range(size):
+                logs[z + i] += jnp.log(backs[0][i] * backs[1][i])
 
     @pl.when(step == pl.num_programs(0) - 1)
     def _():
@@ -301,8 +312,7 @@
         out_specs=VMEM,
         scratch_shapes=[
             pltpu.VMEM((2 * outer - planes, rows, width), jnp.float32),
-            pltpu.VMEM((2, outer, rows, width), jnp.float32),
-            pltpu.VMEM((planes, rows, width), jnp.float32),
+            pltpu.VMEM((groups, outer, rows, width), jnp.float32),
             pltpu.VMEM((planes, rows, width), jnp.float32),
         ],
         compiler_params=PARAMS,
@@ -367,8 +377,7 @@
     rim = (psf_taps.shape[2] - 1) // 2
     planes = depth // members
     me = lax.axis_index("view")
-    odd = lax.axis_index("vol") % 2
-    slab = jnp.where(odd == 1, members - 1 - me, me)
+    slab = slab_index()
     place = jnp.stack([slab // CORES, slab % CORES]).astype(jnp.int32)
 
     near_bit, far_bit = 1, CORES
@@ -379,7 +388,7 @@
     bound, inner = (0, depth - rim), (rim, 2 * planes - rim)
 
     cross_taps = partner(psf_taps, near_bit + far_bit, members)
-    far_bound = resample_bound(place, weights, offsets, raw_views, rim)
+    far_bound = resample_bound(weights, offsets, raw_views, rim)
     far_bound, raw_later, cross_taps = lax.optimization_barrier((far_bound, raw_views, cross_taps))
     far_bound = far(far_bound)
     far_inner, own_bound, own_inner = resample(

time: 98.6 us -> 96.1 us (0.975)
  Pallas kernels: 37 us -> 35 us
    pallas_call x2, Pallas kernels: 24.1 us -> 22.8 us  [update(): pl.pallas_call(functools.partial(update_kernel, paired), grid=(count,), o...]
  transfers between devices with their start and end apart: 16 -> 16, of which waited for: 9 -> 9; matrix products, arithmetic and copies ran while one was open for 1% -> 1% of each run, Pallas kernels for 11% -> 10%
where the time goes in v14:
time: 96.1 us; the launch traced here: 95.9 us
  Pallas kernels  35 us (36%)
  waiting for transfers between devices  23.7 us (25%)
  blocking collectives  19.1 us (20%)
  starting transfers between devices  15.6 us (16%)
  local copies, waits for them, and re-layouts  1.92 us (2%)
    ppermute x13, waiting for transfers between devices, partner(): return lax.ppermute(value, 'view', [(i, i ^ bit) for i in range(members)])  23.7 us
    pallas_call x2, Pallas kernels, update(): pl.pallas_call(functools.partial(update_kernel, paired), grid=(count,), o...  22.8 us
    all_to_all x1, blocking collectives, per_device(): lax.all_to_all(joined, 'vol', split_axis=1, concat_axis=0, tiled=True)  19.1 us
    ppermute x13, starting transfers between devices, partner(): return lax.ppermute(value, 'view', [(i, i ^ bit) for i in range(members)])  13.5 us
    pallas_call x1, Pallas kernels, bands(): pl.pallas_call(bands_kernel, grid=(views,), out_shape=[jax.ShapeDtypeStru...  3.34 us
    pallas_call x1, Pallas kernels, resample_bound(): pl.pallas_call(bound_kernel, grid=(views,), out_shape=jax.ShapeDtypeStruc...  2.86 us
    pallas_call x2, Pallas kernels, gather_views(): pl.pallas_call(functools.partial(gather_kernel, views, planes, rim), grid...  2.6 us
    pallas_call x1, Pallas kernels, resample(): pl.pallas_call(functools.partial(resample_kernel, plan), grid=(views,), o...  2.34 us
  transfers between devices with their start and end apart: 16, of which 9 were waited for; matrix products, arithmetic and copies ran while one was open for 1% of the time, Pallas kernels for 10%

profile of v14, /device:TPU:0, one launch (start us, length us, event | category | flops | bytes accessed | tf_op | source)
XLA Modules:
  0.0 95.9 jit_solution(4690952021824823539)
XLA Ops:
  0.0 0.0 copy-start.2
  0.0 0.0 copy-start.1
  0.0 2.4 %collective-permute-start = (f32[3,3,9]{2,1,0:T(4,128)}, f32[3,3,9]{2,1,0:T(4,128)S(1)}, u32[]{:S(2)}, u32[]{:S(2)}) collective-permute-start(f32[3,3,9]{2,1,0:T(4,128)} %param.7), channel_id=1, source_target_pairs={{0,24},{8,16},{16,8},{24,0},{1,25},{9,17},{17,9},{25,1},{2,26},{10... | collective-permute-start | bytes 980 | tf_op jit(solution)/shard_map/ppermute | solution.py:345
  2.4 0.1 pad_add_fusion.place_ref
  2.5 0.0 copy-start.3
  2.5 2.9 %shard_map.46 = bf16[3,4,64,128]{3,2,1,0:T(8,128)(2,1)} custom-call(f32[3,8,64]{2,1,0:T(8,128)} %bitcast.24, s32[3,64]{1,0:T(4,128)} %offsets_ref.1, bf16[3,32,64,128]{3,2,1,0:T(8,128)(2,1)} %raw_ref), custom_call_target="tpu_custom_call" | custom-call | tf_op jit(solution)/shard_map/pallas_call | solution.py:74
  5.3 0.0 collective-permute-done
  5.3 0.9 collective-permute-start.2
  6.3 0.0 copy-done.2
  6.3 0.0 copy-done.1
  6.3 0.0 copy-start
  6.3 1.4 %copy-done = bf16[3,32,64,128]{3,2,1,0:T(8,128)(2,1)S(1)} copy-done((bf16[3,32,64,128]{3,2,1,0:T(8,128)(2,1)S(1)}, bf16[3,32,64,128]{3,2,1,0:T(8,128)(2,1)}, u32[]{:S(2)}) %copy-start) | copy-done | bytes 1572888
  7.7 2.3 %shard_map.47 = (bf16[3,16,64,128]{3,2,1,0:T(8,128)(2,1)S(1)}, bf16[3,4,64,128]{3,2,1,0:T(8,128)(2,1)S(1)}, bf16[3,16,64,128]{3,2,1,0:T(8,128)(2,1)S(1)}) custom-call(s32[2]{0:T(128)S(1)} %pad_add_fusion.place_ref, f32[3,8,64]{2,1,0:T(8,128)S(1)} %bitcast.25, s32[3,64]{1,0:T(4,128)S(1)} %copy-done.2, bf16[3,32,64,128]{3,2,1,0:T(8,128)(2,1)S(1)} %copy-done), custom_call_target="tpu_custom_call" | custom-call | tf_op jit(solution)/shard_map/pallas_call | solution.py:102
  10.0 0.0 copy-done.3
  10.0 0.1 collective-permute-start.1
  10.1 1.6 %collective-permute-start.4 = (bf16[3,16,64,128]{3,2,1,0:T(8,128)(2,1)S(1)}, bf16[3,16,64,128]{3,2,1,0:T(8,128)(2,1)S(1)}, u32[]{:S(2)}, u32[]{:S(2)}) collective-permute-start(bf16[3,16,64,128]{3,2,1,0:T(8,128)(2,1)S(1)} %get-tuple-element.37), channel_id=1, source_target_pairs={{0,16},{8,24},{16,0},{24,8},{1,17},{9,25},{17,1},{25,9},{2,18},{10... | collective-permute-start | bytes 2359304 | tf_op jit(solution)/shard_map/ppermute | solution.py:345
  11.8 0.0 collective-permute-start.5
  11.8 0.0 collective-permute-done.1
  11.8 0.1 fusion
  11.9 0.1 broadcast_divide_fusion
  12.0 1.1 %collective-permute-done.2 = bf16[3,4,64,128]{3,2,1,0:T(8,128)(2,1)S(1)} collective-permute-done((bf16[3,4,64,128]{3,2,1,0:T(8,128)(2,1)}, bf16[3,4,64,128]{3,2,1,0:T(8,128)(2,1)S(1)}, u32[]{:S(2)}, u32[]{:S(2)}) %collective-permute-start.2) | collective-permute-done | bytes 196640 | tf_op jit(solution)/shard_map/ppermute | solution.py:345
  13.1 0.7 collective-permute-start.3
  13.8 0.3 slice_reduce_fusion
  14.1 0.1 slice_divide_fusion
  14.2 3.3 %shard_map.48 = (bf16[12,2,64,192]{3,2,1,0:T(8,128)(2,1)S(1)}, bf16[12,2,128,256]{3,2,1,0:T(8,128)(2,1)S(1)}) custom-call(f32[12,3,9]{2,1,0:T(4,128)S(1)} %pad_maximum_fusion.1.taps_ref), custom_call_target="tpu_custom_call" | custom-call | tf_op jit(solution)/shard_map/pallas_call | solution.py:140
  17.6 0.1 collective-permute-start.6
  17.6 0.0 collective-permute-done.3.refs_4_.refs_5_
  17.7 0.5 collective-permute-start.7
  18.1 1.2 %collective-permute-done.6.refs_3_.refs_4_ = bf16[6,4,64,128]{3,2,1,0:T(8,128)(2,1)S(1)} collective-permute-done((bf16[6,4,64,128]{3,2,1,0:T(8,128)(2,1)S(1)}, bf16[6,4,64,128]{3,2,1,0:T(8,128)(2,1)S(1)}, u32[]{:S(2)}, u32[]{:S(2)}) %collective-permute-start.6) | collective-permute-done | bytes 393248 | tf_op jit(solution)/shard_map/ppermute | solution.py:345
  19.4 0.0 collective-permute-done.5.refs_1_
  19.4 0.6 collective-permute-done.7.refs_5_.refs_6_
  19.9 1.3 %shard_map.49 = (bf16[2,3,16,64,128]{4,3,2,1,0:T(8,128)(2,1)S(1)}, f32[16,64,128]{2,1,0:T(8,128)S(1)}) custom-call(s32[2]{0:T(128)S(1)} %pad_add_fusion.place_ref, bf16[3,16,64,128]{3,2,1,0:T(8,128)(2,1)S(1)} %get-tuple-element.38.refs_0_, bf16[3,16,64,128]{3,2,1,0:T(8,128)(2,1)S(1)} %collective-permute-done.5.refs_1_, ...), custom_call_target="tpu_custom_call" | custom-call | tf_op jit(solution)/shard_map/pallas_call | solution.py:207
  21.2 9.0 %collective-permute-done.4.refs_1_ = bf16[3,16,64,128]{3,2,1,0:T(8,128)(2,1)S(1)} collective-permute-done((bf16[3,16,64,128]{3,2,1,0:T(8,128)(2,1)S(1)}, bf16[3,16,64,128]{3,2,1,0:T(8,128)(2,1)S(1)}, u32[]{:S(2)}, u32[]{:S(2)}) %collective-permute-start.4) | collective-permute-done | bytes 786464 | tf_op jit(solution)/shard_map/ppermute | solution.py:345
  30.1 0.0 collective-permute-start.8
  30.2 2.3 %collective-permute-done.8.refs_2_ = bf16[3,16,64,128]{3,2,1,0:T(8,128)(2,1)S(1)} collective-permute-done((bf16[3,16,64,128]{3,2,1,0:T(8,128)(2,1)S(1)}, bf16[3,16,64,128]{3,2,1,0:T(8,128)(2,1)S(1)}, u32[]{:S(2)}, u32[]{:S(2)}) %collective-permute-start.8) | collective-permute-done | bytes 786464 | tf_op jit(solution)/shard_map/ppermute | solution.py:345
  32.4 1.3 %shard_map.50 = (bf16[2,3,16,64,128]{4,3,2,1,0:T(8,128)(2,1)S(1)}, f32[16,64,128]{2,1,0:T(8,128)S(1)}, f32[4,64,128]{2,1,0:T(8,128)S(1)}, f32[4,64,128]{2,1,0:T(8,128)S(1)}) custom-call(s32[2]{0:T(128)S(1)} %pad_add_fusion.place_ref, f32[16,64,128]{2,1,0:T(8,128)S(1)} %get-tuple-element.43.refs_0_, ...), custom_call_target="tpu_custom_call" | custom-call | tf_op jit(solution)/shard_map/pallas_call | solution.py:207
  33.8 0.2 collective-permute-start.9
  34.0 0.7 collective-permute-start.10
  34.6 0.5 collective-permute-done.9.refs_2_
  35.2 0.0 collective-permute-done.10.refs_4_
  35.2 11.4 %shard_map.51.refs_3_ = f32[8,64,128]{2,1,0:T(8,128)S(1)} custom-call(s32[2]{0:T(128)S(1)} %pad_add_fusion.place_ref, f32[12,3,9]{2,1,0:T(4,128)S(1)} %pad_maximum_fusion.1.taps_ref, bf16[4,3,2,64,192]{4,3,2,1,0:T(8,128)(2,1)S(1)} %bitcast.19, bf16[4,3,2,128,256]{4,3,2,1,0:T(8,128)(2,1)S(1)} %bitcast.17, ...), custom_call_target="tpu_custom_call" | custom-call | tf_op jit(solution)/shard_map/pallas_call | solution.py:304
  46.6 0.7 collective-permute-start.12
  47.3 7.6 %collective-permute-start.11 = (f32[8,64,128]{2,1,0:T(8,128)S(1)}, f32[8,64,128]{2,1,0:T(8,128)S(1)}, u32[]{:S(2)}, u32[]{:S(2)}) collective-permute-start(f32[8,64,128]{2,1,0:T(8,128)S(1)} %shard_map.51.refs_3_), channel_id=1, source_target_pairs={{0,8},{8,0},{16,24},{24,16},{1,9},{9,1},{17,25},{25,17},{2,10},{10... | collective-permute-start | bytes 786440 | tf_op jit(solution)/shard_map/ppermute | solution.py:345
  54.9 0.0 collective-permute-done.12.refs_4_
  54.9 1.2 %collective-permute-done.11.refs_2_ = f32[8,64,128]{2,1,0:T(8,128)S(1)} collective-permute-done((f32[8,64,128]{2,1,0:T(8,128)S(1)}, f32[8,64,128]{2,1,0:T(8,128)S(1)}, u32[]{:S(2)}, u32[]{:S(2)}) %collective-permute-start.11) | collective-permute-done | bytes 262176 | tf_op jit(solution)/shard_map/ppermute | solution.py:345
  56.1 11.4 %shard_map.52 = f32[8,64,128]{2,1,0:T(8,128)S(1)} custom-call(s32[2]{0:T(128)S(1)} %pad_add_fusion.place_ref, f32[12,3,9]{2,1,0:T(4,128)S(1)} %pad_maximum_fusion.1.taps_ref, bf16[4,3,2,64,192]{4,3,2,1,0:T(8,128)(2,1)S(1)} %bitcast.20, bf16[4,3,2,128,256]{4,3,2,1,0:T(8,128)(2,1)S(1)} %bitcast.18, bf16[2,3,16,64,128]{4,3,2,1,0:T(8,128)(2,1)S(1)} %get-tuple-element.42.refs_0_, ...), custom_call_target="tpu_custom_call" | custom-call | tf_op jit(solution)/shard_map/pallas_call | solution.py:304
  67.5 0.2 copy.7
  67.7 19.1 %all_to_all.18 = f32[8,64,128]{2,0,1:T(8,128)S(1)} all-to-all(f32[8,64,128]{2,0,1:T(8,128)S(1)} %copy.7), channel_id=1, replica_groups=mesh['view'=4,'vol'=8] {'vol'}, dimensions={1} | all-to-all | bytes 524288 | tf_op jit(solution)/shard_map/all_to_all | solution.py:436
  86.8 0.1 collective-permute-start.14
  86.9 0.1 collective-permute-start.13
  87.0 6.3 %collective-permute-done.14.refs_2_ = f32[64,8,128]{2,1,0:T(8,128)S(1)} collective-permute-done((f32[64,8,128]{2,1,0:T(8,128)S(1)}, f32[64,8,128]{2,1,0:T(8,128)S(1)}, u32[]{:S(2)}, u32[]{:S(2)}) %collective-permute-start.14) | collective-permute-done | bytes 262176 | tf_op jit(solution)/shard_map/ppermute | solution.py:345
  93.3 0.0 collective-permute-start.15
  93.3 0.0 collective-permute-done.13.refs_1_
  93.3 1.5 %collective-permute-done.15.refs_3_ = f32[64,8,128]{2,1,0:T(8,128)S(1)} collective-permute-done((f32[64,8,128]{2,1,0:T(8,128)S(1)}, f32[64,8,128]{2,1,0:T(8,128)S(1)}, u32[]{:S(2)}, u32[]{:S(2)}) %collective-permute-start.15) | collective-permute-done | bytes 262176 | tf_op jit(solution)/shard_map/ppermute | solution.py:345
  94.8 1.0 %shard_map.53 = f32[8,4,8,8,128]{4,3,2,1,0:T(8,128)} custom-call(s32[1]{0:T(128)} %bitcast.place_ref, f32[64,8,128]{2,1,0:T(8,128)S(1)} %bitcast.23, f32[64,8,128]{2,1,0:T(8,128)S(1)} %collective-permute-done.13.refs_1_, f32[64,8,128]{2,1,0:T(8,128)S(1)} %collective-permute-done.14.refs_2_, f32[64,8,128]{2,1,0:T(8,128)S(1)} %collective-permute-done.15.refs_3_), custom_call_target="tpu_custom_call" | custom-call | tf_op jit(solution)/shard_map/pallas_call | solution.py:335
  (6 shorter events, 0.1 us)
Async XLA Ops:
  0.0 6.3 %copy-start.2 = (s32[3,64]{1,0:T(4,128)S(1)}, s32[3,64]{1,0:T(4,128)}, u32[]{:S(2)}) copy-start(s32[3,64]{1,0:T(4,128)} %offsets_ref.1) | copy-start | bytes 2308
  0.0 6.3 %copy-start.1 = (f32[3,64,8]{1,2,0:T(8,128)S(1)}, f32[3,64,8]{1,2,0:T(8,128)}, u32[]{:S(2)}) copy-start(f32[3,64,8]{1,2,0:T(8,128)} %param.5) | copy-start | bytes 18436
  0.0 5.3 %collective-permute-start = (f32[3,3,9]{2,1,0:T(4,128)}, f32[3,3,9]{2,1,0:T(4,128)S(1)}, u32[]{:S(2)}, u32[]{:S(2)}) collective-permute-start(f32[3,3,9]{2,1,0:T(4,128)} %param.7), channel_id=1, source_target_pairs={{0,24},{8,16},{16,8},{24,0},{1,25},{9,17},{17,9},{25,1},{2,26},{10... | collective-permute-start | bytes 980 | tf_op jit(solution)/shard_map/ppermute | solution.py:345
  2.5 7.6 %copy-start.3 = (f32[3,3,9]{2,1,0:T(4,128)S(1)}, f32[3,3,9]{2,1,0:T(4,128)}, u32[]{:S(2)}) copy-start(f32[3,3,9]{2,1,0:T(4,128)} %param.7) | copy-start | bytes 976
  5.3 7.8 %collective-permute-start.2 = (bf16[3,4,64,128]{3,2,1,0:T(8,128)(2,1)}, bf16[3,4,64,128]{3,2,1,0:T(8,128)(2,1)S(1)}, u32[]{:S(2)}, u32[]{:S(2)}) collective-permute-start(bf16[3,4,64,128]{3,2,1,0:T(8,128)(2,1)} %shard_map.46), channel_id=1, source_target_pairs={{0,16},{8,24},{16,0},{24,8},{1,17},{9,25},{17,1},{25,9},{2,18},{10... | collective-permute-start | bytes 589832 | tf_op jit(solution)/shard_map/ppermute | solution.py:345
  6.3 1.4 %copy-start = (bf16[3,32,64,128]{3,2,1,0:T(8,128)(2,1)S(1)}, bf16[3,32,64,128]{3,2,1,0:T(8,128)(2,1)}, u32[]{:S(2)}) copy-start(bf16[3,32,64,128]{3,2,1,0:T(8,128)(2,1)} %raw_ref) | copy-start | bytes 4718596
  10.0 1.7 %collective-permute-start.1 = (f32[2,3,3,9]{3,2,1,0:T(4,128)S(1)}, f32[2,3,3,9]{3,2,1,0:T(4,128)S(1)}, u32[]{:S(2)}, u32[]{:S(2)}) collective-permute-start(f32[2,3,3,9]{3,2,1,0:T(4,128)S(1)} %pad_maximum_fusion.2), channel_id=1, source_target_pairs={{0,8},{8,0},{16,24},{24,16},{1,9},{9,1},{17,25},{25,17},{2,10},{10... | collective-permute-start | bytes 1952 | tf_op jit(solution)/shard_map/ppermute | solution.py:345
  10.1 20.0 %collective-permute-start.4 = (bf16[3,16,64,128]{3,2,1,0:T(8,128)(2,1)S(1)}, bf16[3,16,64,128]{3,2,1,0:T(8,128)(2,1)S(1)}, u32[]{:S(2)}, u32[]{:S(2)}) collective-permute-start(bf16[3,16,64,128]{3,2,1,0:T(8,128)(2,1)S(1)} %get-tuple-element.37), channel_id=1, source_target_pairs={{0,16},{8,24},{16,0},{24,8},{1,17},{9,25},{17,1},{25,9},{2,18},{10... | collective-permute-start | bytes 2359304 | tf_op jit(solution)/shard_map/ppermute | solution.py:345
  11.8 7.6 %collective-permute-start.5 = (bf16[3,16,64,128]{3,2,1,0:T(8,128)(2,1)S(1)}, bf16[3,16,64,128]{3,2,1,0:T(8,128)(2,1)S(1)}, u32[]{:S(2)}, u32[]{:S(2)}) collective-permute-start(bf16[3,16,64,128]{3,2,1,0:T(8,128)(2,1)S(1)} %get-tuple-element.38.refs_0_), channel_id=1, source_target_pairs={{0,8},{8,0},{16,24},{24,16},{1,9},{9,1},{17,25},{25,17},{2,10},{10... | collective-permute-start | bytes 2359304 | tf_op jit(solution)/shard_map/ppermute | solution.py:345
  13.1 4.5 %collective-permute-start.3 = (bf16[6,4,64,128]{3,2,1,0:T(8,128)(2,1)S(1)}, bf16[6,4,64,128]{3,2,1,0:T(8,128)(2,1)S(1)}, u32[]{:S(2)}, u32[]{:S(2)}) collective-permute-start(bf16[6,4,64,128]{3,2,1,0:T(8,128)(2,1)S(1)} %constant_dynamic-update-slice_fusion.refs_2_.refs_3_), channel_id=1, source_target_pairs={{24,25},{16,17},{1,2},{9,10},{26,27},{18,19},{3,4},{11,12},{28,29}... | collective-permute-start | bytes 1179656 | tf_op jit(solution)/shard_map/ppermute | solution.py:356
  17.6 1.8 %collective-permute-start.6 = (bf16[6,4,64,128]{3,2,1,0:T(8,128)(2,1)S(1)}, bf16[6,4,64,128]{3,2,1,0:T(8,128)(2,1)S(1)}, u32[]{:S(2)}, u32[]{:S(2)}) collective-permute-start(bf16[6,4,64,128]{3,2,1,0:T(8,128)(2,1)S(1)} %constant_dynamic-update-slice_fusion.refs_2_.refs_3_), channel_id=1, source_target_pairs={{0,8},{8,0},{16,24},{24,16},{1,9},{9,1},{17,25},{25,17},{2,10},{10... | collective-permute-start | bytes 1179656 | tf_op jit(solution)/shard_map/ppermute | solution.py:345
  17.7 2.3 %collective-permute-start.7 = (bf16[6,4,64,128]{3,2,1,0:T(8,128)(2,1)S(1)}, bf16[6,4,64,128]{3,2,1,0:T(8,128)(2,1)S(1)}, u32[]{:S(2)}, u32[]{:S(2)}) collective-permute-start(bf16[6,4,64,128]{3,2,1,0:T(8,128)(2,1)S(1)} %collective-permute-done.3.refs_4_.refs_5_), channel_id=1, source_target_pairs={{0,8},{8,0},{16,24},{24,16},{1,9},{9,1},{17,25},{25,17},{2,10},{10... | collective-permute-start | bytes 1179656 | tf_op jit(solution)/shard_map/ppermute | solution.py:345
  30.1 2.3 %collective-permute-start.8 = (bf16[3,16,64,128]{3,2,1,0:T(8,128)(2,1)S(1)}, bf16[3,16,64,128]{3,2,1,0:T(8,128)(2,1)S(1)}, u32[]{:S(2)}, u32[]{:S(2)}) collective-permute-start(bf16[3,16,64,128]{3,2,1,0:T(8,128)(2,1)S(1)} %collective-permute-done.4.refs_1_), channel_id=1, source_target_pairs={{0,8},{8,0},{16,24},{24,16},{1,9},{9,1},{17,25},{25,17},{2,10},{10... | collective-permute-start | bytes 2359304 | tf_op jit(solution)/shard_map/ppermute | solution.py:345
  33.8 1.4 %collective-permute-start.9 = (f32[4,64,128]{2,1,0:T(8,128)S(1)}, f32[4,64,128]{2,1,0:T(8,128)S(1)}, u32[]{:S(2)}, u32[]{:S(2)}) collective-permute-start(f32[4,64,128]{2,1,0:T(8,128)S(1)} %get-tuple-element.46), channel_id=1, source_target_pairs={{0,8},{8,0},{16,24},{24,16},{1,9},{9,1},{17,25},{25,17},{2,10},{10... | collective-permute-start | bytes 393224 | tf_op jit(solution)/shard_map/ppermute | solution.py:345
  34.0 1.2 %collective-permute-start.10 = (f32[4,64,128]{2,1,0:T(8,128)S(1)}, f32[4,64,128]{2,1,0:T(8,128)S(1)}, u32[]{:S(2)}, u32[]{:S(2)}) collective-permute-start(f32[4,64,128]{2,1,0:T(8,128)S(1)} %get-tuple-element.48), channel_id=1, source_target_pairs={{8,16},{24,25},{17,9},{1,2},{10,18},{26,27},{19,11},{3,4},{12,20},... | collective-permute-start | bytes 393224 | tf_op jit(solution)/shard_map/ppermute | solution.py:356
  46.6 8.3 %collective-permute-start.12 = (f32[8,64,128]{2,1,0:T(8,128)S(1)}, f32[8,64,128]{2,1,0:T(8,128)S(1)}, u32[]{:S(2)}, u32[]{:S(2)}) collective-permute-start(f32[8,64,128]{2,1,0:T(8,128)S(1)} %shard_map.51.refs_3_), channel_id=1, source_target_pairs={{8,16},{24,25},{17,9},{1,2},{10,18},{26,27},{19,11},{3,4},{12,20},... | collective-permute-start | bytes 786440 | tf_op jit(solution)/shard_map/ppermute | solution.py:356
  47.3 8.8 %collective-permute-start.11 = (f32[8,64,128]{2,1,0:T(8,128)S(1)}, f32[8,64,128]{2,1,0:T(8,128)S(1)}, u32[]{:S(2)}, u32[]{:S(2)}) collective-permute-start(f32[8,64,128]{2,1,0:T(8,128)S(1)} %shard_map.51.refs_3_), channel_id=1, source_target_pairs={{0,8},{8,0},{16,24},{24,16},{1,9},{9,1},{17,25},{25,17},{2,10},{10... | collective-permute-start | bytes 786440 | tf_op jit(solution)/shard_map/ppermute | solution.py:345
  86.8 6.4 %collective-permute-start.14 = (f32[64,8,128]{2,1,0:T(8,128)S(1)}, f32[64,8,128]{2,1,0:T(8,128)S(1)}, u32[]{:S(2)}, u32[]{:S(2)}) collective-permute-start(f32[64,8,128]{2,1,0:T(8,128)S(1)} %bitcast.21), channel_id=1, source_target_pairs={{0,16},{8,24},{16,0},{24,8},{1,17},{9,25},{17,1},{25,9},{2,18},{10... | collective-permute-start | bytes 786440 | tf_op jit(solution)/shard_map/ppermute | solution.py:345
  86.9 6.4 %collective-permute-start.13 = (f32[64,8,128]{2,1,0:T(8,128)S(1)}, f32[64,8,128]{2,1,0:T(8,128)S(1)}, u32[]{:S(2)}, u32[]{:S(2)}) collective-permute-start(f32[64,8,128]{2,1,0:T(8,128)S(1)} %bitcast.22), channel_id=1, source_target_pairs={{0,8},{8,0},{16,24},{24,16},{1,9},{9,1},{17,25},{25,17},{2,10},{10... | collective-permute-start | bytes 786440 | tf_op jit(solution)/shard_map/ppermute | solution.py:345
  93.3 1.5 %collective-permute-start.15 = (f32[64,8,128]{2,1,0:T(8,128)S(1)}, f32[64,8,128]{2,1,0:T(8,128)S(1)}, u32[]{:S(2)}, u32[]{:S(2)}) collective-permute-start(f32[64,8,128]{2,1,0:T(8,128)S(1)} %collective-permute-done.14.refs_2_), channel_id=1, source_target_pairs={{0,8},{8,0},{16,24},{24,16},{1,9},{9,1},{17,25},{25,17},{2,10},{10... | collective-permute-start | bytes 786440 | tf_op jit(solution)/shard_map/ppermute | solution.py:345

commit v15 on v14

--- a/solution.py
+++ b/solution.py
@@ -272,20 +272,19 @@
         size = 2 if length % 4 else 4
         return [(z, size) for z in range(0, length, size)]
 
-    for first in range(0, count, 2):
-        pair = (first, first + 1)
-        gains = [[taps_ref[group * pl.num_programs(0) + step, 0, t] for t in range(taps)] for group in pair]
-        for z, size in chunks(outer):
-            for group, gain in zip(pair, gains):
-                fields = chain(volume, gain, lefts_ref[group, 0, 0], rights_ref[group, 0, 0], z, size)
-                for i, blurred in enumerate(fields):
-                    guess = pl.reciprocal(blurred, approx=True)
-                    guess = guess * (2.0 - blurred * guess)
-                    ratios[group, z + i] = bricks[group][0, z + i].astype(jnp.float32) * guess
-        for z, size in chunks(planes):
+    gains = [[taps_ref[group * pl.num_programs(0) + step, 0, t] for t in range(taps)] for group in range(count)]
+    for z, size in chunks(outer):
+        for group, gain in enumerate(gains):
+            fields = chain(volume, gain, lefts_ref[group, 0, 0], rights_ref[group, 0, 0], z, size)
+            for i, blurred in enumerate(fields):
+                guess = pl.reciprocal(blurred, approx=True)
+                guess = guess * (2.0 - blurred * guess)
+                ratios[group, z + i] = bricks[group][0, z + i].astype(jnp.float32) * guess
+    for z, size in chunks(planes):
+        for first in range(0, count, 2):
             backs = [
-                chain(ratios.at[group], gain[::-1], lefts_ref[group, 0, 1], rights_ref[group, 0, 1], z, size)
-                for group, gain in zip(pair, gains)
+                chain(ratios.at[group], gains[group][::-1], lefts_ref[group, 0, 1], rights_ref[group, 0, 1], z, size)
+                for group in (first, first + 1)
             ]
             for i in range(size):
                 logs[z + i] += jnp.log(backs[0][i] * backs[1][i])

time: 96.1 us -> 96 us (level)
  no operation moved by 1% of the time
where the time goes in v15:
time: 96 us; the launch traced here: 95.7 us
  Pallas kernels  34.9 us (36%)
  waiting for transfers between devices  23.7 us (25%)
  blocking collectives  19.1 us (20%)
  starting transfers between devices  15.6 us (16%)
  local copies, waits for them, and re-layouts  1.92 us (2%)
    ppermute x13, waiting for transfers between devices, partner(): return lax.ppermute(value, 'view', [(i, i ^ bit) for i in range(members)])  23.7 us
    pallas_call x2, Pallas kernels, update(): pl.pallas_call(functools.partial(update_kernel, paired), grid=(count,), o...  22.7 us
    all_to_all x1, blocking collectives, per_device(): lax.all_to_all(joined, 'vol', split_axis=1, concat_axis=0, tiled=True)  19.1 us
    ppermute x13, starting transfers between devices, partner(): return lax.ppermute(value, 'view', [(i, i ^ bit) for i in range(members)])  13.5 us
    pallas_call x1, Pallas kernels, bands(): pl.pallas_call(bands_kernel, grid=(views,), out_shape=[jax.ShapeDtypeStru...  3.34 us
    pallas_call x1, Pallas kernels, resample_bound(): pl.pallas_call(bound_kernel, grid=(views,), out_shape=jax.ShapeDtypeStruc...  2.86 us
    pallas_call x2, Pallas kernels, gather_views(): pl.pallas_call(functools.partial(gather_kernel, views, planes, rim), grid...  2.6 us
    pallas_call x1, Pallas kernels, resample(): pl.pallas_call(functools.partial(resample_kernel, plan), grid=(views,), o...  2.34 us
  transfers between devices with their start and end apart: 16, of which 9 were waited for; matrix products, arithmetic and copies ran while one was open for 1% of the time, Pallas kernels for 10%

profile of v15, /device:TPU:0, one launch (start us, length us, event | category | flops | bytes accessed | tf_op | source)
XLA Modules:
  0.0 95.7 jit_solution(8233983741949109271)
XLA Ops:
  0.0 0.0 copy-start.2
  0.0 0.0 copy-start.1
  0.0 2.4 %collective-permute-start = (f32[3,3,9]{2,1,0:T(4,128)}, f32[3,3,9]{2,1,0:T(4,128)S(1)}, u32[]{:S(2)}, u32[]{:S(2)}) collective-permute-start(f32[3,3,9]{2,1,0:T(4,128)} %param.7), channel_id=1, source_target_pairs={{0,24},{8,16},{16,8},{24,0},{1,25},{9,17},{17,9},{25,1},{2,26},{10... | collective-permute-start | bytes 980 | tf_op jit(solution)/shard_map/ppermute | solution.py:344
  2.4 0.1 pad_add_fusion.place_ref
  2.5 0.0 copy-start.3
  2.5 2.9 %shard_map.46 = bf16[3,4,64,128]{3,2,1,0:T(8,128)(2,1)} custom-call(f32[3,8,64]{2,1,0:T(8,128)} %bitcast.24, s32[3,64]{1,0:T(4,128)} %offsets_ref.1, bf16[3,32,64,128]{3,2,1,0:T(8,128)(2,1)} %raw_ref), custom_call_target="tpu_custom_call" | custom-call | tf_op jit(solution)/shard_map/pallas_call | solution.py:74
  5.3 0.0 collective-permute-done
  5.3 0.9 collective-permute-start.2
  6.3 0.0 copy-done.2
  6.3 0.0 copy-done.1
  6.3 0.0 copy-start
  6.3 1.4 %copy-done = bf16[3,32,64,128]{3,2,1,0:T(8,128)(2,1)S(1)} copy-done((bf16[3,32,64,128]{3,2,1,0:T(8,128)(2,1)S(1)}, bf16[3,32,64,128]{3,2,1,0:T(8,128)(2,1)}, u32[]{:S(2)}) %copy-start) | copy-done | bytes 1572888
  7.7 2.3 %shard_map.47 = (bf16[3,16,64,128]{3,2,1,0:T(8,128)(2,1)S(1)}, bf16[3,4,64,128]{3,2,1,0:T(8,128)(2,1)S(1)}, bf16[3,16,64,128]{3,2,1,0:T(8,128)(2,1)S(1)}) custom-call(s32[2]{0:T(128)S(1)} %pad_add_fusion.place_ref, f32[3,8,64]{2,1,0:T(8,128)S(1)} %bitcast.25, s32[3,64]{1,0:T(4,128)S(1)} %copy-done.2, bf16[3,32,64,128]{3,2,1,0:T(8,128)(2,1)S(1)} %copy-done), custom_call_target="tpu_custom_call" | custom-call | tf_op jit(solution)/shard_map/pallas_call | solution.py:102
  10.0 0.0 copy-done.3
  10.0 0.1 collective-permute-start.1
  10.1 1.6 %collective-permute-start.4 = (bf16[3,16,64,128]{3,2,1,0:T(8,128)(2,1)S(1)}, bf16[3,16,64,128]{3,2,1,0:T(8,128)(2,1)S(1)}, u32[]{:S(2)}, u32[]{:S(2)}) collective-permute-start(bf16[3,16,64,128]{3,2,1,0:T(8,128)(2,1)S(1)} %get-tuple-element.37), channel_id=1, source_target_pairs={{0,16},{8,24},{16,0},{24,8},{1,17},{9,25},{17,1},{25,9},{2,18},{10... | collective-permute-start | bytes 2359304 | tf_op jit(solution)/shard_map/ppermute | solution.py:344
  11.8 0.0 collective-permute-start.5
  11.8 0.0 collective-permute-done.1
  11.8 0.1 fusion
  11.9 0.1 broadcast_divide_fusion
  12.0 1.1 %collective-permute-done.2 = bf16[3,4,64,128]{3,2,1,0:T(8,128)(2,1)S(1)} collective-permute-done((bf16[3,4,64,128]{3,2,1,0:T(8,128)(2,1)}, bf16[3,4,64,128]{3,2,1,0:T(8,128)(2,1)S(1)}, u32[]{:S(2)}, u32[]{:S(2)}) %collective-permute-start.2) | collective-permute-done | bytes 196640 | tf_op jit(solution)/shard_map/ppermute | solution.py:344
  13.1 0.7 collective-permute-start.3
  13.8 0.3 slice_reduce_fusion
  14.1 0.1 slice_divide_fusion
  14.2 3.3 %shard_map.48 = (bf16[12,2,64,192]{3,2,1,0:T(8,128)(2,1)S(1)}, bf16[12,2,128,256]{3,2,1,0:T(8,128)(2,1)S(1)}) custom-call(f32[12,3,9]{2,1,0:T(4,128)S(1)} %pad_maximum_fusion.1.taps_ref), custom_call_target="tpu_custom_call" | custom-call | tf_op jit(solution)/shard_map/pallas_call | solution.py:140
  17.6 0.1 collective-permute-start.6
  17.6 0.0 collective-permute-done.3.refs_4_.refs_5_
  17.7 0.5 collective-permute-start.7
  18.1 1.2 %collective-permute-done.6.refs_3_.refs_4_ = bf16[6,4,64,128]{3,2,1,0:T(8,128)(2,1)S(1)} collective-permute-done((bf16[6,4,64,128]{3,2,1,0:T(8,128)(2,1)S(1)}, bf16[6,4,64,128]{3,2,1,0:T(8,128)(2,1)S(1)}, u32[]{:S(2)}, u32[]{:S(2)}) %collective-permute-start.6) | collective-permute-done | bytes 393248 | tf_op jit(solution)/shard_map/ppermute | solution.py:344
  19.4 0.0 collective-permute-done.5.refs_1_
  19.4 0.6 collective-permute-done.7.refs_5_.refs_6_
  19.9 1.3 %shard_map.49 = (bf16[2,3,16,64,128]{4,3,2,1,0:T(8,128)(2,1)S(1)}, f32[16,64,128]{2,1,0:T(8,128)S(1)}) custom-call(s32[2]{0:T(128)S(1)} %pad_add_fusion.place_ref, bf16[3,16,64,128]{3,2,1,0:T(8,128)(2,1)S(1)} %get-tuple-element.38.refs_0_, bf16[3,16,64,128]{3,2,1,0:T(8,128)(2,1)S(1)} %collective-permute-done.5.refs_1_, ...), custom_call_target="tpu_custom_call" | custom-call | tf_op jit(solution)/shard_map/pallas_call | solution.py:207
  21.2 9.0 %collective-permute-done.4.refs_1_ = bf16[3,16,64,128]{3,2,1,0:T(8,128)(2,1)S(1)} collective-permute-done((bf16[3,16,64,128]{3,2,1,0:T(8,128)(2,1)S(1)}, bf16[3,16,64,128]{3,2,1,0:T(8,128)(2,1)S(1)}, u32[]{:S(2)}, u32[]{:S(2)}) %collective-permute-start.4) | collective-permute-done | bytes 786464 | tf_op jit(solution)/shard_map/ppermute | solution.py:344
  30.1 0.0 collective-permute-start.8
  30.2 2.3 %collective-permute-done.8.refs_2_ = bf16[3,16,64,128]{3,2,1,0:T(8,128)(2,1)S(1)} collective-permute-done((bf16[3,16,64,128]{3,2,1,0:T(8,128)(2,1)S(1)}, bf16[3,16,64,128]{3,2,1,0:T(8,128)(2,1)S(1)}, u32[]{:S(2)}, u32[]{:S(2)}) %collective-permute-start.8) | collective-permute-done | bytes 786464 | tf_op jit(solution)/shard_map/ppermute | solution.py:344
  32.4 1.3 %shard_map.50 = (bf16[2,3,16,64,128]{4,3,2,1,0:T(8,128)(2,1)S(1)}, f32[16,64,128]{2,1,0:T(8,128)S(1)}, f32[4,64,128]{2,1,0:T(8,128)S(1)}, f32[4,64,128]{2,1,0:T(8,128)S(1)}) custom-call(s32[2]{0:T(128)S(1)} %pad_add_fusion.place_ref, f32[16,64,128]{2,1,0:T(8,128)S(1)} %get-tuple-element.43.refs_0_, ...), custom_call_target="tpu_custom_call" | custom-call | tf_op jit(solution)/shard_map/pallas_call | solution.py:207
  33.8 0.2 collective-permute-start.9
  34.0 0.7 collective-permute-start.10
  34.6 0.5 collective-permute-done.9.refs_2_
  35.2 0.0 collective-permute-done.10.refs_4_
  35.2 11.3 %shard_map.51.refs_3_ = f32[8,64,128]{2,1,0:T(8,128)S(1)} custom-call(s32[2]{0:T(128)S(1)} %pad_add_fusion.place_ref, f32[12,3,9]{2,1,0:T(4,128)S(1)} %pad_maximum_fusion.1.taps_ref, bf16[4,3,2,64,192]{4,3,2,1,0:T(8,128)(2,1)S(1)} %bitcast.19, bf16[4,3,2,128,256]{4,3,2,1,0:T(8,128)(2,1)S(1)} %bitcast.17, ...), custom_call_target="tpu_custom_call" | custom-call | tf_op jit(solution)/shard_map/pallas_call | solution.py:303
  46.5 0.7 collective-permute-start.12
  47.2 7.6 %collective-permute-start.11 = (f32[8,64,128]{2,1,0:T(8,128)S(1)}, f32[8,64,128]{2,1,0:T(8,128)S(1)}, u32[]{:S(2)}, u32[]{:S(2)}) collective-permute-start(f32[8,64,128]{2,1,0:T(8,128)S(1)} %shard_map.51.refs_3_), channel_id=1, source_target_pairs={{0,8},{8,0},{16,24},{24,16},{1,9},{9,1},{17,25},{25,17},{2,10},{10... | collective-permute-start | bytes 786440 | tf_op jit(solution)/shard_map/ppermute | solution.py:344
  54.9 0.0 collective-permute-done.12.refs_4_
  54.9 1.2 %collective-permute-done.11.refs_2_ = f32[8,64,128]{2,1,0:T(8,128)S(1)} collective-permute-done((f32[8,64,128]{2,1,0:T(8,128)S(1)}, f32[8,64,128]{2,1,0:T(8,128)S(1)}, u32[]{:S(2)}, u32[]{:S(2)}) %collective-permute-start.11) | collective-permute-done | bytes 262176 | tf_op jit(solution)/shard_map/ppermute | solution.py:344
  56.0 11.3 %shard_map.52 = f32[8,64,128]{2,1,0:T(8,128)S(1)} custom-call(s32[2]{0:T(128)S(1)} %pad_add_fusion.place_ref, f32[12,3,9]{2,1,0:T(4,128)S(1)} %pad_maximum_fusion.1.taps_ref, bf16[4,3,2,64,192]{4,3,2,1,0:T(8,128)(2,1)S(1)} %bitcast.20, bf16[4,3,2,128,256]{4,3,2,1,0:T(8,128)(2,1)S(1)} %bitcast.18, bf16[2,3,16,64,128]{4,3,2,1,0:T(8,128)(2,1)S(1)} %get-tuple-element.42.refs_0_, ...), custom_call_target="tpu_custom_call" | custom-call | tf_op jit(solution)/shard_map/pallas_call | solution.py:303
  67.4 0.2 copy.7
  67.5 19.1 %all_to_all.18 = f32[8,64,128]{2,0,1:T(8,128)S(1)} all-to-all(f32[8,64,128]{2,0,1:T(8,128)S(1)} %copy.7), channel_id=1, replica_groups=mesh['view'=4,'vol'=8] {'vol'}, dimensions={1} | all-to-all | bytes 524288 | tf_op jit(solution)/shard_map/all_to_all | solution.py:435
  86.7 0.1 collective-permute-start.14
  86.8 0.1 collective-permute-start.13
  86.9 6.3 %collective-permute-done.14.refs_2_ = f32[64,8,128]{2,1,0:T(8,128)S(1)} collective-permute-done((f32[64,8,128]{2,1,0:T(8,128)S(1)}, f32[64,8,128]{2,1,0:T(8,128)S(1)}, u32[]{:S(2)}, u32[]{:S(2)}) %collective-permute-start.14) | collective-permute-done | bytes 262176 | tf_op jit(solution)/shard_map/ppermute | solution.py:344
  93.2 0.0 collective-permute-start.15
  93.2 0.0 collective-permute-done.13.refs_1_
  93.2 1.5 %collective-permute-done.15.refs_3_ = f32[64,8,128]{2,1,0:T(8,128)S(1)} collective-permute-done((f32[64,8,128]{2,1,0:T(8,128)S(1)}, f32[64,8,128]{2,1,0:T(8,128)S(1)}, u32[]{:S(2)}, u32[]{:S(2)}) %collective-permute-start.15) | collective-permute-done | bytes 262176 | tf_op jit(solution)/shard_map/ppermute | solution.py:344
  94.7 1.0 %shard_map.53 = f32[8,4,8,8,128]{4,3,2,1,0:T(8,128)} custom-call(s32[1]{0:T(128)} %bitcast.place_ref, f32[64,8,128]{2,1,0:T(8,128)S(1)} %bitcast.23, f32[64,8,128]{2,1,0:T(8,128)S(1)} %collective-permute-done.13.refs_1_, f32[64,8,128]{2,1,0:T(8,128)S(1)} %collective-permute-done.14.refs_2_, f32[64,8,128]{2,1,0:T(8,128)S(1)} %collective-permute-done.15.refs_3_), custom_call_target="tpu_custom_call" | custom-call | tf_op jit(solution)/shard_map/pallas_call | solution.py:334
  (6 shorter events, 0.1 us)
Async XLA Ops:
  0.0 6.3 %copy-start.2 = (s32[3,64]{1,0:T(4,128)S(1)}, s32[3,64]{1,0:T(4,128)}, u32[]{:S(2)}) copy-start(s32[3,64]{1,0:T(4,128)} %offsets_ref.1) | copy-start | bytes 2308
  0.0 6.3 %copy-start.1 = (f32[3,64,8]{1,2,0:T(8,128)S(1)}, f32[3,64,8]{1,2,0:T(8,128)}, u32[]{:S(2)}) copy-start(f32[3,64,8]{1,2,0:T(8,128)} %param.5) | copy-start | bytes 18436
  0.0 5.3 %collective-permute-start = (f32[3,3,9]{2,1,0:T(4,128)}, f32[3,3,9]{2,1,0:T(4,128)S(1)}, u32[]{:S(2)}, u32[]{:S(2)}) collective-permute-start(f32[3,3,9]{2,1,0:T(4,128)} %param.7), channel_id=1, source_target_pairs={{0,24},{8,16},{16,8},{24,0},{1,25},{9,17},{17,9},{25,1},{2,26},{10... | collective-permute-start | bytes 980 | tf_op jit(solution)/shard_map/ppermute | solution.py:344
  2.5 7.6 %copy-start.3 = (f32[3,3,9]{2,1,0:T(4,128)S(1)}, f32[3,3,9]{2,1,0:T(4,128)}, u32[]{:S(2)}) copy-start(f32[3,3,9]{2,1,0:T(4,128)} %param.7) | copy-start | bytes 976
  5.3 7.8 %collective-permute-start.2 = (bf16[3,4,64,128]{3,2,1,0:T(8,128)(2,1)}, bf16[3,4,64,128]{3,2,1,0:T(8,128)(2,1)S(1)}, u32[]{:S(2)}, u32[]{:S(2)}) collective-permute-start(bf16[3,4,64,128]{3,2,1,0:T(8,128)(2,1)} %shard_map.46), channel_id=1, source_target_pairs={{0,16},{8,24},{16,0},{24,8},{1,17},{9,25},{17,1},{25,9},{2,18},{10... | collective-permute-start | bytes 589832 | tf_op jit(solution)/shard_map/ppermute | solution.py:344
  6.3 1.4 %copy-start = (bf16[3,32,64,128]{3,2,1,0:T(8,128)(2,1)S(1)}, bf16[3,32,64,128]{3,2,1,0:T(8,128)(2,1)}, u32[]{:S(2)}) copy-start(bf16[3,32,64,128]{3,2,1,0:T(8,128)(2,1)} %raw_ref) | copy-start | bytes 4718596
  10.0 1.7 %collective-permute-start.1 = (f32[2,3,3,9]{3,2,1,0:T(4,128)S(1)}, f32[2,3,3,9]{3,2,1,0:T(4,128)S(1)}, u32[]{:S(2)}, u32[]{:S(2)}) collective-permute-start(f32[2,3,3,9]{3,2,1,0:T(4,128)S(1)} %pad_maximum_fusion.2), channel_id=1, source_target_pairs={{0,8},{8,0},{16,24},{24,16},{1,9},{9,1},{17,25},{25,17},{2,10},{10... | collective-permute-start | bytes 1952 | tf_op jit(solution)/shard_map/ppermute | solution.py:344
  10.1 20.0 %collective-permute-start.4 = (bf16[3,16,64,128]{3,2,1,0:T(8,128)(2,1)S(1)}, bf16[3,16,64,128]{3,2,1,0:T(8,128)(2,1)S(1)}, u32[]{:S(2)}, u32[]{:S(2)}) collective-permute-start(bf16[3,16,64,128]{3,2,1,0:T(8,128)(2,1)S(1)} %get-tuple-element.37), channel_id=1, source_target_pairs={{0,16},{8,24},{16,0},{24,8},{1,17},{9,25},{17,1},{25,9},{2,18},{10... | collective-permute-start | bytes 2359304 | tf_op jit(solution)/shard_map/ppermute | solution.py:344
  11.8 7.6 %collective-permute-start.5 = (bf16[3,16,64,128]{3,2,1,0:T(8,128)(2,1)S(1)}, bf16[3,16,64,128]{3,2,1,0:T(8,128)(2,1)S(1)}, u32[]{:S(2)}, u32[]{:S(2)}) collective-permute-start(bf16[3,16,64,128]{3,2,1,0:T(8,128)(2,1)S(1)} %get-tuple-element.38.refs_0_), channel_id=1, source_target_pairs={{0,8},{8,0},{16,24},{24,16},{1,9},{9,1},{17,25},{25,17},{2,10},{10... | collective-permute-start | bytes 2359304 | tf_op jit(solution)/shard_map/ppermute | solution.py:344
  13.1 4.5 %collective-permute-start.3 = (bf16[6,4,64,128]{3,2,1,0:T(8,128)(2,1)S(1)}, bf16[6,4,64,128]{3,2,1,0:T(8,128)(2,1)S(1)}, u32[]{:S(2)}, u32[]{:S(2)}) collective-permute-start(bf16[6,4,64,128]{3,2,1,0:T(8,128)(2,1)S(1)} %constant_dynamic-update-slice_fusion.refs_2_.refs_3_), channel_id=1, source_target_pairs={{24,25},{16,17},{1,2},{9,10},{26,27},{18,19},{3,4},{11,12},{28,29}... | collective-permute-start | bytes 1179656 | tf_op jit(solution)/shard_map/ppermute | solution.py:355
  17.6 1.8 %collective-permute-start.6 = (bf16[6,4,64,128]{3,2,1,0:T(8,128)(2,1)S(1)}, bf16[6,4,64,128]{3,2,1,0:T(8,128)(2,1)S(1)}, u32[]{:S(2)}, u32[]{:S(2)}) collective-permute-start(bf16[6,4,64,128]{3,2,1,0:T(8,128)(2,1)S(1)} %constant_dynamic-update-slice_fusion.refs_2_.refs_3_), channel_id=1, source_target_pairs={{0,8},{8,0},{16,24},{24,16},{1,9},{9,1},{17,25},{25,17},{2,10},{10... | collective-permute-start | bytes 1179656 | tf_op jit(solution)/shard_map/ppermute | solution.py:344
  17.7 2.3 %collective-permute-start.7 = (bf16[6,4,64,128]{3,2,1,0:T(8,128)(2,1)S(1)}, bf16[6,4,64,128]{3,2,1,0:T(8,128)(2,1)S(1)}, u32[]{:S(2)}, u32[]{:S(2)}) collective-permute-start(bf16[6,4,64,128]{3,2,1,0:T(8,128)(2,1)S(1)} %collective-permute-done.3.refs_4_.refs_5_), channel_id=1, source_target_pairs={{0,8},{8,0},{16,24},{24,16},{1,9},{9,1},{17,25},{25,17},{2,10},{10... | collective-permute-start | bytes 1179656 | tf_op jit(solution)/shard_map/ppermute | solution.py:344
  30.1 2.3 %collective-permute-start.8 = (bf16[3,16,64,128]{3,2,1,0:T(8,128)(2,1)S(1)}, bf16[3,16,64,128]{3,2,1,0:T(8,128)(2,1)S(1)}, u32[]{:S(2)}, u32[]{:S(2)}) collective-permute-start(bf16[3,16,64,128]{3,2,1,0:T(8,128)(2,1)S(1)} %collective-permute-done.4.refs_1_), channel_id=1, source_target_pairs={{0,8},{8,0},{16,24},{24,16},{1,9},{9,1},{17,25},{25,17},{2,10},{10... | collective-permute-start | bytes 2359304 | tf_op jit(solution)/shard_map/ppermute | solution.py:344
  33.8 1.4 %collective-permute-start.9 = (f32[4,64,128]{2,1,0:T(8,128)S(1)}, f32[4,64,128]{2,1,0:T(8,128)S(1)}, u32[]{:S(2)}, u32[]{:S(2)}) collective-permute-start(f32[4,64,128]{2,1,0:T(8,128)S(1)} %get-tuple-element.46), channel_id=1, source_target_pairs={{0,8},{8,0},{16,24},{24,16},{1,9},{9,1},{17,25},{25,17},{2,10},{10... | collective-permute-start | bytes 393224 | tf_op jit(solution)/shard_map/ppermute | solution.py:344
  34.0 1.2 %collective-permute-start.10 = (f32[4,64,128]{2,1,0:T(8,128)S(1)}, f32[4,64,128]{2,1,0:T(8,128)S(1)}, u32[]{:S(2)}, u32[]{:S(2)}) collective-permute-start(f32[4,64,128]{2,1,0:T(8,128)S(1)} %get-tuple-element.48), channel_id=1, source_target_pairs={{8,16},{24,25},{17,9},{1,2},{10,18},{26,27},{19,11},{3,4},{12,20},... | collective-permute-start | bytes 393224 | tf_op jit(solution)/shard_map/ppermute | solution.py:355
  46.5 8.3 %collective-permute-start.12 = (f32[8,64,128]{2,1,0:T(8,128)S(1)}, f32[8,64,128]{2,1,0:T(8,128)S(1)}, u32[]{:S(2)}, u32[]{:S(2)}) collective-permute-start(f32[8,64,128]{2,1,0:T(8,128)S(1)} %shard_map.51.refs_3_), channel_id=1, source_target_pairs={{8,16},{24,25},{17,9},{1,2},{10,18},{26,27},{19,11},{3,4},{12,20},... | collective-permute-start | bytes 786440 | tf_op jit(solution)/shard_map/ppermute | solution.py:355
  47.2 8.8 %collective-permute-start.11 = (f32[8,64,128]{2,1,0:T(8,128)S(1)}, f32[8,64,128]{2,1,0:T(8,128)S(1)}, u32[]{:S(2)}, u32[]{:S(2)}) collective-permute-start(f32[8,64,128]{2,1,0:T(8,128)S(1)} %shard_map.51.refs_3_), channel_id=1, source_target_pairs={{0,8},{8,0},{16,24},{24,16},{1,9},{9,1},{17,25},{25,17},{2,10},{10... | collective-permute-start | bytes 786440 | tf_op jit(solution)/shard_map/ppermute | solution.py:344
  86.7 6.4 %collective-permute-start.14 = (f32[64,8,128]{2,1,0:T(8,128)S(1)}, f32[64,8,128]{2,1,0:T(8,128)S(1)}, u32[]{:S(2)}, u32[]{:S(2)}) collective-permute-start(f32[64,8,128]{2,1,0:T(8,128)S(1)} %bitcast.21), channel_id=1, source_target_pairs={{0,16},{8,24},{16,0},{24,8},{1,17},{9,25},{17,1},{25,9},{2,18},{10... | collective-permute-start | bytes 786440 | tf_op jit(solution)/shard_map/ppermute | solution.py:344
  86.8 6.4 %collective-permute-start.13 = (f32[64,8,128]{2,1,0:T(8,128)S(1)}, f32[64,8,128]{2,1,0:T(8,128)S(1)}, u32[]{:S(2)}, u32[]{:S(2)}) collective-permute-start(f32[64,8,128]{2,1,0:T(8,128)S(1)} %bitcast.22), channel_id=1, source_target_pairs={{0,8},{8,0},{16,24},{24,16},{1,9},{9,1},{17,25},{25,17},{2,10},{10... | collective-permute-start | bytes 786440 | tf_op jit(solution)/shard_map/ppermute | solution.py:344
  93.2 1.5 %collective-permute-start.15 = (f32[64,8,128]{2,1,0:T(8,128)S(1)}, f32[64,8,128]{2,1,0:T(8,128)S(1)}, u32[]{:S(2)}, u32[]{:S(2)}) collective-permute-start(f32[64,8,128]{2,1,0:T(8,128)S(1)} %collective-permute-done.14.refs_2_), channel_id=1, source_target_pairs={{0,8},{8,0},{16,24},{24,16},{1,9},{9,1},{17,25},{25,17},{2,10},{10... | collective-permute-start | bytes 786440 | tf_op jit(solution)/shard_map/ppermute | solution.py:344

commit v16 on v14

--- a/solution.py
+++ b/solution.py
@@ -269,7 +269,7 @@
         return [total[i * rows : (i + 1) * rows] for i in range(length)]
 
     def chunks(length):
-        size = 2 if length % 4 else 4
+        size = next(size for size in (8, 4, 2) if length % size == 0 and length > size or size == 2)
         return [(z, size) for z in range(0, length, size)]
 
     for first in range(0, count, 2):

time: 96.1 us -> 96.6 us (level)
  no operation moved by 1% of the time
where the time goes in v16:
time: 96.6 us; the launch traced here: 96.3 us
  Pallas kernels  35.5 us (37%)
  waiting for transfers between devices  23.7 us (25%)
  blocking collectives  19.1 us (20%)
  starting transfers between devices  15.6 us (16%)
  local copies, waits for them, and re-layouts  1.92 us (2%)
    ppermute x13, waiting for transfers between devices, partner(): return lax.ppermute(value, 'view', [(i, i ^ bit) for i in range(members)])  23.7 us
    pallas_call x2, Pallas kernels, update(): pl.pallas_call(functools.partial(update_kernel, paired), grid=(count,), o...  23.3 us
    all_to_all x1, blocking collectives, per_device(): lax.all_to_all(joined, 'vol', split_axis=1, concat_axis=0, tiled=True)  19.1 us
    ppermute x13, starting transfers between devices, partner(): return lax.ppermute(value, 'view', [(i, i ^ bit) for i in range(members)])  13.5 us
    pallas_call x1, Pallas kernels, bands(): pl.pallas_call(bands_kernel, grid=(views,), out_shape=[jax.ShapeDtypeStru...  3.34 us
    pallas_call x1, Pallas kernels, resample_bound(): pl.pallas_call(bound_kernel, grid=(views,), out_shape=jax.ShapeDtypeStruc...  2.86 us
    pallas_call x2, Pallas kernels, gather_views(): pl.pallas_call(functools.partial(gather_kernel, views, planes, rim), grid...  2.6 us
    pallas_call x1, Pallas kernels, resample(): pl.pallas_call(functools.partial(resample_kernel, plan), grid=(views,), o...  2.34 us
  transfers between devices with their start and end apart: 16, of which 9 were waited for; matrix products, arithmetic and copies ran while one was open for 1% of the time, Pallas kernels for 10%

profile of v16, /device:TPU:0, one launch (start us, length us, event | category | flops | bytes accessed | tf_op | source)
XLA Modules:
  0.0 96.3 jit_solution(17083847078132029494)
XLA Ops:
  0.0 0.0 copy-start.2
  0.0 0.0 copy-start.1
  0.0 2.4 %collective-permute-start = (f32[3,3,9]{2,1,0:T(4,128)}, f32[3,3,9]{2,1,0:T(4,128)S(1)}, u32[]{:S(2)}, u32[]{:S(2)}) collective-permute-start(f32[3,3,9]{2,1,0:T(4,128)} %param.7), channel_id=1, source_target_pairs={{0,24},{8,16},{16,8},{24,0},{1,25},{9,17},{17,9},{25,1},{2,26},{10... | collective-permute-start | bytes 980 | tf_op jit(solution)/shard_map/ppermute | solution.py:345
  2.4 0.1 pad_add_fusion.place_ref
  2.5 0.0 copy-start.3
  2.5 2.9 %shard_map.46 = bf16[3,4,64,128]{3,2,1,0:T(8,128)(2,1)} custom-call(f32[3,8,64]{2,1,0:T(8,128)} %bitcast.24, s32[3,64]{1,0:T(4,128)} %offsets_ref.1, bf16[3,32,64,128]{3,2,1,0:T(8,128)(2,1)} %raw_ref), custom_call_target="tpu_custom_call" | custom-call | tf_op jit(solution)/shard_map/pallas_call | solution.py:74
  5.3 0.0 collective-permute-done
  5.3 0.9 collective-permute-start.2
  6.3 0.0 copy-done.2
  6.3 0.0 copy-done.1
  6.3 0.0 copy-start
  6.3 1.4 %copy-done = bf16[3,32,64,128]{3,2,1,0:T(8,128)(2,1)S(1)} copy-done((bf16[3,32,64,128]{3,2,1,0:T(8,128)(2,1)S(1)}, bf16[3,32,64,128]{3,2,1,0:T(8,128)(2,1)}, u32[]{:S(2)}) %copy-start) | copy-done | bytes 1572888
  7.7 2.3 %shard_map.47 = (bf16[3,16,64,128]{3,2,1,0:T(8,128)(2,1)S(1)}, bf16[3,4,64,128]{3,2,1,0:T(8,128)(2,1)S(1)}, bf16[3,16,64,128]{3,2,1,0:T(8,128)(2,1)S(1)}) custom-call(s32[2]{0:T(128)S(1)} %pad_add_fusion.place_ref, f32[3,8,64]{2,1,0:T(8,128)S(1)} %bitcast.25, s32[3,64]{1,0:T(4,128)S(1)} %copy-done.2, bf16[3,32,64,128]{3,2,1,0:T(8,128)(2,1)S(1)} %copy-done), custom_call_target="tpu_custom_call" | custom-call | tf_op jit(solution)/shard_map/pallas_call | solution.py:102
  10.0 0.0 copy-done.3
  10.0 0.1 collective-permute-start.1
  10.1 1.6 %collective-permute-start.4 = (bf16[3,16,64,128]{3,2,1,0:T(8,128)(2,1)S(1)}, bf16[3,16,64,128]{3,2,1,0:T(8,128)(2,1)S(1)}, u32[]{:S(2)}, u32[]{:S(2)}) collective-permute-start(bf16[3,16,64,128]{3,2,1,0:T(8,128)(2,1)S(1)} %get-tuple-element.37), channel_id=1, source_target_pairs={{0,16},{8,24},{16,0},{24,8},{1,17},{9,25},{17,1},{25,9},{2,18},{10... | collective-permute-start | bytes 2359304 | tf_op jit(solution)/shard_map/ppermute | solution.py:345
  11.8 0.0 collective-permute-start.5
  11.8 0.0 collective-permute-done.1
  11.8 0.1 fusion
  11.9 0.1 broadcast_divide_fusion
  12.0 1.1 %collective-permute-done.2 = bf16[3,4,64,128]{3,2,1,0:T(8,128)(2,1)S(1)} collective-permute-done((bf16[3,4,64,128]{3,2,1,0:T(8,128)(2,1)}, bf16[3,4,64,128]{3,2,1,0:T(8,128)(2,1)S(1)}, u32[]{:S(2)}, u32[]{:S(2)}) %collective-permute-start.2) | collective-permute-done | bytes 196640 | tf_op jit(solution)/shard_map/ppermute | solution.py:345
  13.1 0.7 collective-permute-start.3
  13.8 0.3 slice_reduce_fusion
  14.1 0.1 slice_divide_fusion
  14.2 3.3 %shard_map.48 = (bf16[12,2,64,192]{3,2,1,0:T(8,128)(2,1)S(1)}, bf16[12,2,128,256]{3,2,1,0:T(8,128)(2,1)S(1)}) custom-call(f32[12,3,9]{2,1,0:T(4,128)S(1)} %pad_maximum_fusion.1.taps_ref), custom_call_target="tpu_custom_call" | custom-call | tf_op jit(solution)/shard_map/pallas_call | solution.py:140
  17.6 0.1 collective-permute-start.6
  17.6 0.0 collective-permute-done.3.refs_4_.refs_5_
  17.7 0.5 collective-permute-start.7
  18.1 1.2 %collective-permute-done.6.refs_3_.refs_4_ = bf16[6,4,64,128]{3,2,1,0:T(8,128)(2,1)S(1)} collective-permute-done((bf16[6,4,64,128]{3,2,1,0:T(8,128)(2,1)S(1)}, bf16[6,4,64,128]{3,2,1,0:T(8,128)(2,1)S(1)}, u32[]{:S(2)}, u32[]{:S(2)}) %collective-permute-start.6) | collective-permute-done | bytes 393248 | tf_op jit(solution)/shard_map/ppermute | solution.py:345
  19.4 0.0 collective-permute-done.5.refs_1_
  19.4 0.6 collective-permute-done.7.refs_5_.refs_6_
  19.9 1.3 %shard_map.49 = (bf16[2,3,16,64,128]{4,3,2,1,0:T(8,128)(2,1)S(1)}, f32[16,64,128]{2,1,0:T(8,128)S(1)}) custom-call(s32[2]{0:T(128)S(1)} %pad_add_fusion.place_ref, bf16[3,16,64,128]{3,2,1,0:T(8,128)(2,1)S(1)} %get-tuple-element.38.refs_0_, bf16[3,16,64,128]{3,2,1,0:T(8,128)(2,1)S(1)} %collective-permute-done.5.refs_1_, ...), custom_call_target="tpu_custom_call" | custom-call | tf_op jit(solution)/shard_map/pallas_call | solution.py:207
  21.2 9.0 %collective-permute-done.4.refs_1_ = bf16[3,16,64,128]{3,2,1,0:T(8,128)(2,1)S(1)} collective-permute-done((bf16[3,16,64,128]{3,2,1,0:T(8,128)(2,1)S(1)}, bf16[3,16,64,128]{3,2,1,0:T(8,128)(2,1)S(1)}, u32[]{:S(2)}, u32[]{:S(2)}) %collective-permute-start.4) | collective-permute-done | bytes 786464 | tf_op jit(solution)/shard_map/ppermute | solution.py:345
  30.1 0.0 collective-permute-start.8
  30.2 2.3 %collective-permute-done.8.refs_2_ = bf16[3,16,64,128]{3,2,1,0:T(8,128)(2,1)S(1)} collective-permute-done((bf16[3,16,64,128]{3,2,1,0:T(8,128)(2,1)S(1)}, bf16[3,16,64,128]{3,2,1,0:T(8,128)(2,1)S(1)}, u32[]{:S(2)}, u32[]{:S(2)}) %collective-permute-start.8) | collective-permute-done | bytes 786464 | tf_op jit(solution)/shard_map/ppermute | solution.py:345
  32.4 1.3 %shard_map.50 = (bf16[2,3,16,64,128]{4,3,2,1,0:T(8,128)(2,1)S(1)}, f32[16,64,128]{2,1,0:T(8,128)S(1)}, f32[4,64,128]{2,1,0:T(8,128)S(1)}, f32[4,64,128]{2,1,0:T(8,128)S(1)}) custom-call(s32[2]{0:T(128)S(1)} %pad_add_fusion.place_ref, f32[16,64,128]{2,1,0:T(8,128)S(1)} %get-tuple-element.43.refs_0_, ...), custom_call_target="tpu_custom_call" | custom-call | tf_op jit(solution)/shard_map/pallas_call | solution.py:207
  33.8 0.2 collective-permute-start.9
  34.0 0.7 collective-permute-start.10
  34.6 0.5 collective-permute-done.9.refs_2_
  35.2 0.0 collective-permute-done.10.refs_4_
  35.2 11.6 %shard_map.51.refs_3_ = f32[8,64,128]{2,1,0:T(8,128)S(1)} custom-call(s32[2]{0:T(128)S(1)} %pad_add_fusion.place_ref, f32[12,3,9]{2,1,0:T(4,128)S(1)} %pad_maximum_fusion.1.taps_ref, bf16[4,3,2,64,192]{4,3,2,1,0:T(8,128)(2,1)S(1)} %bitcast.19, bf16[4,3,2,128,256]{4,3,2,1,0:T(8,128)(2,1)S(1)} %bitcast.17, ...), custom_call_target="tpu_custom_call" | custom-call | tf_op jit(solution)/shard_map/pallas_call | solution.py:304
  46.9 0.7 collective-permute-start.12
  47.5 7.6 %collective-permute-start.11 = (f32[8,64,128]{2,1,0:T(8,128)S(1)}, f32[8,64,128]{2,1,0:T(8,128)S(1)}, u32[]{:S(2)}, u32[]{:S(2)}) collective-permute-start(f32[8,64,128]{2,1,0:T(8,128)S(1)} %shard_map.51.refs_3_), channel_id=1, source_target_pairs={{0,8},{8,0},{16,24},{24,16},{1,9},{9,1},{17,25},{25,17},{2,10},{10... | collective-permute-start | bytes 786440 | tf_op jit(solution)/shard_map/ppermute | solution.py:345
  55.2 0.0 collective-permute-done.12.refs_4_
  55.2 1.2 %collective-permute-done.11.refs_2_ = f32[8,64,128]{2,1,0:T(8,128)S(1)} collective-permute-done((f32[8,64,128]{2,1,0:T(8,128)S(1)}, f32[8,64,128]{2,1,0:T(8,128)S(1)}, u32[]{:S(2)}, u32[]{:S(2)}) %collective-permute-start.11) | collective-permute-done | bytes 262176 | tf_op jit(solution)/shard_map/ppermute | solution.py:345
  56.3 11.6 %shard_map.52 = f32[8,64,128]{2,1,0:T(8,128)S(1)} custom-call(s32[2]{0:T(128)S(1)} %pad_add_fusion.place_ref, f32[12,3,9]{2,1,0:T(4,128)S(1)} %pad_maximum_fusion.1.taps_ref, bf16[4,3,2,64,192]{4,3,2,1,0:T(8,128)(2,1)S(1)} %bitcast.20, bf16[4,3,2,128,256]{4,3,2,1,0:T(8,128)(2,1)S(1)} %bitcast.18, bf16[2,3,16,64,128]{4,3,2,1,0:T(8,128)(2,1)S(1)} %get-tuple-element.42.refs_0_, ...), custom_call_target="tpu_custom_call" | custom-call | tf_op jit(solution)/shard_map/pallas_call | solution.py:304
  68.0 0.2 copy.7
  68.2 19.1 %all_to_all.18 = f32[8,64,128]{2,0,1:T(8,128)S(1)} all-to-all(f32[8,64,128]{2,0,1:T(8,128)S(1)} %copy.7), channel_id=1, replica_groups=mesh['view'=4,'vol'=8] {'vol'}, dimensions={1} | all-to-all | bytes 524288 | tf_op jit(solution)/shard_map/all_to_all | solution.py:436
  87.3 0.1 collective-permute-start.14
  87.4 0.1 collective-permute-start.13
  87.5 6.3 %collective-permute-done.14.refs_2_ = f32[64,8,128]{2,1,0:T(8,128)S(1)} collective-permute-done((f32[64,8,128]{2,1,0:T(8,128)S(1)}, f32[64,8,128]{2,1,0:T(8,128)S(1)}, u32[]{:S(2)}, u32[]{:S(2)}) %collective-permute-start.14) | collective-permute-done | bytes 262176 | tf_op jit(solution)/shard_map/ppermute | solution.py:345
  93.8 0.0 collective-permute-start.15
  93.8 0.0 collective-permute-done.13.refs_1_
  93.8 1.5 %collective-permute-done.15.refs_3_ = f32[64,8,128]{2,1,0:T(8,128)S(1)} collective-permute-done((f32[64,8,128]{2,1,0:T(8,128)S(1)}, f32[64,8,128]{2,1,0:T(8,128)S(1)}, u32[]{:S(2)}, u32[]{:S(2)}) %collective-permute-start.15) | collective-permute-done | bytes 262176 | tf_op jit(solution)/shard_map/ppermute | solution.py:345
  95.3 1.0 %shard_map.53 = f32[8,4,8,8,128]{4,3,2,1,0:T(8,128)} custom-call(s32[1]{0:T(128)} %bitcast.place_ref, f32[64,8,128]{2,1,0:T(8,128)S(1)} %bitcast.23, f32[64,8,128]{2,1,0:T(8,128)S(1)} %collective-permute-done.13.refs_1_, f32[64,8,128]{2,1,0:T(8,128)S(1)} %collective-permute-done.14.refs_2_, f32[64,8,128]{2,1,0:T(8,128)S(1)} %collective-permute-done.15.refs_3_), custom_call_target="tpu_custom_call" | custom-call | tf_op jit(solution)/shard_map/pallas_call | solution.py:335
  (6 shorter events, 0.1 us)
Async XLA Ops:
  0.0 6.3 %copy-start.2 = (s32[3,64]{1,0:T(4,128)S(1)}, s32[3,64]{1,0:T(4,128)}, u32[]{:S(2)}) copy-start(s32[3,64]{1,0:T(4,128)} %offsets_ref.1) | copy-start | bytes 2308
  0.0 6.3 %copy-start.1 = (f32[3,64,8]{1,2,0:T(8,128)S(1)}, f32[3,64,8]{1,2,0:T(8,128)}, u32[]{:S(2)}) copy-start(f32[3,64,8]{1,2,0:T(8,128)} %param.5) | copy-start | bytes 18436
  0.0 5.3 %collective-permute-start = (f32[3,3,9]{2,1,0:T(4,128)}, f32[3,3,9]{2,1,0:T(4,128)S(1)}, u32[]{:S(2)}, u32[]{:S(2)}) collective-permute-start(f32[3,3,9]{2,1,0:T(4,128)} %param.7), channel_id=1, source_target_pairs={{0,24},{8,16},{16,8},{24,0},{1,25},{9,17},{17,9},{25,1},{2,26},{10... | collective-permute-start | bytes 980 | tf_op jit(solution)/shard_map/ppermute | solution.py:345
  2.5 7.6 %copy-start.3 = (f32[3,3,9]{2,1,0:T(4,128)S(1)}, f32[3,3,9]{2,1,0:T(4,128)}, u32[]{:S(2)}) copy-start(f32[3,3,9]{2,1,0:T(4,128)} %param.7) | copy-start | bytes 976
  5.3 7.8 %collective-permute-start.2 = (bf16[3,4,64,128]{3,2,1,0:T(8,128)(2,1)}, bf16[3,4,64,128]{3,2,1,0:T(8,128)(2,1)S(1)}, u32[]{:S(2)}, u32[]{:S(2)}) collective-permute-start(bf16[3,4,64,128]{3,2,1,0:T(8,128)(2,1)} %shard_map.46), channel_id=1, source_target_pairs={{0,16},{8,24},{16,0},{24,8},{1,17},{9,25},{17,1},{25,9},{2,18},{10... | collective-permute-start | bytes 589832 | tf_op jit(solution)/shard_map/ppermute | solution.py:345
  6.3 1.4 %copy-start = (bf16[3,32,64,128]{3,2,1,0:T(8,128)(2,1)S(1)}, bf16[3,32,64,128]{3,2,1,0:T(8,128)(2,1)}, u32[]{:S(2)}) copy-start(bf16[3,32,64,128]{3,2,1,0:T(8,128)(2,1)} %raw_ref) | copy-start | bytes 4718596
  10.0 1.7 %collective-permute-start.1 = (f32[2,3,3,9]{3,2,1,0:T(4,128)S(1)}, f32[2,3,3,9]{3,2,1,0:T(4,128)S(1)}, u32[]{:S(2)}, u32[]{:S(2)}) collective-permute-start(f32[2,3,3,9]{3,2,1,0:T(4,128)S(1)} %pad_maximum_fusion.2), channel_id=1, source_target_pairs={{0,8},{8,0},{16,24},{24,16},{1,9},{9,1},{17,25},{25,17},{2,10},{10... | collective-permute-start | bytes 1952 | tf_op jit(solution)/shard_map/ppermute | solution.py:345
  10.1 20.0 %collective-permute-start.4 = (bf16[3,16,64,128]{3,2,1,0:T(8,128)(2,1)S(1)}, bf16[3,16,64,128]{3,2,1,0:T(8,128)(2,1)S(1)}, u32[]{:S(2)}, u32[]{:S(2)}) collective-permute-start(bf16[3,16,64,128]{3,2,1,0:T(8,128)(2,1)S(1)} %get-tuple-element.37), channel_id=1, source_target_pairs={{0,16},{8,24},{16,0},{24,8},{1,17},{9,25},{17,1},{25,9},{2,18},{10... | collective-permute-start | bytes 2359304 | tf_op jit(solution)/shard_map/ppermute | solution.py:345
  11.8 7.6 %collective-permute-start.5 = (bf16[3,16,64,128]{3,2,1,0:T(8,128)(2,1)S(1)}, bf16[3,16,64,128]{3,2,1,0:T(8,128)(2,1)S(1)}, u32[]{:S(2)}, u32[]{:S(2)}) collective-permute-start(bf16[3,16,64,128]{3,2,1,0:T(8,128)(2,1)S(1)} %get-tuple-element.38.refs_0_), channel_id=1, source_target_pairs={{0,8},{8,0},{16,24},{24,16},{1,9},{9,1},{17,25},{25,17},{2,10},{10... | collective-permute-start | bytes 2359304 | tf_op jit(solution)/shard_map/ppermute | solution.py:345
  13.1 4.5 %collective-permute-start.3 = (bf16[6,4,64,128]{3,2,1,0:T(8,128)(2,1)S(1)}, bf16[6,4,64,128]{3,2,1,0:T(8,128)(2,1)S(1)}, u32[]{:S(2)}, u32[]{:S(2)}) collective-permute-start(bf16[6,4,64,128]{3,2,1,0:T(8,128)(2,1)S(1)} %constant_dynamic-update-slice_fusion.refs_2_.refs_3_), channel_id=1, source_target_pairs={{24,25},{16,17},{1,2},{9,10},{26,27},{18,19},{3,4},{11,12},{28,29}... | collective-permute-start | bytes 1179656 | tf_op jit(solution)/shard_map/ppermute | solution.py:356
  17.6 1.8 %collective-permute-start.6 = (bf16[6,4,64,128]{3,2,1,0:T(8,128)(2,1)S(1)}, bf16[6,4,64,128]{3,2,1,0:T(8,128)(2,1)S(1)}, u32[]{:S(2)}, u32[]{:S(2)}) collective-permute-start(bf16[6,4,64,128]{3,2,1,0:T(8,128)(2,1)S(1)} %constant_dynamic-update-slice_fusion.refs_2_.refs_3_), channel_id=1, source_target_pairs={{0,8},{8,0},{16,24},{24,16},{1,9},{9,1},{17,25},{25,17},{2,10},{10... | collective-permute-start | bytes 1179656 | tf_op jit(solution)/shard_map/ppermute | solution.py:345
  17.7 2.3 %collective-permute-start.7 = (bf16[6,4,64,128]{3,2,1,0:T(8,128)(2,1)S(1)}, bf16[6,4,64,128]{3,2,1,0:T(8,128)(2,1)S(1)}, u32[]{:S(2)}, u32[]{:S(2)}) collective-permute-start(bf16[6,4,64,128]{3,2,1,0:T(8,128)(2,1)S(1)} %collective-permute-done.3.refs_4_.refs_5_), channel_id=1, source_target_pairs={{0,8},{8,0},{16,24},{24,16},{1,9},{9,1},{17,25},{25,17},{2,10},{10... | collective-permute-start | bytes 1179656 | tf_op jit(solution)/shard_map/ppermute | solution.py:345
  30.1 2.3 %collective-permute-start.8 = (bf16[3,16,64,128]{3,2,1,0:T(8,128)(2,1)S(1)}, bf16[3,16,64,128]{3,2,1,0:T(8,128)(2,1)S(1)}, u32[]{:S(2)}, u32[]{:S(2)}) collective-permute-start(bf16[3,16,64,128]{3,2,1,0:T(8,128)(2,1)S(1)} %collective-permute-done.4.refs_1_), channel_id=1, source_target_pairs={{0,8},{8,0},{16,24},{24,16},{1,9},{9,1},{17,25},{25,17},{2,10},{10... | collective-permute-start | bytes 2359304 | tf_op jit(solution)/shard_map/ppermute | solution.py:345
  33.8 1.4 %collective-permute-start.9 = (f32[4,64,128]{2,1,0:T(8,128)S(1)}, f32[4,64,128]{2,1,0:T(8,128)S(1)}, u32[]{:S(2)}, u32[]{:S(2)}) collective-permute-start(f32[4,64,128]{2,1,0:T(8,128)S(1)} %get-tuple-element.46), channel_id=1, source_target_pairs={{0,8},{8,0},{16,24},{24,16},{1,9},{9,1},{17,25},{25,17},{2,10},{10... | collective-permute-start | bytes 393224 | tf_op jit(solution)/shard_map/ppermute | solution.py:345
  34.0 1.2 %collective-permute-start.10 = (f32[4,64,128]{2,1,0:T(8,128)S(1)}, f32[4,64,128]{2,1,0:T(8,128)S(1)}, u32[]{:S(2)}, u32[]{:S(2)}) collective-permute-start(f32[4,64,128]{2,1,0:T(8,128)S(1)} %get-tuple-element.48), channel_id=1, source_target_pairs={{8,16},{24,25},{17,9},{1,2},{10,18},{26,27},{19,11},{3,4},{12,20},... | collective-permute-start | bytes 393224 | tf_op jit(solution)/shard_map/ppermute | solution.py:356
  46.9 8.3 %collective-permute-start.12 = (f32[8,64,128]{2,1,0:T(8,128)S(1)}, f32[8,64,128]{2,1,0:T(8,128)S(1)}, u32[]{:S(2)}, u32[]{:S(2)}) collective-permute-start(f32[8,64,128]{2,1,0:T(8,128)S(1)} %shard_map.51.refs_3_), channel_id=1, source_target_pairs={{8,16},{24,25},{17,9},{1,2},{10,18},{26,27},{19,11},{3,4},{12,20},... | collective-permute-start | bytes 786440 | tf_op jit(solution)/shard_map/ppermute | solution.py:356
  47.5 8.8 %collective-permute-start.11 = (f32[8,64,128]{2,1,0:T(8,128)S(1)}, f32[8,64,128]{2,1,0:T(8,128)S(1)}, u32[]{:S(2)}, u32[]{:S(2)}) collective-permute-start(f32[8,64,128]{2,1,0:T(8,128)S(1)} %shard_map.51.refs_3_), channel_id=1, source_target_pairs={{0,8},{8,0},{16,24},{24,16},{1,9},{9,1},{17,25},{25,17},{2,10},{10... | collective-permute-start | bytes 786440 | tf_op jit(solution)/shard_map/ppermute | solution.py:345
  87.3 6.4 %collective-permute-start.14 = (f32[64,8,128]{2,1,0:T(8,128)S(1)}, f32[64,8,128]{2,1,0:T(8,128)S(1)}, u32[]{:S(2)}, u32[]{:S(2)}) collective-permute-start(f32[64,8,128]{2,1,0:T(8,128)S(1)} %bitcast.21), channel_id=1, source_target_pairs={{0,16},{8,24},{16,0},{24,8},{1,17},{9,25},{17,1},{25,9},{2,18},{10... | collective-permute-start | bytes 786440 | tf_op jit(solution)/shard_map/ppermute | solution.py:345
  87.4 6.4 %collective-permute-start.13 = (f32[64,8,128]{2,1,0:T(8,128)S(1)}, f32[64,8,128]{2,1,0:T(8,128)S(1)}, u32[]{:S(2)}, u32[]{:S(2)}) collective-permute-start(f32[64,8,128]{2,1,0:T(8,128)S(1)} %bitcast.22), channel_id=1, source_target_pairs={{0,8},{8,0},{16,24},{24,16},{1,9},{9,1},{17,25},{25,17},{2,10},{10... | collective-permute-start | bytes 786440 | tf_op jit(solution)/shard_map/ppermute | solution.py:345
  93.8 1.5 %collective-permute-start.15 = (f32[64,8,128]{2,1,0:T(8,128)S(1)}, f32[64,8,128]{2,1,0:T(8,128)S(1)}, u32[]{:S(2)}, u32[]{:S(2)}) collective-permute-start(f32[64,8,128]{2,1,0:T(8,128)S(1)} %collective-permute-done.14.refs_2_), channel_id=1, source_target_pairs={{0,8},{8,0},{16,24},{24,16},{1,9},{9,1},{17,25},{25,17},{2,10},{10... | collective-permute-start | bytes 786440 | tf_op jit(solution)/shard_map/ppermute | solution.py:345
